TPU v7x, 32 devices: a whole 2x2x4 slice. The times are simulated.
32 devices in a mesh: ep: 8 (over z, x), tp: 4 (over y, core).
Axes of the slice: x: 2, y: 2, z: 4, core: 2. Of those that a mesh axis runs over, the one named last changes fastest.
Arguments:
- resid: bfloat16 [2048, 1536], P('ep'), may hold values from -6 to 6
- context: bfloat16 [2048, 1536], P('ep', 'tp'), may hold values from -6 to 6
- w_out: bfloat16 [1536, 1536], P('tp'), may hold values from -0.15625 to 0.15625
- pre_gain: bfloat16 [1536], replicated, may hold values from 0.5 to 1.5
- final_gain: bfloat16 [1536], replicated, may hold values from 0.5 to 1.5
- w_router: bfloat16 [1536, 40], replicated, may hold values from -0.03491211 to 0.03491211
- expert_ids: int32 [2048, 8], P('ep'), may hold values from 0 to 39, all different within a row; in each aligned block of 256 rows (0 to 255, 256 to 511, ...) at most 80 rows name the same one
- slot_expert: int32 [40], replicated, may hold values from 0 to 39, as said below
- copy_pick: int32 [8, 40], P('ep'), may hold values from 0 to 7
- w_gate: bfloat16 [40, 1536, 512], P('ep', None, 'tp'), may hold values from -0.15625 to 0.15625
- w_up: bfloat16 [40, 1536, 512], P('ep', None, 'tp'), may hold values from -0.15625 to 0.15625
- w_down: bfloat16 [40, 512, 1536], P('ep', 'tp'), may hold values from -0.25 to 0.25
Outputs:
- layer_out: bfloat16 [2048, 1536], P('ep')
Inputs may be any that keep to these rules, and one draw needn't show every extreme that they name: `expert_ids`: each row names 8 different experts; among the rows of one index of ep no expert is named by more than 80 rows, a bound that some block reaches of them. `slot_expert`: every expert is held by at least one slot.
All inputs are finite; a program needn't handle non-finite values.
Results may differ from a plain program's by a relative error of at most 0.012.
Values may be sent and summed in bfloat16 or wider, within the bound.
No kernel may reach another device: no remote copies, remote signals or barrier semaphores. Data moves between devices by JAX's collectives and lax.ppermute only.
A program may use at most 128 MiB of HBM per device.

v0:
```python
import jax
import jax.numpy as jnp
from jax import lax
from jax.sharding import PartitionSpec as P

CAP = 80


EPSILON = 1e-06


def shortened(value):

    def short(part):
        return part.astype(jnp.bfloat16) if part.dtype == jnp.float32 else part

    return jax.tree.map(short, value)


def rms_scaled(values, gain):
    mean_square = jnp.mean(values * values, axis=-1, keepdims=True)
    return values * lax.rsqrt(mean_square + EPSILON) * gain.astype(jnp.float32)


def slot_of_pick(slot_expert, copy_pick, experts):
    count = slot_expert.shape[0]
    order = jnp.arange(count, dtype=jnp.int32)
    same = slot_expert[:, None] == slot_expert[None, :]
    before = order[None, :] < order[:, None]
    rank = jnp.sum((same & before).astype(jnp.int32), axis=1)
    holds = slot_expert[None, :] == jnp.arange(experts, dtype=jnp.int32)[:, None]
    copies = jnp.sum(holds.astype(jnp.int32), axis=1)
    wanted = copy_pick % copies[None, :]
    match = holds[None, :, :] & (rank[None, None, :] == wanted[:, :, None])
    return jnp.sum(match.astype(jnp.int32) * order[None, None, :], axis=2)


def expert_rows(block, w_gate, w_up, w_down):
    depth, owners, held, width = block.shape
    results = []
    for number in range(held):
        rows_in = block[:, :, number, :].reshape(depth * owners, width)
        gate = jnp.dot(rows_in, w_gate[number], preferred_element_type=jnp.float32)
        upper = jnp.dot(rows_in, w_up[number], preferred_element_type=jnp.float32)
        hidden = (jax.nn.silu(gate) * upper).astype(jnp.bfloat16)
        output = jnp.dot(hidden, w_down[number], preferred_element_type=jnp.float32).astype(
            jnp.bfloat16
        )
        results.append(output.reshape(depth, owners, width))
    return jnp.stack(results, axis=2)


def local(
    resid,
    context,
    w_out,
    pre_gain,
    final_gain,
    w_router,
    expert_ids,
    slot_expert,
    copy_pick,
    w_gate,
    w_up,
    w_down,
):
    owners = lax.axis_size("ep")
    held = w_gate.shape[0]
    row_count, width = resid.shape
    choose = expert_ids.shape[1]
    experts = w_router.shape[1]
    attention = lax.psum(
        jnp.dot(context, w_out, preferred_element_type=jnp.float32).astype(jnp.bfloat16), "tp"
    ).astype(jnp.float32)
    middle = resid.astype(jnp.float32) + attention
    normed = rms_scaled(middle, pre_gain).astype(jnp.bfloat16)
    logits = jnp.dot(normed, w_router, preferred_element_type=jnp.float32)
    onehot = expert_ids[:, :, None] == jnp.arange(experts, dtype=jnp.int32)[None, None, :]
    chosen = jnp.sum(jnp.where(onehot, logits[:, None, :], 0.0), axis=2)
    raised = jnp.exp(chosen)
    weights = (raised / jnp.sum(raised, axis=1, keepdims=True)).astype(jnp.bfloat16)
    table = slot_of_pick(slot_expert, copy_pick, experts)[0]
    slot = jnp.sum(jnp.where(onehot, table[None, None, :], 0), axis=2).reshape(-1)
    flat_hot = onehot.reshape(row_count * choose, experts).astype(jnp.int32)
    earlier = jnp.cumsum(flat_hot, axis=0) - flat_hot
    position = jnp.sum(earlier * flat_hot, axis=1)
    target = slot // held
    local_slot = slot % held
    source_row = jnp.arange(row_count * choose, dtype=jnp.int32) // choose
    flat_index = (position * owners + target) * held + local_slot
    outbound = (
        jnp.zeros((CAP * owners * held, width), jnp.bfloat16).at[flat_index].set(normed[source_row])
    )
    outbound = outbound.reshape(CAP, owners, held, width)
    inbound = lax.all_to_all(outbound, "ep", split_axis=1, concat_axis=1, tiled=True)
    step_rows = 16

    def block_term(number):
        block = lax.dynamic_slice_in_dim(inbound, number * step_rows, step_rows, 0)
        return expert_rows(block, w_gate, w_up, w_down)

    partial_value = lax.map(block_term, jnp.arange(CAP // step_rows, dtype=jnp.int32)).reshape(
        inbound.shape
    )
    returned = lax.all_to_all(
        shortened(partial_value), "ep", split_axis=1, concat_axis=1, tiled=True
    ).astype(partial_value.dtype)
    picked = returned.reshape(-1, width)[flat_index].reshape(row_count, choose, width)
    mixture_lane = jnp.einsum("rk,rkd->rd", weights, picked, preferred_element_type=jnp.float32)
    mixture = lax.psum(mixture_lane.astype(jnp.bfloat16), "tp").astype(jnp.float32)
    return rms_scaled(middle + mixture, final_gain).astype(jnp.bfloat16)


def solution(mesh):
    return jax.shard_map(
        local,
        mesh=mesh,
        in_specs=(
            P("ep", None),
            P("ep", "tp"),
            P("tp", None),
            P(),
            P(),
            P(),
            P("ep", None),
            P(),
            P("ep", None),
            P("ep", None, "tp"),
            P("ep", None, "tp"),
            P("ep", "tp", None),
        ),
        out_specs=P("ep", None),
        check_vma=False,
    )
```

profile of v0, /device:TPU:0, one launch (start us, length us, event | category | flops | bytes accessed | tf_op | source)
XLA Modules:
  0.0 785.6 jit_solution(10528276496376768525)
XLA Ops:
  7.8 2.4 convolution_convert_fusion.5
  12.1 11.3 %reduce-window.6 = s32[40,16,128]{2,1,0:T(8,128)S(1)} reduce-window(s32[40,16,128]{2,1,0:T(8,128)S(1)} %fusion.103, s32[]{:T(128)} %constant.72.clone.1), window={size=1x1x128 pad=0_0x0_0x127_0}, to_apply=%region_4.5 | reduce-window | flops 10403840 | bytes 655364 | tf_op jit(solution)/shard_map/reduce-window
  24.5 23.2 %all-reduce.3.cloned.1.call-done = bf16[256,1536]{1,0:T(8,128)(2,1)} async-done(((bf16[256,1536]{1,0:T(8,128)(2,1)}), bf16[256,1536]{1,0:T(8,128)(2,1)}) %all-reduce.3.cloned.1.call-update) | async-done | bytes 786448 | tf_op jit(solution)/shard_map/psum | solution.py:72
  49.6 36.6 %scatter_custom_fusion = bf16[3200,1536]{1,0:T(8,128)(2,1)} fusion(s32[2048]{0:T(1024)S(1)} %bitcast.212, bf16[256,1536]{1,0:T(8,128)(2,1)S(1)} %multiply_convert_fusion.1, s32[2048]{0:T(1024)S(1)} %broadcast_clamp_fusion.1, bf16[]{:T(256)} %constant.73.clone.1), kind=kCustom, calls=%fused_computation.111 | custom fusion | bytes 9830402 | tf_op jit(solution)/shard_map/scatter | solution.py:92
  86.3 16.7 %reshape.322 = bf16[80,8,5,1536]{3,2,1,0:T(8,128)(2,1)} reshape(bf16[3200,1536]{1,0:T(8,128)(2,1)} %scatter_custom_fusion) | data formatting | bytes 19660800 | tf_op jit(solution)/shard_map/reshape | solution.py:94
  103.0 14.1 %copy.53 = bf16[80,8,5,1536]{3,0,2,1:T(8,128)(2,1)} copy(bf16[80,8,5,1536]{3,2,1,0:T(8,128)(2,1)} %reshape.322) | data formatting | bytes 19660800 | tf_op jit(solution)/shard_map/reshape | solution.py:94
  117.1 5.5 all-to-all-start
  122.6 213.2 %all-to-all-done = bf16[80,8,5,1536]{3,0,2,1:T(8,128)(2,1)} async-done(((bf16[80,8,5,1536]{3,0,2,1:T(8,128)(2,1)}), bf16[80,8,5,1536]{3,0,2,1:T(8,128)(2,1)}, u32[]{:S(2)}, u32[]{:S(2)}) %all-to-all-start) | async-done | bytes 9830432 | tf_op jit(solution)/shard_map/all_to_all | solution.py:95
  335.8 114.4 %while.10 = (s32[]{:T(128)}, bf16[5,16,8,5,1536]{4,2,3,1,0:T(8,128)(2,1)}, s32[5]{0:T(128)S(1)}, bf16[80,8,5,1536]{3,0,2,1:T(8,128)(2,1)}, bf16[5,1536,128]{2,1,...) while((s32[]{:T(128)}, ...), condition=%wide.region_13.14_spmd, body=%wide.region_12.13_spmd.sunk | while | flops 756449280 | bytes 22151720 | solution.py:102
  338.6 2.1 fusion.158
  340.7 2.0 fusion.160
  342.7 2.0 fusion.162
  344.6 2.0 fusion.164
  346.6 2.0 fusion.166
  348.5 1.8 fusion.159
  350.4 1.7 fusion.161
  352.1 1.7 fusion.163
  353.8 1.7 fusion.165
  361.5 2.1 fusion.158
  363.6 2.0 fusion.160
  365.5 2.0 fusion.162
  367.5 2.0 fusion.164
  369.4 2.0 fusion.166
  371.4 1.8 fusion.159
  373.2 1.7 fusion.161
  374.9 1.7 fusion.163
  376.7 1.7 fusion.165
  378.4 1.7 fusion.167
  384.4 2.1 fusion.158
  386.5 2.0 fusion.160
  388.5 2.0 fusion.162
  390.4 2.0 fusion.164
  392.4 2.0 fusion.166
  394.4 1.8 fusion.159
  396.2 1.7 fusion.161
  397.9 1.7 fusion.163
  399.6 1.7 fusion.165
  407.3 2.1 fusion.158
  409.4 2.0 fusion.160
  411.3 2.0 fusion.162
  413.3 2.0 fusion.164
  415.3 2.0 fusion.166
  417.2 1.8 fusion.159
  419.0 1.7 fusion.161
  420.7 1.7 fusion.163
  422.5 1.7 fusion.165
  430.1 2.1 fusion.158
  432.2 2.0 fusion.160
  434.2 2.0 fusion.162
  436.1 2.0 fusion.164
  438.1 2.0 fusion.166
  440.1 1.8 fusion.159
  441.9 1.7 fusion.161
  443.6 1.7 fusion.163
  445.3 1.7 fusion.165
  450.2 10.9 %copy.56 = bf16[80,8,5,1536]{3,0,2,1:T(8,128)(2,1)} copy(bf16[80,8,5,1536]{3,1,2,0:T(8,128)(2,1)} %bitcast.207) | data formatting | bytes 19660800 | tf_op jit(solution)/shard_map/reshape | solution.py:102
  461.1 5.2 all-to-all-start.1
  467.2 211.9 %all-to-all-done.1 = bf16[80,8,5,1536]{3,0,2,1:T(8,128)(2,1)} async-done(((bf16[80,8,5,1536]{3,0,2,1:T(8,128)(2,1)}), bf16[80,8,5,1536]{3,0,2,1:T(8,128)(2,1)}, u32[]{:S(2)}, u32[]{:S(2)}) %all-to-all-start.1) | async-done | bytes 9830432 | tf_op jit(solution)/shard_map/all_to_all | solution.py:105
  679.1 21.9 %copy.57 = bf16[80,8,5,1536]{3,2,1,0:T(8,128)(2,1)} copy(bf16[80,8,5,1536]{3,0,2,1:T(8,128)(2,1)} %all-to-all-done.1) | data formatting | bytes 19660800 | tf_op jit(solution)/shard_map/all_to_all | solution.py:105
  701.0 17.1 %reshape.324 = bf16[3200,1536]{1,0:T(8,128)(2,1)} reshape(bf16[80,8,5,1536]{3,2,1,0:T(8,128)(2,1)} %copy.57) | data formatting | bytes 19660800 | tf_op jit(solution)/shard_map/reshape | solution.py:108
  718.2 18.3 %gather_fusion = bf16[2048,1536]{1,0:T(8,128)(2,1)} fusion(bf16[3200,1536]{1,0:T(8,128)(2,1)} %reshape.324, s32[2048]{0:T(1024)S(1)} %broadcast_clamp_fusion), kind=kCustom, calls=%fused_computation.1 | custom fusion | bytes 12591104 | tf_op jit(solution)/shard_map/gather | solution.py:108
  736.5 4.6 fusion.95
  742.1 33.6 %all-reduce.5.cloned.1.call-done = bf16[256,1536]{1,0:T(8,128)(2,1)} async-done(((bf16[256,1536]{1,0:T(8,128)(2,1)}), bf16[256,1536]{1,0:T(8,128)(2,1)}) %all-reduce.5.cloned.1.call-update) | async-done | bytes 786448 | tf_op jit(solution)/shard_map/psum | solution.py:110
  775.7 1.7 multiply_reduce_fusion
  (134 shorter events, 34.1 us)
Async XLA Ops:
  6.5 1.3 copy-start
  6.5 3.7 copy-start.12
  6.5 3.9 copy-start.15
  6.5 4.2 copy-start.11
  6.5 4.7 copy-start.13
  6.5 41.2 %all-reduce.3.cloned.1.call-start = ((), (), s32[]{:S(2)}) async-start(), calls=%async_computation.2 | async-start | bytes 1572864 | tf_op jit(solution)/shard_map/psum | solution.py:72
  11.1 36.6 %copy-start.2 = (bf16[256,1536]{1,0:T(8,128)(2,1)S(1)}, bf16[256,1536]{1,0:T(8,128)(2,1)}, u32[]{:S(2)}) copy-start(bf16[256,1536]{1,0:T(8,128)(2,1)} %param.14) | copy-start | bytes 2359300
  47.7 1.6 copy-start.4
  49.6 36.6 %copy-start.7 = (bf16[256,1536]{1,0:T(8,128)(2,1)}, bf16[256,1536]{1,0:T(8,128)(2,1)S(1)}, u32[]{:S(2)}) copy-start(bf16[256,1536]{1,0:T(8,128)(2,1)S(1)} %multiply_convert_fusion.1) | copy-start | bytes 2359300
  117.1 218.7 %all-to-all-start = ((bf16[80,8,5,1536]{3,0,2,1:T(8,128)(2,1)}), bf16[80,8,5,1536]{3,0,2,1:T(8,128)(2,1)}, u32[]{:S(2)}, u32[]{:S(2)}) async-start(bf16[80,8,5,1536]{3,0,2,1:T(8,128)(2,1)} %copy.53), calls=%async_computation | async-start | bytes 19660800 | tf_op jit(solution)/shard_map/all_to_all | solution.py:95
  335.8 1.2 copy-start.16
  338.6 8.0 %copy-start.6 = (bf16[16,8,1,1536]{3,0,2,1:T(8,128)(2,1)}, bf16[16,8,1,1536]{3,0,2,1:T(8,128)(2,1)S(1)}, u32[]{:S(2)}) copy-start(bf16[16,8,1,1536]{3,0,2,1:T(8,128)(2,1)S(1)} %get-tuple-element.142) | copy-start | bytes 1179652 | tf_op jit(solution)/shard_map/while
  352.1 3.5 copy-start.18
  357.2 1.4 copy-start.17
  358.6 1.2 copy-start.16
  361.4 8.0 %copy-start.6 = (bf16[16,8,1,1536]{3,0,2,1:T(8,128)(2,1)}, bf16[16,8,1,1536]{3,0,2,1:T(8,128)(2,1)S(1)}, u32[]{:S(2)}) copy-start(bf16[16,8,1,1536]{3,0,2,1:T(8,128)(2,1)S(1)} %get-tuple-element.142) | copy-start | bytes 1179652 | tf_op jit(solution)/shard_map/while
  374.9 3.5 copy-start.18
  380.1 1.5 copy-start.17
  381.6 1.2 copy-start.16
  384.4 8.0 %copy-start.6 = (bf16[16,8,1,1536]{3,0,2,1:T(8,128)(2,1)}, bf16[16,8,1,1536]{3,0,2,1:T(8,128)(2,1)S(1)}, u32[]{:S(2)}) copy-start(bf16[16,8,1,1536]{3,0,2,1:T(8,128)(2,1)S(1)} %get-tuple-element.142) | copy-start | bytes 1179652 | tf_op jit(solution)/shard_map/while
  397.9 3.5 copy-start.18
  403.0 1.4 copy-start.17
  404.4 1.2 copy-start.16
  407.3 8.0 %copy-start.6 = (bf16[16,8,1,1536]{3,0,2,1:T(8,128)(2,1)}, bf16[16,8,1,1536]{3,0,2,1:T(8,128)(2,1)S(1)}, u32[]{:S(2)}) copy-start(bf16[16,8,1,1536]{3,0,2,1:T(8,128)(2,1)S(1)} %get-tuple-element.142) | copy-start | bytes 1179652 | tf_op jit(solution)/shard_map/while
  420.7 3.5 copy-start.18
  425.9 1.4 copy-start.17
  427.3 1.2 copy-start.16
  430.1 8.0 %copy-start.6 = (bf16[16,8,1,1536]{3,0,2,1:T(8,128)(2,1)}, bf16[16,8,1,1536]{3,0,2,1:T(8,128)(2,1)S(1)}, u32[]{:S(2)}) copy-start(bf16[16,8,1,1536]{3,0,2,1:T(8,128)(2,1)S(1)} %get-tuple-element.142) | copy-start | bytes 1179652 | tf_op jit(solution)/shard_map/while
  443.6 3.5 copy-start.18
  448.7 1.4 copy-start.17
  461.1 5.5 copy-start.8
  461.1 5.6 copy-start.10
  461.1 218.0 %all-to-all-start.1 = ((bf16[80,8,5,1536]{3,0,2,1:T(8,128)(2,1)}), bf16[80,8,5,1536]{3,0,2,1:T(8,128)(2,1)}, u32[]{:S(2)}, u32[]{:S(2)}) async-start(bf16[80,8,5,1536]{3,0,2,1:T(8,128)(2,1)} %copy.56), calls=%async_computation.1 | async-start | bytes 19660800 | tf_op jit(solution)/shard_map/all_to_all | solution.py:105
  466.3 309.4 %all-reduce.5.cloned.1.call-start = ((), (), s32[]{:S(2)}) async-start(), calls=%async_computation.3 | async-start | bytes 1572864 | tf_op jit(solution)/shard_map/psum | solution.py:110
  741.1 1.0 copy-start.14
  741.1 34.7 %copy-start.3 = (bf16[256,1536]{1,0:T(8,128)(2,1)S(1)}, bf16[256,1536]{1,0:T(8,128)(2,1)}, u32[]{:S(2)}) copy-start(bf16[256,1536]{1,0:T(8,128)(2,1)} %param.14) | copy-start | bytes 2359300
  741.1 34.6 %copy-start.5 = (bf16[256,1536]{1,0:T(8,128)(2,1)S(1)}, bf16[256,1536]{1,0:T(8,128)(2,1)}, u32[]{:S(2)}) copy-start(bf16[256,1536]{1,0:T(8,128)(2,1)} %all-reduce.3.cloned.1.call-done) | copy-start | bytes 2359300
  775.7 1.7 copy-start.9
  775.7 3.0 copy-start.1
Sparse Core Ops, SparseCore 0:
  10.3 37.3 all-reduce.2
  742.2 33.4 all-reduce.4
where the time goes:
time: 789 us; the launch traced here: 786 us
  waiting for transfers between devices  482 us (61%)
  local copies, waits for them, and re-layouts  158 us (20%)
  matrix products  100 us (13%)
  other arithmetic  17.5 us (2%)
  between operations  13.7 us (2%)
  starting transfers between devices  11.1 us (1%)
    all_to_all x1, waiting for transfers between devices, local(): lax.all_to_all(outbound, 'ep', split_axis=1, concat_axis=1, tiled=True)  213 us
    all_to_all x1, waiting for transfers between devices, local(): lax.all_to_all(shortened(partial_value), 'ep', split_axis=1, concat_axis=...  212 us
    dot_general x25, matrix products, expert_rows(): gate = jnp.dot(rows_in, w_gate[number], preferred_element_type=jnp.float32)  49.7 us
    dot_general x25, matrix products, expert_rows(): jnp.dot(hidden, w_down[number], preferred_element_type=jnp.float32)  43.1 us
    scatter x1, local copies, waits for them, and re-layouts, local(): jnp.zeros((CAP * owners * held, width), jnp.bfloat16).at[flat_index]  36.6 us
    psum x1, waiting for transfers between devices, local(): lax.psum(mixture_lane.astype(jnp.bfloat16), 'tp').astype(jnp.float32)  33.6 us
    reshape x2, local copies, waits for them, and re-layouts, local(): outbound = outbound.reshape(CAP, owners, held, width)  30.8 us
    psum x1, waiting for transfers between devices, local(): lax.psum(jnp.dot(context, w_out, preferred_element_type=jnp.float32).asty...  23.2 us
  transfers between devices with their start and end apart: 4, of which 4 were waited for; matrix products, arithmetic and copies ran while one was open for 2% of the time, Pallas kernels for 0%

commit v1 on v0

v1 whole, which is shorter than its diff:
```python
import functools

import jax
import jax.numpy as jnp
from jax import lax
from jax.experimental import pallas as pl
from jax.experimental.pallas import tpu as pltpu
from jax.sharding import PartitionSpec as P

EPSILON = 1e-06
CHUNKS = 2
LANES = 128
ROW_BLOCK = 512


def slot_of_pick(slot_expert, copy_pick, experts):
    count = slot_expert.shape[0]
    order = jnp.arange(count, dtype=jnp.int32)
    same = slot_expert[:, None] == slot_expert[None, :]
    before = order[None, :] < order[:, None]
    rank = jnp.sum((same & before).astype(jnp.int32), axis=1)
    holds = slot_expert[None, :] == jnp.arange(experts, dtype=jnp.int32)[:, None]
    copies = jnp.sum(holds.astype(jnp.int32), axis=1)
    wanted = copy_pick % copies[None, :]
    match = holds[None, :, :] & (rank[None, None, :] == wanted[:, :, None])
    return jnp.sum(match.astype(jnp.int32) * order[None, None, :], axis=2)


def rms_scaled(values, gain):
    mean_square = jnp.mean(values * values, axis=-1, keepdims=True)
    return values * lax.rsqrt(mean_square + EPSILON) * gain.astype(jnp.float32)


def turn(value, step):
    count = lax.axis_size("ep")
    return lax.ppermute(value, "ep", [(i, (i + 2 * step) % count) for i in range(count)])


def flip_inner(value):
    return lax.ppermute(value, "ep", [(i, i ^ 1) for i in range(lax.axis_size("ep"))])


def flip_upper(value):
    return lax.ppermute(value, "tp", [(i, i ^ 2) for i in range(lax.axis_size("tp"))])


def flip_lower(value):
    return lax.ppermute(value, "tp", [(i, i ^ 1) for i in range(lax.axis_size("tp"))])


VMEM = pl.BlockSpec(memory_space=pltpu.VMEM)
SMEM = pl.BlockSpec(memory_space=pltpu.SMEM)


def attend_kernel(place_ref, context_ref, w_ref, send_ref, keep_ref):
    place = place_ref[0]
    quarter = send_ref.shape[1]
    rows = []
    for lower in (1, 0):
        for upper in (0, 1):
            start = pl.multiple_of((place ^ (upper * 2 + lower)) * quarter, quarter)
            rows.append(context_ref[pl.ds(start, quarter), :])
    rows = jnp.concatenate(rows, axis=0)
    width = w_ref.shape[1]
    tile = 512 if width % 512 == 0 else width
    for left in range(0, width, tile):
        out = jnp.dot(rows, w_ref[:, left : left + tile], preferred_element_type=jnp.float32)
        for upper in (0, 1):
            send_ref[upper, :, left : left + tile] = out[
                upper * quarter : (upper + 1) * quarter
            ].astype(jnp.bfloat16)
            keep_ref[upper, :, left : left + tile] = out[
                (upper + 2) * quarter : (upper + 3) * quarter
            ]


def attend(place, context, w_out):
    rows, _ = context.shape
    width = w_out.shape[1]
    quarter = rows // 4
    return pl.pallas_call(
        attend_kernel,
        out_shape=(
            jax.ShapeDtypeStruct((2, quarter, width), jnp.bfloat16),
            jax.ShapeDtypeStruct((2, quarter, width), jnp.float32),
        ),
        in_specs=[SMEM, VMEM, VMEM],
        out_specs=(VMEM, VMEM),
        name="attend",
    )(place, context, w_out)


def norm_kernel(place_ref, keep_ref, lower_ref, upper_ref, resid_ref, gain_ref, middle_ref, normed_ref):
    attention = (
        keep_ref[0] + lower_ref[0].astype(jnp.float32) + upper_ref[...].astype(jnp.float32)
    )
    middle = resid_ref[...].astype(jnp.float32) + attention
    middle_ref[...] = middle
    normed_ref[...] = rms_scaled(middle, gain_ref[...]).astype(jnp.bfloat16)


def norm_rows(place, keep, from_lower, from_upper, resid, gain, number):
    rows, width = from_upper.shape
    chunks = keep.shape[1] // rows
    return pl.pallas_call(
        norm_kernel,
        out_shape=(
            jax.ShapeDtypeStruct((rows, width), jnp.float32),
            jax.ShapeDtypeStruct((rows, width), jnp.bfloat16),
        ),
        grid_spec=pltpu.PrefetchScalarGridSpec(
            num_scalar_prefetch=1,
            grid=(1,),
            in_specs=[
                pl.BlockSpec((1, rows, width), lambda i, p: (0, number, 0)),
                pl.BlockSpec((1, rows, width), lambda i, p: (0, number, 0)),
                pl.BlockSpec((rows, width), lambda i, p: (0, 0)),
                pl.BlockSpec((rows, width), lambda i, p: (p[0] * chunks + number, 0)),
                pl.BlockSpec((1, width), lambda i, p: (0, 0)),
            ],
            out_specs=[
                pl.BlockSpec((rows, width), lambda i, p: (0, 0)),
                pl.BlockSpec((rows, width), lambda i, p: (0, 0)),
            ],
        ),
        name="norm_rows",
    )(place, keep, from_lower, from_upper, resid, gain)


def expert_kernel(*refs):
    pieces = refs[:4]
    ids_ref, router_ref, gate_ref, up_ref, down_ref, out_ref, rows_ref, hidden_ref = refs[4:]
    held, _, units = gate_ref.shape
    start = 0
    for piece in pieces:
        rows_ref[start : start + piece.shape[0]] = piece[...]
        start += piece.shape[0]
    block = min(ROW_BLOCK, start)

    def one_block(number):
        at = pl.ds(pl.multiple_of(number * block, block), block)
        rows = rows_ref[at, :]
        logits = jnp.dot(rows, router_ref[...], preferred_element_type=jnp.float32)
        lane = lax.broadcasted_iota(jnp.int32, (1, LANES), 1)
        ids = ids_ref[at, :]
        hit = ids[:, 0:1] == lane
        for choice in range(1, ids.shape[1]):
            hit = hit | (ids[:, choice : choice + 1] == lane)
        raised = jnp.where(hit, jnp.exp(logits), 0.0)
        weights = raised / jnp.sum(raised, axis=1, keepdims=True)
        weights = weights.astype(jnp.bfloat16).astype(jnp.float32)
        for slot in range(held):
            both = jnp.concatenate([gate_ref[slot], up_ref[slot]], axis=1)
            out = jnp.dot(rows, both, preferred_element_type=jnp.float32)
            gate, upper = out[:, :units], out[:, units:]
            hidden = jax.nn.silu(gate) * upper * weights[:, slot : slot + 1]
            hidden_ref[:, slot * units : (slot + 1) * units] = hidden.astype(jnp.bfloat16)
        width = out_ref.shape[1]
        tile = 512 if width % 512 == 0 else width
        for left in range(0, width, tile):
            out_ref[at, left : left + tile] = jnp.dot(
                hidden_ref[...],
                down_ref[:, left : left + tile],
                preferred_element_type=jnp.float32,
            ).astype(jnp.bfloat16)

    if start == block:
        one_block(0)
    else:
        pl.loop(0, start // block)(one_block)


def expert_rows(pieces, ids, router, w_gate, w_up, w_down):
    held, width, units = w_gate.shape
    rows = sum(p.shape[0] for p in pieces)
    block = min(ROW_BLOCK, rows)
    return pl.pallas_call(
        expert_kernel,
        out_shape=jax.ShapeDtypeStruct((rows, width), jnp.bfloat16),
        in_specs=[VMEM] * (len(pieces) + 5),
        out_specs=VMEM,
        scratch_shapes=[
            pltpu.VMEM((rows, width), jnp.bfloat16),
            pltpu.VMEM((block, held * units), jnp.bfloat16),
        ],
        compiler_params=pltpu.CompilerParams(vmem_limit_bytes=32 << 20),
        cost_estimate=pl.CostEstimate(
            flops=2 * rows * width * (3 * held * units + LANES),
            bytes_accessed=4 * rows * width + 6 * held * width * units,
            transcendentals=rows * (held * units + LANES),
        ),
        name="expert_rows",
    )(*pieces, ids, router, w_gate, w_up, w_down)


def gather_pieces(rows):
    outer = lax.axis_size("ep") // 2
    half = rows.shape[0] // 2
    ring = [rows] + [turn(rows, step) for step in range(1, outer)]
    first = jnp.concatenate([r[:half] for r in ring], axis=0)
    second = jnp.concatenate([r[half:] for r in ring], axis=0)
    first = jnp.concatenate([first, flip_inner(first)], axis=0)
    second = jnp.concatenate([second, flip_upper(second)], axis=0)
    return [first, flip_upper(first), second, flip_inner(second)]


def wide(value):
    return value.astype(jnp.float32)


def short(value):
    return value.astype(jnp.bfloat16)


def sum_back(own, from_lower):
    outer = lax.axis_size("ep") // 2
    rows = own.shape[0]
    part, quarter, eighth = rows // 2, rows // 4, rows // 8
    half = eighth // outer

    def cut(value, start, size):
        return wide(lax.slice_in_dim(value, start, start + size, axis=0))

    def two(start, size):
        return cut(own, start, size) + cut(from_lower, start, size)

    got_first = flip_upper(short(two(quarter, quarter)))
    got_second = flip_inner(short(two(part + quarter, quarter)))
    next_first = flip_inner(short(two(eighth, eighth) + cut(got_first, eighth, eighth)))
    next_second = flip_upper(short(two(part + eighth, eighth) + cut(got_second, eighth, eighth)))

    def block(number):
        at = number * half
        return jnp.concatenate(
            [
                two(at, half) + cut(got_first, at, half) + cut(next_first, at, half),
                two(part + at, half) + cut(got_second, at, half) + cut(next_second, at, half),
            ],
            axis=0,
        )

    total = block(0)
    for step in range(1, outer):
        total = total + wide(turn(short(block(step)), -step))
    return total


def gather_ids(ids):
    outer = lax.axis_size("ep") // 2
    quarter, choose = ids.shape
    half = quarter // (CHUNKS * 2)
    ring = jnp.stack([ids] + [turn(ids, step) for step in range(1, outer)])
    ring = jnp.stack([ring, flip_inner(ring)])
    ring = jnp.stack([ring, flip_upper(ring)])
    ring = jnp.stack([ring, flip_lower(ring)])
    ring = ring.reshape(2, 2, 2, outer, CHUNKS, 2, half, choose)
    first = jnp.transpose(ring[:, :, :, :, :, 0], (4, 0, 1, 2, 3, 5, 6))
    second = jnp.transpose(ring[:, :, :, :, :, 1], (4, 0, 2, 1, 3, 5, 6))
    both = jnp.stack([first, second], axis=2)
    return both.reshape(CHUNKS, 2, -1, choose)


def local(
    resid,
    context,
    w_out,
    pre_gain,
    final_gain,
    w_router,
    expert_ids,
    slot_expert,
    copy_pick,
    w_gate,
    w_up,
    w_down,
):
    held, width, units = w_gate.shape
    row_count = resid.shape[0]
    choose = expert_ids.shape[1]
    experts = w_router.shape[1]
    slots = slot_expert.shape[0]
    quarter = row_count // 4
    rows = quarter // CHUNKS
    me = lax.axis_index("ep")
    place = lax.axis_index("tp").astype(jnp.int32).reshape(1)

    send, keep = attend(place, context, w_out)

    table = slot_of_pick(slot_expert, copy_pick, experts)[0]
    my_ids = lax.dynamic_slice_in_dim(expert_ids, place[0] * quarter, quarter, axis=0)
    onehot = my_ids[:, :, None] == jnp.arange(experts, dtype=jnp.int32)[None, None, :]
    slot = jnp.sum(jnp.where(onehot, table[None, None, :], 0), axis=2)
    slot = (gather_ids(slot) - me * held) % slots
    rolled = jnp.roll(slot_expert, -me * held)
    column = jnp.arange(experts, dtype=jnp.int32)[:, None] == rolled[None, :]
    router = jnp.dot(w_router, column.astype(jnp.bfloat16), preferred_element_type=jnp.float32)
    router = jnp.pad(router.astype(jnp.bfloat16), ((0, 0), (0, LANES - slots)))
    down = w_down.reshape(held * units, width)

    got = flip_lower(send)
    middles, normeds = [], []
    for number in range(CHUNKS):
        at = slice(number * rows, (number + 1) * rows)
        upper = flip_upper(short(keep[1, at] + wide(got[1, at])))
        middle, normed = norm_rows(place, keep, got, upper, resid, pre_gain.reshape(1, -1), number)
        middles.append(middle)
        normeds.append(normed)

    results = []
    for number in range(CHUNKS):
        pieces = gather_pieces(normeds[number])
        other = [flip_lower(p) for p in pieces]
        own = expert_rows(pieces, slot[number, 0], router, w_gate, w_up, down)
        away = expert_rows(other, slot[number, 1], router, w_gate, w_up, down)
        total = sum_back(own, flip_lower(away))
        results.append(rms_scaled(middles[number] + total, final_gain).astype(jnp.bfloat16))
    result = jnp.concatenate(results, axis=0)
    return lax.all_gather(result, "tp", tiled=True)


def solution(mesh):
    return jax.shard_map(
        local,
        mesh=mesh,
        in_specs=(
            P("ep", None),
            P("ep", "tp"),
            P("tp", None),
            P(),
            P(),
            P(),
            P("ep", None),
            P(),
            P("ep", None),
            P("ep", None, "tp"),
            P("ep", None, "tp"),
            P("ep", "tp", None),
        ),
        out_specs=P("ep", None),
        check_vma=False,
    )
```

time: 789 us -> 150 us (0.19)
  waiting for transfers between devices: 482 us -> 52 us
  local copies, waits for them, and re-layouts: 158 us -> 7.82 us
  matrix products: 100 us -> 0.23 us
  starting transfers between devices: 11.1 us -> 53.6 us
  Pallas kernels: 0 us -> 22.3 us
  between operations: 13.7 us -> 0.63 us
  other arithmetic: 17.5 us -> 4.88 us
  blocking collectives: 0 us -> 8.67 us
    all_to_all x2 -> x0, waiting for transfers between devices: 425 us -> none  [the longest x1 213 us: local(): lax.all_to_all(outbound, 'ep', split_axis=1, concat_axis=1, tiled=True)]
    dot_general x53 -> x1, matrix products: 100 us -> 0.23 us  [local(): jnp.dot(w_router, column.astype(jnp.bfloat16), preferred_element_type=jnp...]
    reshape x4 -> x1, local copies, waits for them, and re-layouts: 58.8 us -> 0.6 us  [local(): pre_gain.reshape(1, -1)]
    psum x2 -> x0, waiting for transfers between devices: 56.8 us -> none  [the longest x1 33.6 us: local(): lax.psum(mixture_lane.astype(jnp.bfloat16), 'tp').astype(jnp.float32)]
    ppermute x0 -> x47, starting transfers between devices: none -> 53.6 us  [the longest x15 29.2 us: turn(): lax.ppermute(value, 'ep', [(i, (i + 2 * step) % count) for i in range(cou...]
    ppermute x0 -> x47, waiting for transfers between devices: none -> 52 us  [the longest x11 21.3 us: flip_upper(): lax.ppermute(value, 'tp', [(i, i ^ 2) for i in range(lax.axis_size('tp'))])]
    scatter x1 -> x0, local copies, waits for them, and re-layouts: 36.6 us -> none  [local(): jnp.zeros((CAP * owners * held, width), jnp.bfloat16).at[flat_index]]
    pallas_call x0 -> x7, Pallas kernels: none -> 22.3 us  [the longest x4 15.6 us: expert_rows(): pl.pallas_call(expert_kernel, out_shape=jax.ShapeDtypeStruct((rows, width...]
  transfers between devices with their start and end apart: 4 -> 47, of which waited for: 4 -> 17; matrix products, arithmetic and copies ran while one was open for 2% -> 4% of each run, Pallas kernels for 0% -> 15%
where the time goes in v1:
time: 150 us
  starting transfers between devices  53.6 us (36%)
  waiting for transfers between devices  52 us (35%)
  Pallas kernels  22.3 us (15%)
  blocking collectives  8.67 us (6%)
  local copies, waits for them, and re-layouts  7.82 us (5%)
  other arithmetic  4.88 us (3%)
    ppermute x15, starting transfers between devices, turn(): lax.ppermute(value, 'ep', [(i, (i + 2 * step) % count) for i in range(cou...  29.2 us
    ppermute x11, waiting for transfers between devices, flip_upper(): lax.ppermute(value, 'tp', [(i, i ^ 2) for i in range(lax.axis_size('tp'))])  21.3 us
    ppermute x9, waiting for transfers between devices, flip_inner(): lax.ppermute(value, 'ep', [(i, i ^ 1) for i in range(lax.axis_size('ep'))])  18.7 us
    pallas_call x4, Pallas kernels, expert_rows(): pl.pallas_call(expert_kernel, out_shape=jax.ShapeDtypeStruct((rows, width...  15.6 us
    ppermute x11, starting transfers between devices, flip_upper(): lax.ppermute(value, 'tp', [(i, i ^ 2) for i in range(lax.axis_size('tp'))])  13.5 us
    ppermute x15, waiting for transfers between devices, turn(): lax.ppermute(value, 'ep', [(i, (i + 2 * step) % count) for i in range(cou...  12 us
    ppermute x9, starting transfers between devices, flip_inner(): lax.ppermute(value, 'ep', [(i, i ^ 1) for i in range(lax.axis_size('ep'))])  9.04 us
    all_gather x1, blocking collectives, local(): return lax.all_gather(result, 'tp', tiled=True)  8.67 us
  transfers between devices with their start and end apart: 47, of which 17 were waited for; matrix products, arithmetic and copies ran while one was open for 4% of the time, Pallas kernels for 15%

profile of v1, /device:TPU:0, one launch (start us, length us, event | category | flops | bytes accessed | tf_op | source)
XLA Modules:
  0.0 150.1 jit_solution(6390967605867152640)
XLA Ops:
  0.0 0.9 convert_reduce_fusion
  0.9 0.8 constant_dynamic-slice_fusion
  1.7 0.8 fusion.13
  2.5 0.8 select_reduce_fusion.1
  3.4 3.1 %collective-permute-start.9 = (s32[64,8]{0,1:T(8,128)S(1)}, s32[64,8]{0,1:T(8,128)S(1)}, u32[]{:S(2)}, u32[]{:S(2)}) collective-permute-start(s32[64,8]{0,1:T(8,128)S(1)} %select_reduce_fusion), channel_id=1, source_target_pairs={{0,8},{4,12},{8,16},{12,20},{16,24},{20,28},{24,0},{28,4},{1,9},{5... | collective-permute-start | bytes 6152 | tf_op jit(solution)/shard_map/ppermute | solution.py:36
  6.5 2.6 %collective-permute-start.10 = (s32[64,8]{0,1:T(8,128)S(1)}, s32[64,8]{0,1:T(8,128)S(1)}, u32[]{:S(2)}, u32[]{:S(2)}) collective-permute-start(s32[64,8]{0,1:T(8,128)S(1)} %select_reduce_fusion), channel_id=1, source_target_pairs={{0,16},{4,20},{8,24},{12,28},{16,0},{20,4},{24,8},{28,12},{1,17},{... | collective-permute-start | bytes 6152 | tf_op jit(solution)/shard_map/ppermute | solution.py:36
  9.1 1.3 collective-permute-start.11
  10.5 0.6 collective-permute-done.10
  11.1 1.7 %collective-permute-done.11 = s32[64,8]{0,1:T(8,128)S(1)} collective-permute-done((s32[64,8]{0,1:T(8,128)S(1)}, s32[64,8]{0,1:T(8,128)S(1)}, u32[]{:S(2)}, u32[]{:S(2)}) %collective-permute-start.11) | collective-permute-done | bytes 2080 | tf_op jit(solution)/shard_map/ppermute | solution.py:36
  12.7 1.5 collective-permute-start.12
  14.2 2.9 %attend.1 = (bf16[2,64,1536]{2,1,0:T(8,128)(2,1)}, f32[2,64,1536]{2,1,0:T(8,128)}) custom-call(s32[1]{0:T(128)} %bitcast.place_ref, bf16[256,384]{1,0:T(8,128)(2,1)} %context_ref.1, bf16[384,1536]{1,0:T(8,128)(2,1)} %w_ref.1), custom_call_target="tpu_custom_call" | custom-call | tf_op jit(solution)/shard_map/attend/pallas_call | solution.py:81
  17.2 1.6 %collective-permute-start.13 = (s32[2,4,64,8]{2,3,1,0:T(8,128)S(1)}, s32[2,4,64,8]{2,3,1,0:T(8,128)S(1)}, u32[]{:S(2)}, u32[]{:S(2)}) collective-permute-start(s32[2,4,64,8]{2,3,1,0:T(8,128)S(1)} %get-tuple-element.88), channel_id=1, source_target_pairs={{0,2},{1,3},{2,0},{3,1},{4,6},{5,7},{6,4},{7,5},{8,10},{9,11},{10,... | collective-permute-start | bytes 49160 | tf_op jit(solution)/shard_map/ppermute | solution.py:44
  18.9 2.2 %collective-permute-done.13 = s32[2,4,64,8]{2,3,1,0:T(8,128)S(1)} collective-permute-done((s32[2,4,64,8]{2,3,1,0:T(8,128)S(1)}, s32[2,4,64,8]{2,3,1,0:T(8,128)S(1)}, u32[]{:S(2)}, u32[]{:S(2)}) %collective-permute-start.13) | collective-permute-done | bytes 16416 | tf_op jit(solution)/shard_map/ppermute | solution.py:44
  21.6 0.6 reshape.184.gain_ref
  23.5 0.7 copy-done.4
  24.2 1.6 %collective-permute-start.27 = (bf16[32,1536]{1,0:T(8,128)(2,1)S(1)}, bf16[32,1536]{1,0:T(8,128)(2,1)S(1)}, u32[]{:S(2)}, u32[]{:S(2)}) collective-permute-start(bf16[32,1536]{1,0:T(8,128)(2,1)S(1)} %get-tuple-element.48), channel_id=1, source_target_pairs={{0,2},{1,3},{2,0},{3,1},{4,6},{5,7},{6,4},{7,5},{8,10},{9,11},{10,... | collective-permute-start | bytes 294920 | tf_op jit(solution)/shard_map/ppermute | solution.py:44
  26.4 0.6 collective-permute-start.1
  27.0 2.7 %collective-permute-done.27.upper_ref = bf16[32,1536]{1,0:T(8,128)(2,1)S(1)} collective-permute-done((bf16[32,1536]{1,0:T(8,128)(2,1)S(1)}, bf16[32,1536]{1,0:T(8,128)(2,1)S(1)}, u32[]{:S(2)}, u32[]{:S(2)}) %collective-permute-start.27) | collective-permute-done | bytes 98336 | tf_op jit(solution)/shard_map/ppermute | solution.py:44
  29.6 0.7 copy-done.9
  30.3 1.9 %norm_rows.3 = (f32[32,1536]{1,0:T(8,128)}, bf16[32,1536]{1,0:T(8,128)(2,1)}) custom-call(s32[1]{0:T(128)} %bitcast.place_ref, f32[2,64,1536]{2,1,0:T(8,128)} %get-tuple-element.11.keep_ref, bf16[2,64,1536]{2,1,0:T(8,128)(2,1)} %copy-done.5, bf16[32,1536]{1,0:T(8,128)(2,1)} %copy-done.9, bf16[256,1536]{1,0:T(8,128)(2,1)} %resid_ref.3, ...), custom_call_target="tpu_custom_call" | custom-call | tf_op jit(solution)/shard_map/norm_rows/pallas_call | solution.py:105
  32.2 0.8 fusion.22
  33.3 3.5 %collective-permute-start.29 = (bf16[32,1536]{1,0:T(8,128)(2,1)}, bf16[32,1536]{1,0:T(8,128)(2,1)S(1)}, u32[]{:S(2)}, u32[]{:S(2)}) collective-permute-start(bf16[32,1536]{1,0:T(8,128)(2,1)} %get-tuple-element.16), channel_id=1, source_target_pairs={{0,16},{4,20},{8,24},{12,28},{16,0},{20,4},{24,8},{28,12},{1,17},{... | collective-permute-start | bytes 294920 | tf_op jit(solution)/shard_map/ppermute | solution.py:36
  37.0 0.6 copy-done.8
  37.6 1.9 %norm_rows.2 = (f32[32,1536]{1,0:T(8,128)}, bf16[32,1536]{1,0:T(8,128)(2,1)}) custom-call(s32[1]{0:T(128)} %bitcast.place_ref, f32[2,64,1536]{2,1,0:T(8,128)} %get-tuple-element.11.keep_ref, bf16[2,64,1536]{2,1,0:T(8,128)(2,1)} %copy-done.5, bf16[32,1536]{1,0:T(8,128)(2,1)} %copy-done.8, bf16[256,1536]{1,0:T(8,128)(2,1)} %resid_ref.3, ...), custom_call_target="tpu_custom_call" | custom-call | tf_op jit(solution)/shard_map/norm_rows/pallas_call | solution.py:105
  39.5 0.8 fusion.18
  40.3 1.9 %collective-permute-start.2 = (bf16[32,1536]{1,0:T(8,128)(2,1)}, bf16[32,1536]{1,0:T(8,128)(2,1)S(1)}, u32[]{:S(2)}, u32[]{:S(2)}) collective-permute-start(bf16[32,1536]{1,0:T(8,128)(2,1)} %get-tuple-element.14), channel_id=1, source_target_pairs={{0,8},{4,12},{8,16},{12,20},{16,24},{20,28},{24,0},{28,4},{1,9},{5... | collective-permute-start | bytes 294920 | tf_op jit(solution)/shard_map/ppermute | solution.py:36
  42.4 2.8 %collective-permute-start.4 = (bf16[32,1536]{1,0:T(8,128)(2,1)}, bf16[32,1536]{1,0:T(8,128)(2,1)S(1)}, u32[]{:S(2)}, u32[]{:S(2)}) collective-permute-start(bf16[32,1536]{1,0:T(8,128)(2,1)} %get-tuple-element.14), channel_id=1, source_target_pairs={{0,24},{4,28},{8,0},{12,4},{16,8},{20,12},{24,16},{28,20},{1,25},{... | collective-permute-start | bytes 294920 | tf_op jit(solution)/shard_map/ppermute | solution.py:36
  45.4 1.8 %collective-permute-start.33 = (bf16[64,1536]{1,0:T(8,128)(2,1)S(1)}, bf16[64,1536]{1,0:T(8,128)(2,1)S(1)}, u32[]{:S(2)}, u32[]{:S(2)}) collective-permute-start(bf16[64,1536]{1,0:T(8,128)(2,1)S(1)} %pad_maximum_fusion.3), channel_id=1, source_target_pairs={{0,2},{1,3},{2,0},{3,1},{4,6},{5,7},{6,4},{7,5},{8,10},{9,11},{10,... | collective-permute-start | bytes 589832 | tf_op jit(solution)/shard_map/ppermute | solution.py:44
  47.2 0.9 collective-permute-start.31
  48.1 3.9 %collective-permute-done.3 = bf16[32,1536]{1,0:T(8,128)(2,1)S(1)} collective-permute-done((bf16[32,1536]{1,0:T(8,128)(2,1)}, bf16[32,1536]{1,0:T(8,128)(2,1)S(1)}, u32[]{:S(2)}, u32[]{:S(2)}) %collective-permute-start.3) | collective-permute-done | bytes 98336 | tf_op jit(solution)/shard_map/ppermute | solution.py:36
  52.1 1.6 %collective-permute-start.7 = (bf16[64,1536]{1,0:T(8,128)(2,1)S(1)}, bf16[64,1536]{1,0:T(8,128)(2,1)S(1)}, u32[]{:S(2)}, u32[]{:S(2)}) collective-permute-start(bf16[64,1536]{1,0:T(8,128)(2,1)S(1)} %pad_maximum_fusion.1), channel_id=1, source_target_pairs={{0,2},{1,3},{2,0},{3,1},{4,6},{5,7},{6,4},{7,5},{8,10},{9,11},{10,... | collective-permute-start | bytes 589832 | tf_op jit(solution)/shard_map/ppermute | solution.py:44
  53.8 0.9 collective-permute-start.5
  54.7 1.3 collective-permute-start.34
  56.0 0.5 collective-permute-start.32
  56.5 2.3 %collective-permute-done.7 = bf16[64,1536]{1,0:T(8,128)(2,1)S(1)} collective-permute-done((bf16[64,1536]{1,0:T(8,128)(2,1)S(1)}, bf16[64,1536]{1,0:T(8,128)(2,1)S(1)}, u32[]{:S(2)}, u32[]{:S(2)}) %collective-permute-start.7) | collective-permute-done | bytes 196640 | tf_op jit(solution)/shard_map/ppermute | solution.py:44
  58.8 2.9 %collective-permute-done.5 = bf16[64,1536]{1,0:T(8,128)(2,1)S(1)} collective-permute-done((bf16[64,1536]{1,0:T(8,128)(2,1)S(1)}, bf16[64,1536]{1,0:T(8,128)(2,1)S(1)}, u32[]{:S(2)}, u32[]{:S(2)}) %collective-permute-start.5) | collective-permute-done | bytes 196640 | tf_op jit(solution)/shard_map/ppermute | solution.py:40
  61.7 0.8 collective-permute-start.8
  62.5 7.6 %collective-permute-done.34.refs_3_ = bf16[128,1536]{1,0:T(8,128)(2,1)S(1)} collective-permute-done((bf16[128,1536]{1,0:T(8,128)(2,1)S(1)}, bf16[128,1536]{1,0:T(8,128)(2,1)S(1)}, u32[]{:S(2)}, u32[]{:S(2)}) %collective-permute-start.34) | collective-permute-done | bytes 393248 | tf_op jit(solution)/shard_map/ppermute | solution.py:40
  71.5 5.5 %collective-permute-done.8.refs_3_ = bf16[128,1536]{1,0:T(8,128)(2,1)S(1)} collective-permute-done((bf16[128,1536]{1,0:T(8,128)(2,1)S(1)}, bf16[128,1536]{1,0:T(8,128)(2,1)S(1)}, u32[]{:S(2)}, u32[]{:S(2)}) %collective-permute-start.8) | collective-permute-done | bytes 393248 | tf_op jit(solution)/shard_map/ppermute | solution.py:40
  77.0 1.1 collective-permute-done.6.refs_1_
  78.7 3.8 %expert_rows.7 = bf16[512,1536]{1,0:T(8,128)(2,1)S(1)} custom-call(bf16[128,1536]{1,0:T(8,128)(2,1)S(1)} %collective-permute-done.35.refs_0_, bf16[128,1536]{1,0:T(8,128)(2,1)S(1)} %collective-permute-done.36.refs_1_, bf16[128,1536]{1,0:T(8,128)(2,1)S(1)} %collective-permute-done.37.refs_2_, bf16[128,1536]{1,0:T(8,128)(2,1)S(1)} %collective-permute-done.38.refs_3_, ...), custom_call_target="tpu_custom_call" | custom-call | flops 3221225472 | bytes 9043968 | tf_op jit(solution)/shard_map/expert_rows/pallas_call | solution.py:177
  82.7 3.8 %expert_rows.5 = bf16[512,1536]{1,0:T(8,128)(2,1)S(1)} custom-call(bf16[128,1536]{1,0:T(8,128)(2,1)S(1)} %collective-permute-done.15.refs_0_, bf16[128,1536]{1,0:T(8,128)(2,1)S(1)} %collective-permute-done.16.refs_1_, bf16[128,1536]{1,0:T(8,128)(2,1)S(1)} %collective-permute-done.17.refs_2_, bf16[128,1536]{1,0:T(8,128)(2,1)S(1)} %collective-permute-done.18.refs_3_, ...), custom_call_target="tpu_custom_call" | custom-call | flops 3221225472 | bytes 9043968 | tf_op jit(solution)/shard_map/expert_rows/pallas_call | solution.py:177
  86.5 0.5 collective-permute-start.19
  87.1 3.8 %expert_rows.6 = bf16[512,1536]{1,0:T(8,128)(2,1)S(1)} custom-call(bf16[128,1536]{1,0:T(8,128)(2,1)S(1)} %constant_dynamic-update-slice_fusion.10.refs_0_, bf16[128,1536]{1,0:T(8,128)(2,1)S(1)} %collective-permute-done.32.refs_1_, bf16[128,1536]{1,0:T(8,128)(2,1)S(1)} %constant_dynamic-update-slice_fusion.15.refs_2_, ...), custom_call_target="tpu_custom_call" | custom-call | flops 3221225472 | bytes 9043968 | tf_op jit(solution)/shard_map/expert_rows/pallas_call | solution.py:177
  90.9 4.1 %expert_rows.4 = bf16[512,1536]{1,0:T(8,128)(2,1)S(1)} custom-call(bf16[128,1536]{1,0:T(8,128)(2,1)S(1)} %constant_dynamic-update-slice_fusion.refs_0_, bf16[128,1536]{1,0:T(8,128)(2,1)S(1)} %collective-permute-done.6.refs_1_, bf16[128,1536]{1,0:T(8,128)(2,1)S(1)} %constant_dynamic-update-slice_fusion.5.refs_2_, ...), custom_call_target="tpu_custom_call" | custom-call | flops 3221225472 | bytes 9043968 | tf_op jit(solution)/shard_map/expert_rows/pallas_call | solution.py:177
  95.2 0.5 collective-permute-start.40
  95.7 0.8 collective-permute-start.42
  96.7 1.6 %collective-permute-start.20 = (bf16[128,1536]{1,0:T(8,128)(2,1)S(1)}, bf16[128,1536]{1,0:T(8,128)(2,1)S(1)}, u32[]{:S(2)}, u32[]{:S(2)}) collective-permute-start(bf16[128,1536]{1,0:T(8,128)(2,1)S(1)} %get-tuple-element.41), channel_id=1, source_target_pairs={{0,2},{1,3},{2,0},{3,1},{4,6},{5,7},{6,4},{7,5},{8,10},{9,11},{10,... | collective-permute-start | bytes 1179656 | tf_op jit(solution)/shard_map/ppermute | solution.py:44
  98.4 1.2 collective-permute-start.22
  99.6 7.7 %collective-permute-done.40 = bf16[128,1536]{1,0:T(8,128)(2,1)S(1)} collective-permute-done((bf16[128,1536]{1,0:T(8,128)(2,1)S(1)}, bf16[128,1536]{1,0:T(8,128)(2,1)S(1)}, u32[]{:S(2)}, u32[]{:S(2)}) %collective-permute-start.40) | collective-permute-done | bytes 393248 | tf_op jit(solution)/shard_map/ppermute | solution.py:44
  107.9 0.9 collective-permute-start.41
  108.8 1.6 %collective-permute-start.43 = (bf16[64,1536]{1,0:T(8,128)(2,1)S(1)}, bf16[64,1536]{1,0:T(8,128)(2,1)S(1)}, u32[]{:S(2)}, u32[]{:S(2)}) collective-permute-start(bf16[64,1536]{1,0:T(8,128)(2,1)S(1)} %get-tuple-element.44), channel_id=1, source_target_pairs={{0,2},{1,3},{2,0},{3,1},{4,6},{5,7},{6,4},{7,5},{8,10},{9,11},{10,... | collective-permute-start | bytes 589832 | tf_op jit(solution)/shard_map/ppermute | solution.py:44
  110.3 5.3 %collective-permute-done.20 = bf16[128,1536]{1,0:T(8,128)(2,1)S(1)} collective-permute-done((bf16[128,1536]{1,0:T(8,128)(2,1)S(1)}, bf16[128,1536]{1,0:T(8,128)(2,1)S(1)}, u32[]{:S(2)}, u32[]{:S(2)}) %collective-permute-start.20) | collective-permute-done | bytes 393248 | tf_op jit(solution)/shard_map/ppermute | solution.py:44
  116.3 0.9 collective-permute-start.21
  117.2 1.6 %collective-permute-start.23 = (bf16[64,1536]{1,0:T(8,128)(2,1)S(1)}, bf16[64,1536]{1,0:T(8,128)(2,1)S(1)}, u32[]{:S(2)}, u32[]{:S(2)}) collective-permute-start(bf16[64,1536]{1,0:T(8,128)(2,1)S(1)} %get-tuple-element.40), channel_id=1, source_target_pairs={{0,2},{1,3},{2,0},{3,1},{4,6},{5,7},{6,4},{7,5},{8,10},{9,11},{10,... | collective-permute-start | bytes 589832 | tf_op jit(solution)/shard_map/ppermute | solution.py:44
  118.8 1.6 %collective-permute-done.41 = bf16[64,1536]{1,0:T(8,128)(2,1)S(1)} collective-permute-done((bf16[64,1536]{1,0:T(8,128)(2,1)S(1)}, bf16[64,1536]{1,0:T(8,128)(2,1)S(1)}, u32[]{:S(2)}, u32[]{:S(2)}) %collective-permute-start.41) | collective-permute-done | bytes 196640 | tf_op jit(solution)/shard_map/ppermute | solution.py:40
  120.6 2.4 %collective-permute-start.44 = (bf16[32,1536]{1,0:T(8,128)(2,1)S(1)}, bf16[32,1536]{1,0:T(8,128)(2,1)S(1)}, u32[]{:S(2)}, u32[]{:S(2)}) collective-permute-start(bf16[32,1536]{1,0:T(8,128)(2,1)S(1)} %pad_maximum_fusion.8), channel_id=1, source_target_pairs={{0,24},{4,28},{8,0},{12,4},{16,8},{20,12},{24,16},{28,20},{1,25},{... | collective-permute-start | bytes 294920 | tf_op jit(solution)/shard_map/ppermute | solution.py:36
  123.0 2.0 %collective-permute-start.45 = (bf16[32,1536]{1,0:T(8,128)(2,1)S(1)}, bf16[32,1536]{1,0:T(8,128)(2,1)S(1)}, u32[]{:S(2)}, u32[]{:S(2)}) collective-permute-start(bf16[32,1536]{1,0:T(8,128)(2,1)S(1)} %pad_maximum_fusion.9), channel_id=1, source_target_pairs={{0,16},{4,20},{8,24},{12,28},{16,0},{20,4},{24,8},{28,12},{1,17},{... | collective-permute-start | bytes 294920 | tf_op jit(solution)/shard_map/ppermute | solution.py:36
  125.4 3.8 %collective-permute-start.24 = (bf16[32,1536]{1,0:T(8,128)(2,1)S(1)}, bf16[32,1536]{1,0:T(8,128)(2,1)S(1)}, u32[]{:S(2)}, u32[]{:S(2)}) collective-permute-start(bf16[32,1536]{1,0:T(8,128)(2,1)S(1)} %pad_maximum_fusion.5), channel_id=1, source_target_pairs={{0,24},{4,28},{8,0},{12,4},{16,8},{20,12},{24,16},{28,20},{1,25},{... | collective-permute-start | bytes 294920 | tf_op jit(solution)/shard_map/ppermute | solution.py:36
  129.3 4.9 %collective-permute-start.26 = (bf16[32,1536]{1,0:T(8,128)(2,1)S(1)}, bf16[32,1536]{1,0:T(8,128)(2,1)S(1)}, u32[]{:S(2)}, u32[]{:S(2)}) collective-permute-start(bf16[32,1536]{1,0:T(8,128)(2,1)S(1)} %pad_maximum_fusion.7), channel_id=1, source_target_pairs={{0,8},{4,12},{8,16},{12,20},{16,24},{20,28},{24,0},{28,4},{1,9},{5... | collective-permute-start | bytes 294920 | tf_op jit(solution)/shard_map/ppermute | solution.py:36
  134.3 3.6 %collective-permute-done.45 = bf16[32,1536]{1,0:T(8,128)(2,1)S(1)} collective-permute-done((bf16[32,1536]{1,0:T(8,128)(2,1)S(1)}, bf16[32,1536]{1,0:T(8,128)(2,1)S(1)}, u32[]{:S(2)}, u32[]{:S(2)}) %collective-permute-start.45) | collective-permute-done | bytes 98336 | tf_op jit(solution)/shard_map/ppermute | solution.py:36
  138.1 2.1 %collective-permute-done.25 = bf16[32,1536]{1,0:T(8,128)(2,1)S(1)} collective-permute-done((bf16[32,1536]{1,0:T(8,128)(2,1)S(1)}, bf16[32,1536]{1,0:T(8,128)(2,1)S(1)}, u32[]{:S(2)}, u32[]{:S(2)}) %collective-permute-start.25) | collective-permute-done | bytes 98336 | tf_op jit(solution)/shard_map/ppermute | solution.py:36
  140.5 8.7 %all_gather.3 = bf16[256,1536]{1,0:T(8,128)(2,1)S(1)} all-gather(bf16[64,1536]{1,0:T(8,128)(2,1)S(1)} %pad_maximum_fusion.4), channel_id=1, replica_groups=mesh['ep'=8,'tp'=4] {'tp'}, dimensions={0}, use_global_device_ids=true | all-gather | bytes 983040 | tf_op jit(solution)/shard_map/all_gather | solution.py:318
  149.2 0.9 copy.52
  (137 shorter events, 8.1 us)
Async XLA Ops:
  0.0 21.2 %copy-start = (bf16[1536,40]{0,1:T(8,128)(2,1)S(1)}, bf16[1536,40]{0,1:T(8,128)(2,1)}, u32[]{:S(2)}) copy-start(bf16[1536,40]{0,1:T(8,128)(2,1)} %param.17) | copy-start | bytes 368644
  0.0 18.8 %copy-start.10 = (s32[40]{0:T(128)S(1)}, s32[40]{0:T(128)}, u32[]{:S(2)}) copy-start(s32[40]{0:T(128)} %param.19) | copy-start | bytes 484
  0.0 21.6 %copy-start.12 = (bf16[1536]{0:T(1024)(128)(2,1)S(1)}, bf16[1536]{0:T(1024)(128)(2,1)}, u32[]{:S(2)}) copy-start(bf16[1536]{0:T(1024)(128)(2,1)} %param.15) | copy-start | bytes 9220
  3.4 7.0 %collective-permute-start.9 = (s32[64,8]{0,1:T(8,128)S(1)}, s32[64,8]{0,1:T(8,128)S(1)}, u32[]{:S(2)}, u32[]{:S(2)}) collective-permute-start(s32[64,8]{0,1:T(8,128)S(1)} %select_reduce_fusion), channel_id=1, source_target_pairs={{0,8},{4,12},{8,16},{12,20},{16,24},{20,28},{24,0},{28,4},{1,9},{5... | collective-permute-start | bytes 6152 | tf_op jit(solution)/shard_map/ppermute | solution.py:36
  6.5 4.5 %collective-permute-start.10 = (s32[64,8]{0,1:T(8,128)S(1)}, s32[64,8]{0,1:T(8,128)S(1)}, u32[]{:S(2)}, u32[]{:S(2)}) collective-permute-start(s32[64,8]{0,1:T(8,128)S(1)} %select_reduce_fusion), channel_id=1, source_target_pairs={{0,16},{4,20},{8,24},{12,28},{16,0},{20,4},{24,8},{28,12},{1,17},{... | collective-permute-start | bytes 6152 | tf_op jit(solution)/shard_map/ppermute | solution.py:36
  9.1 3.6 %collective-permute-start.11 = (s32[64,8]{0,1:T(8,128)S(1)}, s32[64,8]{0,1:T(8,128)S(1)}, u32[]{:S(2)}, u32[]{:S(2)}) collective-permute-start(s32[64,8]{0,1:T(8,128)S(1)} %select_reduce_fusion), channel_id=1, source_target_pairs={{0,24},{4,28},{8,0},{12,4},{16,8},{20,12},{24,16},{28,20},{1,25},{... | collective-permute-start | bytes 6152 | tf_op jit(solution)/shard_map/ppermute | solution.py:36
  12.7 4.4 %collective-permute-start.12 = (s32[4,64,8]{1,2,0:T(8,128)S(1)}, s32[4,64,8]{1,2,0:T(8,128)S(1)}, u32[]{:S(2)}, u32[]{:S(2)}) collective-permute-start(s32[4,64,8]{1,2,0:T(8,128)S(1)} %get-tuple-element.90), channel_id=1, source_target_pairs={{0,4},{4,0},{8,12},{12,8},{16,20},{20,16},{24,28},{28,24},{1,5},{5... | collective-permute-start | bytes 24584 | tf_op jit(solution)/shard_map/ppermute | solution.py:40
  17.1 6.3 %collective-permute-start = (bf16[2,64,1536]{2,1,0:T(8,128)(2,1)}, bf16[2,64,1536]{2,1,0:T(8,128)(2,1)S(1)}, u32[]{:S(2)}, u32[]{:S(2)}) collective-permute-start(bf16[2,64,1536]{2,1,0:T(8,128)(2,1)} %get-tuple-element.12), channel_id=1, source_target_pairs={{0,1},{1,0},{2,3},{3,2},{4,5},{5,4},{6,7},{7,6},{8,9},{9,8},{10,11... | collective-permute-start | bytes 1179656 | tf_op jit(solution)/shard_map/ppermute | solution.py:48
  17.2 4.0 %collective-permute-start.13 = (s32[2,4,64,8]{2,3,1,0:T(8,128)S(1)}, s32[2,4,64,8]{2,3,1,0:T(8,128)S(1)}, u32[]{:S(2)}, u32[]{:S(2)}) collective-permute-start(s32[2,4,64,8]{2,3,1,0:T(8,128)S(1)} %get-tuple-element.88), channel_id=1, source_target_pairs={{0,2},{1,3},{2,0},{3,1},{4,6},{5,7},{6,4},{7,5},{8,10},{9,11},{10,... | collective-permute-start | bytes 49160 | tf_op jit(solution)/shard_map/ppermute | solution.py:44
  21.2 1.9 %collective-permute-start.14 = (s32[2,2,4,64,8]{3,4,2,1,0:T(8,128)S(1)}, s32[2,2,4,64,8]{3,4,2,1,0:T(8,128)S(1)}, u32[]{:S(2)}, u32[]{:S(2)}) collective-permute-start(s32[2,2,4,64,8]{3,4,2,1,0:T(8,128)S(1)} %pad_add_fusion.1), channel_id=1, source_target_pairs={{0,1},{1,0},{2,3},{3,2},{4,5},{5,4},{6,7},{7,6},{8,9},{9,8},{10,11... | collective-permute-start | bytes 98312 | tf_op jit(solution)/shard_map/ppermute | solution.py:48
  23.1 1.1 copy-start.4
  23.5 2.9 %copy-start.5 = (bf16[2,64,1536]{2,1,0:T(8,128)(2,1)}, bf16[2,64,1536]{2,1,0:T(8,128)(2,1)S(1)}, u32[]{:S(2)}) copy-start(bf16[2,64,1536]{2,1,0:T(8,128)(2,1)S(1)} %collective-permute-done.lower_ref) | copy-start | bytes 1179652
  24.2 5.4 %collective-permute-start.27 = (bf16[32,1536]{1,0:T(8,128)(2,1)S(1)}, bf16[32,1536]{1,0:T(8,128)(2,1)S(1)}, u32[]{:S(2)}, u32[]{:S(2)}) collective-permute-start(bf16[32,1536]{1,0:T(8,128)(2,1)S(1)} %get-tuple-element.48), channel_id=1, source_target_pairs={{0,2},{1,3},{2,0},{3,1},{4,6},{5,7},{6,4},{7,5},{8,10},{9,11},{10,... | collective-permute-start | bytes 294920 | tf_op jit(solution)/shard_map/ppermute | solution.py:44
  26.4 10.6 %collective-permute-start.1 = (bf16[32,1536]{1,0:T(8,128)(2,1)S(1)}, bf16[32,1536]{1,0:T(8,128)(2,1)S(1)}, u32[]{:S(2)}, u32[]{:S(2)}) collective-permute-start(bf16[32,1536]{1,0:T(8,128)(2,1)S(1)} %get-tuple-element.47), channel_id=1, source_target_pairs={{0,2},{1,3},{2,0},{3,1},{4,6},{5,7},{6,4},{7,5},{8,10},{9,11},{10,... | collective-permute-start | bytes 294920 | tf_op jit(solution)/shard_map/ppermute | solution.py:44
  29.6 0.7 copy-start.9
  33.0 9.4 %collective-permute-start.28 = (bf16[32,1536]{1,0:T(8,128)(2,1)}, bf16[32,1536]{1,0:T(8,128)(2,1)S(1)}, u32[]{:S(2)}, u32[]{:S(2)}) collective-permute-start(bf16[32,1536]{1,0:T(8,128)(2,1)} %get-tuple-element.16), channel_id=1, source_target_pairs={{0,8},{4,12},{8,16},{12,20},{16,24},{20,28},{24,0},{28,4},{1,9},{5... | collective-permute-start | bytes 294920 | tf_op jit(solution)/shard_map/ppermute | solution.py:36
  33.3 12.0 %collective-permute-start.29 = (bf16[32,1536]{1,0:T(8,128)(2,1)}, bf16[32,1536]{1,0:T(8,128)(2,1)S(1)}, u32[]{:S(2)}, u32[]{:S(2)}) collective-permute-start(bf16[32,1536]{1,0:T(8,128)(2,1)} %get-tuple-element.16), channel_id=1, source_target_pairs={{0,16},{4,20},{8,24},{12,28},{16,0},{20,4},{24,8},{28,12},{1,17},{... | collective-permute-start | bytes 294920 | tf_op jit(solution)/shard_map/ppermute | solution.py:36
  36.8 8.5 %collective-permute-start.30 = (bf16[32,1536]{1,0:T(8,128)(2,1)}, bf16[32,1536]{1,0:T(8,128)(2,1)S(1)}, u32[]{:S(2)}, u32[]{:S(2)}) collective-permute-start(bf16[32,1536]{1,0:T(8,128)(2,1)} %get-tuple-element.16), channel_id=1, source_target_pairs={{0,24},{4,28},{8,0},{12,4},{16,8},{20,12},{24,16},{28,20},{1,25},{... | collective-permute-start | bytes 294920 | tf_op jit(solution)/shard_map/ppermute | solution.py:36
  37.0 0.7 copy-start.8
  40.3 7.8 %collective-permute-start.2 = (bf16[32,1536]{1,0:T(8,128)(2,1)}, bf16[32,1536]{1,0:T(8,128)(2,1)S(1)}, u32[]{:S(2)}, u32[]{:S(2)}) collective-permute-start(bf16[32,1536]{1,0:T(8,128)(2,1)} %get-tuple-element.14), channel_id=1, source_target_pairs={{0,8},{4,12},{8,16},{12,20},{16,24},{20,28},{24,0},{28,4},{1,9},{5... | collective-permute-start | bytes 294920 | tf_op jit(solution)/shard_map/ppermute | solution.py:36
  42.2 9.8 %collective-permute-start.3 = (bf16[32,1536]{1,0:T(8,128)(2,1)}, bf16[32,1536]{1,0:T(8,128)(2,1)S(1)}, u32[]{:S(2)}, u32[]{:S(2)}) collective-permute-start(bf16[32,1536]{1,0:T(8,128)(2,1)} %get-tuple-element.14), channel_id=1, source_target_pairs={{0,16},{4,20},{8,24},{12,28},{16,0},{20,4},{24,8},{28,12},{1,17},{... | collective-permute-start | bytes 294920 | tf_op jit(solution)/shard_map/ppermute | solution.py:36
  42.4 9.7 %collective-permute-start.4 = (bf16[32,1536]{1,0:T(8,128)(2,1)}, bf16[32,1536]{1,0:T(8,128)(2,1)S(1)}, u32[]{:S(2)}, u32[]{:S(2)}) collective-permute-start(bf16[32,1536]{1,0:T(8,128)(2,1)} %get-tuple-element.14), channel_id=1, source_target_pairs={{0,24},{4,28},{8,0},{12,4},{16,8},{20,12},{24,16},{28,20},{1,25},{... | collective-permute-start | bytes 294920 | tf_op jit(solution)/shard_map/ppermute | solution.py:36
  45.4 9.3 %collective-permute-start.33 = (bf16[64,1536]{1,0:T(8,128)(2,1)S(1)}, bf16[64,1536]{1,0:T(8,128)(2,1)S(1)}, u32[]{:S(2)}, u32[]{:S(2)}) collective-permute-start(bf16[64,1536]{1,0:T(8,128)(2,1)S(1)} %pad_maximum_fusion.3), channel_id=1, source_target_pairs={{0,2},{1,3},{2,0},{3,1},{4,6},{5,7},{6,4},{7,5},{8,10},{9,11},{10,... | collective-permute-start | bytes 589832 | tf_op jit(solution)/shard_map/ppermute | solution.py:44
  47.2 8.8 %collective-permute-start.31 = (bf16[64,1536]{1,0:T(8,128)(2,1)S(1)}, bf16[64,1536]{1,0:T(8,128)(2,1)S(1)}, u32[]{:S(2)}, u32[]{:S(2)}) collective-permute-start(bf16[64,1536]{1,0:T(8,128)(2,1)S(1)} %pad_maximum_fusion.2), channel_id=1, source_target_pairs={{0,4},{4,0},{8,12},{12,8},{16,20},{20,16},{24,28},{28,24},{1,5},{5... | collective-permute-start | bytes 589832 | tf_op jit(solution)/shard_map/ppermute | solution.py:40
  52.1 6.6 %collective-permute-start.7 = (bf16[64,1536]{1,0:T(8,128)(2,1)S(1)}, bf16[64,1536]{1,0:T(8,128)(2,1)S(1)}, u32[]{:S(2)}, u32[]{:S(2)}) collective-permute-start(bf16[64,1536]{1,0:T(8,128)(2,1)S(1)} %pad_maximum_fusion.1), channel_id=1, source_target_pairs={{0,2},{1,3},{2,0},{3,1},{4,6},{5,7},{6,4},{7,5},{8,10},{9,11},{10,... | collective-permute-start | bytes 589832 | tf_op jit(solution)/shard_map/ppermute | solution.py:44
  53.8 24.9 %copy-start.3 = (bf16[5,128,1536]{2,1,0:T(8,128)(2,1)S(1)}, bf16[5,128,1536]{2,1,0:T(8,128)(2,1)}, u32[]{:S(2)}) copy-start(bf16[5,128,1536]{2,1,0:T(8,128)(2,1)} %param.23) | copy-start | bytes 5898244
  53.8 7.9 %collective-permute-start.5 = (bf16[64,1536]{1,0:T(8,128)(2,1)S(1)}, bf16[64,1536]{1,0:T(8,128)(2,1)S(1)}, u32[]{:S(2)}, u32[]{:S(2)}) collective-permute-start(bf16[64,1536]{1,0:T(8,128)(2,1)S(1)} %pad_maximum_fusion), channel_id=1, source_target_pairs={{0,4},{4,0},{8,12},{12,8},{16,20},{20,16},{24,28},{28,24},{1,5},{5... | collective-permute-start | bytes 589832 | tf_op jit(solution)/shard_map/ppermute | solution.py:40
  54.7 15.4 %collective-permute-start.34 = (bf16[128,1536]{1,0:T(8,128)(2,1)S(1)}, bf16[128,1536]{1,0:T(8,128)(2,1)S(1)}, u32[]{:S(2)}, u32[]{:S(2)}) collective-permute-start(bf16[128,1536]{1,0:T(8,128)(2,1)S(1)} %constant_dynamic-update-slice_fusion.15.refs_2_), channel_id=1, source_target_pairs={{0,4},{4,0},{8,12},{12,8},{16,20},{20,16},{24,28},{28,24},{1,5},{5... | collective-permute-start | bytes 1179656 | tf_op jit(solution)/shard_map/ppermute | solution.py:40
  56.0 14.6 %collective-permute-start.37 = (bf16[128,1536]{1,0:T(8,128)(2,1)S(1)}, bf16[128,1536]{1,0:T(8,128)(2,1)S(1)}, u32[]{:S(2)}, u32[]{:S(2)}) collective-permute-start(bf16[128,1536]{1,0:T(8,128)(2,1)S(1)} %constant_dynamic-update-slice_fusion.15.refs_2_), channel_id=1, source_target_pairs={{0,1},{1,0},{2,3},{3,2},{4,5},{5,4},{6,7},{7,6},{8,9},{9,8},{10,11... | collective-permute-start | bytes 1179656 | tf_op jit(solution)/shard_map/ppermute | solution.py:48
  56.0 14.6 %collective-permute-start.32 = (bf16[128,1536]{1,0:T(8,128)(2,1)S(1)}, bf16[128,1536]{1,0:T(8,128)(2,1)S(1)}, u32[]{:S(2)}, u32[]{:S(2)}) collective-permute-start(bf16[128,1536]{1,0:T(8,128)(2,1)S(1)} %constant_dynamic-update-slice_fusion.10.refs_0_), channel_id=1, source_target_pairs={{0,2},{1,3},{2,0},{3,1},{4,6},{5,7},{6,4},{7,5},{8,10},{9,11},{10,... | collective-permute-start | bytes 1179656 | tf_op jit(solution)/shard_map/ppermute | solution.py:44
  58.8 12.6 %collective-permute-start.35 = (bf16[128,1536]{1,0:T(8,128)(2,1)S(1)}, bf16[128,1536]{1,0:T(8,128)(2,1)S(1)}, u32[]{:S(2)}, u32[]{:S(2)}) collective-permute-start(bf16[128,1536]{1,0:T(8,128)(2,1)S(1)} %constant_dynamic-update-slice_fusion.10.refs_0_), channel_id=1, source_target_pairs={{0,1},{1,0},{2,3},{3,2},{4,5},{5,4},{6,7},{7,6},{8,9},{9,8},{10,11... | collective-permute-start | bytes 1179656 | tf_op jit(solution)/shard_map/ppermute | solution.py:48
  61.7 15.3 %collective-permute-start.8 = (bf16[128,1536]{1,0:T(8,128)(2,1)S(1)}, bf16[128,1536]{1,0:T(8,128)(2,1)S(1)}, u32[]{:S(2)}, u32[]{:S(2)}) collective-permute-start(bf16[128,1536]{1,0:T(8,128)(2,1)S(1)} %constant_dynamic-update-slice_fusion.5.refs_2_), channel_id=1, source_target_pairs={{0,4},{4,0},{8,12},{12,8},{16,20},{20,16},{24,28},{28,24},{1,5},{5... | collective-permute-start | bytes 1179656 | tf_op jit(solution)/shard_map/ppermute | solution.py:40
  70.1 8.0 %collective-permute-start.6 = (bf16[128,1536]{1,0:T(8,128)(2,1)S(1)}, bf16[128,1536]{1,0:T(8,128)(2,1)S(1)}, u32[]{:S(2)}, u32[]{:S(2)}) collective-permute-start(bf16[128,1536]{1,0:T(8,128)(2,1)S(1)} %constant_dynamic-update-slice_fusion.refs_0_), channel_id=1, source_target_pairs={{0,2},{1,3},{2,0},{3,1},{4,6},{5,7},{6,4},{7,5},{8,10},{9,11},{10,... | collective-permute-start | bytes 1179656 | tf_op jit(solution)/shard_map/ppermute | solution.py:44
  70.6 7.6 %collective-permute-start.38 = (bf16[128,1536]{1,0:T(8,128)(2,1)S(1)}, bf16[128,1536]{1,0:T(8,128)(2,1)S(1)}, u32[]{:S(2)}, u32[]{:S(2)}) collective-permute-start(bf16[128,1536]{1,0:T(8,128)(2,1)S(1)} %collective-permute-done.34.refs_3_), channel_id=1, source_target_pairs={{0,1},{1,0},{2,3},{3,2},{4,5},{5,4},{6,7},{7,6},{8,9},{9,8},{10,11... | collective-permute-start | bytes 1179656 | tf_op jit(solution)/shard_map/ppermute | solution.py:48
  70.6 8.1 %collective-permute-start.36 = (bf16[128,1536]{1,0:T(8,128)(2,1)S(1)}, bf16[128,1536]{1,0:T(8,128)(2,1)S(1)}, u32[]{:S(2)}, u32[]{:S(2)}) collective-permute-start(bf16[128,1536]{1,0:T(8,128)(2,1)S(1)} %collective-permute-done.32.refs_1_), channel_id=1, source_target_pairs={{0,1},{1,0},{2,3},{3,2},{4,5},{5,4},{6,7},{7,6},{8,9},{9,8},{10,11... | collective-permute-start | bytes 1179656 | tf_op jit(solution)/shard_map/ppermute | solution.py:48
  71.1 7.6 %copy-start.2 = (bf16[5,1536,128]{2,1,0:T(8,128)(2,1)S(1)}, bf16[5,1536,128]{2,1,0:T(8,128)(2,1)}, u32[]{:S(2)}) copy-start(bf16[5,1536,128]{2,1,0:T(8,128)(2,1)} %refs_7_.7) | copy-start | bytes 5898244
  71.3 7.4 %copy-start.1 = (bf16[5,1536,128]{2,1,0:T(8,128)(2,1)S(1)}, bf16[5,1536,128]{2,1,0:T(8,128)(2,1)}, u32[]{:S(2)}) copy-start(bf16[5,1536,128]{2,1,0:T(8,128)(2,1)} %refs_6_.7) | copy-start | bytes 5898244
  71.4 11.2 %collective-permute-start.17 = (bf16[128,1536]{1,0:T(8,128)(2,1)S(1)}, bf16[128,1536]{1,0:T(8,128)(2,1)S(1)}, u32[]{:S(2)}, u32[]{:S(2)}) collective-permute-start(bf16[128,1536]{1,0:T(8,128)(2,1)S(1)} %constant_dynamic-update-slice_fusion.5.refs_2_), channel_id=1, source_target_pairs={{0,1},{1,0},{2,3},{3,2},{4,5},{5,4},{6,7},{7,6},{8,9},{9,8},{10,11... | collective-permute-start | bytes 1179656 | tf_op jit(solution)/shard_map/ppermute | solution.py:48
  77.0 5.6 %collective-permute-start.15 = (bf16[128,1536]{1,0:T(8,128)(2,1)S(1)}, bf16[128,1536]{1,0:T(8,128)(2,1)S(1)}, u32[]{:S(2)}, u32[]{:S(2)}) collective-permute-start(bf16[128,1536]{1,0:T(8,128)(2,1)S(1)} %constant_dynamic-update-slice_fusion.refs_0_), channel_id=1, source_target_pairs={{0,1},{1,0},{2,3},{3,2},{4,5},{5,4},{6,7},{7,6},{8,9},{9,8},{10,11... | collective-permute-start | bytes 1179656 | tf_op jit(solution)/shard_map/ppermute | solution.py:48
  78.1 4.5 %collective-permute-start.18 = (bf16[128,1536]{1,0:T(8,128)(2,1)S(1)}, bf16[128,1536]{1,0:T(8,128)(2,1)S(1)}, u32[]{:S(2)}, u32[]{:S(2)}) collective-permute-start(bf16[128,1536]{1,0:T(8,128)(2,1)S(1)} %collective-permute-done.8.refs_3_), channel_id=1, source_target_pairs={{0,1},{1,0},{2,3},{3,2},{4,5},{5,4},{6,7},{7,6},{8,9},{9,8},{10,11... | collective-permute-start | bytes 1179656 | tf_op jit(solution)/shard_map/ppermute | solution.py:48
  78.1 4.5 %collective-permute-start.16 = (bf16[128,1536]{1,0:T(8,128)(2,1)S(1)}, bf16[128,1536]{1,0:T(8,128)(2,1)S(1)}, u32[]{:S(2)}, u32[]{:S(2)}) collective-permute-start(bf16[128,1536]{1,0:T(8,128)(2,1)S(1)} %collective-permute-done.6.refs_1_), channel_id=1, source_target_pairs={{0,1},{1,0},{2,3},{3,2},{4,5},{5,4},{6,7},{7,6},{8,9},{9,8},{10,11... | collective-permute-start | bytes 1179656 | tf_op jit(solution)/shard_map/ppermute | solution.py:48
  82.5 12.5 %collective-permute-start.39 = (bf16[512,1536]{1,0:T(8,128)(2,1)S(1)}, bf16[512,1536]{1,0:T(8,128)(2,1)S(1)}, u32[]{:S(2)}, u32[]{:S(2)}) collective-permute-start(bf16[512,1536]{1,0:T(8,128)(2,1)S(1)} %expert_rows.7), channel_id=1, source_target_pairs={{0,1},{1,0},{2,3},{3,2},{4,5},{5,4},{6,7},{7,6},{8,9},{9,8},{10,11... | collective-permute-start | bytes 4718600 | tf_op jit(solution)/shard_map/ppermute | solution.py:48
  82.6 4.4 %copy-start.11 = (bf16[1536]{0:T(1024)(128)(2,1)S(1)}, bf16[1536]{0:T(1024)(128)(2,1)}, u32[]{:S(2)}) copy-start(bf16[1536]{0:T(1024)(128)(2,1)} %param.16) | copy-start | bytes 9220
  86.5 10.0 %collective-permute-start.19 = (bf16[512,1536]{1,0:T(8,128)(2,1)S(1)}, bf16[512,1536]{1,0:T(8,128)(2,1)S(1)}, u32[]{:S(2)}, u32[]{:S(2)}) collective-permute-start(bf16[512,1536]{1,0:T(8,128)(2,1)S(1)} %expert_rows.5), channel_id=1, source_target_pairs={{0,1},{1,0},{2,3},{3,2},{4,5},{5,4},{6,7},{7,6},{8,9},{9,8},{10,11... | collective-permute-start | bytes 4718600 | tf_op jit(solution)/shard_map/ppermute | solution.py:48
  95.2 12.0 %collective-permute-start.40 = (bf16[128,1536]{1,0:T(8,128)(2,1)S(1)}, bf16[128,1536]{1,0:T(8,128)(2,1)S(1)}, u32[]{:S(2)}, u32[]{:S(2)}) collective-permute-start(bf16[128,1536]{1,0:T(8,128)(2,1)S(1)} %get-tuple-element.45), channel_id=1, source_target_pairs={{0,2},{1,3},{2,0},{3,1},{4,6},{5,7},{6,4},{7,5},{8,10},{9,11},{10,... | collective-permute-start | bytes 1179656 | tf_op jit(solution)/shard_map/ppermute | solution.py:44
  95.7 12.0 %collective-permute-start.42 = (bf16[128,1536]{1,0:T(8,128)(2,1)S(1)}, bf16[128,1536]{1,0:T(8,128)(2,1)S(1)}, u32[]{:S(2)}, u32[]{:S(2)}) collective-permute-start(bf16[128,1536]{1,0:T(8,128)(2,1)S(1)} %get-tuple-element.46), channel_id=1, source_target_pairs={{0,4},{4,0},{8,12},{12,8},{16,20},{20,16},{24,28},{28,24},{1,5},{5... | collective-permute-start | bytes 1179656 | tf_op jit(solution)/shard_map/ppermute | solution.py:40
  96.7 18.9 %collective-permute-start.20 = (bf16[128,1536]{1,0:T(8,128)(2,1)S(1)}, bf16[128,1536]{1,0:T(8,128)(2,1)S(1)}, u32[]{:S(2)}, u32[]{:S(2)}) collective-permute-start(bf16[128,1536]{1,0:T(8,128)(2,1)S(1)} %get-tuple-element.41), channel_id=1, source_target_pairs={{0,2},{1,3},{2,0},{3,1},{4,6},{5,7},{6,4},{7,5},{8,10},{9,11},{10,... | collective-permute-start | bytes 1179656 | tf_op jit(solution)/shard_map/ppermute | solution.py:44
  98.4 17.8 %collective-permute-start.22 = (bf16[128,1536]{1,0:T(8,128)(2,1)S(1)}, bf16[128,1536]{1,0:T(8,128)(2,1)S(1)}, u32[]{:S(2)}, u32[]{:S(2)}) collective-permute-start(bf16[128,1536]{1,0:T(8,128)(2,1)S(1)} %get-tuple-element.42), channel_id=1, source_target_pairs={{0,4},{4,0},{8,12},{12,8},{16,20},{20,16},{24,28},{28,24},{1,5},{5... | collective-permute-start | bytes 1179656 | tf_op jit(solution)/shard_map/ppermute | solution.py:40
  107.9 12.5 %collective-permute-start.41 = (bf16[64,1536]{1,0:T(8,128)(2,1)S(1)}, bf16[64,1536]{1,0:T(8,128)(2,1)S(1)}, u32[]{:S(2)}, u32[]{:S(2)}) collective-permute-start(bf16[64,1536]{1,0:T(8,128)(2,1)S(1)} %get-tuple-element.43), channel_id=1, source_target_pairs={{0,4},{4,0},{8,12},{12,8},{16,20},{20,16},{24,28},{28,24},{1,5},{5... | collective-permute-start | bytes 589832 | tf_op jit(solution)/shard_map/ppermute | solution.py:40
  108.8 11.7 %collective-permute-start.43 = (bf16[64,1536]{1,0:T(8,128)(2,1)S(1)}, bf16[64,1536]{1,0:T(8,128)(2,1)S(1)}, u32[]{:S(2)}, u32[]{:S(2)}) collective-permute-start(bf16[64,1536]{1,0:T(8,128)(2,1)S(1)} %get-tuple-element.44), channel_id=1, source_target_pairs={{0,2},{1,3},{2,0},{3,1},{4,6},{5,7},{6,4},{7,5},{8,10},{9,11},{10,... | collective-permute-start | bytes 589832 | tf_op jit(solution)/shard_map/ppermute | solution.py:44
  116.3 8.8 %collective-permute-start.21 = (bf16[64,1536]{1,0:T(8,128)(2,1)S(1)}, bf16[64,1536]{1,0:T(8,128)(2,1)S(1)}, u32[]{:S(2)}, u32[]{:S(2)}) collective-permute-start(bf16[64,1536]{1,0:T(8,128)(2,1)S(1)} %get-tuple-element.39), channel_id=1, source_target_pairs={{0,4},{4,0},{8,12},{12,8},{16,20},{20,16},{24,28},{28,24},{1,5},{5... | collective-permute-start | bytes 589832 | tf_op jit(solution)/shard_map/ppermute | solution.py:40
  117.2 8.1 %collective-permute-start.23 = (bf16[64,1536]{1,0:T(8,128)(2,1)S(1)}, bf16[64,1536]{1,0:T(8,128)(2,1)S(1)}, u32[]{:S(2)}, u32[]{:S(2)}) collective-permute-start(bf16[64,1536]{1,0:T(8,128)(2,1)S(1)} %get-tuple-element.40), channel_id=1, source_target_pairs={{0,2},{1,3},{2,0},{3,1},{4,6},{5,7},{6,4},{7,5},{8,10},{9,11},{10,... | collective-permute-start | bytes 589832 | tf_op jit(solution)/shard_map/ppermute | solution.py:44
  120.6 17.3 %copy-start.7 = (f32[32,1536]{1,0:T(8,128)S(1)}, f32[32,1536]{1,0:T(8,128)}, u32[]{:S(2)}) copy-start(f32[32,1536]{1,0:T(8,128)} %get-tuple-element.15) | copy-start | bytes 589828
  120.6 8.7 %collective-permute-start.44 = (bf16[32,1536]{1,0:T(8,128)(2,1)S(1)}, bf16[32,1536]{1,0:T(8,128)(2,1)S(1)}, u32[]{:S(2)}, u32[]{:S(2)}) collective-permute-start(bf16[32,1536]{1,0:T(8,128)(2,1)S(1)} %pad_maximum_fusion.8), channel_id=1, source_target_pairs={{0,24},{4,28},{8,0},{12,4},{16,8},{20,12},{24,16},{28,20},{1,25},{... | collective-permute-start | bytes 294920 | tf_op jit(solution)/shard_map/ppermute | solution.py:36
  123.0 14.9 %collective-permute-start.45 = (bf16[32,1536]{1,0:T(8,128)(2,1)S(1)}, bf16[32,1536]{1,0:T(8,128)(2,1)S(1)}, u32[]{:S(2)}, u32[]{:S(2)}) collective-permute-start(bf16[32,1536]{1,0:T(8,128)(2,1)S(1)} %pad_maximum_fusion.9), channel_id=1, source_target_pairs={{0,16},{4,20},{8,24},{12,28},{16,0},{20,4},{24,8},{28,12},{1,17},{... | collective-permute-start | bytes 294920 | tf_op jit(solution)/shard_map/ppermute | solution.py:36
  125.1 15.2 %copy-start.6 = (f32[32,1536]{1,0:T(8,128)S(1)}, f32[32,1536]{1,0:T(8,128)}, u32[]{:S(2)}) copy-start(f32[32,1536]{1,0:T(8,128)} %get-tuple-element.13) | copy-start | bytes 589828
  125.1 12.9 %collective-permute-start.46 = (bf16[32,1536]{1,0:T(8,128)(2,1)S(1)}, bf16[32,1536]{1,0:T(8,128)(2,1)S(1)}, u32[]{:S(2)}, u32[]{:S(2)}) collective-permute-start(bf16[32,1536]{1,0:T(8,128)(2,1)S(1)} %pad_maximum_fusion.10), channel_id=1, source_target_pairs={{0,8},{4,12},{8,16},{12,20},{16,24},{20,28},{24,0},{28,4},{1,9},{5... | collective-permute-start | bytes 294920 | tf_op jit(solution)/shard_map/ppermute | solution.py:36
  125.4 12.7 %collective-permute-start.24 = (bf16[32,1536]{1,0:T(8,128)(2,1)S(1)}, bf16[32,1536]{1,0:T(8,128)(2,1)S(1)}, u32[]{:S(2)}, u32[]{:S(2)}) collective-permute-start(bf16[32,1536]{1,0:T(8,128)(2,1)S(1)} %pad_maximum_fusion.5), channel_id=1, source_target_pairs={{0,24},{4,28},{8,0},{12,4},{16,8},{20,12},{24,16},{28,20},{1,25},{... | collective-permute-start | bytes 294920 | tf_op jit(solution)/shard_map/ppermute | solution.py:36
  129.2 11.0 %collective-permute-start.25 = (bf16[32,1536]{1,0:T(8,128)(2,1)S(1)}, bf16[32,1536]{1,0:T(8,128)(2,1)S(1)}, u32[]{:S(2)}, u32[]{:S(2)}) collective-permute-start(bf16[32,1536]{1,0:T(8,128)(2,1)S(1)} %pad_maximum_fusion.6), channel_id=1, source_target_pairs={{0,16},{4,20},{8,24},{12,28},{16,0},{20,4},{24,8},{28,12},{1,17},{... | collective-permute-start | bytes 294920 | tf_op jit(solution)/shard_map/ppermute | solution.py:36
  129.3 10.9 %collective-permute-start.26 = (bf16[32,1536]{1,0:T(8,128)(2,1)S(1)}, bf16[32,1536]{1,0:T(8,128)(2,1)S(1)}, u32[]{:S(2)}, u32[]{:S(2)}) collective-permute-start(bf16[32,1536]{1,0:T(8,128)(2,1)S(1)} %pad_maximum_fusion.7), channel_id=1, source_target_pairs={{0,8},{4,12},{8,16},{12,20},{16,24},{20,28},{24,0},{28,4},{1,9},{5... | collective-permute-start | bytes 294920 | tf_op jit(solution)/shard_map/ppermute | solution.py:36

commit v2 on v1

v2 whole, which is shorter than its diff:
```python
import functools

import jax
import jax.numpy as jnp
from jax import lax
from jax.experimental import pallas as pl
from jax.experimental.pallas import tpu as pltpu
from jax.sharding import PartitionSpec as P

EPSILON = 1e-06
CHUNKS = 2
LANES = 128
ROW_BLOCK = 512


def slot_of_pick(slot_expert, copy_pick, experts):
    count = slot_expert.shape[0]
    order = jnp.arange(count, dtype=jnp.int32)
    same = slot_expert[:, None] == slot_expert[None, :]
    before = order[None, :] < order[:, None]
    rank = jnp.sum((same & before).astype(jnp.int32), axis=1)
    holds = slot_expert[None, :] == jnp.arange(experts, dtype=jnp.int32)[:, None]
    copies = jnp.sum(holds.astype(jnp.int32), axis=1)
    wanted = copy_pick % copies[None, :]
    match = holds[None, :, :] & (rank[None, None, :] == wanted[:, :, None])
    return jnp.sum(match.astype(jnp.int32) * order[None, None, :], axis=2)


def rms_scaled(values, gain):
    mean_square = jnp.mean(values * values, axis=-1, keepdims=True)
    return values * lax.rsqrt(mean_square + EPSILON) * gain.astype(jnp.float32)


def turn(value, step):
    count = lax.axis_size("ep")
    return lax.ppermute(value, "ep", [(i, (i + 2 * step) % count) for i in range(count)])


def flip_inner(value):
    return lax.ppermute(value, "ep", [(i, i ^ 1) for i in range(lax.axis_size("ep"))])


def flip_upper(value):
    return lax.ppermute(value, "tp", [(i, i ^ 2) for i in range(lax.axis_size("tp"))])


def flip_lower(value):
    return lax.ppermute(value, "tp", [(i, i ^ 1) for i in range(lax.axis_size("tp"))])


VMEM = pl.BlockSpec(memory_space=pltpu.VMEM)
SMEM = pl.BlockSpec(memory_space=pltpu.SMEM)
ANY = pl.BlockSpec(memory_space=pl.ANY)


def attend_kernel(place_ref, context_ref, w_ref, send_ref, keep_ref):
    place = place_ref[0]
    quarter = send_ref.shape[1]
    rows = []
    for lower in (1, 0):
        for upper in (0, 1):
            start = pl.multiple_of((place ^ (upper * 2 + lower)) * quarter, quarter)
            rows.append(context_ref[pl.ds(start, quarter), :])
    rows = jnp.concatenate(rows, axis=0)
    width = w_ref.shape[1]
    tile = 512 if width % 512 == 0 else width
    for left in range(0, width, tile):
        out = jnp.dot(rows, w_ref[:, left : left + tile], preferred_element_type=jnp.float32)
        for upper in (0, 1):
            send_ref[upper, :, left : left + tile] = out[
                upper * quarter : (upper + 1) * quarter
            ].astype(jnp.bfloat16)
            keep_ref[upper, :, left : left + tile] = out[
                (upper + 2) * quarter : (upper + 3) * quarter
            ]


def attend(place, context, w_out):
    rows, _ = context.shape
    width = w_out.shape[1]
    quarter = rows // 4
    return pl.pallas_call(
        attend_kernel,
        out_shape=(
            jax.ShapeDtypeStruct((2, quarter, width), jnp.bfloat16),
            jax.ShapeDtypeStruct((2, quarter, width), jnp.float32),
        ),
        in_specs=[SMEM, VMEM, VMEM],
        out_specs=(VMEM, VMEM),
        compiler_params=pltpu.CompilerParams(vmem_limit_bytes=16 << 20),
        name="attend",
    )(place, context, w_out)


def norm_kernel(
    place_ref,
    keep_ref,
    lower_ref,
    upper_ref,
    resid_ref,
    gain_ref,
    ids_ref,
    router_ref,
    slot_hot_ref,
    middle_ref,
    row_ref,
):
    attention = (
        keep_ref[0] + lower_ref[0].astype(jnp.float32) + upper_ref[...].astype(jnp.float32)
    )
    middle = resid_ref[...].astype(jnp.float32) + attention
    middle_ref[...] = middle
    width = middle.shape[1]
    normed = rms_scaled(middle, gain_ref[...]).astype(jnp.bfloat16)
    row_ref[:, :width] = normed
    logits = jnp.dot(normed, router_ref[...], preferred_element_type=jnp.float32)
    expert = lax.broadcasted_iota(jnp.int32, logits.shape, 1)
    ids = ids_ref[...]
    hit = ids[:, 0:1] == expert
    for choice in range(1, ids.shape[1]):
        hit = hit | (ids[:, choice : choice + 1] == expert)
    raised = jnp.where(hit, jnp.exp(logits), 0.0)
    weights = (raised / jnp.sum(raised, axis=1, keepdims=True)).astype(jnp.bfloat16)
    row_ref[:, width:] = jnp.dot(
        weights, slot_hot_ref[...], preferred_element_type=jnp.float32
    ).astype(jnp.bfloat16)


def norm_rows(place, keep, from_lower, from_upper, resid, gain, ids, router, slot_hot, number):
    rows, width = from_upper.shape
    chunks = keep.shape[1] // rows
    extra = slot_hot.shape[1]

    def whole(array):
        return pl.BlockSpec(array.shape, lambda i, p: (0, 0))

    def mine(array):
        return pl.BlockSpec((rows, array.shape[1]), lambda i, p: (p[0] * chunks + number, 0))

    return pl.pallas_call(
        norm_kernel,
        out_shape=(
            jax.ShapeDtypeStruct((rows, width), jnp.float32),
            jax.ShapeDtypeStruct((rows, width + extra), jnp.bfloat16),
        ),
        grid_spec=pltpu.PrefetchScalarGridSpec(
            num_scalar_prefetch=1,
            grid=(1,),
            in_specs=[
                pl.BlockSpec((1, rows, width), lambda i, p: (0, number, 0)),
                pl.BlockSpec((1, rows, width), lambda i, p: (0, number, 0)),
                whole(from_upper),
                mine(resid),
                whole(gain),
                mine(ids),
                whole(router),
                whole(slot_hot),
            ],
            out_specs=[
                pl.BlockSpec((rows, width), lambda i, p: (0, 0)),
                pl.BlockSpec((rows, width + extra), lambda i, p: (0, 0)),
            ],
        ),
        compiler_params=pltpu.CompilerParams(vmem_limit_bytes=16 << 20),
        name="norm_rows",
    )(place, keep, from_lower, from_upper, resid, gain, ids, router, slot_hot)


def load_kernel(gate_hbm, up_hbm, down_hbm, both_ref, down_ref, sems):
    units = gate_hbm.shape[2]
    copies = [
        pltpu.make_async_copy(gate_hbm, both_ref.at[:, :, pl.ds(0, units)], sems.at[0]),
        pltpu.make_async_copy(up_hbm, both_ref.at[:, :, pl.ds(units, units)], sems.at[1]),
        pltpu.make_async_copy(down_hbm, down_ref, sems.at[2]),
    ]
    for copy in copies:
        copy.start()
    for copy in copies:
        copy.wait()


def load_weights(w_gate, w_up, w_down):
    held, width, units = w_gate.shape
    return pl.pallas_call(
        load_kernel,
        out_shape=(
            pltpu.VMEM((held, width, 2 * units), jnp.bfloat16),
            pltpu.VMEM((held * units, width), jnp.bfloat16),
        ),
        in_specs=[ANY] * 3,
        out_specs=(VMEM, VMEM),
        scratch_shapes=[pltpu.SemaphoreType.DMA((3,))],
        compiler_params=pltpu.CompilerParams(vmem_limit_bytes=2 << 20),
        name="load_weights",
    )(w_gate, w_up, w_down)


def expert_kernel(
    first_ref,
    near_ref,
    far_ref,
    other_near_ref,
    other_far_ref,
    both_ref,
    down_ref,
    near_out,
    far_out,
    other_near_out,
    other_far_out,
    rows_ref,
    hidden_ref,
):
    held, width, units = both_ref.shape
    units = units // 2
    start = 0
    for piece in (near_ref, far_ref, other_near_ref, other_far_ref):
        rows_ref[start : start + piece.shape[0]] = piece[...]
        start += piece.shape[0]
    block = min(ROW_BLOCK, start)
    extra = rows_ref.shape[1] - width
    mine = lax.broadcasted_iota(jnp.int32, (extra, LANES), 1) + first_ref[0]
    mine = (lax.broadcasted_iota(jnp.int32, (extra, LANES), 0) == mine).astype(jnp.bfloat16)
    tile = 512 if width % 512 == 0 else width

    def one_block(at):
        weights = jnp.dot(rows_ref[at, width:], mine, preferred_element_type=jnp.float32)
        for slot in range(held):
            out = jnp.dot(rows_ref[at, :width], both_ref[slot], preferred_element_type=jnp.float32)
            gate, upper = out[:, :units], out[:, units:]
            hidden = jax.nn.silu(gate) * upper * weights[:, slot : slot + 1]
            hidden_ref[:, slot * units : (slot + 1) * units] = hidden.astype(jnp.bfloat16)
        for left in range(0, width, tile):
            out = jnp.dot(
                hidden_ref[...],
                down_ref[:, left : left + tile],
                preferred_element_type=jnp.float32,
            ).astype(jnp.bfloat16)
            give(out, left)

    outs = (near_out, far_out, other_near_out, other_far_out)
    size = start // len(outs)
    for number in range(start // block):

        def give(out, left):
            for first in range(0, block, min(size, block)):
                piece, inside = divmod(number * block + first, size)
                part = min(size, block)
                to = slice(inside, inside + part)
                outs[piece][to, left : left + tile] = out[first : first + part]

        one_block(pl.ds(number * block, block))


def expert_rows(first, pieces, both, down):
    held, width, units = both.shape
    units = units // 2
    rows = sum(p.shape[0] for p in pieces)
    block = min(ROW_BLOCK, rows)
    return pl.pallas_call(
        expert_kernel,
        out_shape=[jax.ShapeDtypeStruct((p.shape[0], width), jnp.bfloat16) for p in pieces],
        in_specs=[SMEM] + [VMEM] * (len(pieces) + 2),
        out_specs=[VMEM] * len(pieces),
        scratch_shapes=[
            pltpu.VMEM((rows, pieces[0].shape[1]), jnp.bfloat16),
            pltpu.VMEM((block, held * units), jnp.bfloat16),
        ],
        compiler_params=pltpu.CompilerParams(vmem_limit_bytes=32 << 20),
        cost_estimate=pl.CostEstimate(
            flops=6 * rows * width * held * units,
            bytes_accessed=4 * rows * width + 6 * held * width * units,
            transcendentals=rows * held * units,
        ),
        name="expert_rows",
    )(first, *pieces, both, down)


def wide(value):
    return value.astype(jnp.float32)


def short(value):
    return value.astype(jnp.bfloat16)


def after(value, *others):
    return lax.optimization_barrier((value, others))[0]


def cut(value, start, size):
    return wide(lax.slice_in_dim(value, start, start + size, axis=0))


class Chunk:
    def __init__(self, rows):
        self.rows = rows
        self.outer = lax.axis_size("ep") // 2
        self.half = rows.shape[0] // 2

    def gather_outer(self, *then):
        rows = after(self.rows, *then)
        ring = [rows] + [turn(rows, step) for step in range(1, self.outer)]
        self.first = jnp.concatenate([r[: self.half] for r in ring], axis=0)
        self.second = jnp.concatenate([r[self.half :] for r in ring], axis=0)

    def gather_near(self, *then):
        first, second = after(self.first, *then), after(self.second, *then)
        self.first = jnp.concatenate([first, flip_inner(first)], axis=0)
        self.second = jnp.concatenate([second, flip_upper(second)], axis=0)

    def gather_far(self):
        self.far_pair = flip_upper(self.first), flip_inner(self.second)

    def gathered_far(self, *then):
        self.pieces = [
            jnp.concatenate([self.first, self.second], axis=0),
            jnp.concatenate(after(self.far_pair, *then), axis=0),
        ]

    def gather_lower(self, *then):
        self.others = [flip_lower(after(p, *then)) for p in self.pieces]

    def back_lower(self):
        self.got = [flip_lower(p) for p in self.away]

    def two(self, number, start, size):
        return cut(self.own[number], start, size) + cut(self.got[number], start, size)

    def back_far(self):
        size = self.own[0].shape[0] // 2
        self.far = short(self.two(1, 0, size)), short(self.two(1, size, size))
        self.far_first, self.far_second = flip_upper(self.far[0]), flip_inner(self.far[1])

    def back_near(self):
        part = self.own[0].shape[0] // 2
        size = part // 2
        first = short(self.two(0, size, size) + cut(self.far_first, size, size))
        second = short(self.two(0, part + size, size) + cut(self.far_second, size, size))
        self.near_first, self.near_second = flip_inner(first), flip_upper(second)

    def block(self, number):
        at, size, part = number * self.half, self.half, self.own[0].shape[0] // 2
        first = self.two(0, at, size) + cut(self.far_first, at, size)
        second = self.two(0, part + at, size) + cut(self.far_second, at, size)
        first = first + cut(self.near_first, at, size)
        second = second + cut(self.near_second, at, size)
        return jnp.concatenate([first, second], axis=0)

    def back_outer(self):
        self.total = self.block(0)
        self.turned = [turn(short(self.block(k)), -k) for k in range(1, self.outer)]

    def finish(self, middle, gain, *then):
        total = middle + self.total
        for turned in after(self.turned, *then):
            total = total + wide(turned)
        return rms_scaled(total, gain).astype(jnp.bfloat16)


def spread(rows):
    size = lax.axis_size("tp")
    both = lax.ppermute(rows, "tp", [(i, i ^ 3) for i in range(size)])
    return [rows, flip_lower(rows), flip_upper(rows), both]


def join_kernel(place_ref, *refs):
    last_ref, out_ref = refs[-2:]
    quarter = out_ref.shape[0] // 4
    size = refs[0].shape[0]
    for number, piece in enumerate(refs[:-2]):
        start = (place_ref[0] ^ number) * quarter
        out_ref[pl.ds(pl.multiple_of(start, size), size), :] = piece[...]
        out_ref[number * quarter + size : (number + 1) * quarter, :] = last_ref[number]


def join(place, pieces, last):
    rows, width = pieces[0].shape
    return pl.pallas_call(
        join_kernel,
        out_shape=jax.ShapeDtypeStruct((rows * 4 * CHUNKS, width), pieces[0].dtype),
        in_specs=[SMEM] + [VMEM] * (len(pieces) + 1),
        out_specs=VMEM,
        compiler_params=pltpu.CompilerParams(vmem_limit_bytes=16 << 20),
        name="join",
    )(place, *pieces, last)


def local(
    resid,
    context,
    w_out,
    pre_gain,
    final_gain,
    w_router,
    expert_ids,
    slot_expert,
    copy_pick,
    w_gate,
    w_up,
    w_down,
):
    held, width, units = w_gate.shape
    row_count = resid.shape[0]
    experts = w_router.shape[1]
    slots = slot_expert.shape[0]
    quarter = row_count // 4
    rows = quarter // CHUNKS
    place = lax.axis_index("tp").astype(jnp.int32).reshape(1)
    first = (lax.axis_index("ep") * held).astype(jnp.int32).reshape(1)
    down = w_down.reshape(held * units, width)

    send, keep = attend(place, context, w_out)
    got = flip_lower(send)
    table = slot_of_pick(after(slot_expert, send), copy_pick, experts)[0]
    lanes = -(-slots // LANES) * LANES
    slot_hot = table[:, None] == jnp.arange(lanes, dtype=jnp.int32)[None, :]
    slot_hot = slot_hot.astype(jnp.bfloat16)

    gain = pre_gain.reshape(1, -1)
    uppers = []
    for number in range(CHUNKS):
        at = slice(number * rows, (number + 1) * rows)
        uppers.append(flip_upper(short(keep[1, at] + wide(got[1, at]))))
    middles, chunks = [], []
    for number in range(CHUNKS):
        middle, row = norm_rows(
            place, keep, got, uppers[number], resid, gain, expert_ids, w_router, slot_hot, number
        )
        middles.append(middle)
        chunks.append(Chunk(row))

    both, down = load_weights(w_gate, w_up, after(down, uppers))

    def serve(chunk, *then):
        pieces = [after(p, *then) for p in chunk.pieces + chunk.others]
        outs = expert_rows(first, pieces, both, down)
        chunk.own, chunk.away = outs[:2], outs[2:]

    one, two = chunks
    one.gather_outer()
    one.gather_near()
    two.gather_outer(one.first)
    one.gather_far()
    two.gather_near()
    one.gathered_far()
    one.gather_lower(one.pieces[1])
    two.gather_far()
    serve(one, two.first, two.second)
    one.back_lower()
    two.gathered_far(one.away)
    two.gather_lower()
    one.back_far()
    serve(two, one.far)
    one.far_first, one.far_second = after((one.far_first, one.far_second), two.away)
    two.back_lower()
    one.back_near()
    two.back_far()
    one.near_first, one.near_second = after((one.near_first, one.near_second), two.far)
    one.back_outer()
    two.back_near()
    two.back_outer()
    result_one = one.finish(middles[0], final_gain)
    ready_one = spread(result_one)
    result_two = two.finish(middles[1], final_gain, result_one)
    return join(place, ready_one, lax.all_gather(result_two, "tp"))


def solution(mesh):
    return jax.shard_map(
        local,
        mesh=mesh,
        in_specs=(
            P("ep", None),
            P("ep", "tp"),
            P("tp", None),
            P(),
            P(),
            P(),
            P("ep", None),
            P(),
            P("ep", None),
            P("ep", None, "tp"),
            P("ep", None, "tp"),
            P("ep", "tp", None),
        ),
        out_specs=P("ep", None),
        check_vma=False,
    )
```

time: 150 us -> 124 us (0.83)
  starting transfers between devices: 53.6 us -> 42.9 us
  waiting for transfers between devices: 52 us -> 44 us
  Pallas kernels: 22.3 us -> 19.6 us
  blocking collectives: 8.67 us -> 6.42 us
  local copies, waits for them, and re-layouts: 7.82 us -> 5.95 us
    ppermute x11, waiting for transfers between devices: 21.3 us -> 6.09 us  [flip_upper(): lax.ppermute(value, 'tp', [(i, i ^ 2) for i in range(lax.axis_size('tp'))])]
    ppermute x15 -> x12, starting transfers between devices: 29.2 us -> 17.7 us  [turn(): lax.ppermute(value, 'ep', [(i, (i + 2 * step) % count) for i in range(cou...]
    ppermute x15 -> x12, waiting for transfers between devices: 12 us -> 16.2 us  [turn(): lax.ppermute(value, 'ep', [(i, (i + 2 * step) % count) for i in range(cou...]
    unnamed x27 -> x24, local copies, waits for them, and re-layouts: 2.92 us -> 5.79 us
    pallas_call x2, Pallas kernels: 3.75 us -> 1.05 us  [norm_rows(): pl.pallas_call(norm_kernel, out_shape=(jax.ShapeDtypeStruct((rows, width)...]
    pallas_call x4, Pallas kernels: 15.6 us -> 18 us  [the longest x2 16.1 us: expert_rows(): pl.pallas_call(expert_kernel, out_shape=[jax.ShapeDtypeStruct((p.shape[0]...]
    ppermute x9 -> x8, waiting for transfers between devices: 18.7 us -> 21.1 us  [flip_inner(): lax.ppermute(value, 'ep', [(i, i ^ 1) for i in range(lax.axis_size('ep'))])]
    pallas_call x1, Pallas kernels: 2.93 us -> 0.56 us  [attend(): pl.pallas_call(attend_kernel, out_shape=(jax.ShapeDtypeStruct((2, quarter...]
  transfers between devices with their start and end apart: 47 -> 42, of which waited for: 17 -> 19; matrix products, arithmetic and copies ran while one was open for 4% -> 4% of each run, Pallas kernels for 15% -> 15%
where the time goes in v2:
time: 124 us
  waiting for transfers between devices  44 us (35%)
  starting transfers between devices  42.9 us (35%)
  Pallas kernels  19.6 us (16%)
  blocking collectives  6.42 us (5%)
  local copies, waits for them, and re-layouts  5.95 us (5%)
  other arithmetic  4.63 us (4%)
    ppermute x8, waiting for transfers between devices, flip_inner(): lax.ppermute(value, 'ep', [(i, i ^ 1) for i in range(lax.axis_size('ep'))])  21.1 us
    ppermute x12, starting transfers between devices, turn(): lax.ppermute(value, 'ep', [(i, (i + 2 * step) % count) for i in range(cou...  17.7 us
    ppermute x12, waiting for transfers between devices, turn(): lax.ppermute(value, 'ep', [(i, (i + 2 * step) % count) for i in range(cou...  16.2 us
    pallas_call x2, Pallas kernels, expert_rows(): pl.pallas_call(expert_kernel, out_shape=[jax.ShapeDtypeStruct((p.shape[0]...  16.1 us
    ppermute x11, starting transfers between devices, flip_upper(): lax.ppermute(value, 'tp', [(i, i ^ 2) for i in range(lax.axis_size('tp'))])  12.4 us
    ppermute x8, starting transfers between devices, flip_inner(): lax.ppermute(value, 'ep', [(i, i ^ 1) for i in range(lax.axis_size('ep'))])  9.92 us
    all_gather x1, blocking collectives, local(): return join(place, ready_one, lax.all_gather(result_two, 'tp'))  6.42 us
    ppermute x11, waiting for transfers between devices, flip_upper(): lax.ppermute(value, 'tp', [(i, i ^ 2) for i in range(lax.axis_size('tp'))])  6.09 us
  transfers between devices with their start and end apart: 42, of which 19 were waited for; matrix products, arithmetic and copies ran while one was open for 4% of the time, Pallas kernels for 15%

profile of v2, /device:TPU:0, one launch (start us, length us, event | category | flops | bytes accessed | tf_op | source)
XLA Modules:
  0.0 124.0 jit_solution(3250187123922466812)
XLA Ops:
  0.0 1.3 %copy-done.4 = bf16[384,1536]{1,0:T(8,128)(2,1)S(1)} copy-done((bf16[384,1536]{1,0:T(8,128)(2,1)S(1)}, bf16[384,1536]{1,0:T(8,128)(2,1)}, u32[]{:S(2)}) %copy-start.4) | copy-done | bytes 1179672
  1.3 0.9 copy-done.5
  2.3 0.6 attend.1
  2.8 0.5 collective-permute-start
  3.4 0.9 convert_reduce_fusion
  4.3 0.8 fusion.11
  5.1 0.8 select_reduce_fusion
  6.0 2.6 %collective-permute-start.1 = (bf16[32,1536]{1,0:T(8,128)(2,1)S(1)}, bf16[32,1536]{1,0:T(8,128)(2,1)S(1)}, u32[]{:S(2)}, u32[]{:S(2)}) collective-permute-start(bf16[32,1536]{1,0:T(8,128)(2,1)S(1)} %get-tuple-element.122), channel_id=1, source_target_pairs={{0,2},{1,3},{2,0},{3,1},{4,6},{5,7},{6,4},{7,5},{8,10},{9,11},{10,... | collective-permute-start | bytes 294920 | tf_op jit(solution)/shard_map/ppermute | solution.py:44
  9.1 2.9 %collective-permute-done.1.upper_ref = bf16[32,1536]{1,0:T(8,128)(2,1)S(1)} collective-permute-done((bf16[32,1536]{1,0:T(8,128)(2,1)S(1)}, bf16[32,1536]{1,0:T(8,128)(2,1)S(1)}, u32[]{:S(2)}, u32[]{:S(2)}) %collective-permute-start.1) | collective-permute-done | bytes 98336 | tf_op jit(solution)/shard_map/ppermute | solution.py:44
  12.0 0.5 norm_rows.2
  12.6 2.1 %collective-permute-start.2 = (bf16[32,1664]{1,0:T(8,128)(2,1)S(1)}, bf16[32,1664]{1,0:T(8,128)(2,1)S(1)}, u32[]{:S(2)}, u32[]{:S(2)}) collective-permute-start(bf16[32,1664]{1,0:T(8,128)(2,1)S(1)} %get-tuple-element.52), channel_id=1, source_target_pairs={{0,8},{4,12},{8,16},{12,20},{16,24},{20,28},{24,0},{28,4},{1,9},{5... | collective-permute-start | bytes 319496 | tf_op jit(solution)/shard_map/ppermute | solution.py:36
  14.6 2.6 %collective-permute-start.3 = (bf16[32,1664]{1,0:T(8,128)(2,1)S(1)}, bf16[32,1664]{1,0:T(8,128)(2,1)S(1)}, u32[]{:S(2)}, u32[]{:S(2)}) collective-permute-start(bf16[32,1664]{1,0:T(8,128)(2,1)S(1)} %get-tuple-element.52), channel_id=1, source_target_pairs={{0,16},{4,20},{8,24},{12,28},{16,0},{20,4},{24,8},{28,12},{1,17},{... | collective-permute-start | bytes 319496 | tf_op jit(solution)/shard_map/ppermute | solution.py:36
  17.2 1.3 %collective-permute-start.4 = (bf16[32,1664]{1,0:T(8,128)(2,1)S(1)}, bf16[32,1664]{1,0:T(8,128)(2,1)S(1)}, u32[]{:S(2)}, u32[]{:S(2)}) collective-permute-start(bf16[32,1664]{1,0:T(8,128)(2,1)S(1)} %get-tuple-element.52), channel_id=1, source_target_pairs={{0,24},{4,28},{8,0},{12,4},{16,8},{20,12},{24,16},{28,20},{1,25},{... | collective-permute-start | bytes 319496 | tf_op jit(solution)/shard_map/ppermute | solution.py:36
  18.6 1.5 %copy-done.2 = bf16[5,1536,128]{2,1,0:T(8,128)(2,1)S(1)} copy-done((bf16[5,1536,128]{2,1,0:T(8,128)(2,1)S(1)}, bf16[5,1536,128]{2,1,0:T(8,128)(2,1)}, u32[]{:S(2)}) %copy-start.2) | copy-done | bytes 1966104
  20.1 1.5 %copy-done.3 = bf16[5,128,1536]{2,1,0:T(8,128)(2,1)S(1)} copy-done((bf16[5,128,1536]{2,1,0:T(8,128)(2,1)S(1)}, bf16[5,128,1536]{2,1,0:T(8,128)(2,1)}, u32[]{:S(2)}) %copy-start.3) | copy-done | bytes 1966104
  21.7 1.0 load_weights.1
  22.7 0.5 norm_rows.3
  23.2 0.7 collective-permute-done.3
  24.0 1.6 %collective-permute-start.5 = (bf16[64,1664]{1,0:T(8,128)(2,1)S(1)}, bf16[64,1664]{1,0:T(8,128)(2,1)S(1)}, u32[]{:S(2)}, u32[]{:S(2)}) collective-permute-start(bf16[64,1664]{1,0:T(8,128)(2,1)S(1)} %pad_maximum_fusion.6), channel_id=1, source_target_pairs={{0,4},{4,0},{8,12},{12,8},{16,20},{20,16},{24,28},{28,24},{1,5},{5... | collective-permute-start | bytes 638984 | tf_op jit(solution)/shard_map/ppermute | solution.py:40
  25.6 1.6 %collective-permute-start.6 = (bf16[64,1664]{1,0:T(8,128)(2,1)S(1)}, bf16[64,1664]{1,0:T(8,128)(2,1)S(1)}, u32[]{:S(2)}, u32[]{:S(2)}) collective-permute-start(bf16[64,1664]{1,0:T(8,128)(2,1)S(1)} %pad_maximum_fusion.7), channel_id=1, source_target_pairs={{0,2},{1,3},{2,0},{3,1},{4,6},{5,7},{6,4},{7,5},{8,10},{9,11},{10,... | collective-permute-start | bytes 638984 | tf_op jit(solution)/shard_map/ppermute | solution.py:44
  27.3 3.8 %collective-permute-done.5 = bf16[64,1664]{1,0:T(8,128)(2,1)S(1)} collective-permute-done((bf16[64,1664]{1,0:T(8,128)(2,1)S(1)}, bf16[64,1664]{1,0:T(8,128)(2,1)S(1)}, u32[]{:S(2)}, u32[]{:S(2)}) %collective-permute-start.5) | collective-permute-done | bytes 213024 | tf_op jit(solution)/shard_map/ppermute | solution.py:40
  31.1 1.4 %collective-permute-start.13 = (bf16[128,1664]{1,0:T(8,128)(2,1)S(1)}, bf16[128,1664]{1,0:T(8,128)(2,1)S(1)}, u32[]{:S(2)}, u32[]{:S(2)}) collective-permute-start(bf16[128,1664]{1,0:T(8,128)(2,1)S(1)} %pad_maximum_fusion.2), channel_id=1, source_target_pairs={{0,2},{1,3},{2,0},{3,1},{4,6},{5,7},{6,4},{7,5},{8,10},{9,11},{10,... | collective-permute-start | bytes 1277960 | tf_op jit(solution)/shard_map/ppermute | solution.py:44
  32.6 2.8 %collective-permute-start.8 = (bf16[32,1664]{1,0:T(8,128)(2,1)S(1)}, bf16[32,1664]{1,0:T(8,128)(2,1)S(1)}, u32[]{:S(2)}, u32[]{:S(2)}) collective-permute-start(bf16[32,1664]{1,0:T(8,128)(2,1)S(1)} %get-tuple-element.54), channel_id=1, source_target_pairs={{0,8},{4,12},{8,16},{12,20},{16,24},{20,28},{24,0},{28,4},{1,9},{5... | collective-permute-start | bytes 319496 | tf_op jit(solution)/shard_map/ppermute | solution.py:36
  35.8 1.9 %collective-permute-start.10 = (bf16[32,1664]{1,0:T(8,128)(2,1)S(1)}, bf16[32,1664]{1,0:T(8,128)(2,1)S(1)}, u32[]{:S(2)}, u32[]{:S(2)}) collective-permute-start(bf16[32,1664]{1,0:T(8,128)(2,1)S(1)} %get-tuple-element.54), channel_id=1, source_target_pairs={{0,24},{4,28},{8,0},{12,4},{16,8},{20,12},{24,16},{28,20},{1,25},{... | collective-permute-start | bytes 319496 | tf_op jit(solution)/shard_map/ppermute | solution.py:36
  37.8 1.6 %collective-permute-start.14 = (bf16[128,1664]{1,0:T(8,128)(2,1)S(1)}, bf16[128,1664]{1,0:T(8,128)(2,1)S(1)}, u32[]{:S(2)}, u32[]{:S(2)}) collective-permute-start(bf16[128,1664]{1,0:T(8,128)(2,1)S(1)} %pad_maximum_fusion.5), channel_id=1, source_target_pairs={{0,4},{4,0},{8,12},{12,8},{16,20},{20,16},{24,28},{28,24},{1,5},{5... | collective-permute-start | bytes 1277960 | tf_op jit(solution)/shard_map/ppermute | solution.py:40
  39.5 0.8 collective-permute-done.8
  40.3 3.2 %collective-permute-done.9 = bf16[32,1664]{1,0:T(8,128)(2,1)S(1)} collective-permute-done((bf16[32,1664]{1,0:T(8,128)(2,1)S(1)}, bf16[32,1664]{1,0:T(8,128)(2,1)S(1)}, u32[]{:S(2)}, u32[]{:S(2)}) %collective-permute-start.9) | collective-permute-done | bytes 106528 | tf_op jit(solution)/shard_map/ppermute | solution.py:36
  43.6 0.7 collective-permute-start.12
  44.3 3.5 %collective-permute-done.14 = bf16[128,1664]{1,0:T(8,128)(2,1)S(1)} collective-permute-done((bf16[128,1664]{1,0:T(8,128)(2,1)S(1)}, bf16[128,1664]{1,0:T(8,128)(2,1)S(1)}, u32[]{:S(2)}, u32[]{:S(2)}) %collective-permute-start.14) | collective-permute-done | bytes 426016 | tf_op jit(solution)/shard_map/ppermute | solution.py:40
  48.0 0.5 collective-permute-start.15
  48.5 1.6 %collective-permute-start.11 = (bf16[64,1664]{1,0:T(8,128)(2,1)S(1)}, bf16[64,1664]{1,0:T(8,128)(2,1)S(1)}, u32[]{:S(2)}, u32[]{:S(2)}) collective-permute-start(bf16[64,1664]{1,0:T(8,128)(2,1)S(1)} %pad_maximum_fusion.8), channel_id=1, source_target_pairs={{0,4},{4,0},{8,12},{12,8},{16,20},{20,16},{24,28},{28,24},{1,5},{5... | collective-permute-start | bytes 638984 | tf_op jit(solution)/shard_map/ppermute | solution.py:40
  50.1 1.0 collective-permute-start.22
  51.1 5.6 %collective-permute-done.11 = bf16[64,1664]{1,0:T(8,128)(2,1)S(1)} collective-permute-done((bf16[64,1664]{1,0:T(8,128)(2,1)S(1)}, bf16[64,1664]{1,0:T(8,128)(2,1)S(1)}, u32[]{:S(2)}, u32[]{:S(2)}) %collective-permute-start.11) | collective-permute-done | bytes 213024 | tf_op jit(solution)/shard_map/ppermute | solution.py:40
  56.7 0.8 collective-permute-start.21
  57.7 8.0 %expert_rows.2 = (bf16[256,1536]{1,0:T(8,128)(2,1)S(1)}, bf16[256,1536]{1,0:T(8,128)(2,1)S(1)}, bf16[256,1536]{1,0:T(8,128)(2,1)S(1)}, bf16[256,1536]{1,0:T(8,128)(2,1)S(1)}) custom-call(s32[1]{0:T(128)} %bitcast.4.first_ref, bf16[256,1664]{1,0:T(8,128)(2,1)S(1)} %pad_maximum_fusion.near_ref, ...), custom_call_target="tpu_custom_call" | custom-call | flops 6039797760 | bytes 12189696 | tf_op jit(solution)/shard_map/expert_rows/pallas_call | solution.py:259
  65.7 0.5 collective-permute-start.18
  66.2 0.6 collective-permute-done.21
  67.0 0.5 collective-permute-start.17
  67.5 0.6 collective-permute-done.18
  68.3 1.3 %collective-permute-start.19 = (bf16[128,1536]{1,0:T(8,128)(2,1)S(1)}, bf16[128,1536]{1,0:T(8,128)(2,1)S(1)}, u32[]{:S(2)}, u32[]{:S(2)}) collective-permute-start(bf16[128,1536]{1,0:T(8,128)(2,1)S(1)} %get-tuple-element.120), channel_id=1, source_target_pairs={{0,2},{1,3},{2,0},{3,1},{4,6},{5,7},{6,4},{7,5},{8,10},{9,11},{10,... | collective-permute-start | bytes 1179656 | tf_op jit(solution)/shard_map/ppermute | solution.py:44
  69.7 1.5 %collective-permute-start.20 = (bf16[128,1536]{1,0:T(8,128)(2,1)S(1)}, bf16[128,1536]{1,0:T(8,128)(2,1)S(1)}, u32[]{:S(2)}, u32[]{:S(2)}) collective-permute-start(bf16[128,1536]{1,0:T(8,128)(2,1)S(1)} %get-tuple-element.119), channel_id=1, source_target_pairs={{0,4},{4,0},{8,12},{12,8},{16,20},{20,16},{24,28},{28,24},{1,5},{5... | collective-permute-start | bytes 1179656 | tf_op jit(solution)/shard_map/ppermute | solution.py:40
  71.2 8.2 %expert_rows.3 = (bf16[256,1536]{1,0:T(8,128)(2,1)S(1)}, bf16[256,1536]{1,0:T(8,128)(2,1)S(1)}, bf16[256,1536]{1,0:T(8,128)(2,1)S(1)}, bf16[256,1536]{1,0:T(8,128)(2,1)S(1)}) custom-call(s32[1]{0:T(128)} %bitcast.4.first_ref, bf16[256,1664]{1,0:T(8,128)(2,1)S(1)} %pad_maximum_fusion.1.near_ref, ...), custom_call_target="tpu_custom_call" | custom-call | flops 6039797760 | bytes 12189696 | tf_op jit(solution)/shard_map/expert_rows/pallas_call | solution.py:259
  79.4 0.5 collective-permute-start.34
  79.9 0.8 collective-permute-done.20
  80.9 1.6 %collective-permute-start.25 = (bf16[64,1536]{1,0:T(8,128)(2,1)S(1)}, bf16[64,1536]{1,0:T(8,128)(2,1)S(1)}, u32[]{:S(2)}, u32[]{:S(2)}) collective-permute-start(bf16[64,1536]{1,0:T(8,128)(2,1)S(1)} %get-tuple-element.118), channel_id=1, source_target_pairs={{0,4},{4,0},{8,12},{12,8},{16,20},{20,16},{24,28},{28,24},{1,5},{5... | collective-permute-start | bytes 589832 | tf_op jit(solution)/shard_map/ppermute | solution.py:40
  82.5 0.5 collective-permute-start.26
  83.2 1.6 %collective-permute-start.35 = (bf16[128,1536]{1,0:T(8,128)(2,1)S(1)}, bf16[128,1536]{1,0:T(8,128)(2,1)S(1)}, u32[]{:S(2)}, u32[]{:S(2)}) collective-permute-start(bf16[128,1536]{1,0:T(8,128)(2,1)S(1)} %get-tuple-element.116), channel_id=1, source_target_pairs={{0,2},{1,3},{2,0},{3,1},{4,6},{5,7},{6,4},{7,5},{8,10},{9,11},{10,... | collective-permute-start | bytes 1179656 | tf_op jit(solution)/shard_map/ppermute | solution.py:44
  84.8 0.5 collective-permute-start.37
  85.3 2.9 %collective-permute-done.25 = bf16[64,1536]{1,0:T(8,128)(2,1)S(1)} collective-permute-done((bf16[64,1536]{1,0:T(8,128)(2,1)S(1)}, bf16[64,1536]{1,0:T(8,128)(2,1)S(1)}, u32[]{:S(2)}, u32[]{:S(2)}) %collective-permute-start.25) | collective-permute-done | bytes 196640 | tf_op jit(solution)/shard_map/ppermute | solution.py:40
  88.2 2.1 %collective-permute-done.26 = bf16[64,1536]{1,0:T(8,128)(2,1)S(1)} collective-permute-done((bf16[64,1536]{1,0:T(8,128)(2,1)S(1)}, bf16[64,1536]{1,0:T(8,128)(2,1)S(1)}, u32[]{:S(2)}, u32[]{:S(2)}) %collective-permute-start.26) | collective-permute-done | bytes 196640 | tf_op jit(solution)/shard_map/ppermute | solution.py:44
  90.6 2.3 %collective-permute-start.29 = (bf16[32,1536]{1,0:T(8,128)(2,1)S(1)}, bf16[32,1536]{1,0:T(8,128)(2,1)S(1)}, u32[]{:S(2)}, u32[]{:S(2)}) collective-permute-start(bf16[32,1536]{1,0:T(8,128)(2,1)S(1)} %pad_maximum_fusion.11), channel_id=1, source_target_pairs={{0,16},{4,20},{8,24},{12,28},{16,0},{20,4},{24,8},{28,12},{1,17},{... | collective-permute-start | bytes 294920 | tf_op jit(solution)/shard_map/ppermute | solution.py:36
  93.0 4.2 %collective-permute-done.30 = bf16[32,1536]{1,0:T(8,128)(2,1)S(1)} collective-permute-done((bf16[32,1536]{1,0:T(8,128)(2,1)S(1)}, bf16[32,1536]{1,0:T(8,128)(2,1)S(1)}, u32[]{:S(2)}, u32[]{:S(2)}) %collective-permute-start.30) | collective-permute-done | bytes 98336 | tf_op jit(solution)/shard_map/ppermute | solution.py:36
  97.4 1.0 collective-permute-done.29
  98.4 3.5 %collective-permute-done.28 = bf16[32,1536]{1,0:T(8,128)(2,1)S(1)} collective-permute-done((bf16[32,1536]{1,0:T(8,128)(2,1)S(1)}, bf16[32,1536]{1,0:T(8,128)(2,1)S(1)}, u32[]{:S(2)}, u32[]{:S(2)}) %collective-permute-start.28) | collective-permute-done | bytes 98336 | tf_op jit(solution)/shard_map/ppermute | solution.py:36
  102.2 0.6 collective-permute-start.36
  102.8 0.8 collective-permute-start.38
  103.6 4.4 %collective-permute-done.36 = bf16[64,1536]{1,0:T(8,128)(2,1)S(1)} collective-permute-done((bf16[64,1536]{1,0:T(8,128)(2,1)S(1)}, bf16[64,1536]{1,0:T(8,128)(2,1)S(1)}, u32[]{:S(2)}, u32[]{:S(2)}) %collective-permute-start.36) | collective-permute-done | bytes 196640 | tf_op jit(solution)/shard_map/ppermute | solution.py:40
  108.7 2.5 %collective-permute-start.40 = (bf16[32,1536]{1,0:T(8,128)(2,1)S(1)}, bf16[32,1536]{1,0:T(8,128)(2,1)S(1)}, u32[]{:S(2)}, u32[]{:S(2)}) collective-permute-start(bf16[32,1536]{1,0:T(8,128)(2,1)S(1)} %pad_maximum_fusion.14), channel_id=1, source_target_pairs={{0,16},{4,20},{8,24},{12,28},{16,0},{20,4},{24,8},{28,12},{1,17},{... | collective-permute-start | bytes 294920 | tf_op jit(solution)/shard_map/ppermute | solution.py:36
  111.1 1.4 %collective-permute-start.39 = (bf16[32,1536]{1,0:T(8,128)(2,1)S(1)}, bf16[32,1536]{1,0:T(8,128)(2,1)S(1)}, u32[]{:S(2)}, u32[]{:S(2)}) collective-permute-start(bf16[32,1536]{1,0:T(8,128)(2,1)S(1)} %pad_maximum_fusion.13), channel_id=1, source_target_pairs={{0,24},{4,28},{8,0},{12,4},{16,8},{20,12},{24,16},{28,20},{1,25},{... | collective-permute-start | bytes 294920 | tf_op jit(solution)/shard_map/ppermute | solution.py:36
  112.8 0.8 collective-permute-start.32
  113.6 1.6 %collective-permute-done.41 = bf16[32,1536]{1,0:T(8,128)(2,1)S(1)} collective-permute-done((bf16[32,1536]{1,0:T(8,128)(2,1)S(1)}, bf16[32,1536]{1,0:T(8,128)(2,1)S(1)}, u32[]{:S(2)}, u32[]{:S(2)}) %collective-permute-start.41) | collective-permute-done | bytes 98336 | tf_op jit(solution)/shard_map/ppermute | solution.py:36
  115.2 1.2 collective-permute-done.40
  116.6 6.4 %all-gather = bf16[128,1536]{1,0:T(8,128)(2,1)S(1)} all-gather(bf16[32,1536]{1,0:T(8,128)(2,1)S(1)} %multiply_convert_fusion), channel_id=2, replica_groups=mesh['ep'=8,'tp'=4] {'tp'}, dimensions={0}, use_global_device_ids=true | all-gather | bytes 491520 | tf_op jit(solution)/shard_map/all_gather | solution.py:465
  123.1 0.9 join.1
  (99 shorter events, 4.4 us)
Async XLA Ops:
  0.0 12.0 %copy-start = (bf16[256,1536]{1,0:T(8,128)(2,1)S(1)}, bf16[256,1536]{1,0:T(8,128)(2,1)}, u32[]{:S(2)}) copy-start(bf16[256,1536]{1,0:T(8,128)(2,1)} %resid_ref.3) | copy-start | bytes 2359300
  0.0 1.3 %copy-start.4 = (bf16[384,1536]{1,0:T(8,128)(2,1)S(1)}, bf16[384,1536]{1,0:T(8,128)(2,1)}, u32[]{:S(2)}) copy-start(bf16[384,1536]{1,0:T(8,128)(2,1)} %w_ref.1) | copy-start | bytes 3538948
  1.3 0.9 copy-start.5
  2.3 6.3 %copy-start.6 = (bf16[1536,40]{0,1:T(8,128)(2,1)S(1)}, bf16[1536,40]{0,1:T(8,128)(2,1)}, u32[]{:S(2)}) copy-start(bf16[1536,40]{0,1:T(8,128)(2,1)} %param.17) | copy-start | bytes 368644
  2.3 6.6 %copy-start.7 = (s32[256,8]{0,1:T(8,128)S(1)}, s32[256,8]{0,1:T(8,128)}, u32[]{:S(2)}) copy-start(s32[256,8]{0,1:T(8,128)} %param.18) | copy-start | bytes 24580
  2.3 6.7 %copy-start.9 = (bf16[1536]{0:T(1024)(128)(2,1)S(1)}, bf16[1536]{0:T(1024)(128)(2,1)}, u32[]{:S(2)}) copy-start(bf16[1536]{0:T(1024)(128)(2,1)} %param.15) | copy-start | bytes 9220
  2.8 3.1 %collective-permute-start = (bf16[2,64,1536]{2,1,0:T(8,128)(2,1)S(1)}, bf16[2,64,1536]{2,1,0:T(8,128)(2,1)S(1)}, u32[]{:S(2)}, u32[]{:S(2)}) collective-permute-start(bf16[2,64,1536]{2,1,0:T(8,128)(2,1)S(1)} %get-tuple-element.49), channel_id=1, source_target_pairs={{0,1},{1,0},{2,3},{3,2},{4,5},{5,4},{6,7},{7,6},{8,9},{9,8},{10,11... | collective-permute-start | bytes 1179656 | tf_op jit(solution)/shard_map/ppermute | solution.py:48
  6.0 6.1 %collective-permute-start.1 = (bf16[32,1536]{1,0:T(8,128)(2,1)S(1)}, bf16[32,1536]{1,0:T(8,128)(2,1)S(1)}, u32[]{:S(2)}, u32[]{:S(2)}) collective-permute-start(bf16[32,1536]{1,0:T(8,128)(2,1)S(1)} %get-tuple-element.122), channel_id=1, source_target_pairs={{0,2},{1,3},{2,0},{3,1},{4,6},{5,7},{6,4},{7,5},{8,10},{9,11},{10,... | collective-permute-start | bytes 294920 | tf_op jit(solution)/shard_map/ppermute | solution.py:44
  9.0 9.5 %copy-start.1 = (bf16[5,1536,128]{2,1,0:T(8,128)(2,1)S(1)}, bf16[5,1536,128]{2,1,0:T(8,128)(2,1)}, u32[]{:S(2)}) copy-start(bf16[5,1536,128]{2,1,0:T(8,128)(2,1)} %gate_hbm.1) | copy-start | bytes 5898244
  9.0 9.5 %collective-permute-start.7 = (bf16[32,1536]{1,0:T(8,128)(2,1)S(1)}, bf16[32,1536]{1,0:T(8,128)(2,1)S(1)}, u32[]{:S(2)}, u32[]{:S(2)}) collective-permute-start(bf16[32,1536]{1,0:T(8,128)(2,1)S(1)} %get-tuple-element.121), channel_id=1, source_target_pairs={{0,2},{1,3},{2,0},{3,1},{4,6},{5,7},{6,4},{7,5},{8,10},{9,11},{10,... | collective-permute-start | bytes 294920 | tf_op jit(solution)/shard_map/ppermute | solution.py:44
  12.6 10.6 %collective-permute-start.2 = (bf16[32,1664]{1,0:T(8,128)(2,1)S(1)}, bf16[32,1664]{1,0:T(8,128)(2,1)S(1)}, u32[]{:S(2)}, u32[]{:S(2)}) collective-permute-start(bf16[32,1664]{1,0:T(8,128)(2,1)S(1)} %get-tuple-element.52), channel_id=1, source_target_pairs={{0,8},{4,12},{8,16},{12,20},{16,24},{20,28},{24,0},{28,4},{1,9},{5... | collective-permute-start | bytes 319496 | tf_op jit(solution)/shard_map/ppermute | solution.py:36
  14.6 9.3 %collective-permute-start.3 = (bf16[32,1664]{1,0:T(8,128)(2,1)S(1)}, bf16[32,1664]{1,0:T(8,128)(2,1)S(1)}, u32[]{:S(2)}, u32[]{:S(2)}) collective-permute-start(bf16[32,1664]{1,0:T(8,128)(2,1)S(1)} %get-tuple-element.52), channel_id=1, source_target_pairs={{0,16},{4,20},{8,24},{12,28},{16,0},{20,4},{24,8},{28,12},{1,17},{... | collective-permute-start | bytes 319496 | tf_op jit(solution)/shard_map/ppermute | solution.py:36
  17.2 6.8 %collective-permute-start.4 = (bf16[32,1664]{1,0:T(8,128)(2,1)S(1)}, bf16[32,1664]{1,0:T(8,128)(2,1)S(1)}, u32[]{:S(2)}, u32[]{:S(2)}) collective-permute-start(bf16[32,1664]{1,0:T(8,128)(2,1)S(1)} %get-tuple-element.52), channel_id=1, source_target_pairs={{0,24},{4,28},{8,0},{12,4},{16,8},{20,12},{24,16},{28,20},{1,25},{... | collective-permute-start | bytes 319496 | tf_op jit(solution)/shard_map/ppermute | solution.py:36
  18.6 1.5 %copy-start.2 = (bf16[5,1536,128]{2,1,0:T(8,128)(2,1)S(1)}, bf16[5,1536,128]{2,1,0:T(8,128)(2,1)}, u32[]{:S(2)}) copy-start(bf16[5,1536,128]{2,1,0:T(8,128)(2,1)} %up_hbm.1) | copy-start | bytes 5898244
  20.1 1.5 %copy-start.3 = (bf16[5,128,1536]{2,1,0:T(8,128)(2,1)S(1)}, bf16[5,128,1536]{2,1,0:T(8,128)(2,1)}, u32[]{:S(2)}) copy-start(bf16[5,128,1536]{2,1,0:T(8,128)(2,1)} %param.23) | copy-start | bytes 5898244
  24.0 7.1 %collective-permute-start.5 = (bf16[64,1664]{1,0:T(8,128)(2,1)S(1)}, bf16[64,1664]{1,0:T(8,128)(2,1)S(1)}, u32[]{:S(2)}, u32[]{:S(2)}) collective-permute-start(bf16[64,1664]{1,0:T(8,128)(2,1)S(1)} %pad_maximum_fusion.6), channel_id=1, source_target_pairs={{0,4},{4,0},{8,12},{12,8},{16,20},{20,16},{24,28},{28,24},{1,5},{5... | collective-permute-start | bytes 638984 | tf_op jit(solution)/shard_map/ppermute | solution.py:40
  25.6 12.1 %collective-permute-start.6 = (bf16[64,1664]{1,0:T(8,128)(2,1)S(1)}, bf16[64,1664]{1,0:T(8,128)(2,1)S(1)}, u32[]{:S(2)}, u32[]{:S(2)}) collective-permute-start(bf16[64,1664]{1,0:T(8,128)(2,1)S(1)} %pad_maximum_fusion.7), channel_id=1, source_target_pairs={{0,2},{1,3},{2,0},{3,1},{4,6},{5,7},{6,4},{7,5},{8,10},{9,11},{10,... | collective-permute-start | bytes 638984 | tf_op jit(solution)/shard_map/ppermute | solution.py:44
  31.1 16.7 %collective-permute-start.13 = (bf16[128,1664]{1,0:T(8,128)(2,1)S(1)}, bf16[128,1664]{1,0:T(8,128)(2,1)S(1)}, u32[]{:S(2)}, u32[]{:S(2)}) collective-permute-start(bf16[128,1664]{1,0:T(8,128)(2,1)S(1)} %pad_maximum_fusion.2), channel_id=1, source_target_pairs={{0,2},{1,3},{2,0},{3,1},{4,6},{5,7},{6,4},{7,5},{8,10},{9,11},{10,... | collective-permute-start | bytes 1277960 | tf_op jit(solution)/shard_map/ppermute | solution.py:44
  32.6 7.7 %collective-permute-start.8 = (bf16[32,1664]{1,0:T(8,128)(2,1)S(1)}, bf16[32,1664]{1,0:T(8,128)(2,1)S(1)}, u32[]{:S(2)}, u32[]{:S(2)}) collective-permute-start(bf16[32,1664]{1,0:T(8,128)(2,1)S(1)} %get-tuple-element.54), channel_id=1, source_target_pairs={{0,8},{4,12},{8,16},{12,20},{16,24},{20,28},{24,0},{28,4},{1,9},{5... | collective-permute-start | bytes 319496 | tf_op jit(solution)/shard_map/ppermute | solution.py:36
  35.4 8.1 %collective-permute-start.9 = (bf16[32,1664]{1,0:T(8,128)(2,1)S(1)}, bf16[32,1664]{1,0:T(8,128)(2,1)S(1)}, u32[]{:S(2)}, u32[]{:S(2)}) collective-permute-start(bf16[32,1664]{1,0:T(8,128)(2,1)S(1)} %get-tuple-element.54), channel_id=1, source_target_pairs={{0,16},{4,20},{8,24},{12,28},{16,0},{20,4},{24,8},{28,12},{1,17},{... | collective-permute-start | bytes 319496 | tf_op jit(solution)/shard_map/ppermute | solution.py:36
  35.8 7.7 %collective-permute-start.10 = (bf16[32,1664]{1,0:T(8,128)(2,1)S(1)}, bf16[32,1664]{1,0:T(8,128)(2,1)S(1)}, u32[]{:S(2)}, u32[]{:S(2)}) collective-permute-start(bf16[32,1664]{1,0:T(8,128)(2,1)S(1)} %get-tuple-element.54), channel_id=1, source_target_pairs={{0,24},{4,28},{8,0},{12,4},{16,8},{20,12},{24,16},{28,20},{1,25},{... | collective-permute-start | bytes 319496 | tf_op jit(solution)/shard_map/ppermute | solution.py:36
  37.8 10.0 %collective-permute-start.14 = (bf16[128,1664]{1,0:T(8,128)(2,1)S(1)}, bf16[128,1664]{1,0:T(8,128)(2,1)S(1)}, u32[]{:S(2)}, u32[]{:S(2)}) collective-permute-start(bf16[128,1664]{1,0:T(8,128)(2,1)S(1)} %pad_maximum_fusion.5), channel_id=1, source_target_pairs={{0,4},{4,0},{8,12},{12,8},{16,20},{20,16},{24,28},{28,24},{1,5},{5... | collective-permute-start | bytes 1277960 | tf_op jit(solution)/shard_map/ppermute | solution.py:40
  43.6 6.5 %collective-permute-start.12 = (bf16[64,1664]{1,0:T(8,128)(2,1)S(1)}, bf16[64,1664]{1,0:T(8,128)(2,1)S(1)}, u32[]{:S(2)}, u32[]{:S(2)}) collective-permute-start(bf16[64,1664]{1,0:T(8,128)(2,1)S(1)} %pad_maximum_fusion.9), channel_id=1, source_target_pairs={{0,2},{1,3},{2,0},{3,1},{4,6},{5,7},{6,4},{7,5},{8,10},{9,11},{10,... | collective-permute-start | bytes 638984 | tf_op jit(solution)/shard_map/ppermute | solution.py:44
  47.9 9.8 %collective-permute-start.16 = (bf16[256,1664]{1,0:T(8,128)(2,1)S(1)}, bf16[256,1664]{1,0:T(8,128)(2,1)S(1)}, u32[]{:S(2)}, u32[]{:S(2)}) collective-permute-start(bf16[256,1664]{1,0:T(8,128)(2,1)S(1)} %constant_dynamic-update-slice_fusion.far_ref), channel_id=1, source_target_pairs={{0,1},{1,0},{2,3},{3,2},{4,5},{5,4},{6,7},{7,6},{8,9},{9,8},{10,11... | collective-permute-start | bytes 2555912 | tf_op jit(solution)/shard_map/ppermute | solution.py:48
  48.0 9.7 %collective-permute-start.15 = (bf16[256,1664]{1,0:T(8,128)(2,1)S(1)}, bf16[256,1664]{1,0:T(8,128)(2,1)S(1)}, u32[]{:S(2)}, u32[]{:S(2)}) collective-permute-start(bf16[256,1664]{1,0:T(8,128)(2,1)S(1)} %pad_maximum_fusion.near_ref), channel_id=1, source_target_pairs={{0,1},{1,0},{2,3},{3,2},{4,5},{5,4},{6,7},{7,6},{8,9},{9,8},{10,11... | collective-permute-start | bytes 2555912 | tf_op jit(solution)/shard_map/ppermute | solution.py:48
  48.5 8.2 %collective-permute-start.11 = (bf16[64,1664]{1,0:T(8,128)(2,1)S(1)}, bf16[64,1664]{1,0:T(8,128)(2,1)S(1)}, u32[]{:S(2)}, u32[]{:S(2)}) collective-permute-start(bf16[64,1664]{1,0:T(8,128)(2,1)S(1)} %pad_maximum_fusion.8), channel_id=1, source_target_pairs={{0,4},{4,0},{8,12},{12,8},{16,20},{20,16},{24,28},{28,24},{1,5},{5... | collective-permute-start | bytes 638984 | tf_op jit(solution)/shard_map/ppermute | solution.py:40
  50.1 16.1 %collective-permute-start.22 = (bf16[128,1664]{1,0:T(8,128)(2,1)S(1)}, bf16[128,1664]{1,0:T(8,128)(2,1)S(1)}, u32[]{:S(2)}, u32[]{:S(2)}) collective-permute-start(bf16[128,1664]{1,0:T(8,128)(2,1)S(1)} %pad_maximum_fusion.4), channel_id=1, source_target_pairs={{0,4},{4,0},{8,12},{12,8},{16,20},{20,16},{24,28},{28,24},{1,5},{5... | collective-permute-start | bytes 1277960 | tf_op jit(solution)/shard_map/ppermute | solution.py:40
  56.7 10.2 %collective-permute-start.21 = (bf16[128,1664]{1,0:T(8,128)(2,1)S(1)}, bf16[128,1664]{1,0:T(8,128)(2,1)S(1)}, u32[]{:S(2)}, u32[]{:S(2)}) collective-permute-start(bf16[128,1664]{1,0:T(8,128)(2,1)S(1)} %pad_maximum_fusion.3), channel_id=1, source_target_pairs={{0,2},{1,3},{2,0},{3,1},{4,6},{5,7},{6,4},{7,5},{8,10},{9,11},{10,... | collective-permute-start | bytes 1277960 | tf_op jit(solution)/shard_map/ppermute | solution.py:44
  57.6 13.5 %collective-permute-start.23 = (bf16[256,1664]{1,0:T(8,128)(2,1)S(1)}, bf16[256,1664]{1,0:T(8,128)(2,1)S(1)}, u32[]{:S(2)}, u32[]{:S(2)}) collective-permute-start(bf16[256,1664]{1,0:T(8,128)(2,1)S(1)} %pad_maximum_fusion.1.near_ref), channel_id=1, source_target_pairs={{0,1},{1,0},{2,3},{3,2},{4,5},{5,4},{6,7},{7,6},{8,9},{9,8},{10,11... | collective-permute-start | bytes 2555912 | tf_op jit(solution)/shard_map/ppermute | solution.py:48
  65.7 2.5 %collective-permute-start.18 = (bf16[256,1536]{1,0:T(8,128)(2,1)S(1)}, bf16[256,1536]{1,0:T(8,128)(2,1)S(1)}, u32[]{:S(2)}, u32[]{:S(2)}) collective-permute-start(bf16[256,1536]{1,0:T(8,128)(2,1)S(1)} %get-tuple-element.69), channel_id=1, source_target_pairs={{0,1},{1,0},{2,3},{3,2},{4,5},{5,4},{6,7},{7,6},{8,9},{9,8},{10,11... | collective-permute-start | bytes 2359304 | tf_op jit(solution)/shard_map/ppermute | solution.py:48
  66.9 4.2 %collective-permute-start.24 = (bf16[256,1664]{1,0:T(8,128)(2,1)S(1)}, bf16[256,1664]{1,0:T(8,128)(2,1)S(1)}, u32[]{:S(2)}, u32[]{:S(2)}) collective-permute-start(bf16[256,1664]{1,0:T(8,128)(2,1)S(1)} %constant_dynamic-update-slice_fusion.2.far_ref), channel_id=1, source_target_pairs={{0,1},{1,0},{2,3},{3,2},{4,5},{5,4},{6,7},{7,6},{8,9},{9,8},{10,11... | collective-permute-start | bytes 2555912 | tf_op jit(solution)/shard_map/ppermute | solution.py:48
  67.0 13.7 %collective-permute-start.17 = (bf16[256,1536]{1,0:T(8,128)(2,1)S(1)}, bf16[256,1536]{1,0:T(8,128)(2,1)S(1)}, u32[]{:S(2)}, u32[]{:S(2)}) collective-permute-start(bf16[256,1536]{1,0:T(8,128)(2,1)S(1)} %get-tuple-element.67), channel_id=1, source_target_pairs={{0,1},{1,0},{2,3},{3,2},{4,5},{5,4},{6,7},{7,6},{8,9},{9,8},{10,11... | collective-permute-start | bytes 2359304 | tf_op jit(solution)/shard_map/ppermute | solution.py:48
  68.3 11.6 %collective-permute-start.19 = (bf16[128,1536]{1,0:T(8,128)(2,1)S(1)}, bf16[128,1536]{1,0:T(8,128)(2,1)S(1)}, u32[]{:S(2)}, u32[]{:S(2)}) collective-permute-start(bf16[128,1536]{1,0:T(8,128)(2,1)S(1)} %get-tuple-element.120), channel_id=1, source_target_pairs={{0,2},{1,3},{2,0},{3,1},{4,6},{5,7},{6,4},{7,5},{8,10},{9,11},{10,... | collective-permute-start | bytes 1179656 | tf_op jit(solution)/shard_map/ppermute | solution.py:44
  69.7 11.1 %collective-permute-start.20 = (bf16[128,1536]{1,0:T(8,128)(2,1)S(1)}, bf16[128,1536]{1,0:T(8,128)(2,1)S(1)}, u32[]{:S(2)}, u32[]{:S(2)}) collective-permute-start(bf16[128,1536]{1,0:T(8,128)(2,1)S(1)} %get-tuple-element.119), channel_id=1, source_target_pairs={{0,4},{4,0},{8,12},{12,8},{16,20},{20,16},{24,28},{28,24},{1,5},{5... | collective-permute-start | bytes 1179656 | tf_op jit(solution)/shard_map/ppermute | solution.py:40
  79.3 3.7 %collective-permute-start.27 = (bf16[256,1536]{1,0:T(8,128)(2,1)S(1)}, bf16[256,1536]{1,0:T(8,128)(2,1)S(1)}, u32[]{:S(2)}, u32[]{:S(2)}) collective-permute-start(bf16[256,1536]{1,0:T(8,128)(2,1)S(1)} %get-tuple-element.77), channel_id=1, source_target_pairs={{0,1},{1,0},{2,3},{3,2},{4,5},{5,4},{6,7},{7,6},{8,9},{9,8},{10,11... | collective-permute-start | bytes 2359304 | tf_op jit(solution)/shard_map/ppermute | solution.py:48
  79.4 22.6 %collective-permute-start.34 = (bf16[256,1536]{1,0:T(8,128)(2,1)S(1)}, bf16[256,1536]{1,0:T(8,128)(2,1)S(1)}, u32[]{:S(2)}, u32[]{:S(2)}) collective-permute-start(bf16[256,1536]{1,0:T(8,128)(2,1)S(1)} %get-tuple-element.76), channel_id=1, source_target_pairs={{0,1},{1,0},{2,3},{3,2},{4,5},{5,4},{6,7},{7,6},{8,9},{9,8},{10,11... | collective-permute-start | bytes 2359304 | tf_op jit(solution)/shard_map/ppermute | solution.py:48
  80.9 7.3 %collective-permute-start.25 = (bf16[64,1536]{1,0:T(8,128)(2,1)S(1)}, bf16[64,1536]{1,0:T(8,128)(2,1)S(1)}, u32[]{:S(2)}, u32[]{:S(2)}) collective-permute-start(bf16[64,1536]{1,0:T(8,128)(2,1)S(1)} %get-tuple-element.118), channel_id=1, source_target_pairs={{0,4},{4,0},{8,12},{12,8},{16,20},{20,16},{24,28},{28,24},{1,5},{5... | collective-permute-start | bytes 589832 | tf_op jit(solution)/shard_map/ppermute | solution.py:40
  82.5 7.8 %collective-permute-start.26 = (bf16[64,1536]{1,0:T(8,128)(2,1)S(1)}, bf16[64,1536]{1,0:T(8,128)(2,1)S(1)}, u32[]{:S(2)}, u32[]{:S(2)}) collective-permute-start(bf16[64,1536]{1,0:T(8,128)(2,1)S(1)} %get-tuple-element.117), channel_id=1, source_target_pairs={{0,2},{1,3},{2,0},{3,1},{4,6},{5,7},{6,4},{7,5},{8,10},{9,11},{10,... | collective-permute-start | bytes 589832 | tf_op jit(solution)/shard_map/ppermute | solution.py:44
  83.2 14.2 %copy-start.8 = (bf16[1536]{0:T(1024)(128)(2,1)S(1)}, bf16[1536]{0:T(1024)(128)(2,1)}, u32[]{:S(2)}) copy-start(bf16[1536]{0:T(1024)(128)(2,1)} %param.16) | copy-start | bytes 9220
  83.2 18.8 %collective-permute-start.35 = (bf16[128,1536]{1,0:T(8,128)(2,1)S(1)}, bf16[128,1536]{1,0:T(8,128)(2,1)S(1)}, u32[]{:S(2)}, u32[]{:S(2)}) collective-permute-start(bf16[128,1536]{1,0:T(8,128)(2,1)S(1)} %get-tuple-element.116), channel_id=1, source_target_pairs={{0,2},{1,3},{2,0},{3,1},{4,6},{5,7},{6,4},{7,5},{8,10},{9,11},{10,... | collective-permute-start | bytes 1179656 | tf_op jit(solution)/shard_map/ppermute | solution.py:44
  84.8 17.2 %collective-permute-start.37 = (bf16[128,1536]{1,0:T(8,128)(2,1)S(1)}, bf16[128,1536]{1,0:T(8,128)(2,1)S(1)}, u32[]{:S(2)}, u32[]{:S(2)}) collective-permute-start(bf16[128,1536]{1,0:T(8,128)(2,1)S(1)} %get-tuple-element.115), channel_id=1, source_target_pairs={{0,4},{4,0},{8,12},{12,8},{16,20},{20,16},{24,28},{28,24},{1,5},{5... | collective-permute-start | bytes 1179656 | tf_op jit(solution)/shard_map/ppermute | solution.py:40
  90.5 6.7 %collective-permute-start.30 = (bf16[32,1536]{1,0:T(8,128)(2,1)S(1)}, bf16[32,1536]{1,0:T(8,128)(2,1)S(1)}, u32[]{:S(2)}, u32[]{:S(2)}) collective-permute-start(bf16[32,1536]{1,0:T(8,128)(2,1)S(1)} %pad_maximum_fusion.12), channel_id=1, source_target_pairs={{0,8},{4,12},{8,16},{12,20},{16,24},{20,28},{24,0},{28,4},{1,9},{5... | collective-permute-start | bytes 294920 | tf_op jit(solution)/shard_map/ppermute | solution.py:36
  90.6 7.7 %collective-permute-start.29 = (bf16[32,1536]{1,0:T(8,128)(2,1)S(1)}, bf16[32,1536]{1,0:T(8,128)(2,1)S(1)}, u32[]{:S(2)}, u32[]{:S(2)}) collective-permute-start(bf16[32,1536]{1,0:T(8,128)(2,1)S(1)} %pad_maximum_fusion.11), channel_id=1, source_target_pairs={{0,16},{4,20},{8,24},{12,28},{16,0},{20,4},{24,8},{28,12},{1,17},{... | collective-permute-start | bytes 294920 | tf_op jit(solution)/shard_map/ppermute | solution.py:36
  97.2 4.6 %collective-permute-start.28 = (bf16[32,1536]{1,0:T(8,128)(2,1)S(1)}, bf16[32,1536]{1,0:T(8,128)(2,1)S(1)}, u32[]{:S(2)}, u32[]{:S(2)}) collective-permute-start(bf16[32,1536]{1,0:T(8,128)(2,1)S(1)} %pad_maximum_fusion.10), channel_id=1, source_target_pairs={{0,24},{4,28},{8,0},{12,4},{16,8},{20,12},{24,16},{28,20},{1,25},{... | collective-permute-start | bytes 294920 | tf_op jit(solution)/shard_map/ppermute | solution.py:36
  102.2 5.7 %collective-permute-start.36 = (bf16[64,1536]{1,0:T(8,128)(2,1)S(1)}, bf16[64,1536]{1,0:T(8,128)(2,1)S(1)}, u32[]{:S(2)}, u32[]{:S(2)}) collective-permute-start(bf16[64,1536]{1,0:T(8,128)(2,1)S(1)} %get-tuple-element.113), channel_id=1, source_target_pairs={{0,4},{4,0},{8,12},{12,8},{16,20},{20,16},{24,28},{28,24},{1,5},{5... | collective-permute-start | bytes 589832 | tf_op jit(solution)/shard_map/ppermute | solution.py:40
  102.8 5.7 %collective-permute-start.38 = (bf16[64,1536]{1,0:T(8,128)(2,1)S(1)}, bf16[64,1536]{1,0:T(8,128)(2,1)S(1)}, u32[]{:S(2)}, u32[]{:S(2)}) collective-permute-start(bf16[64,1536]{1,0:T(8,128)(2,1)S(1)} %get-tuple-element.114), channel_id=1, source_target_pairs={{0,2},{1,3},{2,0},{3,1},{4,6},{5,7},{6,4},{7,5},{8,10},{9,11},{10,... | collective-permute-start | bytes 589832 | tf_op jit(solution)/shard_map/ppermute | solution.py:44
  108.6 6.6 %collective-permute-start.41 = (bf16[32,1536]{1,0:T(8,128)(2,1)S(1)}, bf16[32,1536]{1,0:T(8,128)(2,1)S(1)}, u32[]{:S(2)}, u32[]{:S(2)}) collective-permute-start(bf16[32,1536]{1,0:T(8,128)(2,1)S(1)} %pad_maximum_fusion.15), channel_id=1, source_target_pairs={{0,8},{4,12},{8,16},{12,20},{16,24},{20,28},{24,0},{28,4},{1,9},{5... | collective-permute-start | bytes 294920 | tf_op jit(solution)/shard_map/ppermute | solution.py:36
  108.7 7.7 %collective-permute-start.40 = (bf16[32,1536]{1,0:T(8,128)(2,1)S(1)}, bf16[32,1536]{1,0:T(8,128)(2,1)S(1)}, u32[]{:S(2)}, u32[]{:S(2)}) collective-permute-start(bf16[32,1536]{1,0:T(8,128)(2,1)S(1)} %pad_maximum_fusion.14), channel_id=1, source_target_pairs={{0,16},{4,20},{8,24},{12,28},{16,0},{20,4},{24,8},{28,12},{1,17},{... | collective-permute-start | bytes 294920 | tf_op jit(solution)/shard_map/ppermute | solution.py:36
  111.1 5.2 %collective-permute-start.39 = (bf16[32,1536]{1,0:T(8,128)(2,1)S(1)}, bf16[32,1536]{1,0:T(8,128)(2,1)S(1)}, u32[]{:S(2)}, u32[]{:S(2)}) collective-permute-start(bf16[32,1536]{1,0:T(8,128)(2,1)S(1)} %pad_maximum_fusion.13), channel_id=1, source_target_pairs={{0,24},{4,28},{8,0},{12,4},{16,8},{20,12},{24,16},{28,20},{1,25},{... | collective-permute-start | bytes 294920 | tf_op jit(solution)/shard_map/ppermute | solution.py:36
  112.7 10.4 %collective-permute-start.31 = (bf16[32,1536]{1,0:T(8,128)(2,1)S(1)}, bf16[32,1536]{1,0:T(8,128)(2,1)S(1)}, u32[]{:S(2)}, u32[]{:S(2)}) collective-permute-start(bf16[32,1536]{1,0:T(8,128)(2,1)S(1)} %multiply_convert_fusion.1.refs_0_), channel_id=1, source_target_pairs={{0,1},{1,0},{2,3},{3,2},{4,5},{5,4},{6,7},{7,6},{8,9},{9,8},{10,11... | collective-permute-start | bytes 294920 | tf_op jit(solution)/shard_map/ppermute | solution.py:48
  112.8 10.3 %collective-permute-start.32 = (bf16[32,1536]{1,0:T(8,128)(2,1)S(1)}, bf16[32,1536]{1,0:T(8,128)(2,1)S(1)}, u32[]{:S(2)}, u32[]{:S(2)}) collective-permute-start(bf16[32,1536]{1,0:T(8,128)(2,1)S(1)} %multiply_convert_fusion.1.refs_0_), channel_id=1, source_target_pairs={{0,2},{1,3},{2,0},{3,1},{4,6},{5,7},{6,4},{7,5},{8,10},{9,11},{10,... | collective-permute-start | bytes 294920 | tf_op jit(solution)/shard_map/ppermute | solution.py:44
  115.2 7.9 %collective-permute-start.33 = (bf16[32,1536]{1,0:T(8,128)(2,1)S(1)}, bf16[32,1536]{1,0:T(8,128)(2,1)S(1)}, u32[]{:S(2)}, u32[]{:S(2)}) collective-permute-start(bf16[32,1536]{1,0:T(8,128)(2,1)S(1)} %multiply_convert_fusion.1.refs_0_), channel_id=1, source_target_pairs={{0,3},{1,2},{2,1},{3,0},{4,7},{5,6},{6,5},{7,4},{8,11},{9,10},{10,... | collective-permute-start | bytes 294920 | tf_op jit(solution)/shard_map/ppermute | solution.py:362

commit v3 on v2

--- a/solution.py
+++ b/solution.py
@@ -53,7 +53,7 @@
 ANY = pl.BlockSpec(memory_space=pl.ANY)
 
 
-def attend_kernel(place_ref, context_ref, w_ref, send_ref, keep_ref):
+def attend_kernel(place_ref, first_ref, context_ref, w_ref, send_ref, keep_ref):
     place = place_ref[0]
     quarter = send_ref.shape[1]
     rows = []
@@ -75,7 +75,7 @@
             ]
 
 
-def attend(place, context, w_out):
+def attend(place, first, context, w_out):
     rows, _ = context.shape
     width = w_out.shape[1]
     quarter = rows // 4
@@ -85,11 +85,11 @@
             jax.ShapeDtypeStruct((2, quarter, width), jnp.bfloat16),
             jax.ShapeDtypeStruct((2, quarter, width), jnp.float32),
         ),
-        in_specs=[SMEM, VMEM, VMEM],
+        in_specs=[SMEM, SMEM, VMEM, VMEM],
         out_specs=(VMEM, VMEM),
         compiler_params=pltpu.CompilerParams(vmem_limit_bytes=16 << 20),
         name="attend",
-    )(place, context, w_out)
+    )(place, first, context, w_out)
 
 
 def norm_kernel(
@@ -166,7 +166,7 @@
     )(place, keep, from_lower, from_upper, resid, gain, ids, router, slot_hot)
 
 
-def load_kernel(gate_hbm, up_hbm, down_hbm, both_ref, down_ref, sems):
+def load_kernel(gate_hbm, up_hbm, down_hbm, both_ref, down_ref, mark_ref, sems):
     units = gate_hbm.shape[2]
     copies = [
         pltpu.make_async_copy(gate_hbm, both_ref.at[:, :, pl.ds(0, units)], sems.at[0]),
@@ -175,6 +175,7 @@
     ]
     for copy in copies:
         copy.start()
+    mark_ref[...] = jnp.zeros_like(mark_ref)
     for copy in copies:
         copy.wait()
 
@@ -186,9 +187,10 @@
         out_shape=(
             pltpu.VMEM((held, width, 2 * units), jnp.bfloat16),
             pltpu.VMEM((held * units, width), jnp.bfloat16),
+            jax.ShapeDtypeStruct((8, LANES), jnp.int32),
         ),
         in_specs=[ANY] * 3,
-        out_specs=(VMEM, VMEM),
+        out_specs=(VMEM, VMEM, VMEM),
         scratch_shapes=[pltpu.SemaphoreType.DMA((3,))],
         compiler_params=pltpu.CompilerParams(vmem_limit_bytes=2 << 20),
         name="load_weights",
@@ -203,6 +205,7 @@
     other_far_ref,
     both_ref,
     down_ref,
+    loaded_hbm,
     near_out,
     far_out,
     other_near_out,
@@ -251,7 +254,7 @@
         one_block(pl.ds(number * block, block))
 
 
-def expert_rows(first, pieces, both, down):
+def expert_rows(first, pieces, both, down, loaded):
     held, width, units = both.shape
     units = units // 2
     rows = sum(p.shape[0] for p in pieces)
@@ -259,7 +262,7 @@
     return pl.pallas_call(
         expert_kernel,
         out_shape=[jax.ShapeDtypeStruct((p.shape[0], width), jnp.bfloat16) for p in pieces],
-        in_specs=[SMEM] + [VMEM] * (len(pieces) + 2),
+        in_specs=[SMEM] + [VMEM] * (len(pieces) + 2) + [ANY],
         out_specs=[VMEM] * len(pieces),
         scratch_shapes=[
             pltpu.VMEM((rows, pieces[0].shape[1]), jnp.bfloat16),
@@ -272,7 +275,7 @@
             transcendentals=rows * held * units,
         ),
         name="expert_rows",
-    )(first, *pieces, both, down)
+    )(first, *pieces, both, down, loaded)
 
 
 def wide(value):
@@ -336,6 +339,7 @@
         size = part // 2
         first = short(self.two(0, size, size) + cut(self.far_first, size, size))
         second = short(self.two(0, part + size, size) + cut(self.far_second, size, size))
+        self.near = first, second
         self.near_first, self.near_second = flip_inner(first), flip_upper(second)
 
     def block(self, number):
@@ -409,7 +413,7 @@
     first = (lax.axis_index("ep") * held).astype(jnp.int32).reshape(1)
     down = w_down.reshape(held * units, width)
 
-    send, keep = attend(place, context, w_out)
+    send, keep = attend(place, first, context, w_out)
     got = flip_lower(send)
     table = slot_of_pick(after(slot_expert, send), copy_pick, experts)[0]
     lanes = -(-slots // LANES) * LANES
@@ -429,23 +433,24 @@
         middles.append(middle)
         chunks.append(Chunk(row))
 
-    both, down = load_weights(w_gate, w_up, after(down, uppers))
+    both, down, loaded = load_weights(w_gate, w_up, after(down, uppers))
 
     def serve(chunk, *then):
         pieces = [after(p, *then) for p in chunk.pieces + chunk.others]
-        outs = expert_rows(first, pieces, both, down)
+        outs = expert_rows(first, pieces, both, down, loaded)
         chunk.own, chunk.away = outs[:2], outs[2:]
 
     one, two = chunks
     one.gather_outer()
+    one.first, one.second = after((one.first, one.second), loaded)
+    two.gather_outer(one.first)
     one.gather_near()
-    two.gather_outer(one.first)
     one.gather_far()
     two.gather_near()
-    one.gathered_far()
+    one.gathered_far(two.first, two.second)
     one.gather_lower(one.pieces[1])
     two.gather_far()
-    serve(one, two.first, two.second)
+    serve(one)
     one.back_lower()
     two.gathered_far(one.away)
     two.gather_lower()
@@ -459,7 +464,7 @@
     one.back_outer()
     two.back_near()
     two.back_outer()
-    result_one = one.finish(middles[0], final_gain)
+    result_one = one.finish(middles[0], final_gain, two.near)
     ready_one = spread(result_one)
     result_two = two.finish(middles[1], final_gain, result_one)
     return join(place, ready_one, lax.all_gather(result_two, "tp"))

time: 124 us -> 119 us (0.960)
  waiting for transfers between devices: 44 us -> 34.7 us
  starting transfers between devices: 42.9 us -> 46.9 us
    ppermute x12, waiting for transfers between devices: 16.2 us -> 6.53 us  [turn(): lax.ppermute(value, 'ep', [(i, (i + 2 * step) % count) for i in range(cou...]
    ppermute x11, waiting for transfers between devices: 6.09 us -> 11.6 us  [flip_upper(): lax.ppermute(value, 'tp', [(i, i ^ 2) for i in range(lax.axis_size('tp'))])]
    ppermute x8, waiting for transfers between devices: 21.1 us -> 15.5 us  [flip_inner(): lax.ppermute(value, 'ep', [(i, i ^ 1) for i in range(lax.axis_size('ep'))])]
    ppermute x12, starting transfers between devices: 17.7 us -> 21.9 us  [turn(): lax.ppermute(value, 'ep', [(i, (i + 2 * step) % count) for i in range(cou...]
  transfers between devices with their start and end apart: 42 -> 42, of which waited for: 19 -> 20; matrix products, arithmetic and copies ran while one was open for 4% -> 4% of each run, Pallas kernels for 15% -> 15%
where the time goes in v3:
time: 119 us
  starting transfers between devices  46.9 us (39%)
  waiting for transfers between devices  34.7 us (29%)
  Pallas kernels  19.8 us (17%)
  blocking collectives  6.42 us (5%)
  local copies, waits for them, and re-layouts  5.95 us (5%)
  other arithmetic  4.67 us (4%)
    ppermute x12, starting transfers between devices, turn(): lax.ppermute(value, 'ep', [(i, (i + 2 * step) % count) for i in range(cou...  21.9 us
    pallas_call x2, Pallas kernels, expert_rows(): pl.pallas_call(expert_kernel, out_shape=[jax.ShapeDtypeStruct((p.shape[0]...  16.3 us
    ppermute x8, waiting for transfers between devices, flip_inner(): lax.ppermute(value, 'ep', [(i, i ^ 1) for i in range(lax.axis_size('ep'))])  15.5 us
    ppermute x11, starting transfers between devices, flip_upper(): lax.ppermute(value, 'tp', [(i, i ^ 2) for i in range(lax.axis_size('tp'))])  12.4 us
    ppermute x11, waiting for transfers between devices, flip_upper(): lax.ppermute(value, 'tp', [(i, i ^ 2) for i in range(lax.axis_size('tp'))])  11.6 us
    ppermute x8, starting transfers between devices, flip_inner(): lax.ppermute(value, 'ep', [(i, i ^ 1) for i in range(lax.axis_size('ep'))])  9.65 us
    ppermute x12, waiting for transfers between devices, turn(): lax.ppermute(value, 'ep', [(i, (i + 2 * step) % count) for i in range(cou...  6.53 us
    all_gather x1, blocking collectives, local(): return join(place, ready_one, lax.all_gather(result_two, 'tp'))  6.42 us
  transfers between devices with their start and end apart: 42, of which 20 were waited for; matrix products, arithmetic and copies ran while one was open for 4% of the time, Pallas kernels for 15%

profile of v3, /device:TPU:0, one launch (start us, length us, event | category | flops | bytes accessed | tf_op | source)
XLA Modules:
  0.0 118.8 jit_solution(14862201080906994348)
XLA Ops:
  0.0 1.3 %copy-done.4 = bf16[384,1536]{1,0:T(8,128)(2,1)S(1)} copy-done((bf16[384,1536]{1,0:T(8,128)(2,1)S(1)}, bf16[384,1536]{1,0:T(8,128)(2,1)}, u32[]{:S(2)}) %copy-start.4) | copy-done | bytes 1179672
  1.3 0.9 copy-done.5
  2.3 0.6 attend.1
  2.8 0.5 collective-permute-start
  3.4 0.9 convert_reduce_fusion
  4.3 0.8 fusion.11
  5.1 0.8 select_reduce_fusion
  6.0 2.6 %collective-permute-start.1 = (bf16[32,1536]{1,0:T(8,128)(2,1)S(1)}, bf16[32,1536]{1,0:T(8,128)(2,1)S(1)}, u32[]{:S(2)}, u32[]{:S(2)}) collective-permute-start(bf16[32,1536]{1,0:T(8,128)(2,1)S(1)} %get-tuple-element.120), channel_id=1, source_target_pairs={{0,2},{1,3},{2,0},{3,1},{4,6},{5,7},{6,4},{7,5},{8,10},{9,11},{10,... | collective-permute-start | bytes 294920 | tf_op jit(solution)/shard_map/ppermute | solution.py:44
  9.1 2.9 %collective-permute-done.1.upper_ref = bf16[32,1536]{1,0:T(8,128)(2,1)S(1)} collective-permute-done((bf16[32,1536]{1,0:T(8,128)(2,1)S(1)}, bf16[32,1536]{1,0:T(8,128)(2,1)S(1)}, u32[]{:S(2)}, u32[]{:S(2)}) %collective-permute-start.1) | collective-permute-done | bytes 98336 | tf_op jit(solution)/shard_map/ppermute | solution.py:44
  12.0 0.5 norm_rows.2
  12.6 2.1 %collective-permute-start.2 = (bf16[32,1664]{1,0:T(8,128)(2,1)S(1)}, bf16[32,1664]{1,0:T(8,128)(2,1)S(1)}, u32[]{:S(2)}, u32[]{:S(2)}) collective-permute-start(bf16[32,1664]{1,0:T(8,128)(2,1)S(1)} %get-tuple-element.51), channel_id=1, source_target_pairs={{0,8},{4,12},{8,16},{12,20},{16,24},{20,28},{24,0},{28,4},{1,9},{5... | collective-permute-start | bytes 319496 | tf_op jit(solution)/shard_map/ppermute | solution.py:36
  14.6 2.6 %collective-permute-start.3 = (bf16[32,1664]{1,0:T(8,128)(2,1)S(1)}, bf16[32,1664]{1,0:T(8,128)(2,1)S(1)}, u32[]{:S(2)}, u32[]{:S(2)}) collective-permute-start(bf16[32,1664]{1,0:T(8,128)(2,1)S(1)} %get-tuple-element.51), channel_id=1, source_target_pairs={{0,16},{4,20},{8,24},{12,28},{16,0},{20,4},{24,8},{28,12},{1,17},{... | collective-permute-start | bytes 319496 | tf_op jit(solution)/shard_map/ppermute | solution.py:36
  17.2 1.3 %collective-permute-start.4 = (bf16[32,1664]{1,0:T(8,128)(2,1)S(1)}, bf16[32,1664]{1,0:T(8,128)(2,1)S(1)}, u32[]{:S(2)}, u32[]{:S(2)}) collective-permute-start(bf16[32,1664]{1,0:T(8,128)(2,1)S(1)} %get-tuple-element.51), channel_id=1, source_target_pairs={{0,24},{4,28},{8,0},{12,4},{16,8},{20,12},{24,16},{28,20},{1,25},{... | collective-permute-start | bytes 319496 | tf_op jit(solution)/shard_map/ppermute | solution.py:36
  18.6 1.5 %copy-done.2 = bf16[5,1536,128]{2,1,0:T(8,128)(2,1)S(1)} copy-done((bf16[5,1536,128]{2,1,0:T(8,128)(2,1)S(1)}, bf16[5,1536,128]{2,1,0:T(8,128)(2,1)}, u32[]{:S(2)}) %copy-start.2) | copy-done | bytes 1966104
  20.1 1.5 %copy-done.3 = bf16[5,128,1536]{2,1,0:T(8,128)(2,1)S(1)} copy-done((bf16[5,128,1536]{2,1,0:T(8,128)(2,1)S(1)}, bf16[5,128,1536]{2,1,0:T(8,128)(2,1)}, u32[]{:S(2)}) %copy-start.3) | copy-done | bytes 1966104
  21.7 1.0 load_weights.1
  22.7 0.5 norm_rows.3
  23.2 0.7 collective-permute-done.3
  24.0 2.7 %collective-permute-start.10 = (bf16[32,1664]{1,0:T(8,128)(2,1)S(1)}, bf16[32,1664]{1,0:T(8,128)(2,1)S(1)}, u32[]{:S(2)}, u32[]{:S(2)}) collective-permute-start(bf16[32,1664]{1,0:T(8,128)(2,1)S(1)} %get-tuple-element.57), channel_id=1, source_target_pairs={{0,8},{4,12},{8,16},{12,20},{16,24},{20,28},{24,0},{28,4},{1,9},{5... | collective-permute-start | bytes 319496 | tf_op jit(solution)/shard_map/ppermute | solution.py:36
  26.8 1.6 %collective-permute-start.11 = (bf16[32,1664]{1,0:T(8,128)(2,1)S(1)}, bf16[32,1664]{1,0:T(8,128)(2,1)S(1)}, u32[]{:S(2)}, u32[]{:S(2)}) collective-permute-start(bf16[32,1664]{1,0:T(8,128)(2,1)S(1)} %get-tuple-element.57), channel_id=1, source_target_pairs={{0,16},{4,20},{8,24},{12,28},{16,0},{20,4},{24,8},{28,12},{1,17},{... | collective-permute-start | bytes 319496 | tf_op jit(solution)/shard_map/ppermute | solution.py:36
  28.4 0.8 collective-permute-start.12
  29.2 1.5 %collective-permute-start.7 = (bf16[64,1664]{1,0:T(8,128)(2,1)S(1)}, bf16[64,1664]{1,0:T(8,128)(2,1)S(1)}, u32[]{:S(2)}, u32[]{:S(2)}) collective-permute-start(bf16[64,1664]{1,0:T(8,128)(2,1)S(1)} %get-tuple-element.55), channel_id=1, source_target_pairs={{0,2},{1,3},{2,0},{3,1},{4,6},{5,7},{6,4},{7,5},{8,10},{9,11},{10,... | collective-permute-start | bytes 638984 | tf_op jit(solution)/shard_map/ppermute | solution.py:44
  30.8 1.5 %collective-permute-start.6 = (bf16[64,1664]{1,0:T(8,128)(2,1)S(1)}, bf16[64,1664]{1,0:T(8,128)(2,1)S(1)}, u32[]{:S(2)}, u32[]{:S(2)}) collective-permute-start(bf16[64,1664]{1,0:T(8,128)(2,1)S(1)} %get-tuple-element.54), channel_id=1, source_target_pairs={{0,4},{4,0},{8,12},{12,8},{16,20},{20,16},{24,28},{28,24},{1,5},{5... | collective-permute-start | bytes 638984 | tf_op jit(solution)/shard_map/ppermute | solution.py:40
  32.3 3.0 %collective-permute-done.11 = bf16[32,1664]{1,0:T(8,128)(2,1)S(1)} collective-permute-done((bf16[32,1664]{1,0:T(8,128)(2,1)S(1)}, bf16[32,1664]{1,0:T(8,128)(2,1)S(1)}, u32[]{:S(2)}, u32[]{:S(2)}) %collective-permute-start.11) | collective-permute-done | bytes 106528 | tf_op jit(solution)/shard_map/ppermute | solution.py:36
  35.4 1.6 %collective-permute-start.14 = (bf16[64,1664]{1,0:T(8,128)(2,1)S(1)}, bf16[64,1664]{1,0:T(8,128)(2,1)S(1)}, u32[]{:S(2)}, u32[]{:S(2)}) collective-permute-start(bf16[64,1664]{1,0:T(8,128)(2,1)S(1)} %pad_maximum_fusion.9), channel_id=1, source_target_pairs={{0,2},{1,3},{2,0},{3,1},{4,6},{5,7},{6,4},{7,5},{8,10},{9,11},{10,... | collective-permute-start | bytes 638984 | tf_op jit(solution)/shard_map/ppermute | solution.py:44
  37.0 1.6 %collective-permute-start.13 = (bf16[64,1664]{1,0:T(8,128)(2,1)S(1)}, bf16[64,1664]{1,0:T(8,128)(2,1)S(1)}, u32[]{:S(2)}, u32[]{:S(2)}) collective-permute-start(bf16[64,1664]{1,0:T(8,128)(2,1)S(1)} %pad_maximum_fusion.8), channel_id=1, source_target_pairs={{0,4},{4,0},{8,12},{12,8},{16,20},{20,16},{24,28},{28,24},{1,5},{5... | collective-permute-start | bytes 638984 | tf_op jit(solution)/shard_map/ppermute | solution.py:40
  38.6 0.6 collective-permute-start.9
  39.3 0.5 collective-permute-start.8
  39.9 3.7 %collective-permute-done.14 = bf16[64,1664]{1,0:T(8,128)(2,1)S(1)} collective-permute-done((bf16[64,1664]{1,0:T(8,128)(2,1)S(1)}, bf16[64,1664]{1,0:T(8,128)(2,1)S(1)}, u32[]{:S(2)}, u32[]{:S(2)}) %collective-permute-start.14) | collective-permute-done | bytes 213024 | tf_op jit(solution)/shard_map/ppermute | solution.py:44
  43.6 1.6 %collective-permute-done.13 = bf16[64,1664]{1,0:T(8,128)(2,1)S(1)} collective-permute-done((bf16[64,1664]{1,0:T(8,128)(2,1)S(1)}, bf16[64,1664]{1,0:T(8,128)(2,1)S(1)}, u32[]{:S(2)}, u32[]{:S(2)}) %collective-permute-start.13) | collective-permute-done | bytes 213024 | tf_op jit(solution)/shard_map/ppermute | solution.py:40
  45.3 7.7 %collective-permute-done.9 = bf16[128,1664]{1,0:T(8,128)(2,1)S(1)} collective-permute-done((bf16[128,1664]{1,0:T(8,128)(2,1)S(1)}, bf16[128,1664]{1,0:T(8,128)(2,1)S(1)}, u32[]{:S(2)}, u32[]{:S(2)}) %collective-permute-start.9) | collective-permute-done | bytes 426016 | tf_op jit(solution)/shard_map/ppermute | solution.py:40
  53.2 0.5 collective-permute-start.16
  53.7 1.5 %collective-permute-start.22 = (bf16[128,1664]{1,0:T(8,128)(2,1)S(1)}, bf16[128,1664]{1,0:T(8,128)(2,1)S(1)}, u32[]{:S(2)}, u32[]{:S(2)}) collective-permute-start(bf16[128,1664]{1,0:T(8,128)(2,1)S(1)} %pad_maximum_fusion.5), channel_id=1, source_target_pairs={{0,4},{4,0},{8,12},{12,8},{16,20},{20,16},{24,28},{28,24},{1,5},{5... | collective-permute-start | bytes 1277960 | tf_op jit(solution)/shard_map/ppermute | solution.py:40
  55.8 1.0 collective-permute-done.16.other_far_ref
  56.8 8.0 %expert_rows.2 = (bf16[256,1536]{1,0:T(8,128)(2,1)S(1)}, bf16[256,1536]{1,0:T(8,128)(2,1)S(1)}, bf16[256,1536]{1,0:T(8,128)(2,1)S(1)}, bf16[256,1536]{1,0:T(8,128)(2,1)S(1)}) custom-call(s32[1]{0:T(128)} %bitcast.1.first_ref, bf16[256,1664]{1,0:T(8,128)(2,1)S(1)} %pad_maximum_fusion.near_ref, ...), custom_call_target="tpu_custom_call" | custom-call | flops 6039797760 | bytes 12189696 | tf_op jit(solution)/shard_map/expert_rows/pallas_call | solution.py:262
  65.5 1.2 %collective-permute-done.21 = bf16[128,1664]{1,0:T(8,128)(2,1)S(1)} collective-permute-done((bf16[128,1664]{1,0:T(8,128)(2,1)S(1)}, bf16[128,1664]{1,0:T(8,128)(2,1)S(1)}, u32[]{:S(2)}, u32[]{:S(2)}) %collective-permute-start.21) | collective-permute-done | bytes 426016 | tf_op jit(solution)/shard_map/ppermute | solution.py:44
  66.9 0.5 collective-permute-start.17
  67.6 0.6 collective-permute-start.19
  68.2 1.2 %collective-permute-start.20 = (bf16[128,1536]{1,0:T(8,128)(2,1)S(1)}, bf16[128,1536]{1,0:T(8,128)(2,1)S(1)}, u32[]{:S(2)}, u32[]{:S(2)}) collective-permute-start(bf16[128,1536]{1,0:T(8,128)(2,1)S(1)} %get-tuple-element.117), channel_id=1, source_target_pairs={{0,4},{4,0},{8,12},{12,8},{16,20},{20,16},{24,28},{28,24},{1,5},{5... | collective-permute-start | bytes 1179656 | tf_op jit(solution)/shard_map/ppermute | solution.py:40
  69.4 8.2 %expert_rows.3 = (bf16[256,1536]{1,0:T(8,128)(2,1)S(1)}, bf16[256,1536]{1,0:T(8,128)(2,1)S(1)}, bf16[256,1536]{1,0:T(8,128)(2,1)S(1)}, bf16[256,1536]{1,0:T(8,128)(2,1)S(1)}) custom-call(s32[1]{0:T(128)} %bitcast.1.first_ref, bf16[256,1664]{1,0:T(8,128)(2,1)S(1)} %pad_maximum_fusion.1.near_ref, ...), custom_call_target="tpu_custom_call" | custom-call | flops 6039797760 | bytes 12189696 | tf_op jit(solution)/shard_map/expert_rows/pallas_call | solution.py:262
  77.8 0.5 collective-permute-start.31
  78.2 0.5 collective-permute-done.19
  78.7 0.5 collective-permute-done.20
  79.4 1.1 collective-permute-start.25
  80.5 1.6 %collective-permute-start.26 = (bf16[64,1536]{1,0:T(8,128)(2,1)S(1)}, bf16[64,1536]{1,0:T(8,128)(2,1)S(1)}, u32[]{:S(2)}, u32[]{:S(2)}) collective-permute-start(bf16[64,1536]{1,0:T(8,128)(2,1)S(1)} %get-tuple-element.115), channel_id=1, source_target_pairs={{0,2},{1,3},{2,0},{3,1},{4,6},{5,7},{6,4},{7,5},{8,10},{9,11},{10,... | collective-permute-start | bytes 589832 | tf_op jit(solution)/shard_map/ppermute | solution.py:44
  82.3 0.5 collective-permute-start.32
  82.8 1.0 collective-permute-start.33
  83.8 2.9 %collective-permute-done.25 = bf16[64,1536]{1,0:T(8,128)(2,1)S(1)} collective-permute-done((bf16[64,1536]{1,0:T(8,128)(2,1)S(1)}, bf16[64,1536]{1,0:T(8,128)(2,1)S(1)}, u32[]{:S(2)}, u32[]{:S(2)}) %collective-permute-start.25) | collective-permute-done | bytes 196640 | tf_op jit(solution)/shard_map/ppermute | solution.py:40
  86.7 1.6 %collective-permute-done.26 = bf16[64,1536]{1,0:T(8,128)(2,1)S(1)} collective-permute-done((bf16[64,1536]{1,0:T(8,128)(2,1)S(1)}, bf16[64,1536]{1,0:T(8,128)(2,1)S(1)}, u32[]{:S(2)}, u32[]{:S(2)}) %collective-permute-start.26) | collective-permute-done | bytes 196640 | tf_op jit(solution)/shard_map/ppermute | solution.py:44
  88.6 2.9 %collective-permute-start.30 = (bf16[32,1536]{1,0:T(8,128)(2,1)S(1)}, bf16[32,1536]{1,0:T(8,128)(2,1)S(1)}, u32[]{:S(2)}, u32[]{:S(2)}) collective-permute-start(bf16[32,1536]{1,0:T(8,128)(2,1)S(1)} %pad_maximum_fusion.12), channel_id=1, source_target_pairs={{0,8},{4,12},{8,16},{12,20},{16,24},{20,28},{24,0},{28,4},{1,9},{5... | collective-permute-start | bytes 294920 | tf_op jit(solution)/shard_map/ppermute | solution.py:36
  91.4 0.9 collective-permute-start.29
  92.4 1.6 %collective-permute-start.28 = (bf16[32,1536]{1,0:T(8,128)(2,1)S(1)}, bf16[32,1536]{1,0:T(8,128)(2,1)S(1)}, u32[]{:S(2)}, u32[]{:S(2)}) collective-permute-start(bf16[32,1536]{1,0:T(8,128)(2,1)S(1)} %pad_maximum_fusion.10), channel_id=1, source_target_pairs={{0,24},{4,28},{8,0},{12,4},{16,8},{20,12},{24,16},{28,20},{1,25},{... | collective-permute-start | bytes 294920 | tf_op jit(solution)/shard_map/ppermute | solution.py:36
  93.9 0.6 collective-permute-done.32
  94.8 1.2 %collective-permute-start.37 = (bf16[64,1536]{1,0:T(8,128)(2,1)S(1)}, bf16[64,1536]{1,0:T(8,128)(2,1)S(1)}, u32[]{:S(2)}, u32[]{:S(2)}) collective-permute-start(bf16[64,1536]{1,0:T(8,128)(2,1)S(1)} %get-tuple-element.112), channel_id=1, source_target_pairs={{0,4},{4,0},{8,12},{12,8},{16,20},{20,16},{24,28},{28,24},{1,5},{5... | collective-permute-start | bytes 589832 | tf_op jit(solution)/shard_map/ppermute | solution.py:40
  96.0 1.4 %collective-permute-start.38 = (bf16[64,1536]{1,0:T(8,128)(2,1)S(1)}, bf16[64,1536]{1,0:T(8,128)(2,1)S(1)}, u32[]{:S(2)}, u32[]{:S(2)}) collective-permute-start(bf16[64,1536]{1,0:T(8,128)(2,1)S(1)} %get-tuple-element.111), channel_id=1, source_target_pairs={{0,2},{1,3},{2,0},{3,1},{4,6},{5,7},{6,4},{7,5},{8,10},{9,11},{10,... | collective-permute-start | bytes 589832 | tf_op jit(solution)/shard_map/ppermute | solution.py:44
  98.3 2.2 %collective-permute-done.37 = bf16[64,1536]{1,0:T(8,128)(2,1)S(1)} collective-permute-done((bf16[64,1536]{1,0:T(8,128)(2,1)S(1)}, bf16[64,1536]{1,0:T(8,128)(2,1)S(1)}, u32[]{:S(2)}, u32[]{:S(2)}) %collective-permute-start.37) | collective-permute-done | bytes 196640 | tf_op jit(solution)/shard_map/ppermute | solution.py:40
  100.6 1.0 collective-permute-done.38
  101.7 2.9 %collective-permute-start.41 = (bf16[32,1536]{1,0:T(8,128)(2,1)S(1)}, bf16[32,1536]{1,0:T(8,128)(2,1)S(1)}, u32[]{:S(2)}, u32[]{:S(2)}) collective-permute-start(bf16[32,1536]{1,0:T(8,128)(2,1)S(1)} %pad_maximum_fusion.15), channel_id=1, source_target_pairs={{0,8},{4,12},{8,16},{12,20},{16,24},{20,28},{24,0},{28,4},{1,9},{5... | collective-permute-start | bytes 294920 | tf_op jit(solution)/shard_map/ppermute | solution.py:36
  104.6 0.8 collective-permute-start.40
  105.5 1.7 %collective-permute-start.39 = (bf16[32,1536]{1,0:T(8,128)(2,1)S(1)}, bf16[32,1536]{1,0:T(8,128)(2,1)S(1)}, u32[]{:S(2)}, u32[]{:S(2)}) collective-permute-start(bf16[32,1536]{1,0:T(8,128)(2,1)S(1)} %pad_maximum_fusion.13), channel_id=1, source_target_pairs={{0,24},{4,28},{8,0},{12,4},{16,8},{20,12},{24,16},{28,20},{1,25},{... | collective-permute-start | bytes 294920 | tf_op jit(solution)/shard_map/ppermute | solution.py:36
  107.3 1.5 %collective-permute-start.35 = (bf16[32,1536]{1,0:T(8,128)(2,1)S(1)}, bf16[32,1536]{1,0:T(8,128)(2,1)S(1)}, u32[]{:S(2)}, u32[]{:S(2)}) collective-permute-start(bf16[32,1536]{1,0:T(8,128)(2,1)S(1)} %multiply_convert_fusion.1.refs_0_), channel_id=1, source_target_pairs={{0,2},{1,3},{2,0},{3,1},{4,6},{5,7},{6,4},{7,5},{8,10},{9,11},{10,... | collective-permute-start | bytes 294920 | tf_op jit(solution)/shard_map/ppermute | solution.py:44
  109.2 1.8 %collective-permute-done.40 = bf16[32,1536]{1,0:T(8,128)(2,1)S(1)} collective-permute-done((bf16[32,1536]{1,0:T(8,128)(2,1)S(1)}, bf16[32,1536]{1,0:T(8,128)(2,1)S(1)}, u32[]{:S(2)}, u32[]{:S(2)}) %collective-permute-start.40) | collective-permute-done | bytes 98336 | tf_op jit(solution)/shard_map/ppermute | solution.py:36
  111.5 6.4 %all-gather = bf16[128,1536]{1,0:T(8,128)(2,1)S(1)} all-gather(bf16[32,1536]{1,0:T(8,128)(2,1)S(1)} %multiply_convert_fusion), channel_id=2, replica_groups=mesh['ep'=8,'tp'=4] {'tp'}, dimensions={0}, use_global_device_ids=true | all-gather | bytes 491520 | tf_op jit(solution)/shard_map/all_gather | solution.py:470
  117.9 0.9 join.1
  (98 shorter events, 5.7 us)
Async XLA Ops:
  0.0 12.0 %copy-start = (bf16[256,1536]{1,0:T(8,128)(2,1)S(1)}, bf16[256,1536]{1,0:T(8,128)(2,1)}, u32[]{:S(2)}) copy-start(bf16[256,1536]{1,0:T(8,128)(2,1)} %resid_ref.3) | copy-start | bytes 2359300
  0.0 1.3 %copy-start.4 = (bf16[384,1536]{1,0:T(8,128)(2,1)S(1)}, bf16[384,1536]{1,0:T(8,128)(2,1)}, u32[]{:S(2)}) copy-start(bf16[384,1536]{1,0:T(8,128)(2,1)} %w_ref.1) | copy-start | bytes 3538948
  1.3 0.9 copy-start.5
  2.3 6.3 %copy-start.6 = (bf16[1536,40]{0,1:T(8,128)(2,1)S(1)}, bf16[1536,40]{0,1:T(8,128)(2,1)}, u32[]{:S(2)}) copy-start(bf16[1536,40]{0,1:T(8,128)(2,1)} %param.17) | copy-start | bytes 368644
  2.3 6.6 %copy-start.7 = (s32[256,8]{0,1:T(8,128)S(1)}, s32[256,8]{0,1:T(8,128)}, u32[]{:S(2)}) copy-start(s32[256,8]{0,1:T(8,128)} %param.18) | copy-start | bytes 24580
  2.3 6.7 %copy-start.9 = (bf16[1536]{0:T(1024)(128)(2,1)S(1)}, bf16[1536]{0:T(1024)(128)(2,1)}, u32[]{:S(2)}) copy-start(bf16[1536]{0:T(1024)(128)(2,1)} %param.15) | copy-start | bytes 9220
  2.8 3.1 %collective-permute-start = (bf16[2,64,1536]{2,1,0:T(8,128)(2,1)S(1)}, bf16[2,64,1536]{2,1,0:T(8,128)(2,1)S(1)}, u32[]{:S(2)}, u32[]{:S(2)}) collective-permute-start(bf16[2,64,1536]{2,1,0:T(8,128)(2,1)S(1)} %get-tuple-element.48), channel_id=1, source_target_pairs={{0,1},{1,0},{2,3},{3,2},{4,5},{5,4},{6,7},{7,6},{8,9},{9,8},{10,11... | collective-permute-start | bytes 1179656 | tf_op jit(solution)/shard_map/ppermute | solution.py:48
  6.0 6.1 %collective-permute-start.1 = (bf16[32,1536]{1,0:T(8,128)(2,1)S(1)}, bf16[32,1536]{1,0:T(8,128)(2,1)S(1)}, u32[]{:S(2)}, u32[]{:S(2)}) collective-permute-start(bf16[32,1536]{1,0:T(8,128)(2,1)S(1)} %get-tuple-element.120), channel_id=1, source_target_pairs={{0,2},{1,3},{2,0},{3,1},{4,6},{5,7},{6,4},{7,5},{8,10},{9,11},{10,... | collective-permute-start | bytes 294920 | tf_op jit(solution)/shard_map/ppermute | solution.py:44
  9.0 9.6 %copy-start.1 = (bf16[5,1536,128]{2,1,0:T(8,128)(2,1)S(1)}, bf16[5,1536,128]{2,1,0:T(8,128)(2,1)}, u32[]{:S(2)}) copy-start(bf16[5,1536,128]{2,1,0:T(8,128)(2,1)} %gate_hbm.1) | copy-start | bytes 5898244
  9.0 9.5 %collective-permute-start.5 = (bf16[32,1536]{1,0:T(8,128)(2,1)S(1)}, bf16[32,1536]{1,0:T(8,128)(2,1)S(1)}, u32[]{:S(2)}, u32[]{:S(2)}) collective-permute-start(bf16[32,1536]{1,0:T(8,128)(2,1)S(1)} %get-tuple-element.119), channel_id=1, source_target_pairs={{0,2},{1,3},{2,0},{3,1},{4,6},{5,7},{6,4},{7,5},{8,10},{9,11},{10,... | collective-permute-start | bytes 294920 | tf_op jit(solution)/shard_map/ppermute | solution.py:44
  12.6 10.6 %collective-permute-start.2 = (bf16[32,1664]{1,0:T(8,128)(2,1)S(1)}, bf16[32,1664]{1,0:T(8,128)(2,1)S(1)}, u32[]{:S(2)}, u32[]{:S(2)}) collective-permute-start(bf16[32,1664]{1,0:T(8,128)(2,1)S(1)} %get-tuple-element.51), channel_id=1, source_target_pairs={{0,8},{4,12},{8,16},{12,20},{16,24},{20,28},{24,0},{28,4},{1,9},{5... | collective-permute-start | bytes 319496 | tf_op jit(solution)/shard_map/ppermute | solution.py:36
  14.6 9.3 %collective-permute-start.3 = (bf16[32,1664]{1,0:T(8,128)(2,1)S(1)}, bf16[32,1664]{1,0:T(8,128)(2,1)S(1)}, u32[]{:S(2)}, u32[]{:S(2)}) collective-permute-start(bf16[32,1664]{1,0:T(8,128)(2,1)S(1)} %get-tuple-element.51), channel_id=1, source_target_pairs={{0,16},{4,20},{8,24},{12,28},{16,0},{20,4},{24,8},{28,12},{1,17},{... | collective-permute-start | bytes 319496 | tf_op jit(solution)/shard_map/ppermute | solution.py:36
  17.2 6.8 %collective-permute-start.4 = (bf16[32,1664]{1,0:T(8,128)(2,1)S(1)}, bf16[32,1664]{1,0:T(8,128)(2,1)S(1)}, u32[]{:S(2)}, u32[]{:S(2)}) collective-permute-start(bf16[32,1664]{1,0:T(8,128)(2,1)S(1)} %get-tuple-element.51), channel_id=1, source_target_pairs={{0,24},{4,28},{8,0},{12,4},{16,8},{20,12},{24,16},{28,20},{1,25},{... | collective-permute-start | bytes 319496 | tf_op jit(solution)/shard_map/ppermute | solution.py:36
  18.6 1.5 %copy-start.2 = (bf16[5,1536,128]{2,1,0:T(8,128)(2,1)S(1)}, bf16[5,1536,128]{2,1,0:T(8,128)(2,1)}, u32[]{:S(2)}) copy-start(bf16[5,1536,128]{2,1,0:T(8,128)(2,1)} %up_hbm.1) | copy-start | bytes 5898244
  20.1 1.5 %copy-start.3 = (bf16[5,128,1536]{2,1,0:T(8,128)(2,1)S(1)}, bf16[5,128,1536]{2,1,0:T(8,128)(2,1)}, u32[]{:S(2)}) copy-start(bf16[5,128,1536]{2,1,0:T(8,128)(2,1)} %param.23) | copy-start | bytes 5898244
  24.0 8.2 %collective-permute-start.10 = (bf16[32,1664]{1,0:T(8,128)(2,1)S(1)}, bf16[32,1664]{1,0:T(8,128)(2,1)S(1)}, u32[]{:S(2)}, u32[]{:S(2)}) collective-permute-start(bf16[32,1664]{1,0:T(8,128)(2,1)S(1)} %get-tuple-element.57), channel_id=1, source_target_pairs={{0,8},{4,12},{8,16},{12,20},{16,24},{20,28},{24,0},{28,4},{1,9},{5... | collective-permute-start | bytes 319496 | tf_op jit(solution)/shard_map/ppermute | solution.py:36
  26.8 8.5 %collective-permute-start.11 = (bf16[32,1664]{1,0:T(8,128)(2,1)S(1)}, bf16[32,1664]{1,0:T(8,128)(2,1)S(1)}, u32[]{:S(2)}, u32[]{:S(2)}) collective-permute-start(bf16[32,1664]{1,0:T(8,128)(2,1)S(1)} %get-tuple-element.57), channel_id=1, source_target_pairs={{0,16},{4,20},{8,24},{12,28},{16,0},{20,4},{24,8},{28,12},{1,17},{... | collective-permute-start | bytes 319496 | tf_op jit(solution)/shard_map/ppermute | solution.py:36
  28.4 6.9 %collective-permute-start.12 = (bf16[32,1664]{1,0:T(8,128)(2,1)S(1)}, bf16[32,1664]{1,0:T(8,128)(2,1)S(1)}, u32[]{:S(2)}, u32[]{:S(2)}) collective-permute-start(bf16[32,1664]{1,0:T(8,128)(2,1)S(1)} %get-tuple-element.57), channel_id=1, source_target_pairs={{0,24},{4,28},{8,0},{12,4},{16,8},{20,12},{24,16},{28,20},{1,25},{... | collective-permute-start | bytes 319496 | tf_op jit(solution)/shard_map/ppermute | solution.py:36
  29.2 9.4 %collective-permute-start.7 = (bf16[64,1664]{1,0:T(8,128)(2,1)S(1)}, bf16[64,1664]{1,0:T(8,128)(2,1)S(1)}, u32[]{:S(2)}, u32[]{:S(2)}) collective-permute-start(bf16[64,1664]{1,0:T(8,128)(2,1)S(1)} %get-tuple-element.55), channel_id=1, source_target_pairs={{0,2},{1,3},{2,0},{3,1},{4,6},{5,7},{6,4},{7,5},{8,10},{9,11},{10,... | collective-permute-start | bytes 638984 | tf_op jit(solution)/shard_map/ppermute | solution.py:44
  30.8 8.5 %collective-permute-start.6 = (bf16[64,1664]{1,0:T(8,128)(2,1)S(1)}, bf16[64,1664]{1,0:T(8,128)(2,1)S(1)}, u32[]{:S(2)}, u32[]{:S(2)}) collective-permute-start(bf16[64,1664]{1,0:T(8,128)(2,1)S(1)} %get-tuple-element.54), channel_id=1, source_target_pairs={{0,4},{4,0},{8,12},{12,8},{16,20},{20,16},{24,28},{28,24},{1,5},{5... | collective-permute-start | bytes 638984 | tf_op jit(solution)/shard_map/ppermute | solution.py:40
  35.4 8.2 %collective-permute-start.14 = (bf16[64,1664]{1,0:T(8,128)(2,1)S(1)}, bf16[64,1664]{1,0:T(8,128)(2,1)S(1)}, u32[]{:S(2)}, u32[]{:S(2)}) collective-permute-start(bf16[64,1664]{1,0:T(8,128)(2,1)S(1)} %pad_maximum_fusion.9), channel_id=1, source_target_pairs={{0,2},{1,3},{2,0},{3,1},{4,6},{5,7},{6,4},{7,5},{8,10},{9,11},{10,... | collective-permute-start | bytes 638984 | tf_op jit(solution)/shard_map/ppermute | solution.py:44
  37.0 8.2 %collective-permute-start.13 = (bf16[64,1664]{1,0:T(8,128)(2,1)S(1)}, bf16[64,1664]{1,0:T(8,128)(2,1)S(1)}, u32[]{:S(2)}, u32[]{:S(2)}) collective-permute-start(bf16[64,1664]{1,0:T(8,128)(2,1)S(1)} %pad_maximum_fusion.8), channel_id=1, source_target_pairs={{0,4},{4,0},{8,12},{12,8},{16,20},{20,16},{24,28},{28,24},{1,5},{5... | collective-permute-start | bytes 638984 | tf_op jit(solution)/shard_map/ppermute | solution.py:40
  38.6 14.4 %collective-permute-start.9 = (bf16[128,1664]{1,0:T(8,128)(2,1)S(1)}, bf16[128,1664]{1,0:T(8,128)(2,1)S(1)}, u32[]{:S(2)}, u32[]{:S(2)}) collective-permute-start(bf16[128,1664]{1,0:T(8,128)(2,1)S(1)} %pad_maximum_fusion.3), channel_id=1, source_target_pairs={{0,4},{4,0},{8,12},{12,8},{16,20},{20,16},{24,28},{28,24},{1,5},{5... | collective-permute-start | bytes 1277960 | tf_op jit(solution)/shard_map/ppermute | solution.py:40
  39.3 13.8 %collective-permute-start.8 = (bf16[128,1664]{1,0:T(8,128)(2,1)S(1)}, bf16[128,1664]{1,0:T(8,128)(2,1)S(1)}, u32[]{:S(2)}, u32[]{:S(2)}) collective-permute-start(bf16[128,1664]{1,0:T(8,128)(2,1)S(1)} %pad_maximum_fusion.2), channel_id=1, source_target_pairs={{0,2},{1,3},{2,0},{3,1},{4,6},{5,7},{6,4},{7,5},{8,10},{9,11},{10,... | collective-permute-start | bytes 1277960 | tf_op jit(solution)/shard_map/ppermute | solution.py:44
  53.1 2.7 %collective-permute-start.15 = (bf16[256,1664]{1,0:T(8,128)(2,1)S(1)}, bf16[256,1664]{1,0:T(8,128)(2,1)S(1)}, u32[]{:S(2)}, u32[]{:S(2)}) collective-permute-start(bf16[256,1664]{1,0:T(8,128)(2,1)S(1)} %pad_maximum_fusion.near_ref), channel_id=1, source_target_pairs={{0,1},{1,0},{2,3},{3,2},{4,5},{5,4},{6,7},{7,6},{8,9},{9,8},{10,11... | collective-permute-start | bytes 2555912 | tf_op jit(solution)/shard_map/ppermute | solution.py:48
  53.2 3.6 %collective-permute-start.16 = (bf16[256,1664]{1,0:T(8,128)(2,1)S(1)}, bf16[256,1664]{1,0:T(8,128)(2,1)S(1)}, u32[]{:S(2)}, u32[]{:S(2)}) collective-permute-start(bf16[256,1664]{1,0:T(8,128)(2,1)S(1)} %constant_dynamic-update-slice_fusion.far_ref), channel_id=1, source_target_pairs={{0,1},{1,0},{2,3},{3,2},{4,5},{5,4},{6,7},{7,6},{8,9},{9,8},{10,11... | collective-permute-start | bytes 2555912 | tf_op jit(solution)/shard_map/ppermute | solution.py:48
  53.7 11.8 %collective-permute-start.22 = (bf16[128,1664]{1,0:T(8,128)(2,1)S(1)}, bf16[128,1664]{1,0:T(8,128)(2,1)S(1)}, u32[]{:S(2)}, u32[]{:S(2)}) collective-permute-start(bf16[128,1664]{1,0:T(8,128)(2,1)S(1)} %pad_maximum_fusion.5), channel_id=1, source_target_pairs={{0,4},{4,0},{8,12},{12,8},{16,20},{20,16},{24,28},{28,24},{1,5},{5... | collective-permute-start | bytes 1277960 | tf_op jit(solution)/shard_map/ppermute | solution.py:40
  55.2 11.5 %collective-permute-start.21 = (bf16[128,1664]{1,0:T(8,128)(2,1)S(1)}, bf16[128,1664]{1,0:T(8,128)(2,1)S(1)}, u32[]{:S(2)}, u32[]{:S(2)}) collective-permute-start(bf16[128,1664]{1,0:T(8,128)(2,1)S(1)} %pad_maximum_fusion.4), channel_id=1, source_target_pairs={{0,2},{1,3},{2,0},{3,1},{4,6},{5,7},{6,4},{7,5},{8,10},{9,11},{10,... | collective-permute-start | bytes 1277960 | tf_op jit(solution)/shard_map/ppermute | solution.py:44
  55.7 13.7 %collective-permute-start.23 = (bf16[256,1664]{1,0:T(8,128)(2,1)S(1)}, bf16[256,1664]{1,0:T(8,128)(2,1)S(1)}, u32[]{:S(2)}, u32[]{:S(2)}) collective-permute-start(bf16[256,1664]{1,0:T(8,128)(2,1)S(1)} %pad_maximum_fusion.1.near_ref), channel_id=1, source_target_pairs={{0,1},{1,0},{2,3},{3,2},{4,5},{5,4},{6,7},{7,6},{8,9},{9,8},{10,11... | collective-permute-start | bytes 2555912 | tf_op jit(solution)/shard_map/ppermute | solution.py:48
  64.8 2.5 %collective-permute-start.18 = (bf16[256,1536]{1,0:T(8,128)(2,1)S(1)}, bf16[256,1536]{1,0:T(8,128)(2,1)S(1)}, u32[]{:S(2)}, u32[]{:S(2)}) collective-permute-start(bf16[256,1536]{1,0:T(8,128)(2,1)S(1)} %get-tuple-element.67), channel_id=1, source_target_pairs={{0,1},{1,0},{2,3},{3,2},{4,5},{5,4},{6,7},{7,6},{8,9},{9,8},{10,11... | collective-permute-start | bytes 2359304 | tf_op jit(solution)/shard_map/ppermute | solution.py:48
  66.8 2.6 %collective-permute-start.24 = (bf16[256,1664]{1,0:T(8,128)(2,1)S(1)}, bf16[256,1664]{1,0:T(8,128)(2,1)S(1)}, u32[]{:S(2)}, u32[]{:S(2)}) collective-permute-start(bf16[256,1664]{1,0:T(8,128)(2,1)S(1)} %constant_dynamic-update-slice_fusion.2.far_ref), channel_id=1, source_target_pairs={{0,1},{1,0},{2,3},{3,2},{4,5},{5,4},{6,7},{7,6},{8,9},{9,8},{10,11... | collective-permute-start | bytes 2555912 | tf_op jit(solution)/shard_map/ppermute | solution.py:48
  66.9 12.4 %collective-permute-start.17 = (bf16[256,1536]{1,0:T(8,128)(2,1)S(1)}, bf16[256,1536]{1,0:T(8,128)(2,1)S(1)}, u32[]{:S(2)}, u32[]{:S(2)}) collective-permute-start(bf16[256,1536]{1,0:T(8,128)(2,1)S(1)} %get-tuple-element.65), channel_id=1, source_target_pairs={{0,1},{1,0},{2,3},{3,2},{4,5},{5,4},{6,7},{7,6},{8,9},{9,8},{10,11... | collective-permute-start | bytes 2359304 | tf_op jit(solution)/shard_map/ppermute | solution.py:48
  67.6 10.2 %copy-start.8 = (bf16[1536]{0:T(1024)(128)(2,1)S(1)}, bf16[1536]{0:T(1024)(128)(2,1)}, u32[]{:S(2)}) copy-start(bf16[1536]{0:T(1024)(128)(2,1)} %param.16) | copy-start | bytes 9220
  67.6 11.2 %collective-permute-start.19 = (bf16[128,1536]{1,0:T(8,128)(2,1)S(1)}, bf16[128,1536]{1,0:T(8,128)(2,1)S(1)}, u32[]{:S(2)}, u32[]{:S(2)}) collective-permute-start(bf16[128,1536]{1,0:T(8,128)(2,1)S(1)} %get-tuple-element.118), channel_id=1, source_target_pairs={{0,2},{1,3},{2,0},{3,1},{4,6},{5,7},{6,4},{7,5},{8,10},{9,11},{10,... | collective-permute-start | bytes 1179656 | tf_op jit(solution)/shard_map/ppermute | solution.py:44
  68.2 11.1 %collective-permute-start.20 = (bf16[128,1536]{1,0:T(8,128)(2,1)S(1)}, bf16[128,1536]{1,0:T(8,128)(2,1)S(1)}, u32[]{:S(2)}, u32[]{:S(2)}) collective-permute-start(bf16[128,1536]{1,0:T(8,128)(2,1)S(1)} %get-tuple-element.117), channel_id=1, source_target_pairs={{0,4},{4,0},{8,12},{12,8},{16,20},{20,16},{24,28},{28,24},{1,5},{5... | collective-permute-start | bytes 1179656 | tf_op jit(solution)/shard_map/ppermute | solution.py:40
  77.7 4.4 %collective-permute-start.27 = (bf16[256,1536]{1,0:T(8,128)(2,1)S(1)}, bf16[256,1536]{1,0:T(8,128)(2,1)S(1)}, u32[]{:S(2)}, u32[]{:S(2)}) collective-permute-start(bf16[256,1536]{1,0:T(8,128)(2,1)S(1)} %get-tuple-element.75), channel_id=1, source_target_pairs={{0,1},{1,0},{2,3},{3,2},{4,5},{5,4},{6,7},{7,6},{8,9},{9,8},{10,11... | collective-permute-start | bytes 2359304 | tf_op jit(solution)/shard_map/ppermute | solution.py:48
  77.8 14.6 %collective-permute-start.31 = (bf16[256,1536]{1,0:T(8,128)(2,1)S(1)}, bf16[256,1536]{1,0:T(8,128)(2,1)S(1)}, u32[]{:S(2)}, u32[]{:S(2)}) collective-permute-start(bf16[256,1536]{1,0:T(8,128)(2,1)S(1)} %get-tuple-element.74), channel_id=1, source_target_pairs={{0,1},{1,0},{2,3},{3,2},{4,5},{5,4},{6,7},{7,6},{8,9},{9,8},{10,11... | collective-permute-start | bytes 2359304 | tf_op jit(solution)/shard_map/ppermute | solution.py:48
  79.4 7.3 %collective-permute-start.25 = (bf16[64,1536]{1,0:T(8,128)(2,1)S(1)}, bf16[64,1536]{1,0:T(8,128)(2,1)S(1)}, u32[]{:S(2)}, u32[]{:S(2)}) collective-permute-start(bf16[64,1536]{1,0:T(8,128)(2,1)S(1)} %get-tuple-element.116), channel_id=1, source_target_pairs={{0,4},{4,0},{8,12},{12,8},{16,20},{20,16},{24,28},{28,24},{1,5},{5... | collective-permute-start | bytes 589832 | tf_op jit(solution)/shard_map/ppermute | solution.py:40
  80.5 7.8 %collective-permute-start.26 = (bf16[64,1536]{1,0:T(8,128)(2,1)S(1)}, bf16[64,1536]{1,0:T(8,128)(2,1)S(1)}, u32[]{:S(2)}, u32[]{:S(2)}) collective-permute-start(bf16[64,1536]{1,0:T(8,128)(2,1)S(1)} %get-tuple-element.115), channel_id=1, source_target_pairs={{0,2},{1,3},{2,0},{3,1},{4,6},{5,7},{6,4},{7,5},{8,10},{9,11},{10,... | collective-permute-start | bytes 589832 | tf_op jit(solution)/shard_map/ppermute | solution.py:44
  82.3 12.3 %collective-permute-start.32 = (bf16[128,1536]{1,0:T(8,128)(2,1)S(1)}, bf16[128,1536]{1,0:T(8,128)(2,1)S(1)}, u32[]{:S(2)}, u32[]{:S(2)}) collective-permute-start(bf16[128,1536]{1,0:T(8,128)(2,1)S(1)} %get-tuple-element.114), channel_id=1, source_target_pairs={{0,2},{1,3},{2,0},{3,1},{4,6},{5,7},{6,4},{7,5},{8,10},{9,11},{10,... | collective-permute-start | bytes 1179656 | tf_op jit(solution)/shard_map/ppermute | solution.py:44
  82.8 11.8 %collective-permute-start.33 = (bf16[128,1536]{1,0:T(8,128)(2,1)S(1)}, bf16[128,1536]{1,0:T(8,128)(2,1)S(1)}, u32[]{:S(2)}, u32[]{:S(2)}) collective-permute-start(bf16[128,1536]{1,0:T(8,128)(2,1)S(1)} %get-tuple-element.113), channel_id=1, source_target_pairs={{0,4},{4,0},{8,12},{12,8},{16,20},{20,16},{24,28},{28,24},{1,5},{5... | collective-permute-start | bytes 1179656 | tf_op jit(solution)/shard_map/ppermute | solution.py:40
  88.6 8.8 %collective-permute-start.30 = (bf16[32,1536]{1,0:T(8,128)(2,1)S(1)}, bf16[32,1536]{1,0:T(8,128)(2,1)S(1)}, u32[]{:S(2)}, u32[]{:S(2)}) collective-permute-start(bf16[32,1536]{1,0:T(8,128)(2,1)S(1)} %pad_maximum_fusion.12), channel_id=1, source_target_pairs={{0,8},{4,12},{8,16},{12,20},{16,24},{20,28},{24,0},{28,4},{1,9},{5... | collective-permute-start | bytes 294920 | tf_op jit(solution)/shard_map/ppermute | solution.py:36
  91.4 6.2 %collective-permute-start.29 = (bf16[32,1536]{1,0:T(8,128)(2,1)S(1)}, bf16[32,1536]{1,0:T(8,128)(2,1)S(1)}, u32[]{:S(2)}, u32[]{:S(2)}) collective-permute-start(bf16[32,1536]{1,0:T(8,128)(2,1)S(1)} %pad_maximum_fusion.11), channel_id=1, source_target_pairs={{0,16},{4,20},{8,24},{12,28},{16,0},{20,4},{24,8},{28,12},{1,17},{... | collective-permute-start | bytes 294920 | tf_op jit(solution)/shard_map/ppermute | solution.py:36
  92.4 5.7 %collective-permute-start.28 = (bf16[32,1536]{1,0:T(8,128)(2,1)S(1)}, bf16[32,1536]{1,0:T(8,128)(2,1)S(1)}, u32[]{:S(2)}, u32[]{:S(2)}) collective-permute-start(bf16[32,1536]{1,0:T(8,128)(2,1)S(1)} %pad_maximum_fusion.10), channel_id=1, source_target_pairs={{0,24},{4,28},{8,0},{12,4},{16,8},{20,12},{24,16},{28,20},{1,25},{... | collective-permute-start | bytes 294920 | tf_op jit(solution)/shard_map/ppermute | solution.py:36
  94.8 5.7 %collective-permute-start.37 = (bf16[64,1536]{1,0:T(8,128)(2,1)S(1)}, bf16[64,1536]{1,0:T(8,128)(2,1)S(1)}, u32[]{:S(2)}, u32[]{:S(2)}) collective-permute-start(bf16[64,1536]{1,0:T(8,128)(2,1)S(1)} %get-tuple-element.112), channel_id=1, source_target_pairs={{0,4},{4,0},{8,12},{12,8},{16,20},{20,16},{24,28},{28,24},{1,5},{5... | collective-permute-start | bytes 589832 | tf_op jit(solution)/shard_map/ppermute | solution.py:40
  96.0 5.7 %collective-permute-start.38 = (bf16[64,1536]{1,0:T(8,128)(2,1)S(1)}, bf16[64,1536]{1,0:T(8,128)(2,1)S(1)}, u32[]{:S(2)}, u32[]{:S(2)}) collective-permute-start(bf16[64,1536]{1,0:T(8,128)(2,1)S(1)} %get-tuple-element.111), channel_id=1, source_target_pairs={{0,2},{1,3},{2,0},{3,1},{4,6},{5,7},{6,4},{7,5},{8,10},{9,11},{10,... | collective-permute-start | bytes 589832 | tf_op jit(solution)/shard_map/ppermute | solution.py:44
  101.7 7.0 %collective-permute-start.41 = (bf16[32,1536]{1,0:T(8,128)(2,1)S(1)}, bf16[32,1536]{1,0:T(8,128)(2,1)S(1)}, u32[]{:S(2)}, u32[]{:S(2)}) collective-permute-start(bf16[32,1536]{1,0:T(8,128)(2,1)S(1)} %pad_maximum_fusion.15), channel_id=1, source_target_pairs={{0,8},{4,12},{8,16},{12,20},{16,24},{20,28},{24,0},{28,4},{1,9},{5... | collective-permute-start | bytes 294920 | tf_op jit(solution)/shard_map/ppermute | solution.py:36
  104.6 6.3 %collective-permute-start.40 = (bf16[32,1536]{1,0:T(8,128)(2,1)S(1)}, bf16[32,1536]{1,0:T(8,128)(2,1)S(1)}, u32[]{:S(2)}, u32[]{:S(2)}) collective-permute-start(bf16[32,1536]{1,0:T(8,128)(2,1)S(1)} %pad_maximum_fusion.14), channel_id=1, source_target_pairs={{0,16},{4,20},{8,24},{12,28},{16,0},{20,4},{24,8},{28,12},{1,17},{... | collective-permute-start | bytes 294920 | tf_op jit(solution)/shard_map/ppermute | solution.py:36
  105.5 5.7 %collective-permute-start.39 = (bf16[32,1536]{1,0:T(8,128)(2,1)S(1)}, bf16[32,1536]{1,0:T(8,128)(2,1)S(1)}, u32[]{:S(2)}, u32[]{:S(2)}) collective-permute-start(bf16[32,1536]{1,0:T(8,128)(2,1)S(1)} %pad_maximum_fusion.13), channel_id=1, source_target_pairs={{0,24},{4,28},{8,0},{12,4},{16,8},{20,12},{24,16},{28,20},{1,25},{... | collective-permute-start | bytes 294920 | tf_op jit(solution)/shard_map/ppermute | solution.py:36
  107.2 10.7 %collective-permute-start.34 = (bf16[32,1536]{1,0:T(8,128)(2,1)S(1)}, bf16[32,1536]{1,0:T(8,128)(2,1)S(1)}, u32[]{:S(2)}, u32[]{:S(2)}) collective-permute-start(bf16[32,1536]{1,0:T(8,128)(2,1)S(1)} %multiply_convert_fusion.1.refs_0_), channel_id=1, source_target_pairs={{0,1},{1,0},{2,3},{3,2},{4,5},{5,4},{6,7},{7,6},{8,9},{9,8},{10,11... | collective-permute-start | bytes 294920 | tf_op jit(solution)/shard_map/ppermute | solution.py:48
  107.3 10.6 %collective-permute-start.35 = (bf16[32,1536]{1,0:T(8,128)(2,1)S(1)}, bf16[32,1536]{1,0:T(8,128)(2,1)S(1)}, u32[]{:S(2)}, u32[]{:S(2)}) collective-permute-start(bf16[32,1536]{1,0:T(8,128)(2,1)S(1)} %multiply_convert_fusion.1.refs_0_), channel_id=1, source_target_pairs={{0,2},{1,3},{2,0},{3,1},{4,6},{5,7},{6,4},{7,5},{8,10},{9,11},{10,... | collective-permute-start | bytes 294920 | tf_op jit(solution)/shard_map/ppermute | solution.py:44
  108.8 9.1 %collective-permute-start.36 = (bf16[32,1536]{1,0:T(8,128)(2,1)S(1)}, bf16[32,1536]{1,0:T(8,128)(2,1)S(1)}, u32[]{:S(2)}, u32[]{:S(2)}) collective-permute-start(bf16[32,1536]{1,0:T(8,128)(2,1)S(1)} %multiply_convert_fusion.1.refs_0_), channel_id=1, source_target_pairs={{0,3},{1,2},{2,1},{3,0},{4,7},{5,6},{6,5},{7,4},{8,11},{9,10},{10,... | collective-permute-start | bytes 294920 | tf_op jit(solution)/shard_map/ppermute | solution.py:366

commit v4 on v3

--- a/solution.py
+++ b/solution.py
@@ -201,22 +201,18 @@
     first_ref,
     near_ref,
     far_ref,
-    other_near_ref,
-    other_far_ref,
     both_ref,
     down_ref,
     loaded_hbm,
     near_out,
     far_out,
-    other_near_out,
-    other_far_out,
     rows_ref,
     hidden_ref,
 ):
     held, width, units = both_ref.shape
     units = units // 2
     start = 0
-    for piece in (near_ref, far_ref, other_near_ref, other_far_ref):
+    for piece in (near_ref, far_ref):
         rows_ref[start : start + piece.shape[0]] = piece[...]
         start += piece.shape[0]
     block = min(ROW_BLOCK, start)
@@ -240,7 +236,7 @@
             ).astype(jnp.bfloat16)
             give(out, left)
 
-    outs = (near_out, far_out, other_near_out, other_far_out)
+    outs = (near_out, far_out)
     size = start // len(outs)
     for number in range(start // block):
 
@@ -308,8 +304,9 @@
 
     def gather_near(self, *then):
         first, second = after(self.first, *then), after(self.second, *then)
-        self.first = jnp.concatenate([first, flip_inner(first)], axis=0)
-        self.second = jnp.concatenate([second, flip_upper(second)], axis=0)
+        inner, upper = lax.optimization_barrier((flip_inner(first), flip_upper(second)))
+        self.first = jnp.concatenate([first, inner], axis=0)
+        self.second = jnp.concatenate([second, upper], axis=0)
 
     def gather_far(self):
         self.far_pair = flip_upper(self.first), flip_inner(self.second)
@@ -415,16 +412,17 @@
 
     send, keep = attend(place, first, context, w_out)
     got = flip_lower(send)
-    table = slot_of_pick(after(slot_expert, send), copy_pick, experts)[0]
+    parts = []
+    for number in range(CHUNKS):
+        at = slice(number * rows, (number + 1) * rows)
+        parts.append(short(keep[1, at] + wide(got[1, at])))
+    table = slot_of_pick(after(slot_expert, parts[0]), copy_pick, experts)[0]
     lanes = -(-slots // LANES) * LANES
     slot_hot = table[:, None] == jnp.arange(lanes, dtype=jnp.int32)[None, :]
     slot_hot = slot_hot.astype(jnp.bfloat16)
 
     gain = pre_gain.reshape(1, -1)
-    uppers = []
-    for number in range(CHUNKS):
-        at = slice(number * rows, (number + 1) * rows)
-        uppers.append(flip_upper(short(keep[1, at] + wide(got[1, at]))))
+    uppers = [flip_upper(part) for part in parts]
     middles, chunks = [], []
     for number in range(CHUNKS):
         middle, row = norm_rows(
@@ -435,29 +433,29 @@
 
     both, down, loaded = load_weights(w_gate, w_up, after(down, uppers))
 
-    def serve(chunk, *then):
-        pieces = [after(p, *then) for p in chunk.pieces + chunk.others]
-        outs = expert_rows(first, pieces, both, down, loaded)
-        chunk.own, chunk.away = outs[:2], outs[2:]
+    def serve(pieces, *then):
+        return expert_rows(first, [after(p, *then) for p in pieces], both, down, loaded)
 
     one, two = chunks
     one.gather_outer()
     one.first, one.second = after((one.first, one.second), loaded)
+    one.gather_near()
     two.gather_outer(one.first)
-    one.gather_near()
     one.gather_far()
     two.gather_near()
-    one.gathered_far(two.first, two.second)
+    one.gathered_far()
     one.gather_lower(one.pieces[1])
     two.gather_far()
-    serve(one)
+    one.away = serve(one.others)
     one.back_lower()
-    two.gathered_far(one.away)
+    one.own = serve(one.pieces, one.away)
+    two.gathered_far(one.own)
     two.gather_lower()
     one.back_far()
-    serve(two, one.far)
-    one.far_first, one.far_second = after((one.far_first, one.far_second), two.away)
+    two.away = serve(two.others, one.far)
     two.back_lower()
+    two.own = serve(two.pieces, two.away)
+    one.far_first, one.far_second = after((one.far_first, one.far_second), two.own)
     one.back_near()
     two.back_far()
     one.near_first, one.near_second = after((one.near_first, one.near_second), two.far)

time: 119 us -> 114 us (0.958)
  starting transfers between devices: 46.9 us -> 44.3 us
  other arithmetic: 4.67 us -> 2.63 us
  waiting for transfers between devices: 34.7 us -> 33.1 us
    ppermute x12, starting transfers between devices: 21.9 us -> 19.3 us  [turn(): lax.ppermute(value, 'ep', [(i, (i + 2 * step) % count) for i in range(cou...]
    ppermute x11, waiting for transfers between devices: 11.6 us -> 9 us  [flip_upper(): lax.ppermute(value, 'tp', [(i, i ^ 2) for i in range(lax.axis_size('tp'))])]
    ppermute x11, starting transfers between devices: 12.4 us -> 13.9 us  [flip_upper(): lax.ppermute(value, 'tp', [(i, i ^ 2) for i in range(lax.axis_size('tp'))])]
    ppermute x8, starting transfers between devices: 9.65 us -> 8.22 us  [flip_inner(): lax.ppermute(value, 'ep', [(i, i ^ 1) for i in range(lax.axis_size('ep'))])]
    unnamed x24 -> x26, local copies, waits for them, and re-layouts: 5.79 us -> 6.69 us
    pallas_call x2 -> x4, Pallas kernels: 16.3 us -> 16.7 us  [expert_rows(): pl.pallas_call(expert_kernel, out_shape=[jax.ShapeDtypeStruct((p.shape[0]...]
  transfers between devices with their start and end apart: 42 -> 42, of which waited for: 20 -> 19; matrix products, arithmetic and copies ran while one was open for 4% -> 3% of each run, Pallas kernels for 15% -> 16%
where the time goes in v4:
time: 114 us
  starting transfers between devices  44.3 us (39%)
  waiting for transfers between devices  33.1 us (29%)
  Pallas kernels  20.2 us (18%)
  local copies, waits for them, and re-layouts  6.84 us (6%)
  blocking collectives  6.15 us (5%)
  other arithmetic  2.63 us (2%)
    ppermute x12, starting transfers between devices, turn(): lax.ppermute(value, 'ep', [(i, (i + 2 * step) % count) for i in range(cou...  19.3 us
    pallas_call x4, Pallas kernels, expert_rows(): pl.pallas_call(expert_kernel, out_shape=[jax.ShapeDtypeStruct((p.shape[0]...  16.7 us
    ppermute x8, waiting for transfers between devices, flip_inner(): lax.ppermute(value, 'ep', [(i, i ^ 1) for i in range(lax.axis_size('ep'))])  16.3 us
    ppermute x11, starting transfers between devices, flip_upper(): lax.ppermute(value, 'tp', [(i, i ^ 2) for i in range(lax.axis_size('tp'))])  13.9 us
    ppermute x11, waiting for transfers between devices, flip_upper(): lax.ppermute(value, 'tp', [(i, i ^ 2) for i in range(lax.axis_size('tp'))])  9 us
    ppermute x8, starting transfers between devices, flip_inner(): lax.ppermute(value, 'ep', [(i, i ^ 1) for i in range(lax.axis_size('ep'))])  8.22 us
    ppermute x12, waiting for transfers between devices, turn(): lax.ppermute(value, 'ep', [(i, (i + 2 * step) % count) for i in range(cou...  7.69 us
    unnamed x26, local copies, waits for them, and re-layouts  6.69 us
  transfers between devices with their start and end apart: 42, of which 19 were waited for; matrix products, arithmetic and copies ran while one was open for 3% of the time, Pallas kernels for 16%

profile of v4, /device:TPU:0, one launch (start us, length us, event | category | flops | bytes accessed | tf_op | source)
XLA Modules:
  0.0 113.6 jit_solution(116416834826726088)
XLA Ops:
  0.0 1.3 %copy-done.4 = bf16[384,1536]{1,0:T(8,128)(2,1)S(1)} copy-done((bf16[384,1536]{1,0:T(8,128)(2,1)S(1)}, bf16[384,1536]{1,0:T(8,128)(2,1)}, u32[]{:S(2)}) %copy-start.4) | copy-done | bytes 1179672
  1.3 0.9 copy-done.5
  2.3 0.6 attend.1
  2.9 0.5 collective-permute-start
  3.4 1.1 copy.18.router_ref
  4.8 3.0 %collective-permute-start.1 = (bf16[32,1536]{1,0:T(8,128)(2,1)S(1)}, bf16[32,1536]{1,0:T(8,128)(2,1)S(1)}, u32[]{:S(2)}, u32[]{:S(2)}) collective-permute-start(bf16[32,1536]{1,0:T(8,128)(2,1)S(1)} %get-tuple-element.132), channel_id=1, source_target_pairs={{0,2},{1,3},{2,0},{3,1},{4,6},{5,7},{6,4},{7,5},{8,10},{9,11},{10,... | collective-permute-start | bytes 294920 | tf_op jit(solution)/shard_map/ppermute | solution.py:44
  8.3 2.6 %collective-permute-done.1.upper_ref = bf16[32,1536]{1,0:T(8,128)(2,1)S(1)} collective-permute-done((bf16[32,1536]{1,0:T(8,128)(2,1)S(1)}, bf16[32,1536]{1,0:T(8,128)(2,1)S(1)}, u32[]{:S(2)}, u32[]{:S(2)}) %collective-permute-start.1) | collective-permute-done | bytes 98336 | tf_op jit(solution)/shard_map/ppermute | solution.py:44
  10.9 0.5 norm_rows.2
  11.4 2.0 %collective-permute-start.2 = (bf16[32,1664]{1,0:T(8,128)(2,1)S(1)}, bf16[32,1664]{1,0:T(8,128)(2,1)S(1)}, u32[]{:S(2)}, u32[]{:S(2)}) collective-permute-start(bf16[32,1664]{1,0:T(8,128)(2,1)S(1)} %get-tuple-element.57), channel_id=1, source_target_pairs={{0,8},{4,12},{8,16},{12,20},{16,24},{20,28},{24,0},{28,4},{1,9},{5... | collective-permute-start | bytes 319496 | tf_op jit(solution)/shard_map/ppermute | solution.py:36
  13.4 2.6 %collective-permute-start.3 = (bf16[32,1664]{1,0:T(8,128)(2,1)S(1)}, bf16[32,1664]{1,0:T(8,128)(2,1)S(1)}, u32[]{:S(2)}, u32[]{:S(2)}) collective-permute-start(bf16[32,1664]{1,0:T(8,128)(2,1)S(1)} %get-tuple-element.57), channel_id=1, source_target_pairs={{0,16},{4,20},{8,24},{12,28},{16,0},{20,4},{24,8},{28,12},{1,17},{... | collective-permute-start | bytes 319496 | tf_op jit(solution)/shard_map/ppermute | solution.py:36
  16.0 1.3 %collective-permute-start.4 = (bf16[32,1664]{1,0:T(8,128)(2,1)S(1)}, bf16[32,1664]{1,0:T(8,128)(2,1)S(1)}, u32[]{:S(2)}, u32[]{:S(2)}) collective-permute-start(bf16[32,1664]{1,0:T(8,128)(2,1)S(1)} %get-tuple-element.57), channel_id=1, source_target_pairs={{0,24},{4,28},{8,0},{12,4},{16,8},{20,12},{24,16},{28,20},{1,25},{... | collective-permute-start | bytes 319496 | tf_op jit(solution)/shard_map/ppermute | solution.py:36
  17.4 1.5 %copy-done.2 = bf16[5,1536,128]{2,1,0:T(8,128)(2,1)S(1)} copy-done((bf16[5,1536,128]{2,1,0:T(8,128)(2,1)S(1)}, bf16[5,1536,128]{2,1,0:T(8,128)(2,1)}, u32[]{:S(2)}) %copy-start.2) | copy-done | bytes 1966104
  18.9 1.5 %copy-done.3 = bf16[5,128,1536]{2,1,0:T(8,128)(2,1)S(1)} copy-done((bf16[5,128,1536]{2,1,0:T(8,128)(2,1)S(1)}, bf16[5,128,1536]{2,1,0:T(8,128)(2,1)}, u32[]{:S(2)}) %copy-start.3) | copy-done | bytes 1966104
  20.5 1.0 load_weights.1
  21.5 0.9 collective-permute-done.3
  22.6 1.6 %collective-permute-start.6 = (bf16[64,1664]{1,0:T(8,128)(2,1)S(1)}, bf16[64,1664]{1,0:T(8,128)(2,1)S(1)}, u32[]{:S(2)}, u32[]{:S(2)}) collective-permute-start(bf16[64,1664]{1,0:T(8,128)(2,1)S(1)} %get-tuple-element.60), channel_id=1, source_target_pairs={{0,4},{4,0},{8,12},{12,8},{16,20},{20,16},{24,28},{28,24},{1,5},{5... | collective-permute-start | bytes 638984 | tf_op jit(solution)/shard_map/ppermute | solution.py:40
  24.2 1.7 %collective-permute-start.7 = (bf16[64,1664]{1,0:T(8,128)(2,1)S(1)}, bf16[64,1664]{1,0:T(8,128)(2,1)S(1)}, u32[]{:S(2)}, u32[]{:S(2)}) collective-permute-start(bf16[64,1664]{1,0:T(8,128)(2,1)S(1)} %get-tuple-element.61), channel_id=1, source_target_pairs={{0,2},{1,3},{2,0},{3,1},{4,6},{5,7},{6,4},{7,5},{8,10},{9,11},{10,... | collective-permute-start | bytes 638984 | tf_op jit(solution)/shard_map/ppermute | solution.py:44
  25.9 0.5 norm_rows.3
  26.4 3.0 %collective-permute-done.6 = bf16[64,1664]{1,0:T(8,128)(2,1)S(1)} collective-permute-done((bf16[64,1664]{1,0:T(8,128)(2,1)S(1)}, bf16[64,1664]{1,0:T(8,128)(2,1)S(1)}, u32[]{:S(2)}, u32[]{:S(2)}) %collective-permute-start.6) | collective-permute-done | bytes 213024 | tf_op jit(solution)/shard_map/ppermute | solution.py:40
  29.5 1.1 collective-permute-done.7
  30.6 2.9 %collective-permute-start.16 = (bf16[32,1664]{1,0:T(8,128)(2,1)S(1)}, bf16[32,1664]{1,0:T(8,128)(2,1)S(1)}, u32[]{:S(2)}, u32[]{:S(2)}) collective-permute-start(bf16[32,1664]{1,0:T(8,128)(2,1)S(1)} %get-tuple-element.77), channel_id=1, source_target_pairs={{0,8},{4,12},{8,16},{12,20},{16,24},{20,28},{24,0},{28,4},{1,9},{5... | collective-permute-start | bytes 319496 | tf_op jit(solution)/shard_map/ppermute | solution.py:36
  33.5 0.7 collective-permute-start.17
  34.2 1.7 %collective-permute-start.18 = (bf16[32,1664]{1,0:T(8,128)(2,1)S(1)}, bf16[32,1664]{1,0:T(8,128)(2,1)S(1)}, u32[]{:S(2)}, u32[]{:S(2)}) collective-permute-start(bf16[32,1664]{1,0:T(8,128)(2,1)S(1)} %get-tuple-element.77), channel_id=1, source_target_pairs={{0,24},{4,28},{8,0},{12,4},{16,8},{20,12},{24,16},{28,20},{1,25},{... | collective-permute-start | bytes 319496 | tf_op jit(solution)/shard_map/ppermute | solution.py:36
  36.0 1.3 %collective-permute-start.8 = (bf16[128,1664]{1,0:T(8,128)(2,1)S(1)}, bf16[128,1664]{1,0:T(8,128)(2,1)S(1)}, u32[]{:S(2)}, u32[]{:S(2)}) collective-permute-start(bf16[128,1664]{1,0:T(8,128)(2,1)S(1)} %pad_maximum_fusion.2), channel_id=1, source_target_pairs={{0,2},{1,3},{2,0},{3,1},{4,6},{5,7},{6,4},{7,5},{8,10},{9,11},{10,... | collective-permute-start | bytes 1277960 | tf_op jit(solution)/shard_map/ppermute | solution.py:44
  37.4 0.6 collective-permute-start.9
  38.4 3.3 %collective-permute-done.17 = bf16[32,1664]{1,0:T(8,128)(2,1)S(1)} collective-permute-done((bf16[32,1664]{1,0:T(8,128)(2,1)S(1)}, bf16[32,1664]{1,0:T(8,128)(2,1)S(1)}, u32[]{:S(2)}, u32[]{:S(2)}) %collective-permute-start.17) | collective-permute-done | bytes 106528 | tf_op jit(solution)/shard_map/ppermute | solution.py:36
  41.7 1.2 %collective-permute-start.20 = (bf16[64,1664]{1,0:T(8,128)(2,1)S(1)}, bf16[64,1664]{1,0:T(8,128)(2,1)S(1)}, u32[]{:S(2)}, u32[]{:S(2)}) collective-permute-start(bf16[64,1664]{1,0:T(8,128)(2,1)S(1)} %pad_maximum_fusion.9), channel_id=1, source_target_pairs={{0,2},{1,3},{2,0},{3,1},{4,6},{5,7},{6,4},{7,5},{8,10},{9,11},{10,... | collective-permute-start | bytes 638984 | tf_op jit(solution)/shard_map/ppermute | solution.py:44
  42.9 0.6 collective-permute-start.19
  43.5 5.5 %collective-permute-done.9 = bf16[128,1664]{1,0:T(8,128)(2,1)S(1)} collective-permute-done((bf16[128,1664]{1,0:T(8,128)(2,1)S(1)}, bf16[128,1664]{1,0:T(8,128)(2,1)S(1)}, u32[]{:S(2)}, u32[]{:S(2)}) %collective-permute-start.9) | collective-permute-done | bytes 426016 | tf_op jit(solution)/shard_map/ppermute | solution.py:40
  49.2 0.5 collective-permute-start.11
  49.7 0.8 collective-permute-done.20
  50.5 0.8 collective-permute-done.19
  51.3 0.6 collective-permute-start.23
  52.0 1.3 %collective-permute-start.22 = (bf16[128,1664]{1,0:T(8,128)(2,1)S(1)}, bf16[128,1664]{1,0:T(8,128)(2,1)S(1)}, u32[]{:S(2)}, u32[]{:S(2)}) collective-permute-start(bf16[128,1664]{1,0:T(8,128)(2,1)S(1)} %pad_maximum_fusion.4), channel_id=1, source_target_pairs={{0,2},{1,3},{2,0},{3,1},{4,6},{5,7},{6,4},{7,5},{8,10},{9,11},{10,... | collective-permute-start | bytes 1277960 | tf_op jit(solution)/shard_map/ppermute | solution.py:44
  53.4 4.1 %expert_rows.4 = (bf16[256,1536]{1,0:T(8,128)(2,1)S(1)}, bf16[256,1536]{1,0:T(8,128)(2,1)S(1)}) custom-call(s32[1]{0:T(128)} %bitcast.1.first_ref, bf16[256,1664]{1,0:T(8,128)(2,1)S(1)} %collective-permute-done.10.near_ref, bf16[256,1664]{1,0:T(8,128)(2,1)S(1)} %collective-permute-done.11.far_ref, bf16[5,1536,256]{2,1,0:T(8,128)(2,1)S(1)} %get-tuple-element.68.both_ref, ...), custom_call_target="tpu_custom_call" | custom-call | flops 3019898880 | bytes 9043968 | tf_op jit(solution)/shard_map/expert_rows/pallas_call | solution.py:258
  57.6 0.6 collective-permute-start.13
  58.1 4.1 %expert_rows.5 = (bf16[256,1536]{1,0:T(8,128)(2,1)S(1)}, bf16[256,1536]{1,0:T(8,128)(2,1)S(1)}) custom-call(s32[1]{0:T(128)} %bitcast.1.first_ref, bf16[256,1664]{1,0:T(8,128)(2,1)S(1)} %pad_maximum_fusion.near_ref, bf16[256,1664]{1,0:T(8,128)(2,1)S(1)} %constant_dynamic-update-slice_fusion.far_ref, bf16[5,1536,256]{2,1,0:T(8,128)(2,1)S(1)} %get-tuple-element.68.both_ref, ...), custom_call_target="tpu_custom_call" | custom-call | flops 3019898880 | bytes 9043968 | tf_op jit(solution)/shard_map/expert_rows/pallas_call | solution.py:258
  62.4 0.5 collective-permute-start.12
  63.1 1.0 collective-permute-start.14
  64.1 1.4 %collective-permute-start.15 = (bf16[128,1536]{1,0:T(8,128)(2,1)S(1)}, bf16[128,1536]{1,0:T(8,128)(2,1)S(1)}, u32[]{:S(2)}, u32[]{:S(2)}) collective-permute-start(bf16[128,1536]{1,0:T(8,128)(2,1)S(1)} %get-tuple-element.129), channel_id=1, source_target_pairs={{0,4},{4,0},{8,12},{12,8},{16,20},{20,16},{24,28},{28,24},{1,5},{5... | collective-permute-start | bytes 1179656 | tf_op jit(solution)/shard_map/ppermute | solution.py:40
  65.5 4.1 %expert_rows.6 = (bf16[256,1536]{1,0:T(8,128)(2,1)S(1)}, bf16[256,1536]{1,0:T(8,128)(2,1)S(1)}) custom-call(s32[1]{0:T(128)} %bitcast.1.first_ref, bf16[256,1664]{1,0:T(8,128)(2,1)S(1)} %collective-permute-done.21.near_ref, bf16[256,1664]{1,0:T(8,128)(2,1)S(1)} %collective-permute-done.24.far_ref, bf16[5,1536,256]{2,1,0:T(8,128)(2,1)S(1)} %get-tuple-element.68.both_ref, ...), custom_call_target="tpu_custom_call" | custom-call | flops 3019898880 | bytes 9043968 | tf_op jit(solution)/shard_map/expert_rows/pallas_call | solution.py:258
  69.7 0.5 collective-permute-start.31
  70.2 4.3 %expert_rows.7 = (bf16[256,1536]{1,0:T(8,128)(2,1)S(1)}, bf16[256,1536]{1,0:T(8,128)(2,1)S(1)}) custom-call(s32[1]{0:T(128)} %bitcast.1.first_ref, bf16[256,1664]{1,0:T(8,128)(2,1)S(1)} %pad_maximum_fusion.1.near_ref, bf16[256,1664]{1,0:T(8,128)(2,1)S(1)} %constant_dynamic-update-slice_fusion.2.far_ref, ...), custom_call_target="tpu_custom_call" | custom-call | flops 3019898880 | bytes 9043968 | tf_op jit(solution)/shard_map/expert_rows/pallas_call | solution.py:258
  74.5 0.4 collective-permute-done.15
  75.1 1.4 %collective-permute-start.25 = (bf16[64,1536]{1,0:T(8,128)(2,1)S(1)}, bf16[64,1536]{1,0:T(8,128)(2,1)S(1)}, u32[]{:S(2)}, u32[]{:S(2)}) collective-permute-start(bf16[64,1536]{1,0:T(8,128)(2,1)S(1)} %get-tuple-element.128), channel_id=1, source_target_pairs={{0,4},{4,0},{8,12},{12,8},{16,20},{20,16},{24,28},{28,24},{1,5},{5... | collective-permute-start | bytes 589832 | tf_op jit(solution)/shard_map/ppermute | solution.py:40
  76.5 1.1 collective-permute-start.26
  77.8 1.0 collective-permute-start.32
  78.8 0.7 collective-permute-start.33
  79.5 3.5 %collective-permute-done.25 = bf16[64,1536]{1,0:T(8,128)(2,1)S(1)} collective-permute-done((bf16[64,1536]{1,0:T(8,128)(2,1)S(1)}, bf16[64,1536]{1,0:T(8,128)(2,1)S(1)}, u32[]{:S(2)}, u32[]{:S(2)}) %collective-permute-start.25) | collective-permute-done | bytes 196640 | tf_op jit(solution)/shard_map/ppermute | solution.py:40
  83.0 1.4 %collective-permute-done.26 = bf16[64,1536]{1,0:T(8,128)(2,1)S(1)} collective-permute-done((bf16[64,1536]{1,0:T(8,128)(2,1)S(1)}, bf16[64,1536]{1,0:T(8,128)(2,1)S(1)}, u32[]{:S(2)}, u32[]{:S(2)}) %collective-permute-start.26) | collective-permute-done | bytes 196640 | tf_op jit(solution)/shard_map/ppermute | solution.py:44
  84.7 2.3 %collective-permute-start.29 = (bf16[32,1536]{1,0:T(8,128)(2,1)S(1)}, bf16[32,1536]{1,0:T(8,128)(2,1)S(1)}, u32[]{:S(2)}, u32[]{:S(2)}) collective-permute-start(bf16[32,1536]{1,0:T(8,128)(2,1)S(1)} %pad_maximum_fusion.11), channel_id=1, source_target_pairs={{0,16},{4,20},{8,24},{12,28},{16,0},{20,4},{24,8},{28,12},{1,17},{... | collective-permute-start | bytes 294920 | tf_op jit(solution)/shard_map/ppermute | solution.py:36
  87.0 1.7 %collective-permute-start.28 = (bf16[32,1536]{1,0:T(8,128)(2,1)S(1)}, bf16[32,1536]{1,0:T(8,128)(2,1)S(1)}, u32[]{:S(2)}, u32[]{:S(2)}) collective-permute-start(bf16[32,1536]{1,0:T(8,128)(2,1)S(1)} %pad_maximum_fusion.10), channel_id=1, source_target_pairs={{0,24},{4,28},{8,0},{12,4},{16,8},{20,12},{24,16},{28,20},{1,25},{... | collective-permute-start | bytes 294920 | tf_op jit(solution)/shard_map/ppermute | solution.py:36
  88.6 1.9 %collective-permute-done.32 = bf16[128,1536]{1,0:T(8,128)(2,1)S(1)} collective-permute-done((bf16[128,1536]{1,0:T(8,128)(2,1)S(1)}, bf16[128,1536]{1,0:T(8,128)(2,1)S(1)}, u32[]{:S(2)}, u32[]{:S(2)}) %collective-permute-start.32) | collective-permute-done | bytes 393248 | tf_op jit(solution)/shard_map/ppermute | solution.py:44
  90.7 1.4 %collective-permute-start.37 = (bf16[64,1536]{1,0:T(8,128)(2,1)S(1)}, bf16[64,1536]{1,0:T(8,128)(2,1)S(1)}, u32[]{:S(2)}, u32[]{:S(2)}) collective-permute-start(bf16[64,1536]{1,0:T(8,128)(2,1)S(1)} %get-tuple-element.124), channel_id=1, source_target_pairs={{0,4},{4,0},{8,12},{12,8},{16,20},{20,16},{24,28},{28,24},{1,5},{5... | collective-permute-start | bytes 589832 | tf_op jit(solution)/shard_map/ppermute | solution.py:40
  92.1 1.1 collective-permute-start.38
  93.4 3.1 %collective-permute-done.37 = bf16[64,1536]{1,0:T(8,128)(2,1)S(1)} collective-permute-done((bf16[64,1536]{1,0:T(8,128)(2,1)S(1)}, bf16[64,1536]{1,0:T(8,128)(2,1)S(1)}, u32[]{:S(2)}, u32[]{:S(2)}) %collective-permute-start.37) | collective-permute-done | bytes 196640 | tf_op jit(solution)/shard_map/ppermute | solution.py:40
  96.5 1.2 %collective-permute-done.38 = bf16[64,1536]{1,0:T(8,128)(2,1)S(1)} collective-permute-done((bf16[64,1536]{1,0:T(8,128)(2,1)S(1)}, bf16[64,1536]{1,0:T(8,128)(2,1)S(1)}, u32[]{:S(2)}, u32[]{:S(2)}) %collective-permute-start.38) | collective-permute-done | bytes 196640 | tf_op jit(solution)/shard_map/ppermute | solution.py:44
  97.9 2.3 %collective-permute-start.40 = (bf16[32,1536]{1,0:T(8,128)(2,1)S(1)}, bf16[32,1536]{1,0:T(8,128)(2,1)S(1)}, u32[]{:S(2)}, u32[]{:S(2)}) collective-permute-start(bf16[32,1536]{1,0:T(8,128)(2,1)S(1)} %pad_maximum_fusion.14), channel_id=1, source_target_pairs={{0,16},{4,20},{8,24},{12,28},{16,0},{20,4},{24,8},{28,12},{1,17},{... | collective-permute-start | bytes 294920 | tf_op jit(solution)/shard_map/ppermute | solution.py:36
  100.2 1.7 %collective-permute-start.39 = (bf16[32,1536]{1,0:T(8,128)(2,1)S(1)}, bf16[32,1536]{1,0:T(8,128)(2,1)S(1)}, u32[]{:S(2)}, u32[]{:S(2)}) collective-permute-start(bf16[32,1536]{1,0:T(8,128)(2,1)S(1)} %pad_maximum_fusion.13), channel_id=1, source_target_pairs={{0,24},{4,28},{8,0},{12,4},{16,8},{20,12},{24,16},{28,20},{1,25},{... | collective-permute-start | bytes 294920 | tf_op jit(solution)/shard_map/ppermute | solution.py:36
  102.1 1.2 %collective-permute-start.35 = (bf16[32,1536]{1,0:T(8,128)(2,1)S(1)}, bf16[32,1536]{1,0:T(8,128)(2,1)S(1)}, u32[]{:S(2)}, u32[]{:S(2)}) collective-permute-start(bf16[32,1536]{1,0:T(8,128)(2,1)S(1)} %multiply_convert_fusion.1.refs_0_), channel_id=1, source_target_pairs={{0,2},{1,3},{2,0},{3,1},{4,6},{5,7},{6,4},{7,5},{8,10},{9,11},{10,... | collective-permute-start | bytes 294920 | tf_op jit(solution)/shard_map/ppermute | solution.py:44
  103.2 1.3 %collective-permute-done.41 = bf16[32,1536]{1,0:T(8,128)(2,1)S(1)} collective-permute-done((bf16[32,1536]{1,0:T(8,128)(2,1)S(1)}, bf16[32,1536]{1,0:T(8,128)(2,1)S(1)}, u32[]{:S(2)}, u32[]{:S(2)}) %collective-permute-start.41) | collective-permute-done | bytes 98336 | tf_op jit(solution)/shard_map/ppermute | solution.py:36
  104.5 1.8 %collective-permute-done.40 = bf16[32,1536]{1,0:T(8,128)(2,1)S(1)} collective-permute-done((bf16[32,1536]{1,0:T(8,128)(2,1)S(1)}, bf16[32,1536]{1,0:T(8,128)(2,1)S(1)}, u32[]{:S(2)}, u32[]{:S(2)}) %collective-permute-start.40) | collective-permute-done | bytes 98336 | tf_op jit(solution)/shard_map/ppermute | solution.py:36
  106.5 6.1 %all-gather = bf16[128,1536]{1,0:T(8,128)(2,1)S(1)} all-gather(bf16[32,1536]{1,0:T(8,128)(2,1)S(1)} %multiply_convert_fusion), channel_id=2, replica_groups=mesh['ep'=8,'tp'=4] {'tp'}, dimensions={0}, use_global_device_ids=true | all-gather | bytes 491520 | tf_op jit(solution)/shard_map/all_gather | solution.py:468
  112.7 0.9 join.1
  (102 shorter events, 4.2 us)
Async XLA Ops:
  0.0 10.9 %copy-start = (bf16[256,1536]{1,0:T(8,128)(2,1)S(1)}, bf16[256,1536]{1,0:T(8,128)(2,1)}, u32[]{:S(2)}) copy-start(bf16[256,1536]{1,0:T(8,128)(2,1)} %resid_ref.3) | copy-start | bytes 2359300
  0.0 1.3 %copy-start.4 = (bf16[384,1536]{1,0:T(8,128)(2,1)S(1)}, bf16[384,1536]{1,0:T(8,128)(2,1)}, u32[]{:S(2)}) copy-start(bf16[384,1536]{1,0:T(8,128)(2,1)} %w_ref.1) | copy-start | bytes 3538948
  1.3 0.9 copy-start.5
  2.3 2.2 %copy-start.6 = (s32[256,8]{0,1:T(8,128)S(1)}, s32[256,8]{0,1:T(8,128)}, u32[]{:S(2)}) copy-start(s32[256,8]{0,1:T(8,128)} %param.18) | copy-start | bytes 24580
  2.3 2.4 %copy-start.9 = (bf16[1536]{0:T(1024)(128)(2,1)S(1)}, bf16[1536]{0:T(1024)(128)(2,1)}, u32[]{:S(2)}) copy-start(bf16[1536]{0:T(1024)(128)(2,1)} %param.15) | copy-start | bytes 9220
  2.3 5.4 %copy-start.7 = (s32[40]{0:T(128)S(1)}, s32[40]{0:T(128)}, u32[]{:S(2)}) copy-start(s32[40]{0:T(128)} %param.19) | copy-start | bytes 484
  2.3 5.6 %copy-start.10 = (s32[1,40]{1,0:T(1,128)S(1)}, s32[1,40]{1,0:T(1,128)}, u32[]{:S(2)}) copy-start(s32[1,40]{1,0:T(1,128)} %param.20) | copy-start | bytes 484
  2.9 1.9 %collective-permute-start = (bf16[2,64,1536]{2,1,0:T(8,128)(2,1)S(1)}, bf16[2,64,1536]{2,1,0:T(8,128)(2,1)S(1)}, u32[]{:S(2)}, u32[]{:S(2)}) collective-permute-start(bf16[2,64,1536]{2,1,0:T(8,128)(2,1)S(1)} %get-tuple-element.54), channel_id=1, source_target_pairs={{0,1},{1,0},{2,3},{3,2},{4,5},{5,4},{6,7},{7,6},{8,9},{9,8},{10,11... | collective-permute-start | bytes 1179656 | tf_op jit(solution)/shard_map/ppermute | solution.py:48
  4.7 12.7 %copy-start.1 = (bf16[5,1536,128]{2,1,0:T(8,128)(2,1)S(1)}, bf16[5,1536,128]{2,1,0:T(8,128)(2,1)}, u32[]{:S(2)}) copy-start(bf16[5,1536,128]{2,1,0:T(8,128)(2,1)} %gate_hbm.1) | copy-start | bytes 5898244
  4.8 6.1 %collective-permute-start.1 = (bf16[32,1536]{1,0:T(8,128)(2,1)S(1)}, bf16[32,1536]{1,0:T(8,128)(2,1)S(1)}, u32[]{:S(2)}, u32[]{:S(2)}) collective-permute-start(bf16[32,1536]{1,0:T(8,128)(2,1)S(1)} %get-tuple-element.132), channel_id=1, source_target_pairs={{0,2},{1,3},{2,0},{3,1},{4,6},{5,7},{6,4},{7,5},{8,10},{9,11},{10,... | collective-permute-start | bytes 294920 | tf_op jit(solution)/shard_map/ppermute | solution.py:44
  8.3 9.1 %collective-permute-start.5 = (bf16[32,1536]{1,0:T(8,128)(2,1)S(1)}, bf16[32,1536]{1,0:T(8,128)(2,1)S(1)}, u32[]{:S(2)}, u32[]{:S(2)}) collective-permute-start(bf16[32,1536]{1,0:T(8,128)(2,1)S(1)} %get-tuple-element.131), channel_id=1, source_target_pairs={{0,2},{1,3},{2,0},{3,1},{4,6},{5,7},{6,4},{7,5},{8,10},{9,11},{10,... | collective-permute-start | bytes 294920 | tf_op jit(solution)/shard_map/ppermute | solution.py:44
  11.4 10.1 %collective-permute-start.2 = (bf16[32,1664]{1,0:T(8,128)(2,1)S(1)}, bf16[32,1664]{1,0:T(8,128)(2,1)S(1)}, u32[]{:S(2)}, u32[]{:S(2)}) collective-permute-start(bf16[32,1664]{1,0:T(8,128)(2,1)S(1)} %get-tuple-element.57), channel_id=1, source_target_pairs={{0,8},{4,12},{8,16},{12,20},{16,24},{20,28},{24,0},{28,4},{1,9},{5... | collective-permute-start | bytes 319496 | tf_op jit(solution)/shard_map/ppermute | solution.py:36
  13.4 9.0 %collective-permute-start.3 = (bf16[32,1664]{1,0:T(8,128)(2,1)S(1)}, bf16[32,1664]{1,0:T(8,128)(2,1)S(1)}, u32[]{:S(2)}, u32[]{:S(2)}) collective-permute-start(bf16[32,1664]{1,0:T(8,128)(2,1)S(1)} %get-tuple-element.57), channel_id=1, source_target_pairs={{0,16},{4,20},{8,24},{12,28},{16,0},{20,4},{24,8},{28,12},{1,17},{... | collective-permute-start | bytes 319496 | tf_op jit(solution)/shard_map/ppermute | solution.py:36
  16.0 6.6 %collective-permute-start.4 = (bf16[32,1664]{1,0:T(8,128)(2,1)S(1)}, bf16[32,1664]{1,0:T(8,128)(2,1)S(1)}, u32[]{:S(2)}, u32[]{:S(2)}) collective-permute-start(bf16[32,1664]{1,0:T(8,128)(2,1)S(1)} %get-tuple-element.57), channel_id=1, source_target_pairs={{0,24},{4,28},{8,0},{12,4},{16,8},{20,12},{24,16},{28,20},{1,25},{... | collective-permute-start | bytes 319496 | tf_op jit(solution)/shard_map/ppermute | solution.py:36
  17.4 1.5 %copy-start.2 = (bf16[5,1536,128]{2,1,0:T(8,128)(2,1)S(1)}, bf16[5,1536,128]{2,1,0:T(8,128)(2,1)}, u32[]{:S(2)}) copy-start(bf16[5,1536,128]{2,1,0:T(8,128)(2,1)} %up_hbm.1) | copy-start | bytes 5898244
  18.9 1.5 %copy-start.3 = (bf16[5,128,1536]{2,1,0:T(8,128)(2,1)S(1)}, bf16[5,128,1536]{2,1,0:T(8,128)(2,1)}, u32[]{:S(2)}) copy-start(bf16[5,128,1536]{2,1,0:T(8,128)(2,1)} %param.23) | copy-start | bytes 5898244
  22.6 6.8 %collective-permute-start.6 = (bf16[64,1664]{1,0:T(8,128)(2,1)S(1)}, bf16[64,1664]{1,0:T(8,128)(2,1)S(1)}, u32[]{:S(2)}, u32[]{:S(2)}) collective-permute-start(bf16[64,1664]{1,0:T(8,128)(2,1)S(1)} %get-tuple-element.60), channel_id=1, source_target_pairs={{0,4},{4,0},{8,12},{12,8},{16,20},{20,16},{24,28},{28,24},{1,5},{5... | collective-permute-start | bytes 638984 | tf_op jit(solution)/shard_map/ppermute | solution.py:40
  24.2 6.4 %collective-permute-start.7 = (bf16[64,1664]{1,0:T(8,128)(2,1)S(1)}, bf16[64,1664]{1,0:T(8,128)(2,1)S(1)}, u32[]{:S(2)}, u32[]{:S(2)}) collective-permute-start(bf16[64,1664]{1,0:T(8,128)(2,1)S(1)} %get-tuple-element.61), channel_id=1, source_target_pairs={{0,2},{1,3},{2,0},{3,1},{4,6},{5,7},{6,4},{7,5},{8,10},{9,11},{10,... | collective-permute-start | bytes 638984 | tf_op jit(solution)/shard_map/ppermute | solution.py:44
  30.6 7.7 %collective-permute-start.16 = (bf16[32,1664]{1,0:T(8,128)(2,1)S(1)}, bf16[32,1664]{1,0:T(8,128)(2,1)S(1)}, u32[]{:S(2)}, u32[]{:S(2)}) collective-permute-start(bf16[32,1664]{1,0:T(8,128)(2,1)S(1)} %get-tuple-element.77), channel_id=1, source_target_pairs={{0,8},{4,12},{8,16},{12,20},{16,24},{20,28},{24,0},{28,4},{1,9},{5... | collective-permute-start | bytes 319496 | tf_op jit(solution)/shard_map/ppermute | solution.py:36
  33.5 8.1 %collective-permute-start.17 = (bf16[32,1664]{1,0:T(8,128)(2,1)S(1)}, bf16[32,1664]{1,0:T(8,128)(2,1)S(1)}, u32[]{:S(2)}, u32[]{:S(2)}) collective-permute-start(bf16[32,1664]{1,0:T(8,128)(2,1)S(1)} %get-tuple-element.77), channel_id=1, source_target_pairs={{0,16},{4,20},{8,24},{12,28},{16,0},{20,4},{24,8},{28,12},{1,17},{... | collective-permute-start | bytes 319496 | tf_op jit(solution)/shard_map/ppermute | solution.py:36
  34.2 7.4 %collective-permute-start.18 = (bf16[32,1664]{1,0:T(8,128)(2,1)S(1)}, bf16[32,1664]{1,0:T(8,128)(2,1)S(1)}, u32[]{:S(2)}, u32[]{:S(2)}) collective-permute-start(bf16[32,1664]{1,0:T(8,128)(2,1)S(1)} %get-tuple-element.77), channel_id=1, source_target_pairs={{0,24},{4,28},{8,0},{12,4},{16,8},{20,12},{24,16},{28,20},{1,25},{... | collective-permute-start | bytes 319496 | tf_op jit(solution)/shard_map/ppermute | solution.py:36
  36.0 13.1 %collective-permute-start.8 = (bf16[128,1664]{1,0:T(8,128)(2,1)S(1)}, bf16[128,1664]{1,0:T(8,128)(2,1)S(1)}, u32[]{:S(2)}, u32[]{:S(2)}) collective-permute-start(bf16[128,1664]{1,0:T(8,128)(2,1)S(1)} %pad_maximum_fusion.2), channel_id=1, source_target_pairs={{0,2},{1,3},{2,0},{3,1},{4,6},{5,7},{6,4},{7,5},{8,10},{9,11},{10,... | collective-permute-start | bytes 1277960 | tf_op jit(solution)/shard_map/ppermute | solution.py:44
  37.4 11.6 %collective-permute-start.9 = (bf16[128,1664]{1,0:T(8,128)(2,1)S(1)}, bf16[128,1664]{1,0:T(8,128)(2,1)S(1)}, u32[]{:S(2)}, u32[]{:S(2)}) collective-permute-start(bf16[128,1664]{1,0:T(8,128)(2,1)S(1)} %pad_maximum_fusion.3), channel_id=1, source_target_pairs={{0,4},{4,0},{8,12},{12,8},{16,20},{20,16},{24,28},{28,24},{1,5},{5... | collective-permute-start | bytes 1277960 | tf_op jit(solution)/shard_map/ppermute | solution.py:40
  41.7 8.8 %collective-permute-start.20 = (bf16[64,1664]{1,0:T(8,128)(2,1)S(1)}, bf16[64,1664]{1,0:T(8,128)(2,1)S(1)}, u32[]{:S(2)}, u32[]{:S(2)}) collective-permute-start(bf16[64,1664]{1,0:T(8,128)(2,1)S(1)} %pad_maximum_fusion.9), channel_id=1, source_target_pairs={{0,2},{1,3},{2,0},{3,1},{4,6},{5,7},{6,4},{7,5},{8,10},{9,11},{10,... | collective-permute-start | bytes 638984 | tf_op jit(solution)/shard_map/ppermute | solution.py:44
  42.9 8.4 %collective-permute-start.19 = (bf16[64,1664]{1,0:T(8,128)(2,1)S(1)}, bf16[64,1664]{1,0:T(8,128)(2,1)S(1)}, u32[]{:S(2)}, u32[]{:S(2)}) collective-permute-start(bf16[64,1664]{1,0:T(8,128)(2,1)S(1)} %pad_maximum_fusion.8), channel_id=1, source_target_pairs={{0,4},{4,0},{8,12},{12,8},{16,20},{20,16},{24,28},{28,24},{1,5},{5... | collective-permute-start | bytes 638984 | tf_op jit(solution)/shard_map/ppermute | solution.py:40
  49.1 4.3 %collective-permute-start.10 = (bf16[256,1664]{1,0:T(8,128)(2,1)S(1)}, bf16[256,1664]{1,0:T(8,128)(2,1)S(1)}, u32[]{:S(2)}, u32[]{:S(2)}) collective-permute-start(bf16[256,1664]{1,0:T(8,128)(2,1)S(1)} %pad_maximum_fusion.near_ref), channel_id=1, source_target_pairs={{0,1},{1,0},{2,3},{3,2},{4,5},{5,4},{6,7},{7,6},{8,9},{9,8},{10,11... | collective-permute-start | bytes 2555912 | tf_op jit(solution)/shard_map/ppermute | solution.py:48
  49.2 4.2 %collective-permute-start.11 = (bf16[256,1664]{1,0:T(8,128)(2,1)S(1)}, bf16[256,1664]{1,0:T(8,128)(2,1)S(1)}, u32[]{:S(2)}, u32[]{:S(2)}) collective-permute-start(bf16[256,1664]{1,0:T(8,128)(2,1)S(1)} %constant_dynamic-update-slice_fusion.far_ref), channel_id=1, source_target_pairs={{0,1},{1,0},{2,3},{3,2},{4,5},{5,4},{6,7},{7,6},{8,9},{9,8},{10,11... | collective-permute-start | bytes 2555912 | tf_op jit(solution)/shard_map/ppermute | solution.py:48
  51.3 10.9 %collective-permute-start.23 = (bf16[128,1664]{1,0:T(8,128)(2,1)S(1)}, bf16[128,1664]{1,0:T(8,128)(2,1)S(1)}, u32[]{:S(2)}, u32[]{:S(2)}) collective-permute-start(bf16[128,1664]{1,0:T(8,128)(2,1)S(1)} %pad_maximum_fusion.5), channel_id=1, source_target_pairs={{0,4},{4,0},{8,12},{12,8},{16,20},{20,16},{24,28},{28,24},{1,5},{5... | collective-permute-start | bytes 1277960 | tf_op jit(solution)/shard_map/ppermute | solution.py:40
  52.0 10.2 %collective-permute-start.22 = (bf16[128,1664]{1,0:T(8,128)(2,1)S(1)}, bf16[128,1664]{1,0:T(8,128)(2,1)S(1)}, u32[]{:S(2)}, u32[]{:S(2)}) collective-permute-start(bf16[128,1664]{1,0:T(8,128)(2,1)S(1)} %pad_maximum_fusion.4), channel_id=1, source_target_pairs={{0,2},{1,3},{2,0},{3,1},{4,6},{5,7},{6,4},{7,5},{8,10},{9,11},{10,... | collective-permute-start | bytes 1277960 | tf_op jit(solution)/shard_map/ppermute | solution.py:44
  53.3 12.1 %collective-permute-start.21 = (bf16[256,1664]{1,0:T(8,128)(2,1)S(1)}, bf16[256,1664]{1,0:T(8,128)(2,1)S(1)}, u32[]{:S(2)}, u32[]{:S(2)}) collective-permute-start(bf16[256,1664]{1,0:T(8,128)(2,1)S(1)} %pad_maximum_fusion.1.near_ref), channel_id=1, source_target_pairs={{0,1},{1,0},{2,3},{3,2},{4,5},{5,4},{6,7},{7,6},{8,9},{9,8},{10,11... | collective-permute-start | bytes 2555912 | tf_op jit(solution)/shard_map/ppermute | solution.py:48
  57.6 5.4 %collective-permute-start.13 = (bf16[256,1536]{1,0:T(8,128)(2,1)S(1)}, bf16[256,1536]{1,0:T(8,128)(2,1)S(1)}, u32[]{:S(2)}, u32[]{:S(2)}) collective-permute-start(bf16[256,1536]{1,0:T(8,128)(2,1)S(1)} %get-tuple-element.71), channel_id=1, source_target_pairs={{0,1},{1,0},{2,3},{3,2},{4,5},{5,4},{6,7},{7,6},{8,9},{9,8},{10,11... | collective-permute-start | bytes 2359304 | tf_op jit(solution)/shard_map/ppermute | solution.py:48
  62.4 3.1 %collective-permute-start.24 = (bf16[256,1664]{1,0:T(8,128)(2,1)S(1)}, bf16[256,1664]{1,0:T(8,128)(2,1)S(1)}, u32[]{:S(2)}, u32[]{:S(2)}) collective-permute-start(bf16[256,1664]{1,0:T(8,128)(2,1)S(1)} %constant_dynamic-update-slice_fusion.2.far_ref), channel_id=1, source_target_pairs={{0,1},{1,0},{2,3},{3,2},{4,5},{5,4},{6,7},{7,6},{8,9},{9,8},{10,11... | collective-permute-start | bytes 2555912 | tf_op jit(solution)/shard_map/ppermute | solution.py:48
  62.4 12.5 %collective-permute-start.12 = (bf16[256,1536]{1,0:T(8,128)(2,1)S(1)}, bf16[256,1536]{1,0:T(8,128)(2,1)S(1)}, u32[]{:S(2)}, u32[]{:S(2)}) collective-permute-start(bf16[256,1536]{1,0:T(8,128)(2,1)S(1)} %get-tuple-element.70), channel_id=1, source_target_pairs={{0,1},{1,0},{2,3},{3,2},{4,5},{5,4},{6,7},{7,6},{8,9},{9,8},{10,11... | collective-permute-start | bytes 2359304 | tf_op jit(solution)/shard_map/ppermute | solution.py:48
  63.1 11.4 %collective-permute-start.14 = (bf16[128,1536]{1,0:T(8,128)(2,1)S(1)}, bf16[128,1536]{1,0:T(8,128)(2,1)S(1)}, u32[]{:S(2)}, u32[]{:S(2)}) collective-permute-start(bf16[128,1536]{1,0:T(8,128)(2,1)S(1)} %get-tuple-element.130), channel_id=1, source_target_pairs={{0,2},{1,3},{2,0},{3,1},{4,6},{5,7},{6,4},{7,5},{8,10},{9,11},{10,... | collective-permute-start | bytes 1179656 | tf_op jit(solution)/shard_map/ppermute | solution.py:44
  64.1 5.6 %copy-start.8 = (bf16[1536]{0:T(1024)(128)(2,1)S(1)}, bf16[1536]{0:T(1024)(128)(2,1)}, u32[]{:S(2)}) copy-start(bf16[1536]{0:T(1024)(128)(2,1)} %param.16) | copy-start | bytes 9220
  64.1 10.8 %collective-permute-start.15 = (bf16[128,1536]{1,0:T(8,128)(2,1)S(1)}, bf16[128,1536]{1,0:T(8,128)(2,1)S(1)}, u32[]{:S(2)}, u32[]{:S(2)}) collective-permute-start(bf16[128,1536]{1,0:T(8,128)(2,1)S(1)} %get-tuple-element.129), channel_id=1, source_target_pairs={{0,4},{4,0},{8,12},{12,8},{16,20},{20,16},{24,28},{28,24},{1,5},{5... | collective-permute-start | bytes 1179656 | tf_op jit(solution)/shard_map/ppermute | solution.py:40
  69.6 8.0 %collective-permute-start.27 = (bf16[256,1536]{1,0:T(8,128)(2,1)S(1)}, bf16[256,1536]{1,0:T(8,128)(2,1)S(1)}, u32[]{:S(2)}, u32[]{:S(2)}) collective-permute-start(bf16[256,1536]{1,0:T(8,128)(2,1)S(1)} %get-tuple-element.85), channel_id=1, source_target_pairs={{0,1},{1,0},{2,3},{3,2},{4,5},{5,4},{6,7},{7,6},{8,9},{9,8},{10,11... | collective-permute-start | bytes 2359304 | tf_op jit(solution)/shard_map/ppermute | solution.py:48
  69.7 17.2 %collective-permute-start.31 = (bf16[256,1536]{1,0:T(8,128)(2,1)S(1)}, bf16[256,1536]{1,0:T(8,128)(2,1)S(1)}, u32[]{:S(2)}, u32[]{:S(2)}) collective-permute-start(bf16[256,1536]{1,0:T(8,128)(2,1)S(1)} %get-tuple-element.84), channel_id=1, source_target_pairs={{0,1},{1,0},{2,3},{3,2},{4,5},{5,4},{6,7},{7,6},{8,9},{9,8},{10,11... | collective-permute-start | bytes 2359304 | tf_op jit(solution)/shard_map/ppermute | solution.py:48
  75.1 7.9 %collective-permute-start.25 = (bf16[64,1536]{1,0:T(8,128)(2,1)S(1)}, bf16[64,1536]{1,0:T(8,128)(2,1)S(1)}, u32[]{:S(2)}, u32[]{:S(2)}) collective-permute-start(bf16[64,1536]{1,0:T(8,128)(2,1)S(1)} %get-tuple-element.128), channel_id=1, source_target_pairs={{0,4},{4,0},{8,12},{12,8},{16,20},{20,16},{24,28},{28,24},{1,5},{5... | collective-permute-start | bytes 589832 | tf_op jit(solution)/shard_map/ppermute | solution.py:40
  76.5 7.8 %collective-permute-start.26 = (bf16[64,1536]{1,0:T(8,128)(2,1)S(1)}, bf16[64,1536]{1,0:T(8,128)(2,1)S(1)}, u32[]{:S(2)}, u32[]{:S(2)}) collective-permute-start(bf16[64,1536]{1,0:T(8,128)(2,1)S(1)} %get-tuple-element.127), channel_id=1, source_target_pairs={{0,2},{1,3},{2,0},{3,1},{4,6},{5,7},{6,4},{7,5},{8,10},{9,11},{10,... | collective-permute-start | bytes 589832 | tf_op jit(solution)/shard_map/ppermute | solution.py:44
  77.8 12.7 %collective-permute-start.32 = (bf16[128,1536]{1,0:T(8,128)(2,1)S(1)}, bf16[128,1536]{1,0:T(8,128)(2,1)S(1)}, u32[]{:S(2)}, u32[]{:S(2)}) collective-permute-start(bf16[128,1536]{1,0:T(8,128)(2,1)S(1)} %get-tuple-element.126), channel_id=1, source_target_pairs={{0,2},{1,3},{2,0},{3,1},{4,6},{5,7},{6,4},{7,5},{8,10},{9,11},{10,... | collective-permute-start | bytes 1179656 | tf_op jit(solution)/shard_map/ppermute | solution.py:44
  78.8 11.7 %collective-permute-start.33 = (bf16[128,1536]{1,0:T(8,128)(2,1)S(1)}, bf16[128,1536]{1,0:T(8,128)(2,1)S(1)}, u32[]{:S(2)}, u32[]{:S(2)}) collective-permute-start(bf16[128,1536]{1,0:T(8,128)(2,1)S(1)} %get-tuple-element.125), channel_id=1, source_target_pairs={{0,4},{4,0},{8,12},{12,8},{16,20},{20,16},{24,28},{28,24},{1,5},{5... | collective-permute-start | bytes 1179656 | tf_op jit(solution)/shard_map/ppermute | solution.py:40
  84.6 8.6 %collective-permute-start.30 = (bf16[32,1536]{1,0:T(8,128)(2,1)S(1)}, bf16[32,1536]{1,0:T(8,128)(2,1)S(1)}, u32[]{:S(2)}, u32[]{:S(2)}) collective-permute-start(bf16[32,1536]{1,0:T(8,128)(2,1)S(1)} %pad_maximum_fusion.12), channel_id=1, source_target_pairs={{0,8},{4,12},{8,16},{12,20},{16,24},{20,28},{24,0},{28,4},{1,9},{5... | collective-permute-start | bytes 294920 | tf_op jit(solution)/shard_map/ppermute | solution.py:36
  84.7 8.5 %collective-permute-start.29 = (bf16[32,1536]{1,0:T(8,128)(2,1)S(1)}, bf16[32,1536]{1,0:T(8,128)(2,1)S(1)}, u32[]{:S(2)}, u32[]{:S(2)}) collective-permute-start(bf16[32,1536]{1,0:T(8,128)(2,1)S(1)} %pad_maximum_fusion.11), channel_id=1, source_target_pairs={{0,16},{4,20},{8,24},{12,28},{16,0},{20,4},{24,8},{28,12},{1,17},{... | collective-permute-start | bytes 294920 | tf_op jit(solution)/shard_map/ppermute | solution.py:36
  87.0 6.2 %collective-permute-start.28 = (bf16[32,1536]{1,0:T(8,128)(2,1)S(1)}, bf16[32,1536]{1,0:T(8,128)(2,1)S(1)}, u32[]{:S(2)}, u32[]{:S(2)}) collective-permute-start(bf16[32,1536]{1,0:T(8,128)(2,1)S(1)} %pad_maximum_fusion.10), channel_id=1, source_target_pairs={{0,24},{4,28},{8,0},{12,4},{16,8},{20,12},{24,16},{28,20},{1,25},{... | collective-permute-start | bytes 294920 | tf_op jit(solution)/shard_map/ppermute | solution.py:36
  90.7 5.7 %collective-permute-start.37 = (bf16[64,1536]{1,0:T(8,128)(2,1)S(1)}, bf16[64,1536]{1,0:T(8,128)(2,1)S(1)}, u32[]{:S(2)}, u32[]{:S(2)}) collective-permute-start(bf16[64,1536]{1,0:T(8,128)(2,1)S(1)} %get-tuple-element.124), channel_id=1, source_target_pairs={{0,4},{4,0},{8,12},{12,8},{16,20},{20,16},{24,28},{28,24},{1,5},{5... | collective-permute-start | bytes 589832 | tf_op jit(solution)/shard_map/ppermute | solution.py:40
  92.1 5.7 %collective-permute-start.38 = (bf16[64,1536]{1,0:T(8,128)(2,1)S(1)}, bf16[64,1536]{1,0:T(8,128)(2,1)S(1)}, u32[]{:S(2)}, u32[]{:S(2)}) collective-permute-start(bf16[64,1536]{1,0:T(8,128)(2,1)S(1)} %get-tuple-element.123), channel_id=1, source_target_pairs={{0,2},{1,3},{2,0},{3,1},{4,6},{5,7},{6,4},{7,5},{8,10},{9,11},{10,... | collective-permute-start | bytes 589832 | tf_op jit(solution)/shard_map/ppermute | solution.py:44
  97.9 6.6 %collective-permute-start.41 = (bf16[32,1536]{1,0:T(8,128)(2,1)S(1)}, bf16[32,1536]{1,0:T(8,128)(2,1)S(1)}, u32[]{:S(2)}, u32[]{:S(2)}) collective-permute-start(bf16[32,1536]{1,0:T(8,128)(2,1)S(1)} %pad_maximum_fusion.15), channel_id=1, source_target_pairs={{0,8},{4,12},{8,16},{12,20},{16,24},{20,28},{24,0},{28,4},{1,9},{5... | collective-permute-start | bytes 294920 | tf_op jit(solution)/shard_map/ppermute | solution.py:36
  97.9 8.3 %collective-permute-start.40 = (bf16[32,1536]{1,0:T(8,128)(2,1)S(1)}, bf16[32,1536]{1,0:T(8,128)(2,1)S(1)}, u32[]{:S(2)}, u32[]{:S(2)}) collective-permute-start(bf16[32,1536]{1,0:T(8,128)(2,1)S(1)} %pad_maximum_fusion.14), channel_id=1, source_target_pairs={{0,16},{4,20},{8,24},{12,28},{16,0},{20,4},{24,8},{28,12},{1,17},{... | collective-permute-start | bytes 294920 | tf_op jit(solution)/shard_map/ppermute | solution.py:36
  100.2 6.0 %collective-permute-start.39 = (bf16[32,1536]{1,0:T(8,128)(2,1)S(1)}, bf16[32,1536]{1,0:T(8,128)(2,1)S(1)}, u32[]{:S(2)}, u32[]{:S(2)}) collective-permute-start(bf16[32,1536]{1,0:T(8,128)(2,1)S(1)} %pad_maximum_fusion.13), channel_id=1, source_target_pairs={{0,24},{4,28},{8,0},{12,4},{16,8},{20,12},{24,16},{28,20},{1,25},{... | collective-permute-start | bytes 294920 | tf_op jit(solution)/shard_map/ppermute | solution.py:36
  102.0 10.7 %collective-permute-start.34 = (bf16[32,1536]{1,0:T(8,128)(2,1)S(1)}, bf16[32,1536]{1,0:T(8,128)(2,1)S(1)}, u32[]{:S(2)}, u32[]{:S(2)}) collective-permute-start(bf16[32,1536]{1,0:T(8,128)(2,1)S(1)} %multiply_convert_fusion.1.refs_0_), channel_id=1, source_target_pairs={{0,1},{1,0},{2,3},{3,2},{4,5},{5,4},{6,7},{7,6},{8,9},{9,8},{10,11... | collective-permute-start | bytes 294920 | tf_op jit(solution)/shard_map/ppermute | solution.py:48
  102.1 10.6 %collective-permute-start.35 = (bf16[32,1536]{1,0:T(8,128)(2,1)S(1)}, bf16[32,1536]{1,0:T(8,128)(2,1)S(1)}, u32[]{:S(2)}, u32[]{:S(2)}) collective-permute-start(bf16[32,1536]{1,0:T(8,128)(2,1)S(1)} %multiply_convert_fusion.1.refs_0_), channel_id=1, source_target_pairs={{0,2},{1,3},{2,0},{3,1},{4,6},{5,7},{6,4},{7,5},{8,10},{9,11},{10,... | collective-permute-start | bytes 294920 | tf_op jit(solution)/shard_map/ppermute | solution.py:44
  104.5 8.2 %collective-permute-start.36 = (bf16[32,1536]{1,0:T(8,128)(2,1)S(1)}, bf16[32,1536]{1,0:T(8,128)(2,1)S(1)}, u32[]{:S(2)}, u32[]{:S(2)}) collective-permute-start(bf16[32,1536]{1,0:T(8,128)(2,1)S(1)} %multiply_convert_fusion.1.refs_0_), channel_id=1, source_target_pairs={{0,3},{1,2},{2,1},{3,0},{4,7},{5,6},{6,5},{7,4},{8,11},{9,10},{10,... | collective-permute-start | bytes 294920 | tf_op jit(solution)/shard_map/ppermute | solution.py:363

commit v5 on v4

--- a/solution.py
+++ b/solution.py
@@ -206,63 +206,49 @@
     loaded_hbm,
     near_out,
     far_out,
-    rows_ref,
     hidden_ref,
 ):
     held, width, units = both_ref.shape
     units = units // 2
-    start = 0
-    for piece in (near_ref, far_ref):
-        rows_ref[start : start + piece.shape[0]] = piece[...]
-        start += piece.shape[0]
-    block = min(ROW_BLOCK, start)
-    extra = rows_ref.shape[1] - width
+    extra = near_ref.shape[1] - width
     mine = lax.broadcasted_iota(jnp.int32, (extra, LANES), 1) + first_ref[0]
     mine = (lax.broadcasted_iota(jnp.int32, (extra, LANES), 0) == mine).astype(jnp.bfloat16)
     tile = 512 if width % 512 == 0 else width
-
-    def one_block(at):
-        weights = jnp.dot(rows_ref[at, width:], mine, preferred_element_type=jnp.float32)
-        for slot in range(held):
-            out = jnp.dot(rows_ref[at, :width], both_ref[slot], preferred_element_type=jnp.float32)
+    start = 0
+    spans = []
+    for piece, out in ((near_ref, near_out), (far_ref, far_out)):
+        block = min(ROW_BLOCK, piece.shape[0])
+        for at in range(0, piece.shape[0], block):
+            spans.append((piece, out, pl.ds(at, block), pl.ds(start + at, block)))
+        start += piece.shape[0]
+    scales = [
+        jnp.dot(piece[at, width:], mine, preferred_element_type=jnp.float32)
+        for piece, out, at, to in spans
+    ]
+    for slot in range(held):
+        for (piece, _, at, to), weights in zip(spans, scales):
+            out = jnp.dot(piece[at, :width], both_ref[slot], preferred_element_type=jnp.float32)
             gate, upper = out[:, :units], out[:, units:]
             hidden = jax.nn.silu(gate) * upper * weights[:, slot : slot + 1]
-            hidden_ref[:, slot * units : (slot + 1) * units] = hidden.astype(jnp.bfloat16)
-        for left in range(0, width, tile):
-            out = jnp.dot(
-                hidden_ref[...],
-                down_ref[:, left : left + tile],
-                preferred_element_type=jnp.float32,
+            hidden_ref[to, slot * units : (slot + 1) * units] = hidden.astype(jnp.bfloat16)
+    for left in range(0, width, tile):
+        for _, out_ref, at, to in spans:
+            out_ref[at, left : left + tile] = jnp.dot(
+                hidden_ref[to, :], down_ref[:, left : left + tile], preferred_element_type=jnp.float32
             ).astype(jnp.bfloat16)
-            give(out, left)
-
-    outs = (near_out, far_out)
-    size = start // len(outs)
-    for number in range(start // block):
-
-        def give(out, left):
-            for first in range(0, block, min(size, block)):
-                piece, inside = divmod(number * block + first, size)
-                part = min(size, block)
-                to = slice(inside, inside + part)
-                outs[piece][to, left : left + tile] = out[first : first + part]
-
-        one_block(pl.ds(number * block, block))
 
 
 def expert_rows(first, pieces, both, down, loaded):
     held, width, units = both.shape
     units = units // 2
     rows = sum(p.shape[0] for p in pieces)
-    block = min(ROW_BLOCK, rows)
     return pl.pallas_call(
         expert_kernel,
         out_shape=[jax.ShapeDtypeStruct((p.shape[0], width), jnp.bfloat16) for p in pieces],
         in_specs=[SMEM] + [VMEM] * (len(pieces) + 2) + [ANY],
         out_specs=[VMEM] * len(pieces),
         scratch_shapes=[
-            pltpu.VMEM((rows, pieces[0].shape[1]), jnp.bfloat16),
-            pltpu.VMEM((block, held * units), jnp.bfloat16),
+            pltpu.VMEM((rows, held * units), jnp.bfloat16),
         ],
         compiler_params=pltpu.CompilerParams(vmem_limit_bytes=32 << 20),
         cost_estimate=pl.CostEstimate(

time: 114 us -> 113 us (level)
  Pallas kernels: 20.2 us -> 17.9 us
  waiting for transfers between devices: 33.1 us -> 34.9 us
    pallas_call x4, Pallas kernels: 16.7 us -> 14.4 us  [expert_rows(): pl.pallas_call(expert_kernel, out_shape=[jax.ShapeDtypeStruct((p.shape[0]...]
  transfers between devices with their start and end apart: 42 -> 42, of which waited for: 19 -> 23; matrix products, arithmetic and copies ran while one was open for 3% -> 3% of each run, Pallas kernels for 16% -> 15%
where the time goes in v5:
time: 113 us; the launch traced here: 112 us
  starting transfers between devices  43.3 us (38%)
  waiting for transfers between devices  34.9 us (31%)
  Pallas kernels  17.9 us (16%)
  local copies, waits for them, and re-layouts  6.84 us (6%)
  blocking collectives  6.41 us (6%)
  other arithmetic  2.63 us (2%)
    ppermute x12, starting transfers between devices, turn(): lax.ppermute(value, 'ep', [(i, (i + 2 * step) % count) for i in range(cou...  19.3 us
    ppermute x8, waiting for transfers between devices, flip_inner(): lax.ppermute(value, 'ep', [(i, i ^ 1) for i in range(lax.axis_size('ep'))])  17.4 us
    pallas_call x4, Pallas kernels, expert_rows(): pl.pallas_call(expert_kernel, out_shape=[jax.ShapeDtypeStruct((p.shape[0]...  14.4 us
    ppermute x11, starting transfers between devices, flip_upper(): lax.ppermute(value, 'tp', [(i, i ^ 2) for i in range(lax.axis_size('tp'))])  13.6 us
    ppermute x11, waiting for transfers between devices, flip_upper(): lax.ppermute(value, 'tp', [(i, i ^ 2) for i in range(lax.axis_size('tp'))])  9.88 us
    ppermute x12, waiting for transfers between devices, turn(): lax.ppermute(value, 'ep', [(i, (i + 2 * step) % count) for i in range(cou...  7.57 us
    ppermute x8, starting transfers between devices, flip_inner(): lax.ppermute(value, 'ep', [(i, i ^ 1) for i in range(lax.axis_size('ep'))])  7.56 us
    unnamed x26, local copies, waits for them, and re-layouts  6.69 us
  transfers between devices with their start and end apart: 42, of which 23 were waited for; matrix products, arithmetic and copies ran while one was open for 3% of the time, Pallas kernels for 15%

profile of v5, /device:TPU:0, one launch (start us, length us, event | category | flops | bytes accessed | tf_op | source)
XLA Modules:
  0.0 112.5 jit_solution(5773058338857024501)
XLA Ops:
  0.0 1.3 %copy-done.4 = bf16[384,1536]{1,0:T(8,128)(2,1)S(1)} copy-done((bf16[384,1536]{1,0:T(8,128)(2,1)S(1)}, bf16[384,1536]{1,0:T(8,128)(2,1)}, u32[]{:S(2)}) %copy-start.4) | copy-done | bytes 1179672
  1.3 0.9 copy-done.5
  2.3 0.6 attend.1
  2.9 0.5 collective-permute-start
  3.4 1.1 copy.18.router_ref
  4.8 3.0 %collective-permute-start.1 = (bf16[32,1536]{1,0:T(8,128)(2,1)S(1)}, bf16[32,1536]{1,0:T(8,128)(2,1)S(1)}, u32[]{:S(2)}, u32[]{:S(2)}) collective-permute-start(bf16[32,1536]{1,0:T(8,128)(2,1)S(1)} %get-tuple-element.132), channel_id=1, source_target_pairs={{0,2},{1,3},{2,0},{3,1},{4,6},{5,7},{6,4},{7,5},{8,10},{9,11},{10,... | collective-permute-start | bytes 294920 | tf_op jit(solution)/shard_map/ppermute | solution.py:44
  8.3 2.6 %collective-permute-done.1.upper_ref = bf16[32,1536]{1,0:T(8,128)(2,1)S(1)} collective-permute-done((bf16[32,1536]{1,0:T(8,128)(2,1)S(1)}, bf16[32,1536]{1,0:T(8,128)(2,1)S(1)}, u32[]{:S(2)}, u32[]{:S(2)}) %collective-permute-start.1) | collective-permute-done | bytes 98336 | tf_op jit(solution)/shard_map/ppermute | solution.py:44
  10.9 0.5 norm_rows.2
  11.4 2.0 %collective-permute-start.2 = (bf16[32,1664]{1,0:T(8,128)(2,1)S(1)}, bf16[32,1664]{1,0:T(8,128)(2,1)S(1)}, u32[]{:S(2)}, u32[]{:S(2)}) collective-permute-start(bf16[32,1664]{1,0:T(8,128)(2,1)S(1)} %get-tuple-element.57), channel_id=1, source_target_pairs={{0,8},{4,12},{8,16},{12,20},{16,24},{20,28},{24,0},{28,4},{1,9},{5... | collective-permute-start | bytes 319496 | tf_op jit(solution)/shard_map/ppermute | solution.py:36
  13.4 2.6 %collective-permute-start.3 = (bf16[32,1664]{1,0:T(8,128)(2,1)S(1)}, bf16[32,1664]{1,0:T(8,128)(2,1)S(1)}, u32[]{:S(2)}, u32[]{:S(2)}) collective-permute-start(bf16[32,1664]{1,0:T(8,128)(2,1)S(1)} %get-tuple-element.57), channel_id=1, source_target_pairs={{0,16},{4,20},{8,24},{12,28},{16,0},{20,4},{24,8},{28,12},{1,17},{... | collective-permute-start | bytes 319496 | tf_op jit(solution)/shard_map/ppermute | solution.py:36
  16.0 1.3 %collective-permute-start.4 = (bf16[32,1664]{1,0:T(8,128)(2,1)S(1)}, bf16[32,1664]{1,0:T(8,128)(2,1)S(1)}, u32[]{:S(2)}, u32[]{:S(2)}) collective-permute-start(bf16[32,1664]{1,0:T(8,128)(2,1)S(1)} %get-tuple-element.57), channel_id=1, source_target_pairs={{0,24},{4,28},{8,0},{12,4},{16,8},{20,12},{24,16},{28,20},{1,25},{... | collective-permute-start | bytes 319496 | tf_op jit(solution)/shard_map/ppermute | solution.py:36
  17.4 1.5 %copy-done.2 = bf16[5,1536,128]{2,1,0:T(8,128)(2,1)S(1)} copy-done((bf16[5,1536,128]{2,1,0:T(8,128)(2,1)S(1)}, bf16[5,1536,128]{2,1,0:T(8,128)(2,1)}, u32[]{:S(2)}) %copy-start.2) | copy-done | bytes 1966104
  18.9 1.5 %copy-done.3 = bf16[5,128,1536]{2,1,0:T(8,128)(2,1)S(1)} copy-done((bf16[5,128,1536]{2,1,0:T(8,128)(2,1)S(1)}, bf16[5,128,1536]{2,1,0:T(8,128)(2,1)}, u32[]{:S(2)}) %copy-start.3) | copy-done | bytes 1966104
  20.5 1.0 load_weights.1
  21.5 0.9 collective-permute-done.3
  22.6 1.6 %collective-permute-start.6 = (bf16[64,1664]{1,0:T(8,128)(2,1)S(1)}, bf16[64,1664]{1,0:T(8,128)(2,1)S(1)}, u32[]{:S(2)}, u32[]{:S(2)}) collective-permute-start(bf16[64,1664]{1,0:T(8,128)(2,1)S(1)} %get-tuple-element.60), channel_id=1, source_target_pairs={{0,4},{4,0},{8,12},{12,8},{16,20},{20,16},{24,28},{28,24},{1,5},{5... | collective-permute-start | bytes 638984 | tf_op jit(solution)/shard_map/ppermute | solution.py:40
  24.2 1.7 %collective-permute-start.7 = (bf16[64,1664]{1,0:T(8,128)(2,1)S(1)}, bf16[64,1664]{1,0:T(8,128)(2,1)S(1)}, u32[]{:S(2)}, u32[]{:S(2)}) collective-permute-start(bf16[64,1664]{1,0:T(8,128)(2,1)S(1)} %get-tuple-element.61), channel_id=1, source_target_pairs={{0,2},{1,3},{2,0},{3,1},{4,6},{5,7},{6,4},{7,5},{8,10},{9,11},{10,... | collective-permute-start | bytes 638984 | tf_op jit(solution)/shard_map/ppermute | solution.py:44
  25.9 0.5 norm_rows.3
  26.4 3.0 %collective-permute-done.6 = bf16[64,1664]{1,0:T(8,128)(2,1)S(1)} collective-permute-done((bf16[64,1664]{1,0:T(8,128)(2,1)S(1)}, bf16[64,1664]{1,0:T(8,128)(2,1)S(1)}, u32[]{:S(2)}, u32[]{:S(2)}) %collective-permute-start.6) | collective-permute-done | bytes 213024 | tf_op jit(solution)/shard_map/ppermute | solution.py:40
  29.5 1.1 %collective-permute-done.7 = bf16[64,1664]{1,0:T(8,128)(2,1)S(1)} collective-permute-done((bf16[64,1664]{1,0:T(8,128)(2,1)S(1)}, bf16[64,1664]{1,0:T(8,128)(2,1)S(1)}, u32[]{:S(2)}, u32[]{:S(2)}) %collective-permute-start.7) | collective-permute-done | bytes 213024 | tf_op jit(solution)/shard_map/ppermute | solution.py:44
  30.6 2.9 %collective-permute-start.16 = (bf16[32,1664]{1,0:T(8,128)(2,1)S(1)}, bf16[32,1664]{1,0:T(8,128)(2,1)S(1)}, u32[]{:S(2)}, u32[]{:S(2)}) collective-permute-start(bf16[32,1664]{1,0:T(8,128)(2,1)S(1)} %get-tuple-element.77), channel_id=1, source_target_pairs={{0,8},{4,12},{8,16},{12,20},{16,24},{20,28},{24,0},{28,4},{1,9},{5... | collective-permute-start | bytes 319496 | tf_op jit(solution)/shard_map/ppermute | solution.py:36
  33.5 0.7 collective-permute-start.17
  34.2 1.7 %collective-permute-start.18 = (bf16[32,1664]{1,0:T(8,128)(2,1)S(1)}, bf16[32,1664]{1,0:T(8,128)(2,1)S(1)}, u32[]{:S(2)}, u32[]{:S(2)}) collective-permute-start(bf16[32,1664]{1,0:T(8,128)(2,1)S(1)} %get-tuple-element.77), channel_id=1, source_target_pairs={{0,24},{4,28},{8,0},{12,4},{16,8},{20,12},{24,16},{28,20},{1,25},{... | collective-permute-start | bytes 319496 | tf_op jit(solution)/shard_map/ppermute | solution.py:36
  36.0 1.3 %collective-permute-start.8 = (bf16[128,1664]{1,0:T(8,128)(2,1)S(1)}, bf16[128,1664]{1,0:T(8,128)(2,1)S(1)}, u32[]{:S(2)}, u32[]{:S(2)}) collective-permute-start(bf16[128,1664]{1,0:T(8,128)(2,1)S(1)} %pad_maximum_fusion.2), channel_id=1, source_target_pairs={{0,2},{1,3},{2,0},{3,1},{4,6},{5,7},{6,4},{7,5},{8,10},{9,11},{10,... | collective-permute-start | bytes 1277960 | tf_op jit(solution)/shard_map/ppermute | solution.py:44
  37.4 0.6 collective-permute-start.9
  38.4 3.3 %collective-permute-done.17 = bf16[32,1664]{1,0:T(8,128)(2,1)S(1)} collective-permute-done((bf16[32,1664]{1,0:T(8,128)(2,1)S(1)}, bf16[32,1664]{1,0:T(8,128)(2,1)S(1)}, u32[]{:S(2)}, u32[]{:S(2)}) %collective-permute-start.17) | collective-permute-done | bytes 106528 | tf_op jit(solution)/shard_map/ppermute | solution.py:36
  41.7 1.2 %collective-permute-start.20 = (bf16[64,1664]{1,0:T(8,128)(2,1)S(1)}, bf16[64,1664]{1,0:T(8,128)(2,1)S(1)}, u32[]{:S(2)}, u32[]{:S(2)}) collective-permute-start(bf16[64,1664]{1,0:T(8,128)(2,1)S(1)} %pad_maximum_fusion.9), channel_id=1, source_target_pairs={{0,2},{1,3},{2,0},{3,1},{4,6},{5,7},{6,4},{7,5},{8,10},{9,11},{10,... | collective-permute-start | bytes 638984 | tf_op jit(solution)/shard_map/ppermute | solution.py:44
  42.9 0.6 collective-permute-start.19
  43.5 5.5 %collective-permute-done.9 = bf16[128,1664]{1,0:T(8,128)(2,1)S(1)} collective-permute-done((bf16[128,1664]{1,0:T(8,128)(2,1)S(1)}, bf16[128,1664]{1,0:T(8,128)(2,1)S(1)}, u32[]{:S(2)}, u32[]{:S(2)}) %collective-permute-start.9) | collective-permute-done | bytes 426016 | tf_op jit(solution)/shard_map/ppermute | solution.py:40
  49.2 0.5 collective-permute-start.11
  49.7 0.8 collective-permute-done.20
  50.5 0.8 collective-permute-done.19
  51.3 0.6 collective-permute-start.23
  52.0 1.3 %collective-permute-start.22 = (bf16[128,1664]{1,0:T(8,128)(2,1)S(1)}, bf16[128,1664]{1,0:T(8,128)(2,1)S(1)}, u32[]{:S(2)}, u32[]{:S(2)}) collective-permute-start(bf16[128,1664]{1,0:T(8,128)(2,1)S(1)} %pad_maximum_fusion.4), channel_id=1, source_target_pairs={{0,2},{1,3},{2,0},{3,1},{4,6},{5,7},{6,4},{7,5},{8,10},{9,11},{10,... | collective-permute-start | bytes 1277960 | tf_op jit(solution)/shard_map/ppermute | solution.py:44
  53.4 3.6 %expert_rows.4 = (bf16[256,1536]{1,0:T(8,128)(2,1)S(1)}, bf16[256,1536]{1,0:T(8,128)(2,1)S(1)}) custom-call(s32[1]{0:T(128)} %bitcast.1.first_ref, bf16[256,1664]{1,0:T(8,128)(2,1)S(1)} %collective-permute-done.10.near_ref, bf16[256,1664]{1,0:T(8,128)(2,1)S(1)} %collective-permute-done.11.far_ref, bf16[5,1536,256]{2,1,0:T(8,128)(2,1)S(1)} %get-tuple-element.68.both_ref, ...), custom_call_target="tpu_custom_call" | custom-call | flops 3019898880 | bytes 9043968 | tf_op jit(solution)/shard_map/expert_rows/pallas_call | solution.py:245
  57.0 0.5 collective-permute-start.13
  57.6 3.5 %expert_rows.5 = (bf16[256,1536]{1,0:T(8,128)(2,1)S(1)}, bf16[256,1536]{1,0:T(8,128)(2,1)S(1)}) custom-call(s32[1]{0:T(128)} %bitcast.1.first_ref, bf16[256,1664]{1,0:T(8,128)(2,1)S(1)} %pad_maximum_fusion.near_ref, bf16[256,1664]{1,0:T(8,128)(2,1)S(1)} %constant_dynamic-update-slice_fusion.far_ref, bf16[5,1536,256]{2,1,0:T(8,128)(2,1)S(1)} %get-tuple-element.68.both_ref, ...), custom_call_target="tpu_custom_call" | custom-call | flops 3019898880 | bytes 9043968 | tf_op jit(solution)/shard_map/expert_rows/pallas_call | solution.py:245
  61.1 0.5 collective-permute-done.23
  62.9 1.3 %collective-permute-start.14 = (bf16[128,1536]{1,0:T(8,128)(2,1)S(1)}, bf16[128,1536]{1,0:T(8,128)(2,1)S(1)}, u32[]{:S(2)}, u32[]{:S(2)}) collective-permute-start(bf16[128,1536]{1,0:T(8,128)(2,1)S(1)} %get-tuple-element.130), channel_id=1, source_target_pairs={{0,2},{1,3},{2,0},{3,1},{4,6},{5,7},{6,4},{7,5},{8,10},{9,11},{10,... | collective-permute-start | bytes 1179656 | tf_op jit(solution)/shard_map/ppermute | solution.py:44
  64.1 1.4 %collective-permute-start.15 = (bf16[128,1536]{1,0:T(8,128)(2,1)S(1)}, bf16[128,1536]{1,0:T(8,128)(2,1)S(1)}, u32[]{:S(2)}, u32[]{:S(2)}) collective-permute-start(bf16[128,1536]{1,0:T(8,128)(2,1)S(1)} %get-tuple-element.129), channel_id=1, source_target_pairs={{0,4},{4,0},{8,12},{12,8},{16,20},{20,16},{24,28},{28,24},{1,5},{5... | collective-permute-start | bytes 1179656 | tf_op jit(solution)/shard_map/ppermute | solution.py:40
  65.5 3.6 %expert_rows.6 = (bf16[256,1536]{1,0:T(8,128)(2,1)S(1)}, bf16[256,1536]{1,0:T(8,128)(2,1)S(1)}) custom-call(s32[1]{0:T(128)} %bitcast.1.first_ref, bf16[256,1664]{1,0:T(8,128)(2,1)S(1)} %collective-permute-done.21.near_ref, bf16[256,1664]{1,0:T(8,128)(2,1)S(1)} %collective-permute-done.24.far_ref, bf16[5,1536,256]{2,1,0:T(8,128)(2,1)S(1)} %get-tuple-element.68.both_ref, ...), custom_call_target="tpu_custom_call" | custom-call | flops 3019898880 | bytes 9043968 | tf_op jit(solution)/shard_map/expert_rows/pallas_call | solution.py:245
  69.6 3.8 %expert_rows.7 = (bf16[256,1536]{1,0:T(8,128)(2,1)S(1)}, bf16[256,1536]{1,0:T(8,128)(2,1)S(1)}) custom-call(s32[1]{0:T(128)} %bitcast.1.first_ref, bf16[256,1664]{1,0:T(8,128)(2,1)S(1)} %pad_maximum_fusion.1.near_ref, bf16[256,1664]{1,0:T(8,128)(2,1)S(1)} %constant_dynamic-update-slice_fusion.2.far_ref, ...), custom_call_target="tpu_custom_call" | custom-call | flops 3019898880 | bytes 9043968 | tf_op jit(solution)/shard_map/expert_rows/pallas_call | solution.py:245
  73.4 0.6 collective-permute-done.14
  74.0 0.9 collective-permute-done.15
  75.1 1.4 %collective-permute-start.25 = (bf16[64,1536]{1,0:T(8,128)(2,1)S(1)}, bf16[64,1536]{1,0:T(8,128)(2,1)S(1)}, u32[]{:S(2)}, u32[]{:S(2)}) collective-permute-start(bf16[64,1536]{1,0:T(8,128)(2,1)S(1)} %get-tuple-element.128), channel_id=1, source_target_pairs={{0,4},{4,0},{8,12},{12,8},{16,20},{20,16},{24,28},{28,24},{1,5},{5... | collective-permute-start | bytes 589832 | tf_op jit(solution)/shard_map/ppermute | solution.py:40
  76.5 0.9 collective-permute-start.26
  77.6 1.2 %collective-permute-start.32 = (bf16[128,1536]{1,0:T(8,128)(2,1)S(1)}, bf16[128,1536]{1,0:T(8,128)(2,1)S(1)}, u32[]{:S(2)}, u32[]{:S(2)}) collective-permute-start(bf16[128,1536]{1,0:T(8,128)(2,1)S(1)} %get-tuple-element.126), channel_id=1, source_target_pairs={{0,2},{1,3},{2,0},{3,1},{4,6},{5,7},{6,4},{7,5},{8,10},{9,11},{10,... | collective-permute-start | bytes 1179656 | tf_op jit(solution)/shard_map/ppermute | solution.py:44
  78.8 0.7 collective-permute-start.33
  79.5 2.8 %collective-permute-done.25 = bf16[64,1536]{1,0:T(8,128)(2,1)S(1)} collective-permute-done((bf16[64,1536]{1,0:T(8,128)(2,1)S(1)}, bf16[64,1536]{1,0:T(8,128)(2,1)S(1)}, u32[]{:S(2)}, u32[]{:S(2)}) %collective-permute-start.25) | collective-permute-done | bytes 196640 | tf_op jit(solution)/shard_map/ppermute | solution.py:40
  82.3 2.0 %collective-permute-done.26 = bf16[64,1536]{1,0:T(8,128)(2,1)S(1)} collective-permute-done((bf16[64,1536]{1,0:T(8,128)(2,1)S(1)}, bf16[64,1536]{1,0:T(8,128)(2,1)S(1)}, u32[]{:S(2)}, u32[]{:S(2)}) %collective-permute-start.26) | collective-permute-done | bytes 196640 | tf_op jit(solution)/shard_map/ppermute | solution.py:44
  84.7 2.3 %collective-permute-start.29 = (bf16[32,1536]{1,0:T(8,128)(2,1)S(1)}, bf16[32,1536]{1,0:T(8,128)(2,1)S(1)}, u32[]{:S(2)}, u32[]{:S(2)}) collective-permute-start(bf16[32,1536]{1,0:T(8,128)(2,1)S(1)} %pad_maximum_fusion.11), channel_id=1, source_target_pairs={{0,16},{4,20},{8,24},{12,28},{16,0},{20,4},{24,8},{28,12},{1,17},{... | collective-permute-start | bytes 294920 | tf_op jit(solution)/shard_map/ppermute | solution.py:36
  86.9 1.7 %collective-permute-start.28 = (bf16[32,1536]{1,0:T(8,128)(2,1)S(1)}, bf16[32,1536]{1,0:T(8,128)(2,1)S(1)}, u32[]{:S(2)}, u32[]{:S(2)}) collective-permute-start(bf16[32,1536]{1,0:T(8,128)(2,1)S(1)} %pad_maximum_fusion.10), channel_id=1, source_target_pairs={{0,24},{4,28},{8,0},{12,4},{16,8},{20,12},{24,16},{28,20},{1,25},{... | collective-permute-start | bytes 294920 | tf_op jit(solution)/shard_map/ppermute | solution.py:36
  88.6 1.8 %collective-permute-done.32 = bf16[128,1536]{1,0:T(8,128)(2,1)S(1)} collective-permute-done((bf16[128,1536]{1,0:T(8,128)(2,1)S(1)}, bf16[128,1536]{1,0:T(8,128)(2,1)S(1)}, u32[]{:S(2)}, u32[]{:S(2)}) %collective-permute-start.32) | collective-permute-done | bytes 393248 | tf_op jit(solution)/shard_map/ppermute | solution.py:44
  90.5 0.7 collective-permute-start.37
  91.3 0.8 collective-permute-start.38
  92.5 3.7 %collective-permute-done.37 = bf16[64,1536]{1,0:T(8,128)(2,1)S(1)} collective-permute-done((bf16[64,1536]{1,0:T(8,128)(2,1)S(1)}, bf16[64,1536]{1,0:T(8,128)(2,1)S(1)}, u32[]{:S(2)}, u32[]{:S(2)}) %collective-permute-start.37) | collective-permute-done | bytes 196640 | tf_op jit(solution)/shard_map/ppermute | solution.py:40
  96.4 0.6 collective-permute-done.38
  97.1 2.3 %collective-permute-start.40 = (bf16[32,1536]{1,0:T(8,128)(2,1)S(1)}, bf16[32,1536]{1,0:T(8,128)(2,1)S(1)}, u32[]{:S(2)}, u32[]{:S(2)}) collective-permute-start(bf16[32,1536]{1,0:T(8,128)(2,1)S(1)} %pad_maximum_fusion.14), channel_id=1, source_target_pairs={{0,16},{4,20},{8,24},{12,28},{16,0},{20,4},{24,8},{28,12},{1,17},{... | collective-permute-start | bytes 294920 | tf_op jit(solution)/shard_map/ppermute | solution.py:36
  99.4 1.7 %collective-permute-start.39 = (bf16[32,1536]{1,0:T(8,128)(2,1)S(1)}, bf16[32,1536]{1,0:T(8,128)(2,1)S(1)}, u32[]{:S(2)}, u32[]{:S(2)}) collective-permute-start(bf16[32,1536]{1,0:T(8,128)(2,1)S(1)} %pad_maximum_fusion.13), channel_id=1, source_target_pairs={{0,24},{4,28},{8,0},{12,4},{16,8},{20,12},{24,16},{28,20},{1,25},{... | collective-permute-start | bytes 294920 | tf_op jit(solution)/shard_map/ppermute | solution.py:36
  101.3 0.9 collective-permute-start.35
  102.2 1.5 %collective-permute-done.41 = bf16[32,1536]{1,0:T(8,128)(2,1)S(1)} collective-permute-done((bf16[32,1536]{1,0:T(8,128)(2,1)S(1)}, bf16[32,1536]{1,0:T(8,128)(2,1)S(1)}, u32[]{:S(2)}, u32[]{:S(2)}) %collective-permute-start.41) | collective-permute-done | bytes 98336 | tf_op jit(solution)/shard_map/ppermute | solution.py:36
  103.7 1.1 %collective-permute-done.40 = bf16[32,1536]{1,0:T(8,128)(2,1)S(1)} collective-permute-done((bf16[32,1536]{1,0:T(8,128)(2,1)S(1)}, bf16[32,1536]{1,0:T(8,128)(2,1)S(1)}, u32[]{:S(2)}, u32[]{:S(2)}) %collective-permute-start.40) | collective-permute-done | bytes 98336 | tf_op jit(solution)/shard_map/ppermute | solution.py:36
  105.1 6.4 %all-gather = bf16[128,1536]{1,0:T(8,128)(2,1)S(1)} all-gather(bf16[32,1536]{1,0:T(8,128)(2,1)S(1)} %multiply_convert_fusion), channel_id=2, replica_groups=mesh['ep'=8,'tp'=4] {'tp'}, dimensions={0}, use_global_device_ids=true | all-gather | bytes 491520 | tf_op jit(solution)/shard_map/all_gather | solution.py:454
  111.5 0.9 join.1
  (102 shorter events, 5.8 us)
Async XLA Ops:
  0.0 10.9 %copy-start = (bf16[256,1536]{1,0:T(8,128)(2,1)S(1)}, bf16[256,1536]{1,0:T(8,128)(2,1)}, u32[]{:S(2)}) copy-start(bf16[256,1536]{1,0:T(8,128)(2,1)} %resid_ref.3) | copy-start | bytes 2359300
  0.0 1.3 %copy-start.4 = (bf16[384,1536]{1,0:T(8,128)(2,1)S(1)}, bf16[384,1536]{1,0:T(8,128)(2,1)}, u32[]{:S(2)}) copy-start(bf16[384,1536]{1,0:T(8,128)(2,1)} %w_ref.1) | copy-start | bytes 3538948
  1.3 0.9 copy-start.5
  2.3 2.2 %copy-start.6 = (s32[256,8]{0,1:T(8,128)S(1)}, s32[256,8]{0,1:T(8,128)}, u32[]{:S(2)}) copy-start(s32[256,8]{0,1:T(8,128)} %param.18) | copy-start | bytes 24580
  2.3 2.4 %copy-start.9 = (bf16[1536]{0:T(1024)(128)(2,1)S(1)}, bf16[1536]{0:T(1024)(128)(2,1)}, u32[]{:S(2)}) copy-start(bf16[1536]{0:T(1024)(128)(2,1)} %param.15) | copy-start | bytes 9220
  2.3 5.4 %copy-start.7 = (s32[40]{0:T(128)S(1)}, s32[40]{0:T(128)}, u32[]{:S(2)}) copy-start(s32[40]{0:T(128)} %param.19) | copy-start | bytes 484
  2.3 5.6 %copy-start.10 = (s32[1,40]{1,0:T(1,128)S(1)}, s32[1,40]{1,0:T(1,128)}, u32[]{:S(2)}) copy-start(s32[1,40]{1,0:T(1,128)} %param.20) | copy-start | bytes 484
  2.9 1.9 %collective-permute-start = (bf16[2,64,1536]{2,1,0:T(8,128)(2,1)S(1)}, bf16[2,64,1536]{2,1,0:T(8,128)(2,1)S(1)}, u32[]{:S(2)}, u32[]{:S(2)}) collective-permute-start(bf16[2,64,1536]{2,1,0:T(8,128)(2,1)S(1)} %get-tuple-element.54), channel_id=1, source_target_pairs={{0,1},{1,0},{2,3},{3,2},{4,5},{5,4},{6,7},{7,6},{8,9},{9,8},{10,11... | collective-permute-start | bytes 1179656 | tf_op jit(solution)/shard_map/ppermute | solution.py:48
  4.7 12.7 %copy-start.1 = (bf16[5,1536,128]{2,1,0:T(8,128)(2,1)S(1)}, bf16[5,1536,128]{2,1,0:T(8,128)(2,1)}, u32[]{:S(2)}) copy-start(bf16[5,1536,128]{2,1,0:T(8,128)(2,1)} %gate_hbm.1) | copy-start | bytes 5898244
  4.8 6.1 %collective-permute-start.1 = (bf16[32,1536]{1,0:T(8,128)(2,1)S(1)}, bf16[32,1536]{1,0:T(8,128)(2,1)S(1)}, u32[]{:S(2)}, u32[]{:S(2)}) collective-permute-start(bf16[32,1536]{1,0:T(8,128)(2,1)S(1)} %get-tuple-element.132), channel_id=1, source_target_pairs={{0,2},{1,3},{2,0},{3,1},{4,6},{5,7},{6,4},{7,5},{8,10},{9,11},{10,... | collective-permute-start | bytes 294920 | tf_op jit(solution)/shard_map/ppermute | solution.py:44
  8.3 9.1 %collective-permute-start.5 = (bf16[32,1536]{1,0:T(8,128)(2,1)S(1)}, bf16[32,1536]{1,0:T(8,128)(2,1)S(1)}, u32[]{:S(2)}, u32[]{:S(2)}) collective-permute-start(bf16[32,1536]{1,0:T(8,128)(2,1)S(1)} %get-tuple-element.131), channel_id=1, source_target_pairs={{0,2},{1,3},{2,0},{3,1},{4,6},{5,7},{6,4},{7,5},{8,10},{9,11},{10,... | collective-permute-start | bytes 294920 | tf_op jit(solution)/shard_map/ppermute | solution.py:44
  11.4 10.1 %collective-permute-start.2 = (bf16[32,1664]{1,0:T(8,128)(2,1)S(1)}, bf16[32,1664]{1,0:T(8,128)(2,1)S(1)}, u32[]{:S(2)}, u32[]{:S(2)}) collective-permute-start(bf16[32,1664]{1,0:T(8,128)(2,1)S(1)} %get-tuple-element.57), channel_id=1, source_target_pairs={{0,8},{4,12},{8,16},{12,20},{16,24},{20,28},{24,0},{28,4},{1,9},{5... | collective-permute-start | bytes 319496 | tf_op jit(solution)/shard_map/ppermute | solution.py:36
  13.4 9.0 %collective-permute-start.3 = (bf16[32,1664]{1,0:T(8,128)(2,1)S(1)}, bf16[32,1664]{1,0:T(8,128)(2,1)S(1)}, u32[]{:S(2)}, u32[]{:S(2)}) collective-permute-start(bf16[32,1664]{1,0:T(8,128)(2,1)S(1)} %get-tuple-element.57), channel_id=1, source_target_pairs={{0,16},{4,20},{8,24},{12,28},{16,0},{20,4},{24,8},{28,12},{1,17},{... | collective-permute-start | bytes 319496 | tf_op jit(solution)/shard_map/ppermute | solution.py:36
  16.0 6.6 %collective-permute-start.4 = (bf16[32,1664]{1,0:T(8,128)(2,1)S(1)}, bf16[32,1664]{1,0:T(8,128)(2,1)S(1)}, u32[]{:S(2)}, u32[]{:S(2)}) collective-permute-start(bf16[32,1664]{1,0:T(8,128)(2,1)S(1)} %get-tuple-element.57), channel_id=1, source_target_pairs={{0,24},{4,28},{8,0},{12,4},{16,8},{20,12},{24,16},{28,20},{1,25},{... | collective-permute-start | bytes 319496 | tf_op jit(solution)/shard_map/ppermute | solution.py:36
  17.4 1.5 %copy-start.2 = (bf16[5,1536,128]{2,1,0:T(8,128)(2,1)S(1)}, bf16[5,1536,128]{2,1,0:T(8,128)(2,1)}, u32[]{:S(2)}) copy-start(bf16[5,1536,128]{2,1,0:T(8,128)(2,1)} %up_hbm.1) | copy-start | bytes 5898244
  18.9 1.5 %copy-start.3 = (bf16[5,128,1536]{2,1,0:T(8,128)(2,1)S(1)}, bf16[5,128,1536]{2,1,0:T(8,128)(2,1)}, u32[]{:S(2)}) copy-start(bf16[5,128,1536]{2,1,0:T(8,128)(2,1)} %param.23) | copy-start | bytes 5898244
  22.6 6.8 %collective-permute-start.6 = (bf16[64,1664]{1,0:T(8,128)(2,1)S(1)}, bf16[64,1664]{1,0:T(8,128)(2,1)S(1)}, u32[]{:S(2)}, u32[]{:S(2)}) collective-permute-start(bf16[64,1664]{1,0:T(8,128)(2,1)S(1)} %get-tuple-element.60), channel_id=1, source_target_pairs={{0,4},{4,0},{8,12},{12,8},{16,20},{20,16},{24,28},{28,24},{1,5},{5... | collective-permute-start | bytes 638984 | tf_op jit(solution)/shard_map/ppermute | solution.py:40
  24.2 6.4 %collective-permute-start.7 = (bf16[64,1664]{1,0:T(8,128)(2,1)S(1)}, bf16[64,1664]{1,0:T(8,128)(2,1)S(1)}, u32[]{:S(2)}, u32[]{:S(2)}) collective-permute-start(bf16[64,1664]{1,0:T(8,128)(2,1)S(1)} %get-tuple-element.61), channel_id=1, source_target_pairs={{0,2},{1,3},{2,0},{3,1},{4,6},{5,7},{6,4},{7,5},{8,10},{9,11},{10,... | collective-permute-start | bytes 638984 | tf_op jit(solution)/shard_map/ppermute | solution.py:44
  30.6 7.7 %collective-permute-start.16 = (bf16[32,1664]{1,0:T(8,128)(2,1)S(1)}, bf16[32,1664]{1,0:T(8,128)(2,1)S(1)}, u32[]{:S(2)}, u32[]{:S(2)}) collective-permute-start(bf16[32,1664]{1,0:T(8,128)(2,1)S(1)} %get-tuple-element.77), channel_id=1, source_target_pairs={{0,8},{4,12},{8,16},{12,20},{16,24},{20,28},{24,0},{28,4},{1,9},{5... | collective-permute-start | bytes 319496 | tf_op jit(solution)/shard_map/ppermute | solution.py:36
  33.5 8.1 %collective-permute-start.17 = (bf16[32,1664]{1,0:T(8,128)(2,1)S(1)}, bf16[32,1664]{1,0:T(8,128)(2,1)S(1)}, u32[]{:S(2)}, u32[]{:S(2)}) collective-permute-start(bf16[32,1664]{1,0:T(8,128)(2,1)S(1)} %get-tuple-element.77), channel_id=1, source_target_pairs={{0,16},{4,20},{8,24},{12,28},{16,0},{20,4},{24,8},{28,12},{1,17},{... | collective-permute-start | bytes 319496 | tf_op jit(solution)/shard_map/ppermute | solution.py:36
  34.2 7.4 %collective-permute-start.18 = (bf16[32,1664]{1,0:T(8,128)(2,1)S(1)}, bf16[32,1664]{1,0:T(8,128)(2,1)S(1)}, u32[]{:S(2)}, u32[]{:S(2)}) collective-permute-start(bf16[32,1664]{1,0:T(8,128)(2,1)S(1)} %get-tuple-element.77), channel_id=1, source_target_pairs={{0,24},{4,28},{8,0},{12,4},{16,8},{20,12},{24,16},{28,20},{1,25},{... | collective-permute-start | bytes 319496 | tf_op jit(solution)/shard_map/ppermute | solution.py:36
  36.0 13.1 %collective-permute-start.8 = (bf16[128,1664]{1,0:T(8,128)(2,1)S(1)}, bf16[128,1664]{1,0:T(8,128)(2,1)S(1)}, u32[]{:S(2)}, u32[]{:S(2)}) collective-permute-start(bf16[128,1664]{1,0:T(8,128)(2,1)S(1)} %pad_maximum_fusion.2), channel_id=1, source_target_pairs={{0,2},{1,3},{2,0},{3,1},{4,6},{5,7},{6,4},{7,5},{8,10},{9,11},{10,... | collective-permute-start | bytes 1277960 | tf_op jit(solution)/shard_map/ppermute | solution.py:44
  37.4 11.6 %collective-permute-start.9 = (bf16[128,1664]{1,0:T(8,128)(2,1)S(1)}, bf16[128,1664]{1,0:T(8,128)(2,1)S(1)}, u32[]{:S(2)}, u32[]{:S(2)}) collective-permute-start(bf16[128,1664]{1,0:T(8,128)(2,1)S(1)} %pad_maximum_fusion.3), channel_id=1, source_target_pairs={{0,4},{4,0},{8,12},{12,8},{16,20},{20,16},{24,28},{28,24},{1,5},{5... | collective-permute-start | bytes 1277960 | tf_op jit(solution)/shard_map/ppermute | solution.py:40
  41.7 8.8 %collective-permute-start.20 = (bf16[64,1664]{1,0:T(8,128)(2,1)S(1)}, bf16[64,1664]{1,0:T(8,128)(2,1)S(1)}, u32[]{:S(2)}, u32[]{:S(2)}) collective-permute-start(bf16[64,1664]{1,0:T(8,128)(2,1)S(1)} %pad_maximum_fusion.9), channel_id=1, source_target_pairs={{0,2},{1,3},{2,0},{3,1},{4,6},{5,7},{6,4},{7,5},{8,10},{9,11},{10,... | collective-permute-start | bytes 638984 | tf_op jit(solution)/shard_map/ppermute | solution.py:44
  42.9 8.4 %collective-permute-start.19 = (bf16[64,1664]{1,0:T(8,128)(2,1)S(1)}, bf16[64,1664]{1,0:T(8,128)(2,1)S(1)}, u32[]{:S(2)}, u32[]{:S(2)}) collective-permute-start(bf16[64,1664]{1,0:T(8,128)(2,1)S(1)} %pad_maximum_fusion.8), channel_id=1, source_target_pairs={{0,4},{4,0},{8,12},{12,8},{16,20},{20,16},{24,28},{28,24},{1,5},{5... | collective-permute-start | bytes 638984 | tf_op jit(solution)/shard_map/ppermute | solution.py:40
  49.1 4.3 %collective-permute-start.10 = (bf16[256,1664]{1,0:T(8,128)(2,1)S(1)}, bf16[256,1664]{1,0:T(8,128)(2,1)S(1)}, u32[]{:S(2)}, u32[]{:S(2)}) collective-permute-start(bf16[256,1664]{1,0:T(8,128)(2,1)S(1)} %pad_maximum_fusion.near_ref), channel_id=1, source_target_pairs={{0,1},{1,0},{2,3},{3,2},{4,5},{5,4},{6,7},{7,6},{8,9},{9,8},{10,11... | collective-permute-start | bytes 2555912 | tf_op jit(solution)/shard_map/ppermute | solution.py:48
  49.2 4.2 %collective-permute-start.11 = (bf16[256,1664]{1,0:T(8,128)(2,1)S(1)}, bf16[256,1664]{1,0:T(8,128)(2,1)S(1)}, u32[]{:S(2)}, u32[]{:S(2)}) collective-permute-start(bf16[256,1664]{1,0:T(8,128)(2,1)S(1)} %constant_dynamic-update-slice_fusion.far_ref), channel_id=1, source_target_pairs={{0,1},{1,0},{2,3},{3,2},{4,5},{5,4},{6,7},{7,6},{8,9},{9,8},{10,11... | collective-permute-start | bytes 2555912 | tf_op jit(solution)/shard_map/ppermute | solution.py:48
  51.3 10.3 %collective-permute-start.23 = (bf16[128,1664]{1,0:T(8,128)(2,1)S(1)}, bf16[128,1664]{1,0:T(8,128)(2,1)S(1)}, u32[]{:S(2)}, u32[]{:S(2)}) collective-permute-start(bf16[128,1664]{1,0:T(8,128)(2,1)S(1)} %pad_maximum_fusion.5), channel_id=1, source_target_pairs={{0,4},{4,0},{8,12},{12,8},{16,20},{20,16},{24,28},{28,24},{1,5},{5... | collective-permute-start | bytes 1277960 | tf_op jit(solution)/shard_map/ppermute | solution.py:40
  52.0 10.0 %collective-permute-start.22 = (bf16[128,1664]{1,0:T(8,128)(2,1)S(1)}, bf16[128,1664]{1,0:T(8,128)(2,1)S(1)}, u32[]{:S(2)}, u32[]{:S(2)}) collective-permute-start(bf16[128,1664]{1,0:T(8,128)(2,1)S(1)} %pad_maximum_fusion.4), channel_id=1, source_target_pairs={{0,2},{1,3},{2,0},{3,1},{4,6},{5,7},{6,4},{7,5},{8,10},{9,11},{10,... | collective-permute-start | bytes 1277960 | tf_op jit(solution)/shard_map/ppermute | solution.py:44
  53.3 12.1 %collective-permute-start.21 = (bf16[256,1664]{1,0:T(8,128)(2,1)S(1)}, bf16[256,1664]{1,0:T(8,128)(2,1)S(1)}, u32[]{:S(2)}, u32[]{:S(2)}) collective-permute-start(bf16[256,1664]{1,0:T(8,128)(2,1)S(1)} %pad_maximum_fusion.1.near_ref), channel_id=1, source_target_pairs={{0,1},{1,0},{2,3},{3,2},{4,5},{5,4},{6,7},{7,6},{8,9},{9,8},{10,11... | collective-permute-start | bytes 2555912 | tf_op jit(solution)/shard_map/ppermute | solution.py:48
  57.0 5.6 %collective-permute-start.13 = (bf16[256,1536]{1,0:T(8,128)(2,1)S(1)}, bf16[256,1536]{1,0:T(8,128)(2,1)S(1)}, u32[]{:S(2)}, u32[]{:S(2)}) collective-permute-start(bf16[256,1536]{1,0:T(8,128)(2,1)S(1)} %get-tuple-element.71), channel_id=1, source_target_pairs={{0,1},{1,0},{2,3},{3,2},{4,5},{5,4},{6,7},{7,6},{8,9},{9,8},{10,11... | collective-permute-start | bytes 2359304 | tf_op jit(solution)/shard_map/ppermute | solution.py:48
  62.1 3.4 %collective-permute-start.24 = (bf16[256,1664]{1,0:T(8,128)(2,1)S(1)}, bf16[256,1664]{1,0:T(8,128)(2,1)S(1)}, u32[]{:S(2)}, u32[]{:S(2)}) collective-permute-start(bf16[256,1664]{1,0:T(8,128)(2,1)S(1)} %constant_dynamic-update-slice_fusion.2.far_ref), channel_id=1, source_target_pairs={{0,1},{1,0},{2,3},{3,2},{4,5},{5,4},{6,7},{7,6},{8,9},{9,8},{10,11... | collective-permute-start | bytes 2555912 | tf_op jit(solution)/shard_map/ppermute | solution.py:48
  62.2 12.8 %collective-permute-start.12 = (bf16[256,1536]{1,0:T(8,128)(2,1)S(1)}, bf16[256,1536]{1,0:T(8,128)(2,1)S(1)}, u32[]{:S(2)}, u32[]{:S(2)}) collective-permute-start(bf16[256,1536]{1,0:T(8,128)(2,1)S(1)} %get-tuple-element.70), channel_id=1, source_target_pairs={{0,1},{1,0},{2,3},{3,2},{4,5},{5,4},{6,7},{7,6},{8,9},{9,8},{10,11... | collective-permute-start | bytes 2359304 | tf_op jit(solution)/shard_map/ppermute | solution.py:48
  62.9 11.2 %collective-permute-start.14 = (bf16[128,1536]{1,0:T(8,128)(2,1)S(1)}, bf16[128,1536]{1,0:T(8,128)(2,1)S(1)}, u32[]{:S(2)}, u32[]{:S(2)}) collective-permute-start(bf16[128,1536]{1,0:T(8,128)(2,1)S(1)} %get-tuple-element.130), channel_id=1, source_target_pairs={{0,2},{1,3},{2,0},{3,1},{4,6},{5,7},{6,4},{7,5},{8,10},{9,11},{10,... | collective-permute-start | bytes 1179656 | tf_op jit(solution)/shard_map/ppermute | solution.py:44
  64.1 5.0 %copy-start.8 = (bf16[1536]{0:T(1024)(128)(2,1)S(1)}, bf16[1536]{0:T(1024)(128)(2,1)}, u32[]{:S(2)}) copy-start(bf16[1536]{0:T(1024)(128)(2,1)} %param.16) | copy-start | bytes 9220
  64.1 10.8 %collective-permute-start.15 = (bf16[128,1536]{1,0:T(8,128)(2,1)S(1)}, bf16[128,1536]{1,0:T(8,128)(2,1)S(1)}, u32[]{:S(2)}, u32[]{:S(2)}) collective-permute-start(bf16[128,1536]{1,0:T(8,128)(2,1)S(1)} %get-tuple-element.129), channel_id=1, source_target_pairs={{0,4},{4,0},{8,12},{12,8},{16,20},{20,16},{24,28},{28,24},{1,5},{5... | collective-permute-start | bytes 1179656 | tf_op jit(solution)/shard_map/ppermute | solution.py:40
  69.1 8.4 %collective-permute-start.27 = (bf16[256,1536]{1,0:T(8,128)(2,1)S(1)}, bf16[256,1536]{1,0:T(8,128)(2,1)S(1)}, u32[]{:S(2)}, u32[]{:S(2)}) collective-permute-start(bf16[256,1536]{1,0:T(8,128)(2,1)S(1)} %get-tuple-element.85), channel_id=1, source_target_pairs={{0,1},{1,0},{2,3},{3,2},{4,5},{5,4},{6,7},{7,6},{8,9},{9,8},{10,11... | collective-permute-start | bytes 2359304 | tf_op jit(solution)/shard_map/ppermute | solution.py:48
  69.2 17.8 %collective-permute-start.31 = (bf16[256,1536]{1,0:T(8,128)(2,1)S(1)}, bf16[256,1536]{1,0:T(8,128)(2,1)S(1)}, u32[]{:S(2)}, u32[]{:S(2)}) collective-permute-start(bf16[256,1536]{1,0:T(8,128)(2,1)S(1)} %get-tuple-element.84), channel_id=1, source_target_pairs={{0,1},{1,0},{2,3},{3,2},{4,5},{5,4},{6,7},{7,6},{8,9},{9,8},{10,11... | collective-permute-start | bytes 2359304 | tf_op jit(solution)/shard_map/ppermute | solution.py:48
  75.1 7.2 %collective-permute-start.25 = (bf16[64,1536]{1,0:T(8,128)(2,1)S(1)}, bf16[64,1536]{1,0:T(8,128)(2,1)S(1)}, u32[]{:S(2)}, u32[]{:S(2)}) collective-permute-start(bf16[64,1536]{1,0:T(8,128)(2,1)S(1)} %get-tuple-element.128), channel_id=1, source_target_pairs={{0,4},{4,0},{8,12},{12,8},{16,20},{20,16},{24,28},{28,24},{1,5},{5... | collective-permute-start | bytes 589832 | tf_op jit(solution)/shard_map/ppermute | solution.py:40
  76.5 7.8 %collective-permute-start.26 = (bf16[64,1536]{1,0:T(8,128)(2,1)S(1)}, bf16[64,1536]{1,0:T(8,128)(2,1)S(1)}, u32[]{:S(2)}, u32[]{:S(2)}) collective-permute-start(bf16[64,1536]{1,0:T(8,128)(2,1)S(1)} %get-tuple-element.127), channel_id=1, source_target_pairs={{0,2},{1,3},{2,0},{3,1},{4,6},{5,7},{6,4},{7,5},{8,10},{9,11},{10,... | collective-permute-start | bytes 589832 | tf_op jit(solution)/shard_map/ppermute | solution.py:44
  77.6 12.7 %collective-permute-start.32 = (bf16[128,1536]{1,0:T(8,128)(2,1)S(1)}, bf16[128,1536]{1,0:T(8,128)(2,1)S(1)}, u32[]{:S(2)}, u32[]{:S(2)}) collective-permute-start(bf16[128,1536]{1,0:T(8,128)(2,1)S(1)} %get-tuple-element.126), channel_id=1, source_target_pairs={{0,2},{1,3},{2,0},{3,1},{4,6},{5,7},{6,4},{7,5},{8,10},{9,11},{10,... | collective-permute-start | bytes 1179656 | tf_op jit(solution)/shard_map/ppermute | solution.py:44
  78.8 11.6 %collective-permute-start.33 = (bf16[128,1536]{1,0:T(8,128)(2,1)S(1)}, bf16[128,1536]{1,0:T(8,128)(2,1)S(1)}, u32[]{:S(2)}, u32[]{:S(2)}) collective-permute-start(bf16[128,1536]{1,0:T(8,128)(2,1)S(1)} %get-tuple-element.125), channel_id=1, source_target_pairs={{0,4},{4,0},{8,12},{12,8},{16,20},{20,16},{24,28},{28,24},{1,5},{5... | collective-permute-start | bytes 1179656 | tf_op jit(solution)/shard_map/ppermute | solution.py:40
  84.6 7.5 %collective-permute-start.30 = (bf16[32,1536]{1,0:T(8,128)(2,1)S(1)}, bf16[32,1536]{1,0:T(8,128)(2,1)S(1)}, u32[]{:S(2)}, u32[]{:S(2)}) collective-permute-start(bf16[32,1536]{1,0:T(8,128)(2,1)S(1)} %pad_maximum_fusion.12), channel_id=1, source_target_pairs={{0,8},{4,12},{8,16},{12,20},{16,24},{20,28},{24,0},{28,4},{1,9},{5... | collective-permute-start | bytes 294920 | tf_op jit(solution)/shard_map/ppermute | solution.py:36
  84.7 7.7 %collective-permute-start.29 = (bf16[32,1536]{1,0:T(8,128)(2,1)S(1)}, bf16[32,1536]{1,0:T(8,128)(2,1)S(1)}, u32[]{:S(2)}, u32[]{:S(2)}) collective-permute-start(bf16[32,1536]{1,0:T(8,128)(2,1)S(1)} %pad_maximum_fusion.11), channel_id=1, source_target_pairs={{0,16},{4,20},{8,24},{12,28},{16,0},{20,4},{24,8},{28,12},{1,17},{... | collective-permute-start | bytes 294920 | tf_op jit(solution)/shard_map/ppermute | solution.py:36
  86.9 5.4 %collective-permute-start.28 = (bf16[32,1536]{1,0:T(8,128)(2,1)S(1)}, bf16[32,1536]{1,0:T(8,128)(2,1)S(1)}, u32[]{:S(2)}, u32[]{:S(2)}) collective-permute-start(bf16[32,1536]{1,0:T(8,128)(2,1)S(1)} %pad_maximum_fusion.10), channel_id=1, source_target_pairs={{0,24},{4,28},{8,0},{12,4},{16,8},{20,12},{24,16},{28,20},{1,25},{... | collective-permute-start | bytes 294920 | tf_op jit(solution)/shard_map/ppermute | solution.py:36
  90.5 5.7 %collective-permute-start.37 = (bf16[64,1536]{1,0:T(8,128)(2,1)S(1)}, bf16[64,1536]{1,0:T(8,128)(2,1)S(1)}, u32[]{:S(2)}, u32[]{:S(2)}) collective-permute-start(bf16[64,1536]{1,0:T(8,128)(2,1)S(1)} %get-tuple-element.124), channel_id=1, source_target_pairs={{0,4},{4,0},{8,12},{12,8},{16,20},{20,16},{24,28},{28,24},{1,5},{5... | collective-permute-start | bytes 589832 | tf_op jit(solution)/shard_map/ppermute | solution.py:40
  91.3 5.7 %collective-permute-start.38 = (bf16[64,1536]{1,0:T(8,128)(2,1)S(1)}, bf16[64,1536]{1,0:T(8,128)(2,1)S(1)}, u32[]{:S(2)}, u32[]{:S(2)}) collective-permute-start(bf16[64,1536]{1,0:T(8,128)(2,1)S(1)} %get-tuple-element.123), channel_id=1, source_target_pairs={{0,2},{1,3},{2,0},{3,1},{4,6},{5,7},{6,4},{7,5},{8,10},{9,11},{10,... | collective-permute-start | bytes 589832 | tf_op jit(solution)/shard_map/ppermute | solution.py:44
  97.1 6.6 %collective-permute-start.41 = (bf16[32,1536]{1,0:T(8,128)(2,1)S(1)}, bf16[32,1536]{1,0:T(8,128)(2,1)S(1)}, u32[]{:S(2)}, u32[]{:S(2)}) collective-permute-start(bf16[32,1536]{1,0:T(8,128)(2,1)S(1)} %pad_maximum_fusion.15), channel_id=1, source_target_pairs={{0,8},{4,12},{8,16},{12,20},{16,24},{20,28},{24,0},{28,4},{1,9},{5... | collective-permute-start | bytes 294920 | tf_op jit(solution)/shard_map/ppermute | solution.py:36
  97.1 7.7 %collective-permute-start.40 = (bf16[32,1536]{1,0:T(8,128)(2,1)S(1)}, bf16[32,1536]{1,0:T(8,128)(2,1)S(1)}, u32[]{:S(2)}, u32[]{:S(2)}) collective-permute-start(bf16[32,1536]{1,0:T(8,128)(2,1)S(1)} %pad_maximum_fusion.14), channel_id=1, source_target_pairs={{0,16},{4,20},{8,24},{12,28},{16,0},{20,4},{24,8},{28,12},{1,17},{... | collective-permute-start | bytes 294920 | tf_op jit(solution)/shard_map/ppermute | solution.py:36
  99.4 5.4 %collective-permute-start.39 = (bf16[32,1536]{1,0:T(8,128)(2,1)S(1)}, bf16[32,1536]{1,0:T(8,128)(2,1)S(1)}, u32[]{:S(2)}, u32[]{:S(2)}) collective-permute-start(bf16[32,1536]{1,0:T(8,128)(2,1)S(1)} %pad_maximum_fusion.13), channel_id=1, source_target_pairs={{0,24},{4,28},{8,0},{12,4},{16,8},{20,12},{24,16},{28,20},{1,25},{... | collective-permute-start | bytes 294920 | tf_op jit(solution)/shard_map/ppermute | solution.py:36
  101.2 10.4 %collective-permute-start.34 = (bf16[32,1536]{1,0:T(8,128)(2,1)S(1)}, bf16[32,1536]{1,0:T(8,128)(2,1)S(1)}, u32[]{:S(2)}, u32[]{:S(2)}) collective-permute-start(bf16[32,1536]{1,0:T(8,128)(2,1)S(1)} %multiply_convert_fusion.1.refs_0_), channel_id=1, source_target_pairs={{0,1},{1,0},{2,3},{3,2},{4,5},{5,4},{6,7},{7,6},{8,9},{9,8},{10,11... | collective-permute-start | bytes 294920 | tf_op jit(solution)/shard_map/ppermute | solution.py:48
  101.3 10.3 %collective-permute-start.35 = (bf16[32,1536]{1,0:T(8,128)(2,1)S(1)}, bf16[32,1536]{1,0:T(8,128)(2,1)S(1)}, u32[]{:S(2)}, u32[]{:S(2)}) collective-permute-start(bf16[32,1536]{1,0:T(8,128)(2,1)S(1)} %multiply_convert_fusion.1.refs_0_), channel_id=1, source_target_pairs={{0,2},{1,3},{2,0},{3,1},{4,6},{5,7},{6,4},{7,5},{8,10},{9,11},{10,... | collective-permute-start | bytes 294920 | tf_op jit(solution)/shard_map/ppermute | solution.py:44
  103.7 7.9 %collective-permute-start.36 = (bf16[32,1536]{1,0:T(8,128)(2,1)S(1)}, bf16[32,1536]{1,0:T(8,128)(2,1)S(1)}, u32[]{:S(2)}, u32[]{:S(2)}) collective-permute-start(bf16[32,1536]{1,0:T(8,128)(2,1)S(1)} %multiply_convert_fusion.1.refs_0_), channel_id=1, source_target_pairs={{0,3},{1,2},{2,1},{3,0},{4,7},{5,6},{6,5},{7,4},{8,11},{9,10},{10,... | collective-permute-start | bytes 294920 | tf_op jit(solution)/shard_map/ppermute | solution.py:349

commit v6 on v5

--- a/solution.py
+++ b/solution.py
@@ -54,14 +54,8 @@
 
 
 def attend_kernel(place_ref, first_ref, context_ref, w_ref, send_ref, keep_ref):
-    place = place_ref[0]
     quarter = send_ref.shape[1]
-    rows = []
-    for lower in (1, 0):
-        for upper in (0, 1):
-            start = pl.multiple_of((place ^ (upper * 2 + lower)) * quarter, quarter)
-            rows.append(context_ref[pl.ds(start, quarter), :])
-    rows = jnp.concatenate(rows, axis=0)
+    rows = context_ref[...]
     width = w_ref.shape[1]
     tile = 512 if width % 512 == 0 else width
     for left in range(0, width, tile):
@@ -396,6 +390,11 @@
     first = (lax.axis_index("ep") * held).astype(jnp.int32).reshape(1)
     down = w_down.reshape(held * units, width)
 
+    index = lax.axis_index("tp")
+    blocks = context.reshape(2, 2, quarter, context.shape[1])
+    blocks = jnp.where(index // 2 == 1, blocks[::-1], blocks)
+    blocks = jnp.where(index % 2 == 0, blocks[:, ::-1], blocks)
+    context = jnp.swapaxes(blocks, 0, 1).reshape(context.shape)
     send, keep = attend(place, first, context, w_out)
     got = flip_lower(send)
     parts = []
@@ -430,7 +429,7 @@
     one.gather_far()
     two.gather_near()
     one.gathered_far()
-    one.gather_lower(one.pieces[1])
+    one.gather_lower()
     two.gather_far()
     one.away = serve(one.others)
     one.back_lower()
@@ -441,7 +440,6 @@
     two.away = serve(two.others, one.far)
     two.back_lower()
     two.own = serve(two.pieces, two.away)
-    one.far_first, one.far_second = after((one.far_first, one.far_second), two.own)
     one.back_near()
     two.back_far()
     one.near_first, one.near_second = after((one.near_first, one.near_second), two.far)

time: 113 us -> 111 us (0.982)
  local copies, waits for them, and re-layouts: 6.84 us -> 4.9 us
    unnamed x26, local copies, waits for them, and re-layouts: 6.69 us -> 3.69 us
    ppermute x12, waiting for transfers between devices: 7.57 us -> 6.38 us  [turn(): lax.ppermute(value, 'ep', [(i, (i + 2 * step) % count) for i in range(cou...]
  transfers between devices with their start and end apart: 42 -> 42, of which waited for: 23 -> 21; matrix products, arithmetic and copies ran while one was open for 3% -> 3% of each run, Pallas kernels for 15% -> 15%
where the time goes in v6:
time: 111 us
  starting transfers between devices  43.5 us (39%)
  waiting for transfers between devices  35.4 us (32%)
  Pallas kernels  17.8 us (16%)
  blocking collectives  6.41 us (6%)
  local copies, waits for them, and re-layouts  4.9 us (4%)
  other arithmetic  2.68 us (2%)
    ppermute x12, starting transfers between devices, turn(): lax.ppermute(value, 'ep', [(i, (i + 2 * step) % count) for i in range(cou...  19.4 us
    ppermute x8, waiting for transfers between devices, flip_inner(): lax.ppermute(value, 'ep', [(i, i ^ 1) for i in range(lax.axis_size('ep'))])  17.7 us
    pallas_call x4, Pallas kernels, expert_rows(): pl.pallas_call(expert_kernel, out_shape=[jax.ShapeDtypeStruct((p.shape[0]...  14.2 us
    ppermute x11, starting transfers between devices, flip_upper(): lax.ppermute(value, 'tp', [(i, i ^ 2) for i in range(lax.axis_size('tp'))])  14 us
    ppermute x11, waiting for transfers between devices, flip_upper(): lax.ppermute(value, 'tp', [(i, i ^ 2) for i in range(lax.axis_size('tp'))])  10.3 us
    ppermute x8, starting transfers between devices, flip_inner(): lax.ppermute(value, 'ep', [(i, i ^ 1) for i in range(lax.axis_size('ep'))])  7.76 us
    all_gather x1, blocking collectives, local(): return join(place, ready_one, lax.all_gather(result_two, 'tp'))  6.41 us
    ppermute x12, waiting for transfers between devices, turn(): lax.ppermute(value, 'ep', [(i, (i + 2 * step) % count) for i in range(cou...  6.38 us
  transfers between devices with their start and end apart: 42, of which 21 were waited for; matrix products, arithmetic and copies ran while one was open for 3% of the time, Pallas kernels for 15%

profile of v6, /device:TPU:0, one launch (start us, length us, event | category | flops | bytes accessed | tf_op | source)
XLA Modules:
  0.0 111.2 jit_solution(18384547149640281250)
XLA Ops:
  0.0 1.0 copy.19
  1.4 0.6 attend.1
  1.9 0.5 collective-permute-start
  2.8 1.0 collective-permute-done.lower_ref
  3.8 3.0 %collective-permute-start.1 = (bf16[32,1536]{1,0:T(8,128)(2,1)S(1)}, bf16[32,1536]{1,0:T(8,128)(2,1)S(1)}, u32[]{:S(2)}, u32[]{:S(2)}) collective-permute-start(bf16[32,1536]{1,0:T(8,128)(2,1)S(1)} %get-tuple-element.124), channel_id=1, source_target_pairs={{0,2},{1,3},{2,0},{3,1},{4,6},{5,7},{6,4},{7,5},{8,10},{9,11},{10,... | collective-permute-start | bytes 294920 | tf_op jit(solution)/shard_map/ppermute | solution.py:44
  7.4 2.9 %collective-permute-done.1.upper_ref = bf16[32,1536]{1,0:T(8,128)(2,1)S(1)} collective-permute-done((bf16[32,1536]{1,0:T(8,128)(2,1)S(1)}, bf16[32,1536]{1,0:T(8,128)(2,1)S(1)}, u32[]{:S(2)}, u32[]{:S(2)}) %collective-permute-start.1) | collective-permute-done | bytes 98336 | tf_op jit(solution)/shard_map/ppermute | solution.py:44
  10.4 0.5 norm_rows.2
  10.9 2.1 %collective-permute-start.2 = (bf16[32,1664]{1,0:T(8,128)(2,1)S(1)}, bf16[32,1664]{1,0:T(8,128)(2,1)S(1)}, u32[]{:S(2)}, u32[]{:S(2)}) collective-permute-start(bf16[32,1664]{1,0:T(8,128)(2,1)S(1)} %get-tuple-element.53), channel_id=1, source_target_pairs={{0,8},{4,12},{8,16},{12,20},{16,24},{20,28},{24,0},{28,4},{1,9},{5... | collective-permute-start | bytes 319496 | tf_op jit(solution)/shard_map/ppermute | solution.py:36
  13.0 2.6 %collective-permute-start.3 = (bf16[32,1664]{1,0:T(8,128)(2,1)S(1)}, bf16[32,1664]{1,0:T(8,128)(2,1)S(1)}, u32[]{:S(2)}, u32[]{:S(2)}) collective-permute-start(bf16[32,1664]{1,0:T(8,128)(2,1)S(1)} %get-tuple-element.53), channel_id=1, source_target_pairs={{0,16},{4,20},{8,24},{12,28},{16,0},{20,4},{24,8},{28,12},{1,17},{... | collective-permute-start | bytes 319496 | tf_op jit(solution)/shard_map/ppermute | solution.py:36
  15.6 1.3 %collective-permute-start.4 = (bf16[32,1664]{1,0:T(8,128)(2,1)S(1)}, bf16[32,1664]{1,0:T(8,128)(2,1)S(1)}, u32[]{:S(2)}, u32[]{:S(2)}) collective-permute-start(bf16[32,1664]{1,0:T(8,128)(2,1)S(1)} %get-tuple-element.53), channel_id=1, source_target_pairs={{0,24},{4,28},{8,0},{12,4},{16,8},{20,12},{24,16},{28,20},{1,25},{... | collective-permute-start | bytes 319496 | tf_op jit(solution)/shard_map/ppermute | solution.py:36
  17.0 1.5 %copy-done.2 = bf16[5,1536,128]{2,1,0:T(8,128)(2,1)S(1)} copy-done((bf16[5,1536,128]{2,1,0:T(8,128)(2,1)S(1)}, bf16[5,1536,128]{2,1,0:T(8,128)(2,1)}, u32[]{:S(2)}) %copy-start.2) | copy-done | bytes 1966104
  18.5 1.5 %copy-done.3 = bf16[5,128,1536]{2,1,0:T(8,128)(2,1)S(1)} copy-done((bf16[5,128,1536]{2,1,0:T(8,128)(2,1)S(1)}, bf16[5,128,1536]{2,1,0:T(8,128)(2,1)}, u32[]{:S(2)}) %copy-start.3) | copy-done | bytes 1966104
  20.1 1.0 load_weights.1
  21.1 0.5 collective-permute-done.3
  21.7 1.7 %collective-permute-start.6 = (bf16[64,1664]{1,0:T(8,128)(2,1)S(1)}, bf16[64,1664]{1,0:T(8,128)(2,1)S(1)}, u32[]{:S(2)}, u32[]{:S(2)}) collective-permute-start(bf16[64,1664]{1,0:T(8,128)(2,1)S(1)} %get-tuple-element.56), channel_id=1, source_target_pairs={{0,4},{4,0},{8,12},{12,8},{16,20},{20,16},{24,28},{28,24},{1,5},{5... | collective-permute-start | bytes 638984 | tf_op jit(solution)/shard_map/ppermute | solution.py:40
  23.5 1.5 %collective-permute-start.7 = (bf16[64,1664]{1,0:T(8,128)(2,1)S(1)}, bf16[64,1664]{1,0:T(8,128)(2,1)S(1)}, u32[]{:S(2)}, u32[]{:S(2)}) collective-permute-start(bf16[64,1664]{1,0:T(8,128)(2,1)S(1)} %get-tuple-element.57), channel_id=1, source_target_pairs={{0,2},{1,3},{2,0},{3,1},{4,6},{5,7},{6,4},{7,5},{8,10},{9,11},{10,... | collective-permute-start | bytes 638984 | tf_op jit(solution)/shard_map/ppermute | solution.py:44
  25.0 0.5 norm_rows.3
  25.5 2.9 %collective-permute-done.6 = bf16[64,1664]{1,0:T(8,128)(2,1)S(1)} collective-permute-done((bf16[64,1664]{1,0:T(8,128)(2,1)S(1)}, bf16[64,1664]{1,0:T(8,128)(2,1)S(1)}, u32[]{:S(2)}, u32[]{:S(2)}) %collective-permute-start.6) | collective-permute-done | bytes 213024 | tf_op jit(solution)/shard_map/ppermute | solution.py:40
  28.4 1.0 collective-permute-done.7
  29.4 2.9 %collective-permute-start.18 = (bf16[32,1664]{1,0:T(8,128)(2,1)S(1)}, bf16[32,1664]{1,0:T(8,128)(2,1)S(1)}, u32[]{:S(2)}, u32[]{:S(2)}) collective-permute-start(bf16[32,1664]{1,0:T(8,128)(2,1)S(1)} %get-tuple-element.71), channel_id=1, source_target_pairs={{0,8},{4,12},{8,16},{12,20},{16,24},{20,28},{24,0},{28,4},{1,9},{5... | collective-permute-start | bytes 319496 | tf_op jit(solution)/shard_map/ppermute | solution.py:36
  32.3 1.0 collective-permute-start.19
  33.4 1.4 %collective-permute-start.20 = (bf16[32,1664]{1,0:T(8,128)(2,1)S(1)}, bf16[32,1664]{1,0:T(8,128)(2,1)S(1)}, u32[]{:S(2)}, u32[]{:S(2)}) collective-permute-start(bf16[32,1664]{1,0:T(8,128)(2,1)S(1)} %get-tuple-element.71), channel_id=1, source_target_pairs={{0,24},{4,28},{8,0},{12,4},{16,8},{20,12},{24,16},{28,20},{1,25},{... | collective-permute-start | bytes 319496 | tf_op jit(solution)/shard_map/ppermute | solution.py:36
  34.8 1.5 %collective-permute-start.9 = (bf16[128,1664]{1,0:T(8,128)(2,1)S(1)}, bf16[128,1664]{1,0:T(8,128)(2,1)S(1)}, u32[]{:S(2)}, u32[]{:S(2)}) collective-permute-start(bf16[128,1664]{1,0:T(8,128)(2,1)S(1)} %pad_maximum_fusion.2), channel_id=1, source_target_pairs={{0,2},{1,3},{2,0},{3,1},{4,6},{5,7},{6,4},{7,5},{8,10},{9,11},{10,... | collective-permute-start | bytes 1277960 | tf_op jit(solution)/shard_map/ppermute | solution.py:44
  36.4 0.6 collective-permute-start.10
  37.0 3.3 %collective-permute-done.19 = bf16[32,1664]{1,0:T(8,128)(2,1)S(1)} collective-permute-done((bf16[32,1664]{1,0:T(8,128)(2,1)S(1)}, bf16[32,1664]{1,0:T(8,128)(2,1)S(1)}, u32[]{:S(2)}, u32[]{:S(2)}) %collective-permute-start.19) | collective-permute-done | bytes 106528 | tf_op jit(solution)/shard_map/ppermute | solution.py:36
  40.4 1.5 %collective-permute-start.22 = (bf16[64,1664]{1,0:T(8,128)(2,1)S(1)}, bf16[64,1664]{1,0:T(8,128)(2,1)S(1)}, u32[]{:S(2)}, u32[]{:S(2)}) collective-permute-start(bf16[64,1664]{1,0:T(8,128)(2,1)S(1)} %pad_maximum_fusion.9), channel_id=1, source_target_pairs={{0,2},{1,3},{2,0},{3,1},{4,6},{5,7},{6,4},{7,5},{8,10},{9,11},{10,... | collective-permute-start | bytes 638984 | tf_op jit(solution)/shard_map/ppermute | solution.py:44
  42.0 0.6 collective-permute-start.21
  42.6 5.4 %collective-permute-done.10 = bf16[128,1664]{1,0:T(8,128)(2,1)S(1)} collective-permute-done((bf16[128,1664]{1,0:T(8,128)(2,1)S(1)}, bf16[128,1664]{1,0:T(8,128)(2,1)S(1)}, u32[]{:S(2)}, u32[]{:S(2)}) %collective-permute-start.10) | collective-permute-done | bytes 426016 | tf_op jit(solution)/shard_map/ppermute | solution.py:40
  48.1 0.8 collective-permute-done.22
  48.9 1.3 %collective-permute-done.21 = bf16[64,1664]{1,0:T(8,128)(2,1)S(1)} collective-permute-done((bf16[64,1664]{1,0:T(8,128)(2,1)S(1)}, bf16[64,1664]{1,0:T(8,128)(2,1)S(1)}, u32[]{:S(2)}, u32[]{:S(2)}) %collective-permute-start.21) | collective-permute-done | bytes 213024 | tf_op jit(solution)/shard_map/ppermute | solution.py:40
  50.3 0.6 collective-permute-start.25
  50.9 1.1 collective-permute-start.24
  52.2 3.5 %expert_rows.4 = (bf16[256,1536]{1,0:T(8,128)(2,1)S(1)}, bf16[256,1536]{1,0:T(8,128)(2,1)S(1)}) custom-call(s32[1]{0:T(128)} %bitcast.1.first_ref, bf16[256,1664]{1,0:T(8,128)(2,1)S(1)} %collective-permute-done.8.near_ref, bf16[256,1664]{1,0:T(8,128)(2,1)S(1)} %collective-permute-done.11.far_ref, bf16[5,1536,256]{2,1,0:T(8,128)(2,1)S(1)} %get-tuple-element.62.both_ref, ...), custom_call_target="tpu_custom_call" | custom-call | flops 3019898880 | bytes 9043968 | tf_op jit(solution)/shard_map/expert_rows/pallas_call | solution.py:239
  55.7 0.5 collective-permute-start.13
  56.3 3.5 %expert_rows.5 = (bf16[256,1536]{1,0:T(8,128)(2,1)S(1)}, bf16[256,1536]{1,0:T(8,128)(2,1)S(1)}) custom-call(s32[1]{0:T(128)} %bitcast.1.first_ref, bf16[256,1664]{1,0:T(8,128)(2,1)S(1)} %pad_maximum_fusion.near_ref, bf16[256,1664]{1,0:T(8,128)(2,1)S(1)} %constant_dynamic-update-slice_fusion.far_ref, bf16[5,1536,256]{2,1,0:T(8,128)(2,1)S(1)} %get-tuple-element.62.both_ref, ...), custom_call_target="tpu_custom_call" | custom-call | flops 3019898880 | bytes 9043968 | tf_op jit(solution)/shard_map/expert_rows/pallas_call | solution.py:239
  59.8 0.7 collective-permute-done.25
  61.0 0.5 collective-permute-start.12
  61.7 1.1 collective-permute-start.14
  62.8 1.0 collective-permute-start.16
  63.9 3.5 %expert_rows.6 = (bf16[256,1536]{1,0:T(8,128)(2,1)S(1)}, bf16[256,1536]{1,0:T(8,128)(2,1)S(1)}) custom-call(s32[1]{0:T(128)} %bitcast.1.first_ref, bf16[256,1664]{1,0:T(8,128)(2,1)S(1)} %collective-permute-done.23.near_ref, bf16[256,1664]{1,0:T(8,128)(2,1)S(1)} %collective-permute-done.26.far_ref, bf16[5,1536,256]{2,1,0:T(8,128)(2,1)S(1)} %get-tuple-element.62.both_ref, ...), custom_call_target="tpu_custom_call" | custom-call | flops 3019898880 | bytes 9043968 | tf_op jit(solution)/shard_map/expert_rows/pallas_call | solution.py:239
  67.5 0.5 collective-permute-start.31
  68.0 3.7 %expert_rows.7 = (bf16[256,1536]{1,0:T(8,128)(2,1)S(1)}, bf16[256,1536]{1,0:T(8,128)(2,1)S(1)}) custom-call(s32[1]{0:T(128)} %bitcast.1.first_ref, bf16[256,1664]{1,0:T(8,128)(2,1)S(1)} %pad_maximum_fusion.1.near_ref, bf16[256,1664]{1,0:T(8,128)(2,1)S(1)} %constant_dynamic-update-slice_fusion.2.far_ref, ...), custom_call_target="tpu_custom_call" | custom-call | flops 3019898880 | bytes 9043968 | tf_op jit(solution)/shard_map/expert_rows/pallas_call | solution.py:239
  71.7 1.2 %collective-permute-done.14 = bf16[128,1536]{1,0:T(8,128)(2,1)S(1)} collective-permute-done((bf16[128,1536]{1,0:T(8,128)(2,1)S(1)}, bf16[128,1536]{1,0:T(8,128)(2,1)S(1)}, u32[]{:S(2)}, u32[]{:S(2)}) %collective-permute-start.14) | collective-permute-done | bytes 393248 | tf_op jit(solution)/shard_map/ppermute | solution.py:44
  72.9 0.8 collective-permute-done.16
  73.8 1.1 %collective-permute-start.15 = (bf16[64,1536]{1,0:T(8,128)(2,1)S(1)}, bf16[64,1536]{1,0:T(8,128)(2,1)S(1)}, u32[]{:S(2)}, u32[]{:S(2)}) collective-permute-start(bf16[64,1536]{1,0:T(8,128)(2,1)S(1)} %get-tuple-element.120), channel_id=1, source_target_pairs={{0,4},{4,0},{8,12},{12,8},{16,20},{20,16},{24,28},{28,24},{1,5},{5... | collective-permute-start | bytes 589832 | tf_op jit(solution)/shard_map/ppermute | solution.py:40
  74.9 1.4 %collective-permute-start.17 = (bf16[64,1536]{1,0:T(8,128)(2,1)S(1)}, bf16[64,1536]{1,0:T(8,128)(2,1)S(1)}, u32[]{:S(2)}, u32[]{:S(2)}) collective-permute-start(bf16[64,1536]{1,0:T(8,128)(2,1)S(1)} %get-tuple-element.119), channel_id=1, source_target_pairs={{0,2},{1,3},{2,0},{3,1},{4,6},{5,7},{6,4},{7,5},{8,10},{9,11},{10,... | collective-permute-start | bytes 589832 | tf_op jit(solution)/shard_map/ppermute | solution.py:44
  76.5 0.7 collective-permute-start.32
  77.2 1.0 collective-permute-start.33
  78.2 3.2 %collective-permute-done.15 = bf16[64,1536]{1,0:T(8,128)(2,1)S(1)} collective-permute-done((bf16[64,1536]{1,0:T(8,128)(2,1)S(1)}, bf16[64,1536]{1,0:T(8,128)(2,1)S(1)}, u32[]{:S(2)}, u32[]{:S(2)}) %collective-permute-start.15) | collective-permute-done | bytes 196640 | tf_op jit(solution)/shard_map/ppermute | solution.py:40
  81.4 1.4 %collective-permute-done.17 = bf16[64,1536]{1,0:T(8,128)(2,1)S(1)} collective-permute-done((bf16[64,1536]{1,0:T(8,128)(2,1)S(1)}, bf16[64,1536]{1,0:T(8,128)(2,1)S(1)}, u32[]{:S(2)}, u32[]{:S(2)}) %collective-permute-start.17) | collective-permute-done | bytes 196640 | tf_op jit(solution)/shard_map/ppermute | solution.py:44
  83.0 2.3 %collective-permute-start.29 = (bf16[32,1536]{1,0:T(8,128)(2,1)S(1)}, bf16[32,1536]{1,0:T(8,128)(2,1)S(1)}, u32[]{:S(2)}, u32[]{:S(2)}) collective-permute-start(bf16[32,1536]{1,0:T(8,128)(2,1)S(1)} %pad_maximum_fusion.11), channel_id=1, source_target_pairs={{0,16},{4,20},{8,24},{12,28},{16,0},{20,4},{24,8},{28,12},{1,17},{... | collective-permute-start | bytes 294920 | tf_op jit(solution)/shard_map/ppermute | solution.py:36
  85.3 1.7 %collective-permute-start.28 = (bf16[32,1536]{1,0:T(8,128)(2,1)S(1)}, bf16[32,1536]{1,0:T(8,128)(2,1)S(1)}, u32[]{:S(2)}, u32[]{:S(2)}) collective-permute-start(bf16[32,1536]{1,0:T(8,128)(2,1)S(1)} %pad_maximum_fusion.10), channel_id=1, source_target_pairs={{0,24},{4,28},{8,0},{12,4},{16,8},{20,12},{24,16},{28,20},{1,25},{... | collective-permute-start | bytes 294920 | tf_op jit(solution)/shard_map/ppermute | solution.py:36
  87.0 1.8 %collective-permute-done.32 = bf16[128,1536]{1,0:T(8,128)(2,1)S(1)} collective-permute-done((bf16[128,1536]{1,0:T(8,128)(2,1)S(1)}, bf16[128,1536]{1,0:T(8,128)(2,1)S(1)}, u32[]{:S(2)}, u32[]{:S(2)}) %collective-permute-start.32) | collective-permute-done | bytes 393248 | tf_op jit(solution)/shard_map/ppermute | solution.py:44
  88.9 1.0 collective-permute-start.37
  90.0 1.0 collective-permute-start.38
  91.1 3.5 %collective-permute-done.37 = bf16[64,1536]{1,0:T(8,128)(2,1)S(1)} collective-permute-done((bf16[64,1536]{1,0:T(8,128)(2,1)S(1)}, bf16[64,1536]{1,0:T(8,128)(2,1)S(1)}, u32[]{:S(2)}, u32[]{:S(2)}) %collective-permute-start.37) | collective-permute-done | bytes 196640 | tf_op jit(solution)/shard_map/ppermute | solution.py:40
  94.7 0.9 collective-permute-done.38
  95.8 2.3 %collective-permute-start.40 = (bf16[32,1536]{1,0:T(8,128)(2,1)S(1)}, bf16[32,1536]{1,0:T(8,128)(2,1)S(1)}, u32[]{:S(2)}, u32[]{:S(2)}) collective-permute-start(bf16[32,1536]{1,0:T(8,128)(2,1)S(1)} %pad_maximum_fusion.14), channel_id=1, source_target_pairs={{0,16},{4,20},{8,24},{12,28},{16,0},{20,4},{24,8},{28,12},{1,17},{... | collective-permute-start | bytes 294920 | tf_op jit(solution)/shard_map/ppermute | solution.py:36
  98.1 1.7 %collective-permute-start.39 = (bf16[32,1536]{1,0:T(8,128)(2,1)S(1)}, bf16[32,1536]{1,0:T(8,128)(2,1)S(1)}, u32[]{:S(2)}, u32[]{:S(2)}) collective-permute-start(bf16[32,1536]{1,0:T(8,128)(2,1)S(1)} %pad_maximum_fusion.13), channel_id=1, source_target_pairs={{0,24},{4,28},{8,0},{12,4},{16,8},{20,12},{24,16},{28,20},{1,25},{... | collective-permute-start | bytes 294920 | tf_op jit(solution)/shard_map/ppermute | solution.py:36
  99.9 1.1 collective-permute-start.35
  101.0 1.4 %collective-permute-done.41 = bf16[32,1536]{1,0:T(8,128)(2,1)S(1)} collective-permute-done((bf16[32,1536]{1,0:T(8,128)(2,1)S(1)}, bf16[32,1536]{1,0:T(8,128)(2,1)S(1)}, u32[]{:S(2)}, u32[]{:S(2)}) %collective-permute-start.41) | collective-permute-done | bytes 98336 | tf_op jit(solution)/shard_map/ppermute | solution.py:36
  102.4 1.1 %collective-permute-done.40 = bf16[32,1536]{1,0:T(8,128)(2,1)S(1)} collective-permute-done((bf16[32,1536]{1,0:T(8,128)(2,1)S(1)}, bf16[32,1536]{1,0:T(8,128)(2,1)S(1)}, u32[]{:S(2)}, u32[]{:S(2)}) %collective-permute-start.40) | collective-permute-done | bytes 98336 | tf_op jit(solution)/shard_map/ppermute | solution.py:36
  103.8 6.4 %all-gather = bf16[128,1536]{1,0:T(8,128)(2,1)S(1)} all-gather(bf16[32,1536]{1,0:T(8,128)(2,1)S(1)} %multiply_convert_fusion), channel_id=2, replica_groups=mesh['ep'=8,'tp'=4] {'tp'}, dimensions={0}, use_global_device_ids=true | all-gather | bytes 491520 | tf_op jit(solution)/shard_map/all_gather | solution.py:452
  110.2 0.9 join.1
  (105 shorter events, 4.5 us)
Async XLA Ops:
  0.0 1.4 %copy-start.4 = (bf16[384,1536]{1,0:T(8,128)(2,1)S(1)}, bf16[384,1536]{1,0:T(8,128)(2,1)}, u32[]{:S(2)}) copy-start(bf16[384,1536]{1,0:T(8,128)(2,1)} %w_ref.1) | copy-start | bytes 3538948
  0.0 2.4 %copy-start.5 = (bf16[1536,40]{0,1:T(8,128)(2,1)S(1)}, bf16[1536,40]{0,1:T(8,128)(2,1)}, u32[]{:S(2)}) copy-start(bf16[1536,40]{0,1:T(8,128)(2,1)} %param.17) | copy-start | bytes 368644
  0.0 2.7 %copy-start.6 = (s32[256,8]{0,1:T(8,128)S(1)}, s32[256,8]{0,1:T(8,128)}, u32[]{:S(2)}) copy-start(s32[256,8]{0,1:T(8,128)} %param.18) | copy-start | bytes 24580
  0.0 2.8 %copy-start.9 = (bf16[1536]{0:T(1024)(128)(2,1)S(1)}, bf16[1536]{0:T(1024)(128)(2,1)}, u32[]{:S(2)}) copy-start(bf16[1536]{0:T(1024)(128)(2,1)} %param.15) | copy-start | bytes 9220
  1.1 5.8 %copy-start.7 = (s32[40]{0:T(128)S(1)}, s32[40]{0:T(128)}, u32[]{:S(2)}) copy-start(s32[40]{0:T(128)} %param.19) | copy-start | bytes 484
  1.1 5.9 %copy-start.10 = (s32[1,40]{1,0:T(1,128)S(1)}, s32[1,40]{1,0:T(1,128)}, u32[]{:S(2)}) copy-start(s32[1,40]{1,0:T(1,128)} %param.20) | copy-start | bytes 484
  1.1 9.2 %copy-start = (bf16[256,1536]{1,0:T(8,128)(2,1)S(1)}, bf16[256,1536]{1,0:T(8,128)(2,1)}, u32[]{:S(2)}) copy-start(bf16[256,1536]{1,0:T(8,128)(2,1)} %resid_ref.3) | copy-start | bytes 2359300
  1.9 1.9 %collective-permute-start = (bf16[2,64,1536]{2,1,0:T(8,128)(2,1)S(1)}, bf16[2,64,1536]{2,1,0:T(8,128)(2,1)S(1)}, u32[]{:S(2)}, u32[]{:S(2)}) collective-permute-start(bf16[2,64,1536]{2,1,0:T(8,128)(2,1)S(1)} %get-tuple-element.50), channel_id=1, source_target_pairs={{0,1},{1,0},{2,3},{3,2},{4,5},{5,4},{6,7},{7,6},{8,9},{9,8},{10,11... | collective-permute-start | bytes 1179656 | tf_op jit(solution)/shard_map/ppermute | solution.py:48
  3.8 13.2 %copy-start.1 = (bf16[5,1536,128]{2,1,0:T(8,128)(2,1)S(1)}, bf16[5,1536,128]{2,1,0:T(8,128)(2,1)}, u32[]{:S(2)}) copy-start(bf16[5,1536,128]{2,1,0:T(8,128)(2,1)} %gate_hbm.1) | copy-start | bytes 5898244
  3.8 6.5 %collective-permute-start.1 = (bf16[32,1536]{1,0:T(8,128)(2,1)S(1)}, bf16[32,1536]{1,0:T(8,128)(2,1)S(1)}, u32[]{:S(2)}, u32[]{:S(2)}) collective-permute-start(bf16[32,1536]{1,0:T(8,128)(2,1)S(1)} %get-tuple-element.124), channel_id=1, source_target_pairs={{0,2},{1,3},{2,0},{3,1},{4,6},{5,7},{6,4},{7,5},{8,10},{9,11},{10,... | collective-permute-start | bytes 294920 | tf_op jit(solution)/shard_map/ppermute | solution.py:44
  6.8 10.2 %collective-permute-start.5 = (bf16[32,1536]{1,0:T(8,128)(2,1)S(1)}, bf16[32,1536]{1,0:T(8,128)(2,1)S(1)}, u32[]{:S(2)}, u32[]{:S(2)}) collective-permute-start(bf16[32,1536]{1,0:T(8,128)(2,1)S(1)} %get-tuple-element.123), channel_id=1, source_target_pairs={{0,2},{1,3},{2,0},{3,1},{4,6},{5,7},{6,4},{7,5},{8,10},{9,11},{10,... | collective-permute-start | bytes 294920 | tf_op jit(solution)/shard_map/ppermute | solution.py:44
  10.9 10.2 %collective-permute-start.2 = (bf16[32,1664]{1,0:T(8,128)(2,1)S(1)}, bf16[32,1664]{1,0:T(8,128)(2,1)S(1)}, u32[]{:S(2)}, u32[]{:S(2)}) collective-permute-start(bf16[32,1664]{1,0:T(8,128)(2,1)S(1)} %get-tuple-element.53), channel_id=1, source_target_pairs={{0,8},{4,12},{8,16},{12,20},{16,24},{20,28},{24,0},{28,4},{1,9},{5... | collective-permute-start | bytes 319496 | tf_op jit(solution)/shard_map/ppermute | solution.py:36
  13.0 8.6 %collective-permute-start.3 = (bf16[32,1664]{1,0:T(8,128)(2,1)S(1)}, bf16[32,1664]{1,0:T(8,128)(2,1)S(1)}, u32[]{:S(2)}, u32[]{:S(2)}) collective-permute-start(bf16[32,1664]{1,0:T(8,128)(2,1)S(1)} %get-tuple-element.53), channel_id=1, source_target_pairs={{0,16},{4,20},{8,24},{12,28},{16,0},{20,4},{24,8},{28,12},{1,17},{... | collective-permute-start | bytes 319496 | tf_op jit(solution)/shard_map/ppermute | solution.py:36
  15.6 6.1 %collective-permute-start.4 = (bf16[32,1664]{1,0:T(8,128)(2,1)S(1)}, bf16[32,1664]{1,0:T(8,128)(2,1)S(1)}, u32[]{:S(2)}, u32[]{:S(2)}) collective-permute-start(bf16[32,1664]{1,0:T(8,128)(2,1)S(1)} %get-tuple-element.53), channel_id=1, source_target_pairs={{0,24},{4,28},{8,0},{12,4},{16,8},{20,12},{24,16},{28,20},{1,25},{... | collective-permute-start | bytes 319496 | tf_op jit(solution)/shard_map/ppermute | solution.py:36
  17.0 1.5 %copy-start.2 = (bf16[5,1536,128]{2,1,0:T(8,128)(2,1)S(1)}, bf16[5,1536,128]{2,1,0:T(8,128)(2,1)}, u32[]{:S(2)}) copy-start(bf16[5,1536,128]{2,1,0:T(8,128)(2,1)} %up_hbm.1) | copy-start | bytes 5898244
  18.5 1.5 %copy-start.3 = (bf16[5,128,1536]{2,1,0:T(8,128)(2,1)S(1)}, bf16[5,128,1536]{2,1,0:T(8,128)(2,1)}, u32[]{:S(2)}) copy-start(bf16[5,128,1536]{2,1,0:T(8,128)(2,1)} %param.23) | copy-start | bytes 5898244
  21.7 6.7 %collective-permute-start.6 = (bf16[64,1664]{1,0:T(8,128)(2,1)S(1)}, bf16[64,1664]{1,0:T(8,128)(2,1)S(1)}, u32[]{:S(2)}, u32[]{:S(2)}) collective-permute-start(bf16[64,1664]{1,0:T(8,128)(2,1)S(1)} %get-tuple-element.56), channel_id=1, source_target_pairs={{0,4},{4,0},{8,12},{12,8},{16,20},{20,16},{24,28},{28,24},{1,5},{5... | collective-permute-start | bytes 638984 | tf_op jit(solution)/shard_map/ppermute | solution.py:40
  23.5 5.9 %collective-permute-start.7 = (bf16[64,1664]{1,0:T(8,128)(2,1)S(1)}, bf16[64,1664]{1,0:T(8,128)(2,1)S(1)}, u32[]{:S(2)}, u32[]{:S(2)}) collective-permute-start(bf16[64,1664]{1,0:T(8,128)(2,1)S(1)} %get-tuple-element.57), channel_id=1, source_target_pairs={{0,2},{1,3},{2,0},{3,1},{4,6},{5,7},{6,4},{7,5},{8,10},{9,11},{10,... | collective-permute-start | bytes 638984 | tf_op jit(solution)/shard_map/ppermute | solution.py:44
  29.4 7.6 %collective-permute-start.18 = (bf16[32,1664]{1,0:T(8,128)(2,1)S(1)}, bf16[32,1664]{1,0:T(8,128)(2,1)S(1)}, u32[]{:S(2)}, u32[]{:S(2)}) collective-permute-start(bf16[32,1664]{1,0:T(8,128)(2,1)S(1)} %get-tuple-element.71), channel_id=1, source_target_pairs={{0,8},{4,12},{8,16},{12,20},{16,24},{20,28},{24,0},{28,4},{1,9},{5... | collective-permute-start | bytes 319496 | tf_op jit(solution)/shard_map/ppermute | solution.py:36
  32.3 8.0 %collective-permute-start.19 = (bf16[32,1664]{1,0:T(8,128)(2,1)S(1)}, bf16[32,1664]{1,0:T(8,128)(2,1)S(1)}, u32[]{:S(2)}, u32[]{:S(2)}) collective-permute-start(bf16[32,1664]{1,0:T(8,128)(2,1)S(1)} %get-tuple-element.71), channel_id=1, source_target_pairs={{0,16},{4,20},{8,24},{12,28},{16,0},{20,4},{24,8},{28,12},{1,17},{... | collective-permute-start | bytes 319496 | tf_op jit(solution)/shard_map/ppermute | solution.py:36
  33.4 7.0 %collective-permute-start.20 = (bf16[32,1664]{1,0:T(8,128)(2,1)S(1)}, bf16[32,1664]{1,0:T(8,128)(2,1)S(1)}, u32[]{:S(2)}, u32[]{:S(2)}) collective-permute-start(bf16[32,1664]{1,0:T(8,128)(2,1)S(1)} %get-tuple-element.71), channel_id=1, source_target_pairs={{0,24},{4,28},{8,0},{12,4},{16,8},{20,12},{24,16},{28,20},{1,25},{... | collective-permute-start | bytes 319496 | tf_op jit(solution)/shard_map/ppermute | solution.py:36
  34.8 13.2 %collective-permute-start.9 = (bf16[128,1664]{1,0:T(8,128)(2,1)S(1)}, bf16[128,1664]{1,0:T(8,128)(2,1)S(1)}, u32[]{:S(2)}, u32[]{:S(2)}) collective-permute-start(bf16[128,1664]{1,0:T(8,128)(2,1)S(1)} %pad_maximum_fusion.2), channel_id=1, source_target_pairs={{0,2},{1,3},{2,0},{3,1},{4,6},{5,7},{6,4},{7,5},{8,10},{9,11},{10,... | collective-permute-start | bytes 1277960 | tf_op jit(solution)/shard_map/ppermute | solution.py:44
  36.4 11.6 %collective-permute-start.10 = (bf16[128,1664]{1,0:T(8,128)(2,1)S(1)}, bf16[128,1664]{1,0:T(8,128)(2,1)S(1)}, u32[]{:S(2)}, u32[]{:S(2)}) collective-permute-start(bf16[128,1664]{1,0:T(8,128)(2,1)S(1)} %pad_maximum_fusion.3), channel_id=1, source_target_pairs={{0,4},{4,0},{8,12},{12,8},{16,20},{20,16},{24,28},{28,24},{1,5},{5... | collective-permute-start | bytes 1277960 | tf_op jit(solution)/shard_map/ppermute | solution.py:40
  37.0 15.2 %collective-permute-start.8 = (bf16[256,1664]{1,0:T(8,128)(2,1)S(1)}, bf16[256,1664]{1,0:T(8,128)(2,1)S(1)}, u32[]{:S(2)}, u32[]{:S(2)}) collective-permute-start(bf16[256,1664]{1,0:T(8,128)(2,1)S(1)} %pad_maximum_fusion.near_ref), channel_id=1, source_target_pairs={{0,1},{1,0},{2,3},{3,2},{4,5},{5,4},{6,7},{7,6},{8,9},{9,8},{10,11... | collective-permute-start | bytes 2555912 | tf_op jit(solution)/shard_map/ppermute | solution.py:48
  40.4 8.6 %collective-permute-start.22 = (bf16[64,1664]{1,0:T(8,128)(2,1)S(1)}, bf16[64,1664]{1,0:T(8,128)(2,1)S(1)}, u32[]{:S(2)}, u32[]{:S(2)}) collective-permute-start(bf16[64,1664]{1,0:T(8,128)(2,1)S(1)} %pad_maximum_fusion.9), channel_id=1, source_target_pairs={{0,2},{1,3},{2,0},{3,1},{4,6},{5,7},{6,4},{7,5},{8,10},{9,11},{10,... | collective-permute-start | bytes 638984 | tf_op jit(solution)/shard_map/ppermute | solution.py:44
  42.0 8.3 %collective-permute-start.21 = (bf16[64,1664]{1,0:T(8,128)(2,1)S(1)}, bf16[64,1664]{1,0:T(8,128)(2,1)S(1)}, u32[]{:S(2)}, u32[]{:S(2)}) collective-permute-start(bf16[64,1664]{1,0:T(8,128)(2,1)S(1)} %pad_maximum_fusion.8), channel_id=1, source_target_pairs={{0,4},{4,0},{8,12},{12,8},{16,20},{20,16},{24,28},{28,24},{1,5},{5... | collective-permute-start | bytes 638984 | tf_op jit(solution)/shard_map/ppermute | solution.py:40
  48.0 4.2 %collective-permute-start.11 = (bf16[256,1664]{1,0:T(8,128)(2,1)S(1)}, bf16[256,1664]{1,0:T(8,128)(2,1)S(1)}, u32[]{:S(2)}, u32[]{:S(2)}) collective-permute-start(bf16[256,1664]{1,0:T(8,128)(2,1)S(1)} %constant_dynamic-update-slice_fusion.far_ref), channel_id=1, source_target_pairs={{0,1},{1,0},{2,3},{3,2},{4,5},{5,4},{6,7},{7,6},{8,9},{9,8},{10,11... | collective-permute-start | bytes 2555912 | tf_op jit(solution)/shard_map/ppermute | solution.py:48
  50.3 10.2 %collective-permute-start.25 = (bf16[128,1664]{1,0:T(8,128)(2,1)S(1)}, bf16[128,1664]{1,0:T(8,128)(2,1)S(1)}, u32[]{:S(2)}, u32[]{:S(2)}) collective-permute-start(bf16[128,1664]{1,0:T(8,128)(2,1)S(1)} %pad_maximum_fusion.5), channel_id=1, source_target_pairs={{0,4},{4,0},{8,12},{12,8},{16,20},{20,16},{24,28},{28,24},{1,5},{5... | collective-permute-start | bytes 1277960 | tf_op jit(solution)/shard_map/ppermute | solution.py:40
  50.9 9.9 %collective-permute-start.24 = (bf16[128,1664]{1,0:T(8,128)(2,1)S(1)}, bf16[128,1664]{1,0:T(8,128)(2,1)S(1)}, u32[]{:S(2)}, u32[]{:S(2)}) collective-permute-start(bf16[128,1664]{1,0:T(8,128)(2,1)S(1)} %pad_maximum_fusion.4), channel_id=1, source_target_pairs={{0,2},{1,3},{2,0},{3,1},{4,6},{5,7},{6,4},{7,5},{8,10},{9,11},{10,... | collective-permute-start | bytes 1277960 | tf_op jit(solution)/shard_map/ppermute | solution.py:44
  52.1 11.7 %collective-permute-start.23 = (bf16[256,1664]{1,0:T(8,128)(2,1)S(1)}, bf16[256,1664]{1,0:T(8,128)(2,1)S(1)}, u32[]{:S(2)}, u32[]{:S(2)}) collective-permute-start(bf16[256,1664]{1,0:T(8,128)(2,1)S(1)} %pad_maximum_fusion.1.near_ref), channel_id=1, source_target_pairs={{0,1},{1,0},{2,3},{3,2},{4,5},{5,4},{6,7},{7,6},{8,9},{9,8},{10,11... | collective-permute-start | bytes 2555912 | tf_op jit(solution)/shard_map/ppermute | solution.py:48
  55.7 5.8 %collective-permute-start.13 = (bf16[256,1536]{1,0:T(8,128)(2,1)S(1)}, bf16[256,1536]{1,0:T(8,128)(2,1)S(1)}, u32[]{:S(2)}, u32[]{:S(2)}) collective-permute-start(bf16[256,1536]{1,0:T(8,128)(2,1)S(1)} %get-tuple-element.65), channel_id=1, source_target_pairs={{0,1},{1,0},{2,3},{3,2},{4,5},{5,4},{6,7},{7,6},{8,9},{9,8},{10,11... | collective-permute-start | bytes 2359304 | tf_op jit(solution)/shard_map/ppermute | solution.py:48
  60.9 2.9 %collective-permute-start.26 = (bf16[256,1664]{1,0:T(8,128)(2,1)S(1)}, bf16[256,1664]{1,0:T(8,128)(2,1)S(1)}, u32[]{:S(2)}, u32[]{:S(2)}) collective-permute-start(bf16[256,1664]{1,0:T(8,128)(2,1)S(1)} %constant_dynamic-update-slice_fusion.2.far_ref), channel_id=1, source_target_pairs={{0,1},{1,0},{2,3},{3,2},{4,5},{5,4},{6,7},{7,6},{8,9},{9,8},{10,11... | collective-permute-start | bytes 2555912 | tf_op jit(solution)/shard_map/ppermute | solution.py:48
  61.0 10.7 %collective-permute-start.12 = (bf16[256,1536]{1,0:T(8,128)(2,1)S(1)}, bf16[256,1536]{1,0:T(8,128)(2,1)S(1)}, u32[]{:S(2)}, u32[]{:S(2)}) collective-permute-start(bf16[256,1536]{1,0:T(8,128)(2,1)S(1)} %get-tuple-element.64), channel_id=1, source_target_pairs={{0,1},{1,0},{2,3},{3,2},{4,5},{5,4},{6,7},{7,6},{8,9},{9,8},{10,11... | collective-permute-start | bytes 2359304 | tf_op jit(solution)/shard_map/ppermute | solution.py:48
  61.7 11.2 %collective-permute-start.14 = (bf16[128,1536]{1,0:T(8,128)(2,1)S(1)}, bf16[128,1536]{1,0:T(8,128)(2,1)S(1)}, u32[]{:S(2)}, u32[]{:S(2)}) collective-permute-start(bf16[128,1536]{1,0:T(8,128)(2,1)S(1)} %get-tuple-element.121), channel_id=1, source_target_pairs={{0,2},{1,3},{2,0},{3,1},{4,6},{5,7},{6,4},{7,5},{8,10},{9,11},{10,... | collective-permute-start | bytes 1179656 | tf_op jit(solution)/shard_map/ppermute | solution.py:44
  62.8 4.6 %copy-start.8 = (bf16[1536]{0:T(1024)(128)(2,1)S(1)}, bf16[1536]{0:T(1024)(128)(2,1)}, u32[]{:S(2)}) copy-start(bf16[1536]{0:T(1024)(128)(2,1)} %param.16) | copy-start | bytes 9220
  62.8 10.8 %collective-permute-start.16 = (bf16[128,1536]{1,0:T(8,128)(2,1)S(1)}, bf16[128,1536]{1,0:T(8,128)(2,1)S(1)}, u32[]{:S(2)}, u32[]{:S(2)}) collective-permute-start(bf16[128,1536]{1,0:T(8,128)(2,1)S(1)} %get-tuple-element.122), channel_id=1, source_target_pairs={{0,4},{4,0},{8,12},{12,8},{16,20},{20,16},{24,28},{28,24},{1,5},{5... | collective-permute-start | bytes 1179656 | tf_op jit(solution)/shard_map/ppermute | solution.py:40
  67.4 8.9 %collective-permute-start.27 = (bf16[256,1536]{1,0:T(8,128)(2,1)S(1)}, bf16[256,1536]{1,0:T(8,128)(2,1)S(1)}, u32[]{:S(2)}, u32[]{:S(2)}) collective-permute-start(bf16[256,1536]{1,0:T(8,128)(2,1)S(1)} %get-tuple-element.79), channel_id=1, source_target_pairs={{0,1},{1,0},{2,3},{3,2},{4,5},{5,4},{6,7},{7,6},{8,9},{9,8},{10,11... | collective-permute-start | bytes 2359304 | tf_op jit(solution)/shard_map/ppermute | solution.py:48
  67.5 17.8 %collective-permute-start.31 = (bf16[256,1536]{1,0:T(8,128)(2,1)S(1)}, bf16[256,1536]{1,0:T(8,128)(2,1)S(1)}, u32[]{:S(2)}, u32[]{:S(2)}) collective-permute-start(bf16[256,1536]{1,0:T(8,128)(2,1)S(1)} %get-tuple-element.78), channel_id=1, source_target_pairs={{0,1},{1,0},{2,3},{3,2},{4,5},{5,4},{6,7},{7,6},{8,9},{9,8},{10,11... | collective-permute-start | bytes 2359304 | tf_op jit(solution)/shard_map/ppermute | solution.py:48
  73.8 7.6 %collective-permute-start.15 = (bf16[64,1536]{1,0:T(8,128)(2,1)S(1)}, bf16[64,1536]{1,0:T(8,128)(2,1)S(1)}, u32[]{:S(2)}, u32[]{:S(2)}) collective-permute-start(bf16[64,1536]{1,0:T(8,128)(2,1)S(1)} %get-tuple-element.120), channel_id=1, source_target_pairs={{0,4},{4,0},{8,12},{12,8},{16,20},{20,16},{24,28},{28,24},{1,5},{5... | collective-permute-start | bytes 589832 | tf_op jit(solution)/shard_map/ppermute | solution.py:40
  74.9 7.8 %collective-permute-start.17 = (bf16[64,1536]{1,0:T(8,128)(2,1)S(1)}, bf16[64,1536]{1,0:T(8,128)(2,1)S(1)}, u32[]{:S(2)}, u32[]{:S(2)}) collective-permute-start(bf16[64,1536]{1,0:T(8,128)(2,1)S(1)} %get-tuple-element.119), channel_id=1, source_target_pairs={{0,2},{1,3},{2,0},{3,1},{4,6},{5,7},{6,4},{7,5},{8,10},{9,11},{10,... | collective-permute-start | bytes 589832 | tf_op jit(solution)/shard_map/ppermute | solution.py:44
  76.5 12.3 %collective-permute-start.32 = (bf16[128,1536]{1,0:T(8,128)(2,1)S(1)}, bf16[128,1536]{1,0:T(8,128)(2,1)S(1)}, u32[]{:S(2)}, u32[]{:S(2)}) collective-permute-start(bf16[128,1536]{1,0:T(8,128)(2,1)S(1)} %get-tuple-element.118), channel_id=1, source_target_pairs={{0,2},{1,3},{2,0},{3,1},{4,6},{5,7},{6,4},{7,5},{8,10},{9,11},{10,... | collective-permute-start | bytes 1179656 | tf_op jit(solution)/shard_map/ppermute | solution.py:44
  77.2 11.6 %collective-permute-start.33 = (bf16[128,1536]{1,0:T(8,128)(2,1)S(1)}, bf16[128,1536]{1,0:T(8,128)(2,1)S(1)}, u32[]{:S(2)}, u32[]{:S(2)}) collective-permute-start(bf16[128,1536]{1,0:T(8,128)(2,1)S(1)} %get-tuple-element.117), channel_id=1, source_target_pairs={{0,4},{4,0},{8,12},{12,8},{16,20},{20,16},{24,28},{28,24},{1,5},{5... | collective-permute-start | bytes 1179656 | tf_op jit(solution)/shard_map/ppermute | solution.py:40
  82.9 8.0 %collective-permute-start.30 = (bf16[32,1536]{1,0:T(8,128)(2,1)S(1)}, bf16[32,1536]{1,0:T(8,128)(2,1)S(1)}, u32[]{:S(2)}, u32[]{:S(2)}) collective-permute-start(bf16[32,1536]{1,0:T(8,128)(2,1)S(1)} %pad_maximum_fusion.12), channel_id=1, source_target_pairs={{0,8},{4,12},{8,16},{12,20},{16,24},{20,28},{24,0},{28,4},{1,9},{5... | collective-permute-start | bytes 294920 | tf_op jit(solution)/shard_map/ppermute | solution.py:36
  83.0 7.9 %collective-permute-start.29 = (bf16[32,1536]{1,0:T(8,128)(2,1)S(1)}, bf16[32,1536]{1,0:T(8,128)(2,1)S(1)}, u32[]{:S(2)}, u32[]{:S(2)}) collective-permute-start(bf16[32,1536]{1,0:T(8,128)(2,1)S(1)} %pad_maximum_fusion.11), channel_id=1, source_target_pairs={{0,16},{4,20},{8,24},{12,28},{16,0},{20,4},{24,8},{28,12},{1,17},{... | collective-permute-start | bytes 294920 | tf_op jit(solution)/shard_map/ppermute | solution.py:36
  85.3 5.6 %collective-permute-start.28 = (bf16[32,1536]{1,0:T(8,128)(2,1)S(1)}, bf16[32,1536]{1,0:T(8,128)(2,1)S(1)}, u32[]{:S(2)}, u32[]{:S(2)}) collective-permute-start(bf16[32,1536]{1,0:T(8,128)(2,1)S(1)} %pad_maximum_fusion.10), channel_id=1, source_target_pairs={{0,24},{4,28},{8,0},{12,4},{16,8},{20,12},{24,16},{28,20},{1,25},{... | collective-permute-start | bytes 294920 | tf_op jit(solution)/shard_map/ppermute | solution.py:36
  88.9 5.7 %collective-permute-start.37 = (bf16[64,1536]{1,0:T(8,128)(2,1)S(1)}, bf16[64,1536]{1,0:T(8,128)(2,1)S(1)}, u32[]{:S(2)}, u32[]{:S(2)}) collective-permute-start(bf16[64,1536]{1,0:T(8,128)(2,1)S(1)} %get-tuple-element.116), channel_id=1, source_target_pairs={{0,4},{4,0},{8,12},{12,8},{16,20},{20,16},{24,28},{28,24},{1,5},{5... | collective-permute-start | bytes 589832 | tf_op jit(solution)/shard_map/ppermute | solution.py:40
  90.0 5.7 %collective-permute-start.38 = (bf16[64,1536]{1,0:T(8,128)(2,1)S(1)}, bf16[64,1536]{1,0:T(8,128)(2,1)S(1)}, u32[]{:S(2)}, u32[]{:S(2)}) collective-permute-start(bf16[64,1536]{1,0:T(8,128)(2,1)S(1)} %get-tuple-element.115), channel_id=1, source_target_pairs={{0,2},{1,3},{2,0},{3,1},{4,6},{5,7},{6,4},{7,5},{8,10},{9,11},{10,... | collective-permute-start | bytes 589832 | tf_op jit(solution)/shard_map/ppermute | solution.py:44
  95.7 6.6 %collective-permute-start.41 = (bf16[32,1536]{1,0:T(8,128)(2,1)S(1)}, bf16[32,1536]{1,0:T(8,128)(2,1)S(1)}, u32[]{:S(2)}, u32[]{:S(2)}) collective-permute-start(bf16[32,1536]{1,0:T(8,128)(2,1)S(1)} %pad_maximum_fusion.15), channel_id=1, source_target_pairs={{0,8},{4,12},{8,16},{12,20},{16,24},{20,28},{24,0},{28,4},{1,9},{5... | collective-permute-start | bytes 294920 | tf_op jit(solution)/shard_map/ppermute | solution.py:36
  95.8 7.7 %collective-permute-start.40 = (bf16[32,1536]{1,0:T(8,128)(2,1)S(1)}, bf16[32,1536]{1,0:T(8,128)(2,1)S(1)}, u32[]{:S(2)}, u32[]{:S(2)}) collective-permute-start(bf16[32,1536]{1,0:T(8,128)(2,1)S(1)} %pad_maximum_fusion.14), channel_id=1, source_target_pairs={{0,16},{4,20},{8,24},{12,28},{16,0},{20,4},{24,8},{28,12},{1,17},{... | collective-permute-start | bytes 294920 | tf_op jit(solution)/shard_map/ppermute | solution.py:36
  98.1 5.4 %collective-permute-start.39 = (bf16[32,1536]{1,0:T(8,128)(2,1)S(1)}, bf16[32,1536]{1,0:T(8,128)(2,1)S(1)}, u32[]{:S(2)}, u32[]{:S(2)}) collective-permute-start(bf16[32,1536]{1,0:T(8,128)(2,1)S(1)} %pad_maximum_fusion.13), channel_id=1, source_target_pairs={{0,24},{4,28},{8,0},{12,4},{16,8},{20,12},{24,16},{28,20},{1,25},{... | collective-permute-start | bytes 294920 | tf_op jit(solution)/shard_map/ppermute | solution.py:36
  99.9 10.4 %collective-permute-start.34 = (bf16[32,1536]{1,0:T(8,128)(2,1)S(1)}, bf16[32,1536]{1,0:T(8,128)(2,1)S(1)}, u32[]{:S(2)}, u32[]{:S(2)}) collective-permute-start(bf16[32,1536]{1,0:T(8,128)(2,1)S(1)} %multiply_convert_fusion.1.refs_0_), channel_id=1, source_target_pairs={{0,1},{1,0},{2,3},{3,2},{4,5},{5,4},{6,7},{7,6},{8,9},{9,8},{10,11... | collective-permute-start | bytes 294920 | tf_op jit(solution)/shard_map/ppermute | solution.py:48
  99.9 10.3 %collective-permute-start.35 = (bf16[32,1536]{1,0:T(8,128)(2,1)S(1)}, bf16[32,1536]{1,0:T(8,128)(2,1)S(1)}, u32[]{:S(2)}, u32[]{:S(2)}) collective-permute-start(bf16[32,1536]{1,0:T(8,128)(2,1)S(1)} %multiply_convert_fusion.1.refs_0_), channel_id=1, source_target_pairs={{0,2},{1,3},{2,0},{3,1},{4,6},{5,7},{6,4},{7,5},{8,10},{9,11},{10,... | collective-permute-start | bytes 294920 | tf_op jit(solution)/shard_map/ppermute | solution.py:44
  102.4 7.9 %collective-permute-start.36 = (bf16[32,1536]{1,0:T(8,128)(2,1)S(1)}, bf16[32,1536]{1,0:T(8,128)(2,1)S(1)}, u32[]{:S(2)}, u32[]{:S(2)}) collective-permute-start(bf16[32,1536]{1,0:T(8,128)(2,1)S(1)} %multiply_convert_fusion.1.refs_0_), channel_id=1, source_target_pairs={{0,3},{1,2},{2,1},{3,0},{4,7},{5,6},{6,5},{7,4},{8,11},{9,10},{10,... | collective-permute-start | bytes 294920 | tf_op jit(solution)/shard_map/ppermute | solution.py:343
